TPU v7x, 32 devices: a whole 2x2x4 slice. The times are simulated.
32 devices in a mesh: pos: 4 (over y, x), slab: 8 (over z, core).
Axes of the slice: x: 2, y: 2, z: 4, core: 2. Of those that a mesh axis runs over, the one named last changes fastest.
Arguments:
- labels: int32 [16, 256, 256], P('slab'), may hold values from 0 to 3
- magnet_mask: int32 [16, 256, 256], P('slab'), may hold values 0 or 1
- reluctivity: float32 [4], replicated, may hold values from 0.3 to 3
- rotor_shift: int32 [4], P('pos'), may hold values from 0 to 255
- potential: float32 [4, 16, 256, 256], P('pos', 'slab'), may hold values from -6 to 6
- adjoint_load: float32 [4, 16, 256, 256], P('pos', 'slab'), may hold values from -40 to 40
Outputs:
- shape_gradient: float32 [16, 256, 256], P('slab')
- adjoint: float32 [4, 16, 256, 256], P('pos', 'slab')
All inputs are finite; a program needn't handle non-finite values. No bound on the sum of `magnet_mask` on one device may be relied on, other than what follows from the above.
Results may differ from a plain program's by a relative error of at most 0.0003.
Values sent between devices are 32-bit elements; how exact they have to be, the bound alone decides.
No kernel may reach another device: no remote copies, remote signals or barrier semaphores. Data moves between devices by JAX's collectives and lax.ppermute only.
A program may use at most 64 MiB of HBM per device.

v0:
```python
import jax
import jax.numpy as jnp
from jax import lax
from jax.sharding import PartitionSpec as P

ITERS = 2


diagonal_shift = 0.5


def padded(shard, sides, width):
    for axis, dim in sides:
        size, length = (lax.axis_size(axis), shard.shape[dim])
        up = [(i, (i + 1) % size) for i in range(size - 1)]
        down = [(j, i) for i, j in up]
        last = lax.slice_in_dim(shard, length - width, length, axis=dim)
        first = lax.slice_in_dim(shard, 0, width, axis=dim)
        before = lax.ppermute(last, axis, up)
        after = lax.ppermute(first, axis, down)
        shard = jnp.concatenate([before, shard, after], axis=dim)
    return shard


def material_field(labels, reluctivity, offset):
    rotated = jnp.roll(labels, offset, axis=2)
    radial = lax.broadcasted_iota(jnp.int32, labels.shape, 1)
    material = jnp.where(radial < labels.shape[1] // 2, rotated, labels)
    result = jnp.zeros(labels.shape, jnp.float32)
    for index in range(4):
        result = result + (material == index).astype(jnp.float32) * reluctivity[index]
    return result


def apply_operator(field, padded_field, relief, padded_relief):
    result = diagonal_shift * field
    result = result + 0.5 * (relief + padded_relief[2:]) * (field - padded_field[2:])
    result = result + 0.5 * (relief + padded_relief[:-2]) * (field - padded_field[:-2])
    radial_field = jnp.pad(field, ((0, 0), (1, 1), (0, 0)))
    radial_relief = jnp.pad(relief, ((0, 0), (1, 1), (0, 0)))
    result = result + 0.5 * (relief + radial_relief[:, 2:]) * (field - radial_field[:, 2:])
    result = result + 0.5 * (relief + radial_relief[:, :-2]) * (field - radial_field[:, :-2])
    for offset in (1, -1):
        result = result + 0.5 * (relief + jnp.roll(relief, offset, 2)) * (
            field - jnp.roll(field, offset, 2)
        )
    return result


def gradient_term(stacked, padded_stack, relief, magnet_mask):
    axial = 0.5 * (padded_stack[:, 2:] - padded_stack[:, :-2])
    radial_pad = jnp.pad(stacked, ((0, 0), (0, 0), (1, 1), (0, 0)))
    radial = 0.5 * (radial_pad[:, :, 2:] - radial_pad[:, :, :-2])
    angular = 0.5 * (jnp.roll(stacked, -1, 3) - jnp.roll(stacked, 1, 3))
    inner = axial[0] * axial[1] + radial[0] * radial[1] + angular[0] * angular[1]
    square = axial[0] * axial[0] + radial[0] * radial[0] + angular[0] * angular[0]
    return magnet_mask.astype(jnp.float32) * relief * (inner + 0.5 * square)


def squares(residual):
    return lax.psum(jnp.sum(residual * residual), "slab")


def local(labels, magnet_mask, reluctivity, rotor_shift, potential, adjoint_load):
    relief = material_field(labels, reluctivity, rotor_shift[0])
    padded_relief = padded(relief, (("slab", 0),), 1)
    solution = jnp.zeros(relief.shape, jnp.float32)
    residual = adjoint_load[0]
    direction = residual
    norm_now = squares(residual)
    for iteration in range(ITERS):
        padded_field = padded(direction, (("slab", 0),), 1)
        image = apply_operator(direction, padded_field, relief, padded_relief)
        alpha = norm_now / lax.psum(jnp.sum(direction * image), "slab")
        solution = solution + alpha * direction
        residual = residual - alpha * image
        norm_next = squares(residual)
        direction = residual + norm_next / norm_now * direction
        norm_now = norm_next
    stacked = jnp.stack([potential[0], solution])
    padded_stack = padded(stacked, (("slab", 1),), 1)
    contribution = gradient_term(stacked, padded_stack, relief, magnet_mask)
    summed = lax.psum(contribution, "pos")
    return (summed / lax.axis_size("pos"), solution[None])


def solution(mesh):
    return jax.shard_map(
        local,
        mesh=mesh,
        in_specs=(
            P("slab", None, None),
            P("slab", None, None),
            P(),
            P("pos"),
            P("pos", "slab", None, None),
            P("pos", "slab", None, None),
        ),
        out_specs=(P("slab", None, None), P("pos", "slab", None, None)),
        check_vma=False,
    )
```

profile of v0, /device:TPU:0, one launch (start us, length us, event | category | flops | bytes accessed | tf_op | source)
XLA Modules:
  0.0 160.0 jit_solution(3972374283325124673)
XLA Ops:
  7.2 1.1 slice_bitcast_fusion.1
  8.3 3.1 %collective-permute-start.3 = (f32[1,256,256]{2,1,0:T(8,128)S(1)}, f32[1,256,256]{2,1,0:T(8,128)}, u32[]{:S(2)}, u32[]{:S(2)}) collective-permute-start(f32[1,256,256]{2,1,0:T(8,128)S(1)} %get-tuple-element.24), channel_id=1, source_target_pairs={{0,1},{1,2},{2,3},{3,4},{4,5},{5,6},{6,7},{8,9},{9,10},{10,11},{11... | collective-permute-start | bytes 786440 | tf_op jit(solution)/shard_map/ppermute | solution.py:19
  12.1 0.7 fusion.57
  12.8 3.0 %select_add_fusion = f32[2,256,256]{2,1,0:T(8,128)S(1)} fusion(s32[2,256,256]{2,1,0:T(8,128)S(1)} %copy-done.3, s32[]{:T(128)S(6)} %select_n.18, f32[]{:T(128)} %bitcast.4, f32[]{:T(128)} %bitcast.3, f32[]{:T(128)} %bitcast.2, f32[]{:T(128)} %bitcast.1, pred[256]{0:T(512)(128)(4,1)S(1)} %iota_compare_fusion), kind=kLoop, calls=%fused_computation.91 | loop fusion | flops 1703936 | bytes 1048852 | tf_op jit(solution)/shard_map/add | solution.py:31
  15.9 3.9 %collective-permute-start.2 = (f32[1,256,256]{2,1,0:T(8,128)S(1)}, f32[1,256,256]{2,1,0:T(8,128)S(1)}, u32[]{:S(2)}, u32[]{:S(2)}) collective-permute-start(f32[1,256,256]{2,1,0:T(8,128)S(1)} %get-tuple-element.22), channel_id=1, source_target_pairs={{0,1},{1,2},{2,3},{3,4},{4,5},{5,6},{6,7},{8,9},{9,10},{10,11},{11... | collective-permute-start | bytes 786440 | tf_op jit(solution)/shard_map/ppermute | solution.py:19
  19.8 1.3 collective-permute-start.1
  21.1 1.3 collective-permute-start
  23.2 1.9 %collective-permute-done = f32[1,256,256]{2,1,0:T(8,128)S(1)} collective-permute-done((f32[1,256,256]{2,1,0:T(8,128)S(1)}, f32[1,256,256]{2,1,0:T(8,128)S(1)}, u32[]{:S(2)}, u32[]{:S(2)}) %collective-permute-start) | collective-permute-done | bytes 262176 | tf_op jit(solution)/shard_map/ppermute | solution.py:20
  25.1 2.6 %multiply_reduce_fusion.1 = (f32[]{:T(128)}, f32[]{:T(128)}, f32[2,256,256]{2,1,0:T(8,128)S(1)}) fusion(f32[1,2,256,256]{3,2,1,0:T(8,128)S(1)} %copy-done, f32[2,256,256]{2,1,0:T(8,128)S(1)} %bitcast.26, f32[2,256,1]{2,1,0:T(8,128)S(1)} %get-tuple-element.37, f32[2,256,255]{2,1,0:T(8,128)S(1)} %get-tuple-element.39, f32[2,256,256]{2,1,0:T(8,128)S(1)} %select_add_fusion, ...), kind=kLoop, calls=%fused_computation.87 | loop fusion | flops 5636094 | bytes 5242888 | tf_op jit(solution)/shard_map/reduce_sum | solution.py:74
  27.7 19.4 %all-reduce.4 = (f32[]{:T(128)}, f32[]{:T(128)}) all-reduce(f32[]{:T(128)} %get-tuple-element.3, f32[]{:T(128)} %get-tuple-element.2), channel_id=1, replica_groups=mesh['pos'=4,'slab'=8] {'slab'}, use_global_device_ids=true, to_apply=%region_1.2 | all-reduce | flops 2 | bytes 16 | tf_op jit(solution)/shard_map/psum | solution.py:61
  48.4 0.7 multiply_reduce_fusion
  49.2 14.2 %psum.37 = f32[]{:T(128)} all-reduce(f32[]{:T(128)} %multiply_reduce_fusion), channel_id=1, replica_groups=mesh['pos'=4,'slab'=8] {'slab'}, use_global_device_ids=true, to_apply=%region_5.6 | all-reduce | flops 1 | bytes 8 | tf_op jit(solution)/shard_map/psum | solution.py:61
  64.9 1.8 %collective-permute-start.5 = (f32[1,256,256]{2,1,0:T(8,128)S(1)}, f32[1,256,256]{2,1,0:T(8,128)S(1)}, u32[]{:S(2)}, u32[]{:S(2)}) collective-permute-start(f32[1,256,256]{2,1,0:T(8,128)S(1)} %get-tuple-element.16), channel_id=1, source_target_pairs={{0,1},{1,2},{2,3},{3,4},{4,5},{5,6},{6,7},{8,9},{9,10},{10,11},{11... | collective-permute-start | bytes 786440 | tf_op jit(solution)/shard_map/ppermute | solution.py:19
  66.8 1.4 collective-permute-start.4
  68.4 1.9 %collective-permute-done.4 = f32[1,256,256]{2,1,0:T(8,128)S(1)} collective-permute-done((f32[1,256,256]{2,1,0:T(8,128)S(1)}, f32[1,256,256]{2,1,0:T(8,128)S(1)}, u32[]{:S(2)}, u32[]{:S(2)}) %collective-permute-start.4) | collective-permute-done | bytes 262176 | tf_op jit(solution)/shard_map/ppermute | solution.py:20
  70.3 1.5 fusion.47
  71.8 18.5 %psum.38 = f32[]{:T(128)} all-reduce(f32[]{:T(128)} %fusion.47), channel_id=1, replica_groups=mesh['pos'=4,'slab'=8] {'slab'}, use_global_device_ids=true, to_apply=%region_7.8 | all-reduce | flops 1 | bytes 8 | tf_op jit(solution)/shard_map/psum | solution.py:74
  91.9 1.3 collective-permute-start.7
  93.2 1.3 collective-permute-start.6
  95.5 1.5 collective-permute-done.6
  97.5 0.8 copy-done.4
  98.4 4.0 %fusion.14 = f32[2,256,256]{2,1,0:T(8,128)} fusion(f32[2,2,256,256]{3,2,1,0:T(8,128)S(1)} %fusion.4, f32[2,2,256,256]{3,2,1,0:T(8,128)S(1)} %subtract_multiply_fusion, f32[2,2,256,256]{3,2,1,0:T(8,128)S(1)} %get-tuple-element.7, s32[2,256,256]{2,1,0:T(8,128)S(1)} %copy-done.7, f32[]{:T(128)} %bitcast.4, f32[]{:T(128)} %bitcast.3, f32[]{:T(128)} %bitcast.2, ...), kind=kLoop, calls=%fused_computation.36 | loop fusion | flops 3670016 | bytes 4718868 | tf_op jit(solution)/shard_map/mul | solution.py:57
  102.4 48.9 %all-reduce.7.cloned.1.call-done = f32[2,256,256]{2,1,0:T(8,128)} async-done(((f32[2,256,256]{2,1,0:T(8,128)}), f32[2,256,256]{2,1,0:T(8,128)}) %all-reduce.7.cloned.1.call-update) | async-done | bytes 524304 | tf_op jit(solution)/shard_map/psum | solution.py:83
  151.3 1.9 %broadcast_multiply_fusion = f32[2,256,256]{2,1,0:T(8,128)} fusion(f32[2,256,256]{2,1,0:T(8,128)} %all-reduce.7.cloned.1.call-done), kind=kLoop, calls=%fused_computation.93 | loop fusion | flops 131072 | bytes 1048576 | tf_op jit(solution)/shard_map/div | solution.py:84
  (39 shorter events, 3.2 us)
Async XLA Ops:
  7.2 5.0 %copy-start.8 = (f32[4]{0:T(128)S(1)}, f32[4]{0:T(128)}, u32[]{:S(2)}) copy-start(f32[4]{0:T(128)} %param.8) | copy-start | bytes 52
  7.2 5.6 %copy-start.3 = (s32[2,256,256]{2,1,0:T(8,128)S(1)}, s32[2,256,256]{2,1,0:T(8,128)}, u32[]{:S(2)}) copy-start(s32[2,256,256]{2,1,0:T(8,128)} %param.6) | copy-start | bytes 1572868
  7.2 144.1 %all-reduce.7.cloned.1.call-start = ((), (), s32[]{:S(2)}) async-start(), calls=%async_computation | async-start | bytes 1048576 | tf_op jit(solution)/shard_map/psum | solution.py:83
  8.3 14.6 %collective-permute-start.3 = (f32[1,256,256]{2,1,0:T(8,128)S(1)}, f32[1,256,256]{2,1,0:T(8,128)}, u32[]{:S(2)}, u32[]{:S(2)}) collective-permute-start(f32[1,256,256]{2,1,0:T(8,128)S(1)} %get-tuple-element.24), channel_id=1, source_target_pairs={{0,1},{1,2},{2,3},{3,4},{4,5},{5,6},{6,7},{8,9},{9,10},{10,11},{11... | collective-permute-start | bytes 786440 | tf_op jit(solution)/shard_map/ppermute | solution.py:19
  12.8 9.6 %copy-start = (f32[1,2,256,256]{3,2,1,0:T(8,128)S(1)}, f32[1,2,256,256]{3,2,1,0:T(8,128)}, u32[]{:S(2)}) copy-start(f32[1,2,256,256]{3,2,1,0:T(8,128)} %param.11) | copy-start | bytes 1572868
  15.9 7.1 %collective-permute-start.2 = (f32[1,256,256]{2,1,0:T(8,128)S(1)}, f32[1,256,256]{2,1,0:T(8,128)S(1)}, u32[]{:S(2)}, u32[]{:S(2)}) collective-permute-start(f32[1,256,256]{2,1,0:T(8,128)S(1)} %get-tuple-element.22), channel_id=1, source_target_pairs={{0,1},{1,2},{2,3},{3,4},{4,5},{5,6},{6,7},{8,9},{9,10},{10,11},{11... | collective-permute-start | bytes 786440 | tf_op jit(solution)/shard_map/ppermute | solution.py:19
  19.8 3.4 %collective-permute-start.1 = (f32[1,256,256]{2,1,0:T(8,128)S(1)}, f32[1,256,256]{2,1,0:T(8,128)S(1)}, u32[]{:S(2)}, u32[]{:S(2)}) collective-permute-start(f32[1,256,256]{2,1,0:T(8,128)S(1)} %get-tuple-element.23), channel_id=1, source_target_pairs={{1,0},{2,1},{3,2},{4,3},{5,4},{6,5},{7,6},{9,8},{10,9},{11,10},{12... | collective-permute-start | bytes 786440 | tf_op jit(solution)/shard_map/ppermute | solution.py:20
  21.1 4.1 %collective-permute-start = (f32[1,256,256]{2,1,0:T(8,128)S(1)}, f32[1,256,256]{2,1,0:T(8,128)S(1)}, u32[]{:S(2)}, u32[]{:S(2)}) collective-permute-start(f32[1,256,256]{2,1,0:T(8,128)S(1)} %get-tuple-element.21), channel_id=1, source_target_pairs={{1,0},{2,1},{3,2},{4,3},{5,4},{6,5},{7,6},{9,8},{10,9},{11,10},{12... | collective-permute-start | bytes 786440 | tf_op jit(solution)/shard_map/ppermute | solution.py:20
  25.1 2.6 %copy-start.5 = (f32[1,256,256]{2,1,0:T(8,128)}, f32[1,256,256]{2,1,0:T(8,128)S(1)}, u32[]{:S(2)}) copy-start(f32[1,256,256]{2,1,0:T(8,128)S(1)} %collective-permute-done) | copy-start | bytes 786436
  64.9 3.5 %collective-permute-start.5 = (f32[1,256,256]{2,1,0:T(8,128)S(1)}, f32[1,256,256]{2,1,0:T(8,128)S(1)}, u32[]{:S(2)}, u32[]{:S(2)}) collective-permute-start(f32[1,256,256]{2,1,0:T(8,128)S(1)} %get-tuple-element.16), channel_id=1, source_target_pairs={{0,1},{1,2},{2,3},{3,4},{4,5},{5,6},{6,7},{8,9},{9,10},{10,11},{11... | collective-permute-start | bytes 786440 | tf_op jit(solution)/shard_map/ppermute | solution.py:19
  66.8 3.6 %copy-start.6 = (f32[1,256,256]{2,1,0:T(8,128)S(1)}, f32[1,256,256]{2,1,0:T(8,128)}, u32[]{:S(2)}) copy-start(f32[1,256,256]{2,1,0:T(8,128)} %copy-done.5) | copy-start | bytes 786436
  66.8 3.6 %collective-permute-start.4 = (f32[1,256,256]{2,1,0:T(8,128)S(1)}, f32[1,256,256]{2,1,0:T(8,128)S(1)}, u32[]{:S(2)}, u32[]{:S(2)}) collective-permute-start(f32[1,256,256]{2,1,0:T(8,128)S(1)} %get-tuple-element.15), channel_id=1, source_target_pairs={{1,0},{2,1},{3,2},{4,3},{5,4},{6,5},{7,6},{9,8},{10,9},{11,10},{12... | collective-permute-start | bytes 786440 | tf_op jit(solution)/shard_map/ppermute | solution.py:20
  71.8 19.9 %copy-start.2 = (f32[1,2,256,256]{3,2,1,0:T(8,128)S(1)}, f32[1,2,256,256]{3,2,1,0:T(8,128)}, u32[]{:S(2)}) copy-start(f32[1,2,256,256]{3,2,1,0:T(8,128)} %param.10) | copy-start | bytes 1572868
  91.8 5.2 %copy-start.1 = (f32[1,2,256,256]{3,2,1,0:T(8,128)}, f32[1,2,256,256]{3,2,1,0:T(8,128)S(1)}, u32[]{:S(2)}) copy-start(f32[1,2,256,256]{3,2,1,0:T(8,128)S(1)} %add_bitcast_fusion) | copy-start | bytes 1572868
  91.9 3.7 %collective-permute-start.7 = (f32[2,1,256,256]{3,2,1,0:T(8,128)S(1)}, f32[2,1,256,256]{3,2,1,0:T(8,128)S(1)}, u32[]{:S(2)}, u32[]{:S(2)}) collective-permute-start(f32[2,1,256,256]{3,2,1,0:T(8,128)S(1)} %get-tuple-element.10), channel_id=1, source_target_pairs={{0,1},{1,2},{2,3},{3,4},{4,5},{5,6},{6,7},{8,9},{9,10},{10,11},{11... | collective-permute-start | bytes 1572872 | tf_op jit(solution)/shard_map/ppermute | solution.py:19
  93.2 3.8 %collective-permute-start.6 = (f32[2,1,256,256]{3,2,1,0:T(8,128)S(1)}, f32[2,1,256,256]{3,2,1,0:T(8,128)S(1)}, u32[]{:S(2)}, u32[]{:S(2)}) collective-permute-start(f32[2,1,256,256]{3,2,1,0:T(8,128)S(1)} %get-tuple-element.9), channel_id=1, source_target_pairs={{1,0},{2,1},{3,2},{4,3},{5,4},{6,5},{7,6},{9,8},{10,9},{11,10},{12... | collective-permute-start | bytes 1572872 | tf_op jit(solution)/shard_map/ppermute | solution.py:20
  97.2 1.0 copy-start.4
  97.2 1.2 copy-start.7
Sparse Core Ops, SparseCore 0:
  102.6 48.6 all-reduce.6
where the time goes:
time: 161 us; the launch traced here: 160 us
  waiting for transfers between devices  54.4 us (34%)
  blocking collectives  52 us (32%)
  between operations  18.9 us (12%)
  starting transfers between devices  15.4 us (10%)
  other arithmetic  15.4 us (10%)
  local copies, waits for them, and re-layouts  3.74 us (2%)
    psum x1, waiting for transfers between devices, local(): summed = lax.psum(contribution, 'pos')  48.9 us
    psum x2, blocking collectives, squares(): return lax.psum(jnp.sum(residual * residual), 'slab')  33.6 us
    psum x1, blocking collectives, local(): alpha = norm_now / lax.psum(jnp.sum(direction * image), 'slab')  18.5 us
    ppermute x4, starting transfers between devices, padded(): before = lax.ppermute(last, axis, up)  10.1 us
    ppermute x4, waiting for transfers between devices, padded(): after = lax.ppermute(first, axis, down)  5.56 us
    ppermute x4, starting transfers between devices, padded(): after = lax.ppermute(first, axis, down)  5.3 us
    reduce_sum x2, other arithmetic, local(): alpha = norm_now / lax.psum(jnp.sum(direction * image), 'slab')  4.07 us
    mul x1, other arithmetic, gradient_term(): return magnet_mask.astype(jnp.float32) * relief * (inner + 0.5 * square)  3.97 us
  transfers between devices with their start and end apart: 9, of which 5 were waited for; matrix products, arithmetic and copies ran while one was open for 3% of the time, Pallas kernels for 0%

commit v1 on v0

v1 whole, which is shorter than its diff:
```python
import functools

import jax
import jax.numpy as jnp
from jax import lax
from jax.experimental import pallas as pl
from jax.experimental.pallas import tpu as pltpu
from jax.sharding import PartitionSpec as P


ROWS = 16
VMEM = pltpu.VMEM
SMEM = pltpu.SMEM
SUMS = 5


def params(**kw):
    return pltpu.CompilerParams(vmem_limit_bytes=40 * 1024 * 1024, **kw)


def shifted(ref, index, start, offset):
    total, columns = ref.shape[-2:]
    zero = jnp.zeros((1, columns), jnp.float32)
    if start + offset < 0:
        return jnp.concatenate([zero, ref[index, 0 : ROWS - 1, :]], axis=0)
    if start + offset + ROWS > total:
        return jnp.concatenate([ref[index, start + 1 : total, :], zero], axis=0)
    return ref[index, start + offset : start + offset + ROWS, :]


def turn(value, offset):
    return pltpu.roll(value, offset % value.shape[1], 1)


def in_plane(nu_ref, nu_index, ref, index, start):
    nu = nu_ref[nu_index, start : start + ROWS, :]
    v = ref[index, start : start + ROWS, :]
    flux = (nu + turn(nu, -1)) * (v - turn(v, -1))
    total = flux - turn(flux, 1)
    for offset in (-1, 1):
        total = total + (nu + shifted(nu_ref, nu_index, start, offset)) * (
            v - shifted(ref, index, start, offset)
        )
    return nu, v, total


def place():
    slab = lax.axis_index("slab")
    return slab, lax.rem(slab, 2)


def open_kernel(reluctivity, shift, labels, load, potential, far, near, far_potential):
    _, even = place()
    total = labels.shape[1]
    r0, r1, r2, r3 = (reluctivity[i] for i in range(4))
    offset = shift[0]
    for layer, out in ((even, far), (1 - even, near)):
        for start in range(0, total, ROWS):
            rows = slice(start, start + ROWS)
            material = labels[layer, rows, :]
            if start < total // 2:
                material = pltpu.roll(material, offset, 1)
            out[0, rows, :] = jnp.where(
                material < 2,
                jnp.where(material == 0, r0, r1),
                jnp.where(material == 2, r2, r3),
            )
            out[1, rows, :] = load[layer, rows, :]
            moved = potential[layer, rows, :]
            if out is far:
                far_potential[0, rows, :] = moved
            else:
                out[3, rows, :] = moved
    for own, other in ((far, near), (near, far)):
        for start in range(0, total, ROWS):
            rows = slice(start, start + ROWS)
            nu, v, total_flux = in_plane(own, 0, own, 1, start)
            total_flux = total_flux + (nu + other[0, rows, :]) * (v - other[1, rows, :])
            own[2, rows, :] = 0.5 * (v + total_flux)


def fold(value):
    return jnp.sum(value.reshape(ROWS // 8, 8, value.shape[1]), axis=0)


def sums_kernel(far, near, far_in, near_in, image, image_in, sums):
    slab, _ = place()
    count = lax.axis_size("slab")
    total, columns = far.shape[1:]
    beyond = jnp.where((slab > 0) & (slab < count - 1), 1.0, 0.0).astype(jnp.float32)
    sides = ((far, far_in, beyond), (near, near_in, None))
    nil = jnp.zeros((8, columns), jnp.float32)
    m0, m1 = nil, nil
    for side, (own, halo, keep) in enumerate(sides):
        for start in range(0, total, ROWS):
            rows = slice(start, start + ROWS)
            v = own[1, rows, :]
            flux = 0.5 * (own[0, rows, :] + halo[0, rows, :]) * (v - halo[1, rows, :])
            y = own[2, rows, :] + flux
            outer = halo[2, rows, :] - flux
            image[side, rows, :] = y
            image_in[side, rows, :] = outer if keep is None else keep * outer
            m0 = m0 + fold(v * v)
            m1 = m1 + fold(v * y)
    m0 = jnp.sum(m0, keepdims=True)
    m1 = jnp.sum(m1, keepdims=True)
    c = jnp.where(m0 > 0, m1 / m0, 0.0)
    q, s, t = nil, nil, nil
    for side, (own, halo, _) in enumerate(sides):
        for start in range(0, total, ROWS):
            rows = slice(start, start + ROWS)
            nu, y, total_flux = in_plane(own, 0, image, side, start)
            other = (near, far)[side]
            total_flux = total_flux + (nu + other[0, rows, :]) * (y - image[1 - side, rows, :])
            total_flux = total_flux + (nu + halo[0, rows, :]) * (y - image_in[side, rows, :])
            z = 0.5 * (y + total_flux)
            v = own[1, rows, :]
            w = y - c * v
            u = z - c * y
            q = q + fold(w * w)
            s = s + fold(w * u)
            t = t + fold(v * u)
    here = lax.broadcasted_iota(jnp.int32, sums.shape[1:], 0) == slab
    for index, value in enumerate((m0, m1, q, s, t)):
        value = jnp.sum(value, keepdims=True) if index > 1 else value
        sums[index] = jnp.where(here, value, 0.0)


def finish_kernel(
    sums, far, near, far_in, near_in, image, image_in, potential, far_potential, mask, adjoint, term, mixed, mixed_in
):
    _, even = place()
    total = far.shape[1]
    m0_d, m1_d, q_d, s_d, t_d = (sums[i] for i in range(SUMS))
    m0 = jnp.sum(m0_d, axis=0, keepdims=True)
    m1 = jnp.sum(m1_d, axis=0, keepdims=True)
    c = m1 / m0
    delta = jnp.where(m0_d > 0, m1_d / m0_d, 0.0) - c
    ww = jnp.sum(q_d + delta * delta * m0_d, axis=0, keepdims=True)
    waw = jnp.sum(s_d + delta * (q_d + t_d) + delta * delta * m1_d, axis=0, keepdims=True)
    alpha0 = m0 / m1
    beta = alpha0 * (ww * alpha0 / m0)
    divisor = waw - ww * (ww / m1)
    alpha1 = jnp.where(divisor == 0, 0.0, ww / divisor)
    a = (alpha0 + alpha1 * (1.0 + beta))[:, 0:1]
    b = (-alpha1 * alpha0)[:, 0:1]
    scale = 0.25 / lax.axis_size("pos")
    sides = ((far, even, far_in, far_potential, 0), (near, 1 - even, near_in, near_in, 3))
    for side, (own, layer, halo, halo_potential, at) in enumerate(sides):
        for start in range(0, total, ROWS):
            rows = slice(start, start + ROWS)
            out = a * own[1, rows, :] + b * image[side, rows, :]
            adjoint[layer, rows, :] = out
            mixed[side, rows, :] = out + 0.5 * potential[layer, rows, :]
            outer = a * halo[1, rows, :] + b * image_in[side, rows, :]
            mixed_in[side, rows, :] = outer + 0.5 * halo_potential[at, rows, :]
    for side, (own, layer, halo, halo_potential, at) in enumerate(sides):
        for start in range(0, total, ROWS):
            rows = slice(start, start + ROWS)
            g = potential[layer, rows, :]
            f = mixed[side, rows, :]
            result = (halo_potential[at, rows, :] - potential[1 - layer, rows, :]) * (
                mixed_in[side, rows, :] - mixed[1 - side, rows, :]
            )
            result = result + (turn(g, -1) - turn(g, 1)) * (turn(f, -1) - turn(f, 1))
            result = result + (
                shifted(potential, layer, start, 1) - shifted(potential, layer, start, -1)
            ) * (shifted(mixed, side, start, 1) - shifted(mixed, side, start, -1))
            weight = mask[layer, rows, :].astype(jnp.float32) * own[0, rows, :]
            term[layer, rows, :] = weight * (scale * result)


def pairs(size, first):
    out = []
    for i in range(first, size - 1, 2):
        out += [(i, i + 1), (i + 1, i)]
    return out


def gather_sums(sums, axis, size):
    if size & (size - 1):
        return lax.psum(sums, axis)
    step = 1
    while step < size:
        sums = sums + lax.ppermute(sums, axis, [(i, i ^ step) for i in range(size)])
        step *= 2
    return sums


def sum_positions(term, positions, slabs):
    if positions & (positions - 1):
        return lax.psum(term, "pos")
    bits = positions.bit_length() - 1
    for step in range(bits):
        route = []
        for p in range(positions):
            for s in range(slabs):
                bit = step if s % 2 == 0 else bits - 1 - step
                route.append((p * slabs + s, (p ^ (1 << bit)) * slabs + s))
        term = term + lax.ppermute(term, ("pos", "slab"), route)
    return term


def local(labels, magnet_mask, reluctivity, rotor_shift, potential, adjoint_load):
    layers, radial, angular = labels.shape
    positions, slabs = lax.axis_size("pos"), lax.axis_size("slab")
    if layers != 2 or slabs % 2 or radial % (2 * ROWS):
        raise ValueError("unsupported sizes")
    potential, load = potential[0], adjoint_load[0]
    f32 = functools.partial(jax.ShapeDtypeStruct, dtype=jnp.float32)
    plane = (radial, angular)
    vmem = pl.BlockSpec(memory_space=VMEM)
    smem = pl.BlockSpec(memory_space=SMEM)
    far, near, far_potential = pl.pallas_call(
        open_kernel,
        out_shape=(f32((3,) + plane), f32((4,) + plane), f32((1,) + plane)),
        in_specs=[smem, smem, vmem, vmem, vmem],
        out_specs=(vmem,) * 3,
        compiler_params=params(),
        name="open",
    )(reluctivity, rotor_shift, labels, load, potential)
    far_in = lax.ppermute(far, "slab", pairs(slabs, 1))
    near_in = lax.ppermute(near, "slab", pairs(slabs, 0))
    far_potential = lax.ppermute(far_potential, "slab", pairs(slabs, 1))
    image, image_in, sums = pl.pallas_call(
        sums_kernel,
        out_shape=(f32((2,) + plane), f32((2,) + plane), f32((SUMS, slabs, 128))),
        in_specs=[vmem] * 4,
        out_specs=(vmem,) * 3,
        compiler_params=params(),
        name="sums",
    )(far, near, far_in, near_in)
    sums = gather_sums(sums, "slab", slabs)
    adjoint, term = pl.pallas_call(
        finish_kernel,
        out_shape=(f32((2,) + plane), f32((2,) + plane)),
        in_specs=[vmem] * 10,
        out_specs=(vmem,) * 2,
        scratch_shapes=[VMEM((2,) + plane, jnp.float32)] * 2,
        compiler_params=params(),
        name="finish",
    )(sums, far, near, far_in, near_in, image, image_in, potential, far_potential, magnet_mask)
    return sum_positions(term, positions, slabs), adjoint[None]


def solution(mesh):
    return jax.shard_map(
        local,
        mesh=mesh,
        in_specs=(
            P("slab", None, None),
            P("slab", None, None),
            P(),
            P("pos"),
            P("pos", "slab", None, None),
            P("pos", "slab", None, None),
        ),
        out_specs=(P("slab", None, None), P("pos", "slab", None, None)),
        check_vma=False,
    )
```

time: 161 us -> 55.5 us (0.34)
  blocking collectives: 52 us -> 0 us
  waiting for transfers between devices: 54.4 us -> 20.5 us
  between operations: 18.9 us -> 1.36 us
  other arithmetic: 15.4 us -> 0.94 us
  starting transfers between devices: 15.4 us -> 22.5 us
  Pallas kernels: 0 us -> 6.09 us
    psum x3 -> x0, blocking collectives: 52 us -> none  [the longest x2 33.6 us: squares(): return lax.psum(jnp.sum(residual * residual), 'slab')]
    psum x1 -> x0, waiting for transfers between devices: 48.9 us -> none  [local(): summed = lax.psum(contribution, 'pos')]
    ppermute x8, waiting for transfers between devices: 5.57 us -> 20.5 us  [the longest x2 15.3 us: sum_positions(): term = term + lax.ppermute(term, ('pos', 'slab'), route)]
    ppermute x8, starting transfers between devices: 15.4 us -> 22.5 us  [the longest x3 17.5 us: gather_sums(): sums = sums + lax.ppermute(sums, axis, [(i, i ^ step) for i in range(size)])]
    pallas_call x0 -> x3, Pallas kernels: none -> 6.09 us  [the longest x1 2.51 us: local(): pl.pallas_call(open_kernel, out_shape=(f32((3,) + plane), f32((4,) + plan...]
    mul x4 -> x0, other arithmetic: 4.88 us -> none  [the longest x1 3.97 us: gradient_term(): return magnet_mask.astype(jnp.float32) * relief * (inner + 0.5 * square)]
    reduce_sum x3 -> x0, other arithmetic: 4.81 us -> none  [the longest x2 4.07 us: local(): alpha = norm_now / lax.psum(jnp.sum(direction * image), 'slab')]
    unnamed x18 -> x12, local copies, waits for them, and re-layouts: 1.01 us -> 3.78 us
  transfers between devices with their start and end apart: 9 -> 8, of which waited for: 5 -> 6; matrix products, arithmetic and copies ran while one was open for 3% -> 0% of each run, Pallas kernels for 0% -> 4%
where the time goes in v1:
time: 55.5 us; the launch traced here: 55.2 us
  starting transfers between devices  22.5 us (41%)
  waiting for transfers between devices  20.5 us (37%)
  Pallas kernels  6.09 us (11%)
  local copies, waits for them, and re-layouts  3.78 us (7%)
  between operations  1.36 us (2%)
  other arithmetic  0.94 us (2%)
    ppermute x3, starting transfers between devices, gather_sums(): sums = sums + lax.ppermute(sums, axis, [(i, i ^ step) for i in range(size)])  17.5 us
    ppermute x2, waiting for transfers between devices, sum_positions(): term = term + lax.ppermute(term, ('pos', 'slab'), route)  15.3 us
    ppermute x3, waiting for transfers between devices, gather_sums(): sums = sums + lax.ppermute(sums, axis, [(i, i ^ step) for i in range(size)])  4.36 us
    unnamed x12, local copies, waits for them, and re-layouts  3.78 us
    ppermute x2, starting transfers between devices, sum_positions(): term = term + lax.ppermute(term, ('pos', 'slab'), route)  3.15 us
    pallas_call x1, Pallas kernels, local(): pl.pallas_call(open_kernel, out_shape=(f32((3,) + plane), f32((4,) + plan...  2.51 us
    pallas_call x1, Pallas kernels, local(): pl.pallas_call(sums_kernel, out_shape=(f32((2,) + plane), f32((2,) + plan...  1.99 us
    pallas_call x1, Pallas kernels, local(): pl.pallas_call(finish_kernel, out_shape=(f32((2,) + plane), f32((2,) + pl...  1.58 us
  transfers between devices with their start and end apart: 8, of which 6 were waited for; matrix products, arithmetic and copies ran while one was open for 0% of the time, Pallas kernels for 4%

profile of v1, /device:TPU:0, one launch (start us, length us, event | category | flops | bytes accessed | tf_op | source)
XLA Modules:
  0.0 55.2 jit_solution(5074891195909335003)
XLA Ops:
  1.3 0.6 %copy-done.5 = f32[4]{0:T(128)S(1)} copy-done((f32[4]{0:T(128)S(1)}, f32[4]{0:T(128)}, u32[]{:S(2)}) %copy-start.5) | copy-done | bytes 40
  1.9 1.0 %copy-done = f32[1,2,256,256]{3,2,1,0:T(8,128)S(1)} copy-done((f32[1,2,256,256]{3,2,1,0:T(8,128)S(1)}, f32[1,2,256,256]{3,2,1,0:T(8,128)}, u32[]{:S(2)}) %copy-start) | copy-done | bytes 524312
  3.0 1.0 %copy-done.3 = s32[2,256,256]{2,1,0:T(8,128)S(1)} copy-done((s32[2,256,256]{2,1,0:T(8,128)S(1)}, s32[2,256,256]{2,1,0:T(8,128)}, u32[]{:S(2)}) %copy-start.3) | copy-done | bytes 524312
  4.0 1.0 %copy-done.4 = f32[1,2,256,256]{3,2,1,0:T(8,128)S(1)} copy-done((f32[1,2,256,256]{3,2,1,0:T(8,128)S(1)}, f32[1,2,256,256]{3,2,1,0:T(8,128)}, u32[]{:S(2)}) %copy-start.4) | copy-done | bytes 524312
  5.1 2.5 %open.1 = (f32[3,256,256]{2,1,0:T(8,128)S(1)}, f32[4,256,256]{2,1,0:T(8,128)S(1)}, f32[1,256,256]{2,1,0:T(8,128)S(1)}) custom-call(f32[4]{0:T(128)S(1)} %copy-done.5, s32[1]{0:T(128)S(6)} %copy.8.shift, s32[2,256,256]{2,1,0:T(8,128)S(1)} %copy-done.3, f32[2,256,256]{2,1,0:T(8,128)S(1)} %bitcast.5, f32[2,256,256]{2,1,0:T(8,128)S(1)} %bitcast.3), custom_call_target="tpu_custom_call" | custom-call | tf_op jit(solution)/shard_map/open/pallas_call | solution.py:214
  7.6 0.5 collective-permute-start.1
  8.1 0.7 %collective-permute-start = (f32[3,256,256]{2,1,0:T(8,128)S(1)}, f32[3,256,256]{2,1,0:T(8,128)S(1)}, u32[]{:S(2)}, u32[]{:S(2)}) collective-permute-start(f32[3,256,256]{2,1,0:T(8,128)S(1)} %get-tuple-element.10.far), channel_id=1, source_target_pairs={{1,2},{2,1},{3,4},{4,3},{5,6},{6,5},{9,10},{10,9},{11,12},{12,11},... | collective-permute-start | bytes 2359304 | tf_op jit(solution)/shard_map/ppermute | solution.py:222
  8.8 0.7 %collective-permute-start.5 = (f32[1,256,256]{2,1,0:T(8,128)S(1)}, f32[1,256,256]{2,1,0:T(8,128)S(1)}, u32[]{:S(2)}, u32[]{:S(2)}) collective-permute-start(f32[1,256,256]{2,1,0:T(8,128)S(1)} %get-tuple-element.15), channel_id=1, source_target_pairs={{1,2},{2,1},{3,4},{4,3},{5,6},{6,5},{9,10},{10,9},{11,12},{12,11},... | collective-permute-start | bytes 786440 | tf_op jit(solution)/shard_map/ppermute | solution.py:224
  9.5 0.0 collective-permute-done.far_in
  9.5 0.9 %collective-permute-done.1.near_in = f32[4,256,256]{2,1,0:T(8,128)S(1)} collective-permute-done((f32[4,256,256]{2,1,0:T(8,128)S(1)}, f32[4,256,256]{2,1,0:T(8,128)S(1)}, u32[]{:S(2)}, u32[]{:S(2)}) %collective-permute-start.1) | collective-permute-done | bytes 1048608 | tf_op jit(solution)/shard_map/ppermute | solution.py:223
  10.4 2.0 %sums.1 = (f32[2,256,256]{2,1,0:T(8,128)S(1)}, f32[2,256,256]{2,1,0:T(8,128)S(1)}, f32[5,8,128]{2,1,0:T(8,128)S(1)}) custom-call(f32[3,256,256]{2,1,0:T(8,128)S(1)} %get-tuple-element.10.far, f32[4,256,256]{2,1,0:T(8,128)S(1)} %get-tuple-element.11.near, f32[3,256,256]{2,1,0:T(8,128)S(1)} %collective-permute-done.far_in, ...), custom_call_target="tpu_custom_call" | custom-call | tf_op jit(solution)/shard_map/sums/pallas_call | solution.py:225
  12.4 12.1 %collective-permute-start.2 = (f32[5,8,128]{2,1,0:T(8,128)S(1)}, f32[5,8,128]{2,1,0:T(8,128)S(1)}, u32[]{:S(2)}, u32[]{:S(2)}) collective-permute-start(f32[5,8,128]{2,1,0:T(8,128)S(1)} %get-tuple-element.12), channel_id=1, source_target_pairs={{0,1},{1,0},{2,3},{3,2},{4,5},{5,4},{6,7},{7,6},{8,9},{9,8},{10,11... | collective-permute-start | bytes 61448 | tf_op jit(solution)/shard_map/ppermute | solution.py:185
  24.4 0.8 %collective-permute-done.2 = f32[5,8,128]{2,1,0:T(8,128)S(1)} collective-permute-done((f32[5,8,128]{2,1,0:T(8,128)S(1)}, f32[5,8,128]{2,1,0:T(8,128)S(1)}, u32[]{:S(2)}, u32[]{:S(2)}) %collective-permute-start.2) | collective-permute-done | bytes 20512 | tf_op jit(solution)/shard_map/ppermute | solution.py:185
  25.3 2.4 %collective-permute-start.3 = (f32[5,8,128]{2,1,0:T(8,128)S(1)}, f32[5,8,128]{2,1,0:T(8,128)S(1)}, u32[]{:S(2)}, u32[]{:S(2)}) collective-permute-start(f32[5,8,128]{2,1,0:T(8,128)S(1)} %add.15), channel_id=1, source_target_pairs={{0,2},{1,3},{2,0},{3,1},{4,6},{5,7},{6,4},{7,5},{8,10},{9,11},{10,... | collective-permute-start | bytes 61448 | tf_op jit(solution)/shard_map/ppermute | solution.py:185
  27.7 1.8 %collective-permute-done.3 = f32[5,8,128]{2,1,0:T(8,128)S(1)} collective-permute-done((f32[5,8,128]{2,1,0:T(8,128)S(1)}, f32[5,8,128]{2,1,0:T(8,128)S(1)}, u32[]{:S(2)}, u32[]{:S(2)}) %collective-permute-start.3) | collective-permute-done | bytes 20512 | tf_op jit(solution)/shard_map/ppermute | solution.py:185
  29.5 3.0 %collective-permute-start.4 = (f32[5,8,128]{2,1,0:T(8,128)S(1)}, f32[5,8,128]{2,1,0:T(8,128)S(1)}, u32[]{:S(2)}, u32[]{:S(2)}) collective-permute-start(f32[5,8,128]{2,1,0:T(8,128)S(1)} %add.16), channel_id=1, source_target_pairs={{0,4},{1,5},{2,6},{3,7},{4,0},{5,1},{6,2},{7,3},{8,12},{9,13},{10,... | collective-permute-start | bytes 61448 | tf_op jit(solution)/shard_map/ppermute | solution.py:185
  32.5 1.8 %collective-permute-done.4 = f32[5,8,128]{2,1,0:T(8,128)S(1)} collective-permute-done((f32[5,8,128]{2,1,0:T(8,128)S(1)}, f32[5,8,128]{2,1,0:T(8,128)S(1)}, u32[]{:S(2)}, u32[]{:S(2)}) %collective-permute-start.4) | collective-permute-done | bytes 20512 | tf_op jit(solution)/shard_map/ppermute | solution.py:185
  34.3 1.6 %finish.1 = (f32[2,256,256]{2,1,0:T(8,128)}, f32[2,256,256]{2,1,0:T(8,128)S(1)}) custom-call(f32[5,8,128]{2,1,0:T(8,128)S(1)} %add.17.sums, f32[3,256,256]{2,1,0:T(8,128)S(1)} %get-tuple-element.10.far, f32[4,256,256]{2,1,0:T(8,128)S(1)} %get-tuple-element.11.near, f32[3,256,256]{2,1,0:T(8,128)S(1)} %collective-permute-done.far_in, ...), custom_call_target="tpu_custom_call" | custom-call | tf_op jit(solution)/shard_map/finish/pallas_call | solution.py:234
  35.9 1.5 %collective-permute-start.6 = (f32[2,256,256]{2,1,0:T(8,128)S(1)}, f32[2,256,256]{2,1,0:T(8,128)S(1)}, u32[]{:S(2)}, u32[]{:S(2)}) collective-permute-start(f32[2,256,256]{2,1,0:T(8,128)S(1)} %get-tuple-element.16), channel_id=1, source_target_pairs={{0,8},{1,17},{2,10},{3,19},{4,12},{5,21},{6,14},{7,23},{8,0},{9,25... | collective-permute-start | bytes 1572872 | tf_op jit(solution)/shard_map/ppermute | solution.py:200
  37.4 7.7 %collective-permute-done.6 = f32[2,256,256]{2,1,0:T(8,128)S(1)} collective-permute-done((f32[2,256,256]{2,1,0:T(8,128)S(1)}, f32[2,256,256]{2,1,0:T(8,128)S(1)}, u32[]{:S(2)}, u32[]{:S(2)}) %collective-permute-start.6) | collective-permute-done | bytes 524320 | tf_op jit(solution)/shard_map/ppermute | solution.py:200
  45.0 0.1 add.18
  45.1 1.6 %collective-permute-start.7 = (f32[2,256,256]{2,1,0:T(8,128)S(1)}, f32[2,256,256]{2,1,0:T(8,128)S(1)}, u32[]{:S(2)}, u32[]{:S(2)}) collective-permute-start(f32[2,256,256]{2,1,0:T(8,128)S(1)} %add.18), channel_id=1, source_target_pairs={{0,16},{1,9},{2,18},{3,11},{4,20},{5,13},{6,22},{7,15},{8,24},{9,1... | collective-permute-start | bytes 1572872 | tf_op jit(solution)/shard_map/ppermute | solution.py:200
  46.7 7.6 %collective-permute-done.7 = f32[2,256,256]{2,1,0:T(8,128)S(1)} collective-permute-done((f32[2,256,256]{2,1,0:T(8,128)S(1)}, f32[2,256,256]{2,1,0:T(8,128)S(1)}, u32[]{:S(2)}, u32[]{:S(2)}) %collective-permute-start.7) | collective-permute-done | bytes 524320 | tf_op jit(solution)/shard_map/ppermute | solution.py:200
  54.4 0.9 %add.19 = f32[2,256,256]{2,1,0:T(8,128)} add(f32[2,256,256]{2,1,0:T(8,128)S(1)} %add.18, f32[2,256,256]{2,1,0:T(8,128)S(1)} %collective-permute-done.7) | non-fusion elementwise | flops 131072 | bytes 1572864 | tf_op jit(solution)/shard_map/add | solution.py:200
  (12 shorter events, 0.0 us)
Async XLA Ops:
  1.3 0.7 %copy-start.5 = (f32[4]{0:T(128)S(1)}, f32[4]{0:T(128)}, u32[]{:S(2)}) copy-start(f32[4]{0:T(128)} %reluctivity.1) | copy-start | bytes 52
  1.9 1.0 %copy-start = (f32[1,2,256,256]{3,2,1,0:T(8,128)S(1)}, f32[1,2,256,256]{3,2,1,0:T(8,128)}, u32[]{:S(2)}) copy-start(f32[1,2,256,256]{3,2,1,0:T(8,128)} %param.10) | copy-start | bytes 1572868
  3.0 1.0 %copy-start.3 = (s32[2,256,256]{2,1,0:T(8,128)S(1)}, s32[2,256,256]{2,1,0:T(8,128)}, u32[]{:S(2)}) copy-start(s32[2,256,256]{2,1,0:T(8,128)} %labels.1) | copy-start | bytes 1572868
  4.0 1.0 %copy-start.4 = (f32[1,2,256,256]{3,2,1,0:T(8,128)S(1)}, f32[1,2,256,256]{3,2,1,0:T(8,128)}, u32[]{:S(2)}) copy-start(f32[1,2,256,256]{3,2,1,0:T(8,128)} %param.11) | copy-start | bytes 1572868
  7.6 2.8 %collective-permute-start.1 = (f32[4,256,256]{2,1,0:T(8,128)S(1)}, f32[4,256,256]{2,1,0:T(8,128)S(1)}, u32[]{:S(2)}, u32[]{:S(2)}) collective-permute-start(f32[4,256,256]{2,1,0:T(8,128)S(1)} %get-tuple-element.11.near), channel_id=1, source_target_pairs={{0,1},{1,0},{2,3},{3,2},{4,5},{5,4},{6,7},{7,6},{8,9},{9,8},{10,11... | collective-permute-start | bytes 3145736 | tf_op jit(solution)/shard_map/ppermute | solution.py:223
  8.1 1.4 %collective-permute-start = (f32[3,256,256]{2,1,0:T(8,128)S(1)}, f32[3,256,256]{2,1,0:T(8,128)S(1)}, u32[]{:S(2)}, u32[]{:S(2)}) collective-permute-start(f32[3,256,256]{2,1,0:T(8,128)S(1)} %get-tuple-element.10.far), channel_id=1, source_target_pairs={{1,2},{2,1},{3,4},{4,3},{5,6},{6,5},{9,10},{10,9},{11,12},{12,11},... | collective-permute-start | bytes 2359304 | tf_op jit(solution)/shard_map/ppermute | solution.py:222
  8.8 25.5 %collective-permute-start.5 = (f32[1,256,256]{2,1,0:T(8,128)S(1)}, f32[1,256,256]{2,1,0:T(8,128)S(1)}, u32[]{:S(2)}, u32[]{:S(2)}) collective-permute-start(f32[1,256,256]{2,1,0:T(8,128)S(1)} %get-tuple-element.15), channel_id=1, source_target_pairs={{1,2},{2,1},{3,4},{4,3},{5,6},{6,5},{9,10},{10,9},{11,12},{12,11},... | collective-permute-start | bytes 786440 | tf_op jit(solution)/shard_map/ppermute | solution.py:224
  10.4 23.9 %copy-start.1 = (f32[1,2,256,256]{3,2,1,0:T(8,128)S(1)}, f32[1,2,256,256]{3,2,1,0:T(8,128)}, u32[]{:S(2)}) copy-start(f32[1,2,256,256]{3,2,1,0:T(8,128)} %param.10) | copy-start | bytes 1572868
  10.4 23.9 %copy-start.2 = (s32[2,256,256]{2,1,0:T(8,128)S(1)}, s32[2,256,256]{2,1,0:T(8,128)}, u32[]{:S(2)}) copy-start(s32[2,256,256]{2,1,0:T(8,128)} %mask.1) | copy-start | bytes 1572868
  12.4 12.9 %collective-permute-start.2 = (f32[5,8,128]{2,1,0:T(8,128)S(1)}, f32[5,8,128]{2,1,0:T(8,128)S(1)}, u32[]{:S(2)}, u32[]{:S(2)}) collective-permute-start(f32[5,8,128]{2,1,0:T(8,128)S(1)} %get-tuple-element.12), channel_id=1, source_target_pairs={{0,1},{1,0},{2,3},{3,2},{4,5},{5,4},{6,7},{7,6},{8,9},{9,8},{10,11... | collective-permute-start | bytes 61448 | tf_op jit(solution)/shard_map/ppermute | solution.py:185
  25.3 4.2 %collective-permute-start.3 = (f32[5,8,128]{2,1,0:T(8,128)S(1)}, f32[5,8,128]{2,1,0:T(8,128)S(1)}, u32[]{:S(2)}, u32[]{:S(2)}) collective-permute-start(f32[5,8,128]{2,1,0:T(8,128)S(1)} %add.15), channel_id=1, source_target_pairs={{0,2},{1,3},{2,0},{3,1},{4,6},{5,7},{6,4},{7,5},{8,10},{9,11},{10,... | collective-permute-start | bytes 61448 | tf_op jit(solution)/shard_map/ppermute | solution.py:185
  29.5 4.8 %collective-permute-start.4 = (f32[5,8,128]{2,1,0:T(8,128)S(1)}, f32[5,8,128]{2,1,0:T(8,128)S(1)}, u32[]{:S(2)}, u32[]{:S(2)}) collective-permute-start(f32[5,8,128]{2,1,0:T(8,128)S(1)} %add.16), channel_id=1, source_target_pairs={{0,4},{1,5},{2,6},{3,7},{4,0},{5,1},{6,2},{7,3},{8,12},{9,13},{10,... | collective-permute-start | bytes 61448 | tf_op jit(solution)/shard_map/ppermute | solution.py:185
  35.9 9.2 %collective-permute-start.6 = (f32[2,256,256]{2,1,0:T(8,128)S(1)}, f32[2,256,256]{2,1,0:T(8,128)S(1)}, u32[]{:S(2)}, u32[]{:S(2)}) collective-permute-start(f32[2,256,256]{2,1,0:T(8,128)S(1)} %get-tuple-element.16), channel_id=1, source_target_pairs={{0,8},{1,17},{2,10},{3,19},{4,12},{5,21},{6,14},{7,23},{8,0},{9,25... | collective-permute-start | bytes 1572872 | tf_op jit(solution)/shard_map/ppermute | solution.py:200
  45.1 9.2 %collective-permute-start.7 = (f32[2,256,256]{2,1,0:T(8,128)S(1)}, f32[2,256,256]{2,1,0:T(8,128)S(1)}, u32[]{:S(2)}, u32[]{:S(2)}) collective-permute-start(f32[2,256,256]{2,1,0:T(8,128)S(1)} %add.18), channel_id=1, source_target_pairs={{0,16},{1,9},{2,18},{3,11},{4,20},{5,13},{6,22},{7,15},{8,24},{9,1... | collective-permute-start | bytes 1572872 | tf_op jit(solution)/shard_map/ppermute | solution.py:200

commit v2 on v1

--- a/solution.py
+++ b/solution.py
@@ -12,10 +12,11 @@
 VMEM = pltpu.VMEM
 SMEM = pltpu.SMEM
 SUMS = 5
-
-
-def params(**kw):
-    return pltpu.CompilerParams(vmem_limit_bytes=40 * 1024 * 1024, **kw)
+CHUNKS = 2
+
+
+def params():
+    return pltpu.CompilerParams(vmem_limit_bytes=40 * 1024 * 1024)
 
 
 def shifted(ref, index, start, offset):
@@ -49,15 +50,30 @@
     return slab, lax.rem(slab, 2)
 
 
-def open_kernel(reluctivity, shift, labels, load, potential, far, near, far_potential):
+def open_kernel(reluctivity, shift, labels, load, potential, far, near, far_potential, held, table, sems):
     _, even = place()
+    odd = 1 - even
     total = labels.shape[1]
-    r0, r1, r2, r3 = (reluctivity[i] for i in range(4))
+    moves = (
+        (labels.at[even], held.at[0]),
+        (labels.at[odd], held.at[1]),
+        (load.at[even], far.at[1]),
+        (load.at[odd], near.at[1]),
+        (potential.at[even], far_potential.at[0]),
+        (potential.at[odd], near.at[3]),
+        (reluctivity, table),
+    )
+    copies = [pltpu.make_async_copy(src, dst, sems.at[i]) for i, (src, dst) in enumerate(moves)]
+    for copy in copies:
+        copy.start()
+    copies[-1].wait()
+    r0, r1, r2, r3 = (table[i] for i in range(4))
     offset = shift[0]
-    for layer, out in ((even, far), (1 - even, near)):
-        for start in range(0, total, ROWS):
-            rows = slice(start, start + ROWS)
-            material = labels[layer, rows, :]
+    for side, out in enumerate((far, near)):
+        copies[side].wait()
+        for start in range(0, total, ROWS):
+            rows = slice(start, start + ROWS)
+            material = held[side, rows, :]
             if start < total // 2:
                 material = pltpu.roll(material, offset, 1)
             out[0, rows, :] = jnp.where(
@@ -65,12 +81,8 @@
                 jnp.where(material == 0, r0, r1),
                 jnp.where(material == 2, r2, r3),
             )
-            out[1, rows, :] = load[layer, rows, :]
-            moved = potential[layer, rows, :]
-            if out is far:
-                far_potential[0, rows, :] = moved
-            else:
-                out[3, rows, :] = moved
+    for copy in copies[2:-1]:
+        copy.wait()
     for own, other in ((far, near), (near, far)):
         for start in range(0, total, ROWS):
             rows = slice(start, start + ROWS)
@@ -127,8 +139,9 @@
 
 
 def finish_kernel(
-    sums, far, near, far_in, near_in, image, image_in, potential, far_potential, mask, adjoint, term, mixed, mixed_in
+    sums, far, near, far_in, near_in, image, image_in, potential, far_potential, mask, adjoint, *rest
 ):
+    *terms, mixed, mixed_in = rest
     _, even = place()
     total = far.shape[1]
     m0_d, m1_d, q_d, s_d, t_d = (sums[i] for i in range(SUMS))
@@ -167,7 +180,12 @@
                 shifted(potential, layer, start, 1) - shifted(potential, layer, start, -1)
             ) * (shifted(mixed, side, start, 1) - shifted(mixed, side, start, -1))
             weight = mask[layer, rows, :].astype(jnp.float32) * own[0, rows, :]
-            term[layer, rows, :] = weight * (scale * result)
+            span = total // CHUNKS
+            terms[start // span][layer, start % span : start % span + ROWS, :] = weight * (scale * result)
+
+
+def in_hbm(x):
+    return pltpu.with_memory_space_constraint(x, pltpu.HBM)
 
 
 def pairs(size, first):
@@ -204,21 +222,27 @@
 def local(labels, magnet_mask, reluctivity, rotor_shift, potential, adjoint_load):
     layers, radial, angular = labels.shape
     positions, slabs = lax.axis_size("pos"), lax.axis_size("slab")
-    if layers != 2 or slabs % 2 or radial % (2 * ROWS):
+    if layers != 2 or slabs % 2 or radial % (2 * CHUNKS * ROWS):
         raise ValueError("unsupported sizes")
     potential, load = potential[0], adjoint_load[0]
     f32 = functools.partial(jax.ShapeDtypeStruct, dtype=jnp.float32)
     plane = (radial, angular)
     vmem = pl.BlockSpec(memory_space=VMEM)
     smem = pl.BlockSpec(memory_space=SMEM)
+    hbm = pl.BlockSpec(memory_space=pltpu.HBM)
     far, near, far_potential = pl.pallas_call(
         open_kernel,
-        out_shape=(f32((3,) + plane), f32((4,) + plane), f32((1,) + plane)),
-        in_specs=[smem, smem, vmem, vmem, vmem],
+        out_shape=tuple(pltpu.VMEM((k,) + plane, jnp.float32) for k in (3, 4, 1)),
+        in_specs=[hbm, smem, hbm, hbm, hbm],
         out_specs=(vmem,) * 3,
+        scratch_shapes=[
+            VMEM((2,) + plane, jnp.int32),
+            SMEM(reluctivity.shape, jnp.float32),
+            pltpu.SemaphoreType.DMA((7,)),
+        ],
         compiler_params=params(),
         name="open",
-    )(reluctivity, rotor_shift, labels, load, potential)
+    )(in_hbm(reluctivity), rotor_shift, in_hbm(labels), in_hbm(load), in_hbm(potential))
     far_in = lax.ppermute(far, "slab", pairs(slabs, 1))
     near_in = lax.ppermute(near, "slab", pairs(slabs, 0))
     far_potential = lax.ppermute(far_potential, "slab", pairs(slabs, 1))
@@ -231,16 +255,18 @@
         name="sums",
     )(far, near, far_in, near_in)
     sums = gather_sums(sums, "slab", slabs)
-    adjoint, term = pl.pallas_call(
+    adjoint, *terms = pl.pallas_call(
         finish_kernel,
-        out_shape=(f32((2,) + plane), f32((2,) + plane)),
+        out_shape=(pltpu.VMEM((2,) + plane, jnp.float32),)
+        + (f32((2, radial // CHUNKS, angular)),) * CHUNKS,
         in_specs=[vmem] * 10,
-        out_specs=(vmem,) * 2,
+        out_specs=(vmem,) * (1 + CHUNKS),
         scratch_shapes=[VMEM((2,) + plane, jnp.float32)] * 2,
         compiler_params=params(),
         name="finish",
     )(sums, far, near, far_in, near_in, image, image_in, potential, far_potential, magnet_mask)
-    return sum_positions(term, positions, slabs), adjoint[None]
+    gradient = [sum_positions(term, positions, slabs) for term in terms]
+    return jnp.concatenate(gradient, axis=1), adjoint[None]
 
 
 def solution(mesh):

time: 55.5 us -> 51.6 us (0.930)
  waiting for transfers between devices: 20.5 us -> 17.3 us
  local copies, waits for them, and re-layouts: 3.78 us -> 0.8 us
  starting transfers between devices: 22.5 us -> 24.8 us
    ppermute x2 -> x4, waiting for transfers between devices: 15.3 us -> 12 us  [sum_positions(): term = term + lax.ppermute(term, ('pos', 'slab'), route)]
    unnamed x12 -> x5, local copies, waits for them, and re-layouts: 3.78 us -> 0.8 us
    ppermute x2 -> x4, starting transfers between devices: 3.15 us -> 5.37 us  [sum_positions(): term = term + lax.ppermute(term, ('pos', 'slab'), route)]
    concatenate x0 -> x1, other arithmetic: none -> 0.83 us  [local(): return (jnp.concatenate(gradient, axis=1), adjoint[None])]
    add x2 -> x4, other arithmetic: 0.93 us -> 0.13 us  [sum_positions(): term = term + lax.ppermute(term, ('pos', 'slab'), route)]
  transfers between devices with their start and end apart: 8 -> 10, of which waited for: 6 -> 7; matrix products, arithmetic and copies ran while one was open for 0% -> 2% of each run, Pallas kernels for 4% -> 4%
where the time goes in v2:
time: 51.6 us; the launch traced here: 51.4 us
  starting transfers between devices  24.8 us (48%)
  waiting for transfers between devices  17.3 us (34%)
  Pallas kernels  6.24 us (12%)
  between operations  1.37 us (3%)
  other arithmetic  0.98 us (2%)
  local copies, waits for them, and re-layouts  0.8 us (2%)
    ppermute x3, starting transfers between devices, gather_sums(): sums = sums + lax.ppermute(sums, axis, [(i, i ^ step) for i in range(size)])  17.5 us
    ppermute x4, waiting for transfers between devices, sum_positions(): term = term + lax.ppermute(term, ('pos', 'slab'), route)  12 us
    ppermute x4, starting transfers between devices, sum_positions(): term = term + lax.ppermute(term, ('pos', 'slab'), route)  5.37 us
    ppermute x3, waiting for transfers between devices, gather_sums(): sums = sums + lax.ppermute(sums, axis, [(i, i ^ step) for i in range(size)])  4.36 us
    pallas_call x1, Pallas kernels, local(): pl.pallas_call(open_kernel, out_shape=tuple((pltpu.VMEM((k,) + plane, jnp...  3.37 us
    pallas_call x1, Pallas kernels, local(): pl.pallas_call(sums_kernel, out_shape=(f32((2,) + plane), f32((2,) + plan...  1.99 us
  transfers between devices with their start and end apart: 10, of which 7 were waited for; matrix products, arithmetic and copies ran while one was open for 2% of the time, Pallas kernels for 4%

profile of v2, /device:TPU:0, one launch (start us, length us, event | category | flops | bytes accessed | tf_op | source)
XLA Modules:
  0.0 51.4 jit_solution(1410775389360156701)
XLA Ops:
  1.3 3.4 %open.1 = (f32[3,256,256]{2,1,0:T(8,128)S(1)}, f32[4,256,256]{2,1,0:T(8,128)S(1)}, f32[1,256,256]{2,1,0:T(8,128)S(1)}) custom-call(f32[4]{0:T(128)} %reluctivity.1, s32[1]{0:T(128)S(6)} %copy.9.shift, s32[2,256,256]{2,1,0:T(8,128)} %labels.1, f32[2,256,256]{2,1,0:T(8,128)} %bitcast.6, f32[2,256,256]{2,1,0:T(8,128)} %bitcast.4), custom_call_target="tpu_custom_call" | custom-call | tf_op jit(solution)/shard_map/open/pallas_call | solution.py:233
  4.6 0.5 %collective-permute-start.1 = (f32[4,256,256]{2,1,0:T(8,128)S(1)}, f32[4,256,256]{2,1,0:T(8,128)S(1)}, u32[]{:S(2)}, u32[]{:S(2)}) collective-permute-start(f32[4,256,256]{2,1,0:T(8,128)S(1)} %get-tuple-element.12.near), channel_id=1, source_target_pairs={{0,1},{1,0},{2,3},{3,2},{4,5},{5,4},{6,7},{7,6},{8,9},{9,8},{10,11... | collective-permute-start | bytes 3145736 | tf_op jit(solution)/shard_map/ppermute | solution.py:247
  5.2 0.7 %collective-permute-start = (f32[3,256,256]{2,1,0:T(8,128)S(1)}, f32[3,256,256]{2,1,0:T(8,128)S(1)}, u32[]{:S(2)}, u32[]{:S(2)}) collective-permute-start(f32[3,256,256]{2,1,0:T(8,128)S(1)} %get-tuple-element.11.far), channel_id=1, source_target_pairs={{1,2},{2,1},{3,4},{4,3},{5,6},{6,5},{9,10},{10,9},{11,12},{12,11},... | collective-permute-start | bytes 2359304 | tf_op jit(solution)/shard_map/ppermute | solution.py:246
  5.9 0.7 %collective-permute-start.5 = (f32[1,256,256]{2,1,0:T(8,128)S(1)}, f32[1,256,256]{2,1,0:T(8,128)S(1)}, u32[]{:S(2)}, u32[]{:S(2)}) collective-permute-start(f32[1,256,256]{2,1,0:T(8,128)S(1)} %get-tuple-element.16), channel_id=1, source_target_pairs={{1,2},{2,1},{3,4},{4,3},{5,6},{6,5},{9,10},{10,9},{11,12},{12,11},... | collective-permute-start | bytes 786440 | tf_op jit(solution)/shard_map/ppermute | solution.py:248
  6.6 0.0 collective-permute-done.far_in
  6.6 0.9 %collective-permute-done.1.near_in = f32[4,256,256]{2,1,0:T(8,128)S(1)} collective-permute-done((f32[4,256,256]{2,1,0:T(8,128)S(1)}, f32[4,256,256]{2,1,0:T(8,128)S(1)}, u32[]{:S(2)}, u32[]{:S(2)}) %collective-permute-start.1) | collective-permute-done | bytes 1048608 | tf_op jit(solution)/shard_map/ppermute | solution.py:247
  7.5 2.0 %sums.1 = (f32[2,256,256]{2,1,0:T(8,128)S(1)}, f32[2,256,256]{2,1,0:T(8,128)S(1)}, f32[5,8,128]{2,1,0:T(8,128)S(1)}) custom-call(f32[3,256,256]{2,1,0:T(8,128)S(1)} %get-tuple-element.11.far, f32[4,256,256]{2,1,0:T(8,128)S(1)} %get-tuple-element.12.near, f32[3,256,256]{2,1,0:T(8,128)S(1)} %collective-permute-done.far_in, ...), custom_call_target="tpu_custom_call" | custom-call | tf_op jit(solution)/shard_map/sums/pallas_call | solution.py:249
  9.5 12.1 %collective-permute-start.2 = (f32[5,8,128]{2,1,0:T(8,128)S(1)}, f32[5,8,128]{2,1,0:T(8,128)S(1)}, u32[]{:S(2)}, u32[]{:S(2)}) collective-permute-start(f32[5,8,128]{2,1,0:T(8,128)S(1)} %get-tuple-element.13), channel_id=1, source_target_pairs={{0,1},{1,0},{2,3},{3,2},{4,5},{5,4},{6,7},{7,6},{8,9},{9,8},{10,11... | collective-permute-start | bytes 61448 | tf_op jit(solution)/shard_map/ppermute | solution.py:203
  21.5 0.8 %collective-permute-done.2 = f32[5,8,128]{2,1,0:T(8,128)S(1)} collective-permute-done((f32[5,8,128]{2,1,0:T(8,128)S(1)}, f32[5,8,128]{2,1,0:T(8,128)S(1)}, u32[]{:S(2)}, u32[]{:S(2)}) %collective-permute-start.2) | collective-permute-done | bytes 20512 | tf_op jit(solution)/shard_map/ppermute | solution.py:203
  22.4 2.4 %collective-permute-start.3 = (f32[5,8,128]{2,1,0:T(8,128)S(1)}, f32[5,8,128]{2,1,0:T(8,128)S(1)}, u32[]{:S(2)}, u32[]{:S(2)}) collective-permute-start(f32[5,8,128]{2,1,0:T(8,128)S(1)} %add.21), channel_id=1, source_target_pairs={{0,2},{1,3},{2,0},{3,1},{4,6},{5,7},{6,4},{7,5},{8,10},{9,11},{10,... | collective-permute-start | bytes 61448 | tf_op jit(solution)/shard_map/ppermute | solution.py:203
  24.8 1.8 %collective-permute-done.3 = f32[5,8,128]{2,1,0:T(8,128)S(1)} collective-permute-done((f32[5,8,128]{2,1,0:T(8,128)S(1)}, f32[5,8,128]{2,1,0:T(8,128)S(1)}, u32[]{:S(2)}, u32[]{:S(2)}) %collective-permute-start.3) | collective-permute-done | bytes 20512 | tf_op jit(solution)/shard_map/ppermute | solution.py:203
  26.5 3.0 %collective-permute-start.4 = (f32[5,8,128]{2,1,0:T(8,128)S(1)}, f32[5,8,128]{2,1,0:T(8,128)S(1)}, u32[]{:S(2)}, u32[]{:S(2)}) collective-permute-start(f32[5,8,128]{2,1,0:T(8,128)S(1)} %add.22), channel_id=1, source_target_pairs={{0,4},{1,5},{2,6},{3,7},{4,0},{5,1},{6,2},{7,3},{8,12},{9,13},{10,... | collective-permute-start | bytes 61448 | tf_op jit(solution)/shard_map/ppermute | solution.py:203
  29.6 1.8 %collective-permute-done.4 = f32[5,8,128]{2,1,0:T(8,128)S(1)} collective-permute-done((f32[5,8,128]{2,1,0:T(8,128)S(1)}, f32[5,8,128]{2,1,0:T(8,128)S(1)}, u32[]{:S(2)}, u32[]{:S(2)}) %collective-permute-start.4) | collective-permute-done | bytes 20512 | tf_op jit(solution)/shard_map/ppermute | solution.py:203
  31.4 0.9 %finish.1 = (f32[2,256,256]{2,1,0:T(8,128)S(1)}, f32[2,128,256]{2,1,0:T(8,128)S(1)}, f32[2,128,256]{2,1,0:T(8,128)S(1)}) custom-call(f32[5,8,128]{2,1,0:T(8,128)S(1)} %add.23.sums, f32[3,256,256]{2,1,0:T(8,128)S(1)} %get-tuple-element.11.far, f32[4,256,256]{2,1,0:T(8,128)S(1)} %get-tuple-element.12.near, f32[3,256,256]{2,1,0:T(8,128)S(1)} %collective-permute-done.far_in, ...), custom_call_target="tpu_custom_call" | custom-call | tf_op jit(solution)/shard_map/finish/pallas_call | solution.py:258
  32.2 1.6 %collective-permute-start.6 = (f32[2,128,256]{2,1,0:T(8,128)S(1)}, f32[2,128,256]{2,1,0:T(8,128)S(1)}, u32[]{:S(2)}, u32[]{:S(2)}) collective-permute-start(f32[2,128,256]{2,1,0:T(8,128)S(1)} %get-tuple-element.17), channel_id=1, source_target_pairs={{0,8},{1,17},{2,10},{3,19},{4,12},{5,21},{6,14},{7,23},{8,0},{9,25... | collective-permute-start | bytes 786440 | tf_op jit(solution)/shard_map/ppermute | solution.py:218
  33.8 0.5 collective-permute-start.8
  34.3 4.3 %collective-permute-done.6 = f32[2,128,256]{2,1,0:T(8,128)S(1)} collective-permute-done((f32[2,128,256]{2,1,0:T(8,128)S(1)}, f32[2,128,256]{2,1,0:T(8,128)S(1)}, u32[]{:S(2)}, u32[]{:S(2)}) %collective-permute-start.6) | collective-permute-done | bytes 262176 | tf_op jit(solution)/shard_map/ppermute | solution.py:218
  38.7 1.6 %collective-permute-start.7 = (f32[2,128,256]{2,1,0:T(8,128)S(1)}, f32[2,128,256]{2,1,0:T(8,128)S(1)}, u32[]{:S(2)}, u32[]{:S(2)}) collective-permute-start(f32[2,128,256]{2,1,0:T(8,128)S(1)} %add.24), channel_id=1, source_target_pairs={{0,16},{1,9},{2,18},{3,11},{4,20},{5,13},{6,22},{7,15},{8,24},{9,1... | collective-permute-start | bytes 786440 | tf_op jit(solution)/shard_map/ppermute | solution.py:218
  40.3 3.7 %collective-permute-done.8 = f32[2,128,256]{2,1,0:T(8,128)S(1)} collective-permute-done((f32[2,128,256]{2,1,0:T(8,128)S(1)}, f32[2,128,256]{2,1,0:T(8,128)S(1)}, u32[]{:S(2)}, u32[]{:S(2)}) %collective-permute-start.8) | collective-permute-done | bytes 262176 | tf_op jit(solution)/shard_map/ppermute | solution.py:218
  44.1 1.7 %collective-permute-start.9 = (f32[2,128,256]{2,1,0:T(8,128)S(1)}, f32[2,128,256]{2,1,0:T(8,128)S(1)}, u32[]{:S(2)}, u32[]{:S(2)}) collective-permute-start(f32[2,128,256]{2,1,0:T(8,128)S(1)} %add.26), channel_id=1, source_target_pairs={{0,16},{1,9},{2,18},{3,11},{4,20},{5,13},{6,22},{7,15},{8,24},{9,1... | collective-permute-start | bytes 786440 | tf_op jit(solution)/shard_map/ppermute | solution.py:218
  45.8 0.8 %copy.8 = f32[1,2,256,256]{3,2,1,0:T(8,128)} copy(f32[1,2,256,256]{3,2,1,0:T(8,128)S(1)} %bitcast.3) | data formatting | bytes 1048576
  46.6 0.0 collective-permute-done.7
  46.6 3.9 %collective-permute-done.9 = f32[2,128,256]{2,1,0:T(8,128)S(1)} collective-permute-done((f32[2,128,256]{2,1,0:T(8,128)S(1)}, f32[2,128,256]{2,1,0:T(8,128)S(1)}, u32[]{:S(2)}, u32[]{:S(2)}) %collective-permute-start.9) | collective-permute-done | bytes 262176 | tf_op jit(solution)/shard_map/ppermute | solution.py:218
  50.6 0.8 %pad_maximum_fusion = f32[2,256,256]{2,1,0:T(8,128)} fusion(f32[2,128,256]{2,1,0:T(8,128)S(1)} %add.27, f32[2,128,256]{2,1,0:T(8,128)S(1)} %add.25), kind=kLoop, calls=%fused_computation | loop fusion | flops 131072 | bytes 1048576 | tf_op jit(solution)/shard_map/concatenate | solution.py:269
  (12 shorter events, 0.2 us)
Async XLA Ops:
  4.6 2.8 %collective-permute-start.1 = (f32[4,256,256]{2,1,0:T(8,128)S(1)}, f32[4,256,256]{2,1,0:T(8,128)S(1)}, u32[]{:S(2)}, u32[]{:S(2)}) collective-permute-start(f32[4,256,256]{2,1,0:T(8,128)S(1)} %get-tuple-element.12.near), channel_id=1, source_target_pairs={{0,1},{1,0},{2,3},{3,2},{4,5},{5,4},{6,7},{7,6},{8,9},{9,8},{10,11... | collective-permute-start | bytes 3145736 | tf_op jit(solution)/shard_map/ppermute | solution.py:247
  5.2 1.4 %collective-permute-start = (f32[3,256,256]{2,1,0:T(8,128)S(1)}, f32[3,256,256]{2,1,0:T(8,128)S(1)}, u32[]{:S(2)}, u32[]{:S(2)}) collective-permute-start(f32[3,256,256]{2,1,0:T(8,128)S(1)} %get-tuple-element.11.far), channel_id=1, source_target_pairs={{1,2},{2,1},{3,4},{4,3},{5,6},{6,5},{9,10},{10,9},{11,12},{12,11},... | collective-permute-start | bytes 2359304 | tf_op jit(solution)/shard_map/ppermute | solution.py:246
  5.9 25.5 %collective-permute-start.5 = (f32[1,256,256]{2,1,0:T(8,128)S(1)}, f32[1,256,256]{2,1,0:T(8,128)S(1)}, u32[]{:S(2)}, u32[]{:S(2)}) collective-permute-start(f32[1,256,256]{2,1,0:T(8,128)S(1)} %get-tuple-element.16), channel_id=1, source_target_pairs={{1,2},{2,1},{3,4},{4,3},{5,6},{6,5},{9,10},{10,9},{11,12},{12,11},... | collective-permute-start | bytes 786440 | tf_op jit(solution)/shard_map/ppermute | solution.py:248
  7.5 23.9 %copy-start = (f32[1,2,256,256]{3,2,1,0:T(8,128)S(1)}, f32[1,2,256,256]{3,2,1,0:T(8,128)}, u32[]{:S(2)}) copy-start(f32[1,2,256,256]{3,2,1,0:T(8,128)} %param.10) | copy-start | bytes 1572868
  7.5 23.9 %copy-start.1 = (s32[2,256,256]{2,1,0:T(8,128)S(1)}, s32[2,256,256]{2,1,0:T(8,128)}, u32[]{:S(2)}) copy-start(s32[2,256,256]{2,1,0:T(8,128)} %mask.1) | copy-start | bytes 1572868
  9.5 12.9 %collective-permute-start.2 = (f32[5,8,128]{2,1,0:T(8,128)S(1)}, f32[5,8,128]{2,1,0:T(8,128)S(1)}, u32[]{:S(2)}, u32[]{:S(2)}) collective-permute-start(f32[5,8,128]{2,1,0:T(8,128)S(1)} %get-tuple-element.13), channel_id=1, source_target_pairs={{0,1},{1,0},{2,3},{3,2},{4,5},{5,4},{6,7},{7,6},{8,9},{9,8},{10,11... | collective-permute-start | bytes 61448 | tf_op jit(solution)/shard_map/ppermute | solution.py:203
  22.4 4.2 %collective-permute-start.3 = (f32[5,8,128]{2,1,0:T(8,128)S(1)}, f32[5,8,128]{2,1,0:T(8,128)S(1)}, u32[]{:S(2)}, u32[]{:S(2)}) collective-permute-start(f32[5,8,128]{2,1,0:T(8,128)S(1)} %add.21), channel_id=1, source_target_pairs={{0,2},{1,3},{2,0},{3,1},{4,6},{5,7},{6,4},{7,5},{8,10},{9,11},{10,... | collective-permute-start | bytes 61448 | tf_op jit(solution)/shard_map/ppermute | solution.py:203
  26.5 4.8 %collective-permute-start.4 = (f32[5,8,128]{2,1,0:T(8,128)S(1)}, f32[5,8,128]{2,1,0:T(8,128)S(1)}, u32[]{:S(2)}, u32[]{:S(2)}) collective-permute-start(f32[5,8,128]{2,1,0:T(8,128)S(1)} %add.22), channel_id=1, source_target_pairs={{0,4},{1,5},{2,6},{3,7},{4,0},{5,1},{6,2},{7,3},{8,12},{9,13},{10,... | collective-permute-start | bytes 61448 | tf_op jit(solution)/shard_map/ppermute | solution.py:203
  32.2 6.4 %collective-permute-start.6 = (f32[2,128,256]{2,1,0:T(8,128)S(1)}, f32[2,128,256]{2,1,0:T(8,128)S(1)}, u32[]{:S(2)}, u32[]{:S(2)}) collective-permute-start(f32[2,128,256]{2,1,0:T(8,128)S(1)} %get-tuple-element.17), channel_id=1, source_target_pairs={{0,8},{1,17},{2,10},{3,19},{4,12},{5,21},{6,14},{7,23},{8,0},{9,25... | collective-permute-start | bytes 786440 | tf_op jit(solution)/shard_map/ppermute | solution.py:218
  33.8 10.2 %collective-permute-start.8 = (f32[2,128,256]{2,1,0:T(8,128)S(1)}, f32[2,128,256]{2,1,0:T(8,128)S(1)}, u32[]{:S(2)}, u32[]{:S(2)}) collective-permute-start(f32[2,128,256]{2,1,0:T(8,128)S(1)} %get-tuple-element.18), channel_id=1, source_target_pairs={{0,8},{1,17},{2,10},{3,19},{4,12},{5,21},{6,14},{7,23},{8,0},{9,25... | collective-permute-start | bytes 786440 | tf_op jit(solution)/shard_map/ppermute | solution.py:218
  38.7 7.8 %collective-permute-start.7 = (f32[2,128,256]{2,1,0:T(8,128)S(1)}, f32[2,128,256]{2,1,0:T(8,128)S(1)}, u32[]{:S(2)}, u32[]{:S(2)}) collective-permute-start(f32[2,128,256]{2,1,0:T(8,128)S(1)} %add.24), channel_id=1, source_target_pairs={{0,16},{1,9},{2,18},{3,11},{4,20},{5,13},{6,22},{7,15},{8,24},{9,1... | collective-permute-start | bytes 786440 | tf_op jit(solution)/shard_map/ppermute | solution.py:218
  44.1 6.4 %collective-permute-start.9 = (f32[2,128,256]{2,1,0:T(8,128)S(1)}, f32[2,128,256]{2,1,0:T(8,128)S(1)}, u32[]{:S(2)}, u32[]{:S(2)}) collective-permute-start(f32[2,128,256]{2,1,0:T(8,128)S(1)} %add.26), channel_id=1, source_target_pairs={{0,16},{1,9},{2,18},{3,11},{4,20},{5,13},{6,22},{7,15},{8,24},{9,1... | collective-permute-start | bytes 786440 | tf_op jit(solution)/shard_map/ppermute | solution.py:218

commit v3 on v2

--- a/solution.py
+++ b/solution.py
@@ -12,7 +12,7 @@
 VMEM = pltpu.VMEM
 SMEM = pltpu.SMEM
 SUMS = 5
-CHUNKS = 2
+CHUNKS = 4
 
 
 def params():
@@ -60,7 +60,7 @@
         (load.at[even], far.at[1]),
         (load.at[odd], near.at[1]),
         (potential.at[even], far_potential.at[0]),
-        (potential.at[odd], near.at[3]),
+        (potential.at[odd], near.at[2]),
         (reluctivity, table),
     )
     copies = [pltpu.make_async_copy(src, dst, sems.at[i]) for i, (src, dst) in enumerate(moves)]
@@ -83,33 +83,37 @@
             )
     for copy in copies[2:-1]:
         copy.wait()
-    for own, other in ((far, near), (near, far)):
+
+
+def part_kernel(far, near, far_part, near_part):
+    total = far.shape[1]
+    for own, other, out in ((far, near, far_part), (near, far, near_part)):
         for start in range(0, total, ROWS):
             rows = slice(start, start + ROWS)
             nu, v, total_flux = in_plane(own, 0, own, 1, start)
             total_flux = total_flux + (nu + other[0, rows, :]) * (v - other[1, rows, :])
-            own[2, rows, :] = 0.5 * (v + total_flux)
+            out[0, rows, :] = 0.5 * (v + total_flux)
 
 
 def fold(value):
     return jnp.sum(value.reshape(ROWS // 8, 8, value.shape[1]), axis=0)
 
 
-def sums_kernel(far, near, far_in, near_in, image, image_in, sums):
+def sums_kernel(far, near, far_part, near_part, far_in, near_in, far_part_in, near_part_in, image, image_in, sums):
     slab, _ = place()
     count = lax.axis_size("slab")
     total, columns = far.shape[1:]
     beyond = jnp.where((slab > 0) & (slab < count - 1), 1.0, 0.0).astype(jnp.float32)
-    sides = ((far, far_in, beyond), (near, near_in, None))
+    sides = ((far, far_part, far_in, far_part_in, beyond), (near, near_part, near_in, near_part_in, None))
     nil = jnp.zeros((8, columns), jnp.float32)
     m0, m1 = nil, nil
-    for side, (own, halo, keep) in enumerate(sides):
+    for side, (own, part, halo, part_in, keep) in enumerate(sides):
         for start in range(0, total, ROWS):
             rows = slice(start, start + ROWS)
             v = own[1, rows, :]
             flux = 0.5 * (own[0, rows, :] + halo[0, rows, :]) * (v - halo[1, rows, :])
-            y = own[2, rows, :] + flux
-            outer = halo[2, rows, :] - flux
+            y = part[0, rows, :] + flux
+            outer = part_in[0, rows, :] - flux
             image[side, rows, :] = y
             image_in[side, rows, :] = outer if keep is None else keep * outer
             m0 = m0 + fold(v * v)
@@ -118,7 +122,7 @@
     m1 = jnp.sum(m1, keepdims=True)
     c = jnp.where(m0 > 0, m1 / m0, 0.0)
     q, s, t = nil, nil, nil
-    for side, (own, halo, _) in enumerate(sides):
+    for side, (own, _, halo, _, _) in enumerate(sides):
         for start in range(0, total, ROWS):
             rows = slice(start, start + ROWS)
             nu, y, total_flux = in_plane(own, 0, image, side, start)
@@ -158,7 +162,7 @@
     a = (alpha0 + alpha1 * (1.0 + beta))[:, 0:1]
     b = (-alpha1 * alpha0)[:, 0:1]
     scale = 0.25 / lax.axis_size("pos")
-    sides = ((far, even, far_in, far_potential, 0), (near, 1 - even, near_in, near_in, 3))
+    sides = ((far, even, far_in, far_potential, 0), (near, 1 - even, near_in, near_in, 2))
     for side, (own, layer, halo, halo_potential, at) in enumerate(sides):
         for start in range(0, total, ROWS):
             rows = slice(start, start + ROWS)
@@ -188,6 +192,14 @@
     return pltpu.with_memory_space_constraint(x, pltpu.HBM)
 
 
+def close_kernel(start, total, arrived, *rest):
+    gradient, held, sem = rest[-3:]
+    held[...] = total[...] + arrived[...]
+    copy = pltpu.make_async_copy(held, gradient.at[:, pl.ds(start, total.shape[1]), :], sem)
+    copy.start()
+    copy.wait()
+
+
 def pairs(size, first):
     out = []
     for i in range(first, size - 1, 2):
@@ -206,17 +218,19 @@
 
 
 def sum_positions(term, positions, slabs):
-    if positions & (positions - 1):
-        return lax.psum(term, "pos")
+    if positions & (positions - 1) or positions == 1:
+        return lax.psum(term, "pos"), jnp.zeros_like(term)
     bits = positions.bit_length() - 1
+    arrived = None
     for step in range(bits):
+        term = term if arrived is None else term + arrived
         route = []
         for p in range(positions):
             for s in range(slabs):
                 bit = step if s % 2 == 0 else bits - 1 - step
                 route.append((p * slabs + s, (p ^ (1 << bit)) * slabs + s))
-        term = term + lax.ppermute(term, ("pos", "slab"), route)
-    return term
+        arrived = lax.ppermute(term, ("pos", "slab"), route)
+    return term, arrived
 
 
 def local(labels, magnet_mask, reluctivity, rotor_shift, potential, adjoint_load):
@@ -232,7 +246,7 @@
     hbm = pl.BlockSpec(memory_space=pltpu.HBM)
     far, near, far_potential = pl.pallas_call(
         open_kernel,
-        out_shape=tuple(pltpu.VMEM((k,) + plane, jnp.float32) for k in (3, 4, 1)),
+        out_shape=tuple(pltpu.VMEM((k,) + plane, jnp.float32) for k in (2, 3, 1)),
         in_specs=[hbm, smem, hbm, hbm, hbm],
         out_specs=(vmem,) * 3,
         scratch_shapes=[
@@ -245,15 +259,25 @@
     )(in_hbm(reluctivity), rotor_shift, in_hbm(labels), in_hbm(load), in_hbm(potential))
     far_in = lax.ppermute(far, "slab", pairs(slabs, 1))
     near_in = lax.ppermute(near, "slab", pairs(slabs, 0))
+    far_part, near_part = pl.pallas_call(
+        part_kernel,
+        out_shape=(pltpu.VMEM((1,) + plane, jnp.float32),) * 2,
+        in_specs=[vmem] * 2,
+        out_specs=(vmem,) * 2,
+        compiler_params=params(),
+        name="part",
+    )(far, near)
+    far_part_in = lax.ppermute(far_part, "slab", pairs(slabs, 1))
+    near_part_in = lax.ppermute(near_part, "slab", pairs(slabs, 0))
     far_potential = lax.ppermute(far_potential, "slab", pairs(slabs, 1))
     image, image_in, sums = pl.pallas_call(
         sums_kernel,
         out_shape=(f32((2,) + plane), f32((2,) + plane), f32((SUMS, slabs, 128))),
-        in_specs=[vmem] * 4,
+        in_specs=[vmem] * 8,
         out_specs=(vmem,) * 3,
         compiler_params=params(),
         name="sums",
-    )(far, near, far_in, near_in)
+    )(far, near, far_part, near_part, far_in, near_in, far_part_in, near_part_in)
     sums = gather_sums(sums, "slab", slabs)
     adjoint, *terms = pl.pallas_call(
         finish_kernel,
@@ -265,8 +289,20 @@
         compiler_params=params(),
         name="finish",
     )(sums, far, near, far_in, near_in, image, image_in, potential, far_potential, magnet_mask)
-    gradient = [sum_positions(term, positions, slabs) for term in terms]
-    return jnp.concatenate(gradient, axis=1), adjoint[None]
+    span = radial // CHUNKS
+    gradient = ()
+    for index, (total, arrived) in enumerate([sum_positions(term, positions, slabs) for term in terms]):
+        gradient = pl.pallas_call(
+            functools.partial(close_kernel, index * span),
+            out_shape=pltpu.HBM((2,) + plane, jnp.float32),
+            in_specs=[vmem] * 2 + [hbm] * (index > 0),
+            out_specs=hbm,
+            scratch_shapes=[VMEM((2, span, angular), jnp.float32), pltpu.SemaphoreType.DMA(())],
+            input_output_aliases={2: 0} if index else {},
+            compiler_params=params(),
+            name="close",
+        )(total, arrived, *((gradient,) if index else ()))
+    return gradient, adjoint[None]
 
 
 def solution(mesh):

time: 51.6 us -> 49.8 us (0.965)
  waiting for transfers between devices: 17.3 us -> 9.77 us
  starting transfers between devices: 24.8 us -> 28.6 us
  Pallas kernels: 6.24 us -> 8.93 us
  other arithmetic: 0.98 us -> 0.08 us
    ppermute x4 -> x10, starting transfers between devices: 5.37 us -> 16.7 us  [the longest x8 10.8 us: sum_positions(): arrived = lax.ppermute(term, ('pos', 'slab'), route)]
    ppermute x3, starting transfers between devices: 17.5 us -> 10.1 us  [gather_sums(): sums = sums + lax.ppermute(sums, axis, [(i, i ^ step) for i in range(size)])]
    ppermute x4 -> x10, waiting for transfers between devices: 12 us -> 5.4 us  [the longest x8 4.92 us: sum_positions(): arrived = lax.ppermute(term, ('pos', 'slab'), route)]
    pallas_call x0 -> x5, Pallas kernels: none -> 4.67 us  [the longest x4 2.72 us: local(): pl.pallas_call(functools.partial(close_kernel, index * span), out_shape=p...]
    pallas_call x1, Pallas kernels: 3.37 us -> 1.42 us  [local(): pl.pallas_call(open_kernel, out_shape=tuple((pltpu.VMEM((k,) + plane, jnp...]
    ppermute x1, waiting for transfers between devices: 0.88 us -> 0.01 us  [local(): near_in = lax.ppermute(near, 'slab', pairs(slabs, 0))]
    concatenate x1 -> x0, other arithmetic: 0.83 us -> none  [local(): return (jnp.concatenate(gradient, axis=1), adjoint[None])]
  transfers between devices with their start and end apart: 10 -> 16, of which waited for: 7 -> 9; matrix products, arithmetic and copies ran while one was open for 2% -> 2% of each run, Pallas kernels for 4% -> 12%
where the time goes in v3:
time: 49.8 us; the launch traced here: 49.6 us
  starting transfers between devices  28.6 us (57%)
  waiting for transfers between devices  9.77 us (20%)
  Pallas kernels  8.93 us (18%)
  between operations  1.43 us (3%)
  local copies, waits for them, and re-layouts  0.8 us (2%)
    ppermute x8, starting transfers between devices, sum_positions(): arrived = lax.ppermute(term, ('pos', 'slab'), route)  10.8 us
    ppermute x3, starting transfers between devices, gather_sums(): sums = sums + lax.ppermute(sums, axis, [(i, i ^ step) for i in range(size)])  10.1 us
    ppermute x1, starting transfers between devices, local(): near_part_in = lax.ppermute(near_part, 'slab', pairs(slabs, 0))  5.23 us
    ppermute x8, waiting for transfers between devices, sum_positions(): arrived = lax.ppermute(term, ('pos', 'slab'), route)  4.92 us
    ppermute x3, waiting for transfers between devices, gather_sums(): sums = sums + lax.ppermute(sums, axis, [(i, i ^ step) for i in range(size)])  4.36 us
    pallas_call x4, Pallas kernels, local(): pl.pallas_call(functools.partial(close_kernel, index * span), out_shape=p...  2.72 us
    pallas_call x1, Pallas kernels, local(): pl.pallas_call(sums_kernel, out_shape=(f32((2,) + plane), f32((2,) + plan...  2 us
    pallas_call x1, Pallas kernels, local(): pl.pallas_call(part_kernel, out_shape=(pltpu.VMEM((1,) + plane, jnp.float...  1.95 us
  transfers between devices with their start and end apart: 16, of which 9 were waited for; matrix products, arithmetic and copies ran while one was open for 2% of the time, Pallas kernels for 12%

profile of v3, /device:TPU:0, one launch (start us, length us, event | category | flops | bytes accessed | tf_op | source)
XLA Modules:
  0.0 49.6 jit_solution(16996040203791604738)
XLA Ops:
  1.3 1.4 %open.1 = (f32[2,256,256]{2,1,0:T(8,128)S(1)}, f32[3,256,256]{2,1,0:T(8,128)S(1)}, f32[1,256,256]{2,1,0:T(8,128)S(1)}) custom-call(f32[4]{0:T(128)} %reluctivity.1, s32[1]{0:T(128)S(6)} %copy.15.shift, s32[2,256,256]{2,1,0:T(8,128)} %labels.1, f32[2,256,256]{2,1,0:T(8,128)} %bitcast.6, f32[2,256,256]{2,1,0:T(8,128)} %bitcast.4), custom_call_target="tpu_custom_call" | custom-call | tf_op jit(solution)/shard_map/open/pallas_call | solution.py:247
  3.2 0.7 %collective-permute-start = (f32[2,256,256]{2,1,0:T(8,128)S(1)}, f32[2,256,256]{2,1,0:T(8,128)S(1)}, u32[]{:S(2)}, u32[]{:S(2)}) collective-permute-start(f32[2,256,256]{2,1,0:T(8,128)S(1)} %get-tuple-element.15.far), channel_id=1, source_target_pairs={{1,2},{2,1},{3,4},{4,3},{5,6},{6,5},{9,10},{10,9},{11,12},{12,11},... | collective-permute-start | bytes 1572872 | tf_op jit(solution)/shard_map/ppermute | solution.py:260
  3.9 1.9 %part.1 = (f32[1,256,256]{2,1,0:T(8,128)S(1)}, f32[1,256,256]{2,1,0:T(8,128)S(1)}) custom-call(f32[2,256,256]{2,1,0:T(8,128)S(1)} %get-tuple-element.15.far, f32[3,256,256]{2,1,0:T(8,128)S(1)} %get-tuple-element.16.near), custom_call_target="tpu_custom_call" | custom-call | tf_op jit(solution)/shard_map/part/pallas_call | solution.py:262
  6.5 5.2 %collective-permute-start.3 = (f32[1,256,256]{2,1,0:T(8,128)S(1)}, f32[1,256,256]{2,1,0:T(8,128)S(1)}, u32[]{:S(2)}, u32[]{:S(2)}) collective-permute-start(f32[1,256,256]{2,1,0:T(8,128)S(1)} %get-tuple-element.18.near_part), channel_id=1, source_target_pairs={{0,1},{1,0},{2,3},{3,2},{4,5},{5,4},{6,7},{7,6},{8,9},{9,8},{10,11... | collective-permute-start | bytes 786440 | tf_op jit(solution)/shard_map/ppermute | solution.py:271
  13.0 2.0 %sums.1 = (f32[2,256,256]{2,1,0:T(8,128)S(1)}, f32[2,256,256]{2,1,0:T(8,128)S(1)}, f32[5,8,128]{2,1,0:T(8,128)S(1)}) custom-call(f32[2,256,256]{2,1,0:T(8,128)S(1)} %get-tuple-element.15.far, f32[3,256,256]{2,1,0:T(8,128)S(1)} %get-tuple-element.16.near, f32[1,256,256]{2,1,0:T(8,128)S(1)} %get-tuple-element.17.far_part, ...), custom_call_target="tpu_custom_call" | custom-call | tf_op jit(solution)/shard_map/sums/pallas_call | solution.py:273
  15.0 4.6 %collective-permute-start.4 = (f32[5,8,128]{2,1,0:T(8,128)S(1)}, f32[5,8,128]{2,1,0:T(8,128)S(1)}, u32[]{:S(2)}, u32[]{:S(2)}) collective-permute-start(f32[5,8,128]{2,1,0:T(8,128)S(1)} %get-tuple-element.19), channel_id=1, source_target_pairs={{0,1},{1,0},{2,3},{3,2},{4,5},{5,4},{6,7},{7,6},{8,9},{9,8},{10,11... | collective-permute-start | bytes 61448 | tf_op jit(solution)/shard_map/ppermute | solution.py:215
  19.6 0.8 %collective-permute-done.4 = f32[5,8,128]{2,1,0:T(8,128)S(1)} collective-permute-done((f32[5,8,128]{2,1,0:T(8,128)S(1)}, f32[5,8,128]{2,1,0:T(8,128)S(1)}, u32[]{:S(2)}, u32[]{:S(2)}) %collective-permute-start.4) | collective-permute-done | bytes 20512 | tf_op jit(solution)/shard_map/ppermute | solution.py:215
  20.4 2.4 %collective-permute-start.5 = (f32[5,8,128]{2,1,0:T(8,128)S(1)}, f32[5,8,128]{2,1,0:T(8,128)S(1)}, u32[]{:S(2)}, u32[]{:S(2)}) collective-permute-start(f32[5,8,128]{2,1,0:T(8,128)S(1)} %add.21), channel_id=1, source_target_pairs={{0,2},{1,3},{2,0},{3,1},{4,6},{5,7},{6,4},{7,5},{8,10},{9,11},{10,... | collective-permute-start | bytes 61448 | tf_op jit(solution)/shard_map/ppermute | solution.py:215
  22.8 1.8 %collective-permute-done.5 = f32[5,8,128]{2,1,0:T(8,128)S(1)} collective-permute-done((f32[5,8,128]{2,1,0:T(8,128)S(1)}, f32[5,8,128]{2,1,0:T(8,128)S(1)}, u32[]{:S(2)}, u32[]{:S(2)}) %collective-permute-start.5) | collective-permute-done | bytes 20512 | tf_op jit(solution)/shard_map/ppermute | solution.py:215
  24.6 3.0 %collective-permute-start.6 = (f32[5,8,128]{2,1,0:T(8,128)S(1)}, f32[5,8,128]{2,1,0:T(8,128)S(1)}, u32[]{:S(2)}, u32[]{:S(2)}) collective-permute-start(f32[5,8,128]{2,1,0:T(8,128)S(1)} %add.22), channel_id=1, source_target_pairs={{0,4},{1,5},{2,6},{3,7},{4,0},{5,1},{6,2},{7,3},{8,12},{9,13},{10,... | collective-permute-start | bytes 61448 | tf_op jit(solution)/shard_map/ppermute | solution.py:215
  27.6 1.8 %collective-permute-done.6 = f32[5,8,128]{2,1,0:T(8,128)S(1)} collective-permute-done((f32[5,8,128]{2,1,0:T(8,128)S(1)}, f32[5,8,128]{2,1,0:T(8,128)S(1)}, u32[]{:S(2)}, u32[]{:S(2)}) %collective-permute-start.6) | collective-permute-done | bytes 20512 | tf_op jit(solution)/shard_map/ppermute | solution.py:215
  29.4 0.9 %finish.1 = (f32[2,256,256]{2,1,0:T(8,128)S(1)}, f32[2,64,256]{2,1,0:T(8,128)S(1)}, f32[2,64,256]{2,1,0:T(8,128)S(1)}, f32[2,64,256]{2,1,0:T(8,128)S(1)}, f32[2,64,256]{2,1,0:T(8,128)S(1)}) custom-call(f32[5,8,128]{2,1,0:T(8,128)S(1)} %add.23.sums, f32[2,256,256]{2,1,0:T(8,128)S(1)} %get-tuple-element.15.far, f32[3,256,256]{2,1,0:T(8,128)S(1)} %get-tuple-element.16.near, ...), custom_call_target="tpu_custom_call" | custom-call | tf_op jit(solution)/shard_map/finish/pallas_call | solution.py:282
  30.3 1.6 %collective-permute-start.12 = (f32[2,64,256]{2,1,0:T(8,128)S(1)}, f32[2,64,256]{2,1,0:T(8,128)S(1)}, u32[]{:S(2)}, u32[]{:S(2)}) collective-permute-start(f32[2,64,256]{2,1,0:T(8,128)S(1)} %get-tuple-element.25), channel_id=1, source_target_pairs={{0,8},{1,17},{2,10},{3,19},{4,12},{5,21},{6,14},{7,23},{8,0},{9,25... | collective-permute-start | bytes 393224 | tf_op jit(solution)/shard_map/ppermute | solution.py:232
  32.4 1.5 %collective-permute-start.10 = (f32[2,64,256]{2,1,0:T(8,128)S(1)}, f32[2,64,256]{2,1,0:T(8,128)S(1)}, u32[]{:S(2)}, u32[]{:S(2)}) collective-permute-start(f32[2,64,256]{2,1,0:T(8,128)S(1)} %get-tuple-element.24), channel_id=1, source_target_pairs={{0,8},{1,17},{2,10},{3,19},{4,12},{5,21},{6,14},{7,23},{8,0},{9,25... | collective-permute-start | bytes 393224 | tf_op jit(solution)/shard_map/ppermute | solution.py:232
  34.4 1.0 %collective-permute-done.12 = f32[2,64,256]{2,1,0:T(8,128)S(1)} collective-permute-done((f32[2,64,256]{2,1,0:T(8,128)S(1)}, f32[2,64,256]{2,1,0:T(8,128)S(1)}, u32[]{:S(2)}, u32[]{:S(2)}) %collective-permute-start.12) | collective-permute-done | bytes 131104 | tf_op jit(solution)/shard_map/ppermute | solution.py:232
  35.5 1.7 %collective-permute-start.13 = (f32[2,64,256]{2,1,0:T(8,128)S(1)}, f32[2,64,256]{2,1,0:T(8,128)S(1)}, u32[]{:S(2)}, u32[]{:S(2)}) collective-permute-start(f32[2,64,256]{2,1,0:T(8,128)S(1)} %add.26.total), channel_id=1, source_target_pairs={{0,16},{1,9},{2,18},{3,11},{4,20},{5,13},{6,22},{7,15},{8,24},{9,1... | collective-permute-start | bytes 393224 | tf_op jit(solution)/shard_map/ppermute | solution.py:232
  37.1 1.1 %collective-permute-done.14 = f32[2,64,256]{2,1,0:T(8,128)S(1)} collective-permute-done((f32[2,64,256]{2,1,0:T(8,128)S(1)}, f32[2,64,256]{2,1,0:T(8,128)S(1)}, u32[]{:S(2)}, u32[]{:S(2)}) %collective-permute-start.14) | collective-permute-done | bytes 131104 | tf_op jit(solution)/shard_map/ppermute | solution.py:232
  38.3 1.7 %collective-permute-start.15 = (f32[2,64,256]{2,1,0:T(8,128)S(1)}, f32[2,64,256]{2,1,0:T(8,128)S(1)}, u32[]{:S(2)}, u32[]{:S(2)}) collective-permute-start(f32[2,64,256]{2,1,0:T(8,128)S(1)} %add.27.total), channel_id=1, source_target_pairs={{0,16},{1,9},{2,18},{3,11},{4,20},{5,13},{6,22},{7,15},{8,24},{9,1... | collective-permute-start | bytes 393224 | tf_op jit(solution)/shard_map/ppermute | solution.py:232
  39.9 1.1 %collective-permute-done.10 = f32[2,64,256]{2,1,0:T(8,128)S(1)} collective-permute-done((f32[2,64,256]{2,1,0:T(8,128)S(1)}, f32[2,64,256]{2,1,0:T(8,128)S(1)}, u32[]{:S(2)}, u32[]{:S(2)}) %collective-permute-start.10) | collective-permute-done | bytes 131104 | tf_op jit(solution)/shard_map/ppermute | solution.py:232
  41.1 1.7 %collective-permute-start.11 = (f32[2,64,256]{2,1,0:T(8,128)S(1)}, f32[2,64,256]{2,1,0:T(8,128)S(1)}, u32[]{:S(2)}, u32[]{:S(2)}) collective-permute-start(f32[2,64,256]{2,1,0:T(8,128)S(1)} %add.25.total), channel_id=1, source_target_pairs={{0,16},{1,9},{2,18},{3,11},{4,20},{5,13},{6,22},{7,15},{8,24},{9,1... | collective-permute-start | bytes 393224 | tf_op jit(solution)/shard_map/ppermute | solution.py:232
  42.7 1.1 %collective-permute-done.8 = f32[2,64,256]{2,1,0:T(8,128)S(1)} collective-permute-done((f32[2,64,256]{2,1,0:T(8,128)S(1)}, f32[2,64,256]{2,1,0:T(8,128)S(1)}, u32[]{:S(2)}, u32[]{:S(2)}) %collective-permute-start.8) | collective-permute-done | bytes 131104 | tf_op jit(solution)/shard_map/ppermute | solution.py:232
  43.9 1.7 %collective-permute-start.9 = (f32[2,64,256]{2,1,0:T(8,128)S(1)}, f32[2,64,256]{2,1,0:T(8,128)S(1)}, u32[]{:S(2)}, u32[]{:S(2)}) collective-permute-start(f32[2,64,256]{2,1,0:T(8,128)S(1)} %add.24.total), channel_id=1, source_target_pairs={{0,16},{1,9},{2,18},{3,11},{4,20},{5,13},{6,22},{7,15},{8,24},{9,1... | collective-permute-start | bytes 393224 | tf_op jit(solution)/shard_map/ppermute | solution.py:232
  45.6 0.8 %copy.14 = f32[1,2,256,256]{3,2,1,0:T(8,128)} copy(f32[1,2,256,256]{3,2,1,0:T(8,128)S(1)} %bitcast.3) | data formatting | bytes 1048576
  47.1 0.7 %close.5.rest_0_ = f32[2,256,256]{2,1,0:T(8,128)} custom-call(f32[2,64,256]{2,1,0:T(8,128)S(1)} %add.26.total, f32[2,64,256]{2,1,0:T(8,128)S(1)} %collective-permute-done.13.arrived, f32[2,256,256]{2,1,0:T(8,128)} %close.4.rest_0_), custom_call_target="tpu_custom_call", output_to_operand_aliasing={{}: (2, {})} | custom-call | tf_op jit(solution)/shard_map/close/pallas_call | solution.py:295
  (28 shorter events, 6.0 us)
Async XLA Ops:
  2.7 10.3 %collective-permute-start.1 = (f32[3,256,256]{2,1,0:T(8,128)S(1)}, f32[3,256,256]{2,1,0:T(8,128)S(1)}, u32[]{:S(2)}, u32[]{:S(2)}) collective-permute-start(f32[3,256,256]{2,1,0:T(8,128)S(1)} %get-tuple-element.16.near), channel_id=1, source_target_pairs={{0,1},{1,0},{2,3},{3,2},{4,5},{5,4},{6,7},{7,6},{8,9},{9,8},{10,11... | collective-permute-start | bytes 2359304 | tf_op jit(solution)/shard_map/ppermute | solution.py:261
  3.2 9.7 %collective-permute-start = (f32[2,256,256]{2,1,0:T(8,128)S(1)}, f32[2,256,256]{2,1,0:T(8,128)S(1)}, u32[]{:S(2)}, u32[]{:S(2)}) collective-permute-start(f32[2,256,256]{2,1,0:T(8,128)S(1)} %get-tuple-element.15.far), channel_id=1, source_target_pairs={{1,2},{2,1},{3,4},{4,3},{5,6},{6,5},{9,10},{10,9},{11,12},{12,11},... | collective-permute-start | bytes 1572872 | tf_op jit(solution)/shard_map/ppermute | solution.py:260
  5.9 6.6 %collective-permute-start.2 = (f32[1,256,256]{2,1,0:T(8,128)S(1)}, f32[1,256,256]{2,1,0:T(8,128)S(1)}, u32[]{:S(2)}, u32[]{:S(2)}) collective-permute-start(f32[1,256,256]{2,1,0:T(8,128)S(1)} %get-tuple-element.17.far_part), channel_id=1, source_target_pairs={{1,2},{2,1},{3,4},{4,3},{5,6},{6,5},{9,10},{10,9},{11,12},{12,11},... | collective-permute-start | bytes 786440 | tf_op jit(solution)/shard_map/ppermute | solution.py:270
  6.5 6.4 %collective-permute-start.3 = (f32[1,256,256]{2,1,0:T(8,128)S(1)}, f32[1,256,256]{2,1,0:T(8,128)S(1)}, u32[]{:S(2)}, u32[]{:S(2)}) collective-permute-start(f32[1,256,256]{2,1,0:T(8,128)S(1)} %get-tuple-element.18.near_part), channel_id=1, source_target_pairs={{0,1},{1,0},{2,3},{3,2},{4,5},{5,4},{6,7},{7,6},{8,9},{9,8},{10,11... | collective-permute-start | bytes 786440 | tf_op jit(solution)/shard_map/ppermute | solution.py:271
  11.8 17.6 %collective-permute-start.7 = (f32[1,256,256]{2,1,0:T(8,128)S(1)}, f32[1,256,256]{2,1,0:T(8,128)S(1)}, u32[]{:S(2)}, u32[]{:S(2)}) collective-permute-start(f32[1,256,256]{2,1,0:T(8,128)S(1)} %get-tuple-element.22), channel_id=1, source_target_pairs={{1,2},{2,1},{3,4},{4,3},{5,6},{6,5},{9,10},{10,9},{11,12},{12,11},... | collective-permute-start | bytes 786440 | tf_op jit(solution)/shard_map/ppermute | solution.py:272
  13.0 16.5 %copy-start = (f32[1,2,256,256]{3,2,1,0:T(8,128)S(1)}, f32[1,2,256,256]{3,2,1,0:T(8,128)}, u32[]{:S(2)}) copy-start(f32[1,2,256,256]{3,2,1,0:T(8,128)} %param.10) | copy-start | bytes 1572868
  13.0 16.5 %copy-start.1 = (s32[2,256,256]{2,1,0:T(8,128)S(1)}, s32[2,256,256]{2,1,0:T(8,128)}, u32[]{:S(2)}) copy-start(s32[2,256,256]{2,1,0:T(8,128)} %mask.1) | copy-start | bytes 1572868
  15.0 5.5 %collective-permute-start.4 = (f32[5,8,128]{2,1,0:T(8,128)S(1)}, f32[5,8,128]{2,1,0:T(8,128)S(1)}, u32[]{:S(2)}, u32[]{:S(2)}) collective-permute-start(f32[5,8,128]{2,1,0:T(8,128)S(1)} %get-tuple-element.19), channel_id=1, source_target_pairs={{0,1},{1,0},{2,3},{3,2},{4,5},{5,4},{6,7},{7,6},{8,9},{9,8},{10,11... | collective-permute-start | bytes 61448 | tf_op jit(solution)/shard_map/ppermute | solution.py:215
  20.4 4.2 %collective-permute-start.5 = (f32[5,8,128]{2,1,0:T(8,128)S(1)}, f32[5,8,128]{2,1,0:T(8,128)S(1)}, u32[]{:S(2)}, u32[]{:S(2)}) collective-permute-start(f32[5,8,128]{2,1,0:T(8,128)S(1)} %add.21), channel_id=1, source_target_pairs={{0,2},{1,3},{2,0},{3,1},{4,6},{5,7},{6,4},{7,5},{8,10},{9,11},{10,... | collective-permute-start | bytes 61448 | tf_op jit(solution)/shard_map/ppermute | solution.py:215
  24.6 4.8 %collective-permute-start.6 = (f32[5,8,128]{2,1,0:T(8,128)S(1)}, f32[5,8,128]{2,1,0:T(8,128)S(1)}, u32[]{:S(2)}, u32[]{:S(2)}) collective-permute-start(f32[5,8,128]{2,1,0:T(8,128)S(1)} %add.22), channel_id=1, source_target_pairs={{0,4},{1,5},{2,6},{3,7},{4,0},{5,1},{6,2},{7,3},{8,12},{9,13},{10,... | collective-permute-start | bytes 61448 | tf_op jit(solution)/shard_map/ppermute | solution.py:215
  30.3 5.1 %collective-permute-start.12 = (f32[2,64,256]{2,1,0:T(8,128)S(1)}, f32[2,64,256]{2,1,0:T(8,128)S(1)}, u32[]{:S(2)}, u32[]{:S(2)}) collective-permute-start(f32[2,64,256]{2,1,0:T(8,128)S(1)} %get-tuple-element.25), channel_id=1, source_target_pairs={{0,8},{1,17},{2,10},{3,19},{4,12},{5,21},{6,14},{7,23},{8,0},{9,25... | collective-permute-start | bytes 393224 | tf_op jit(solution)/shard_map/ppermute | solution.py:232
  31.9 6.4 %collective-permute-start.14 = (f32[2,64,256]{2,1,0:T(8,128)S(1)}, f32[2,64,256]{2,1,0:T(8,128)S(1)}, u32[]{:S(2)}, u32[]{:S(2)}) collective-permute-start(f32[2,64,256]{2,1,0:T(8,128)S(1)} %get-tuple-element.26), channel_id=1, source_target_pairs={{0,8},{1,17},{2,10},{3,19},{4,12},{5,21},{6,14},{7,23},{8,0},{9,25... | collective-permute-start | bytes 393224 | tf_op jit(solution)/shard_map/ppermute | solution.py:232
  32.4 8.7 %collective-permute-start.10 = (f32[2,64,256]{2,1,0:T(8,128)S(1)}, f32[2,64,256]{2,1,0:T(8,128)S(1)}, u32[]{:S(2)}, u32[]{:S(2)}) collective-permute-start(f32[2,64,256]{2,1,0:T(8,128)S(1)} %get-tuple-element.24), channel_id=1, source_target_pairs={{0,8},{1,17},{2,10},{3,19},{4,12},{5,21},{6,14},{7,23},{8,0},{9,25... | collective-permute-start | bytes 393224 | tf_op jit(solution)/shard_map/ppermute | solution.py:232
  33.9 10.0 %collective-permute-start.8 = (f32[2,64,256]{2,1,0:T(8,128)S(1)}, f32[2,64,256]{2,1,0:T(8,128)S(1)}, u32[]{:S(2)}, u32[]{:S(2)}) collective-permute-start(f32[2,64,256]{2,1,0:T(8,128)S(1)} %get-tuple-element.23), channel_id=1, source_target_pairs={{0,8},{1,17},{2,10},{3,19},{4,12},{5,21},{6,14},{7,23},{8,0},{9,25... | collective-permute-start | bytes 393224 | tf_op jit(solution)/shard_map/ppermute | solution.py:232
  35.5 11.6 %collective-permute-start.13 = (f32[2,64,256]{2,1,0:T(8,128)S(1)}, f32[2,64,256]{2,1,0:T(8,128)S(1)}, u32[]{:S(2)}, u32[]{:S(2)}) collective-permute-start(f32[2,64,256]{2,1,0:T(8,128)S(1)} %add.26.total), channel_id=1, source_target_pairs={{0,16},{1,9},{2,18},{3,11},{4,20},{5,13},{6,22},{7,15},{8,24},{9,1... | collective-permute-start | bytes 393224 | tf_op jit(solution)/shard_map/ppermute | solution.py:232
  38.3 8.1 %collective-permute-start.15 = (f32[2,64,256]{2,1,0:T(8,128)S(1)}, f32[2,64,256]{2,1,0:T(8,128)S(1)}, u32[]{:S(2)}, u32[]{:S(2)}) collective-permute-start(f32[2,64,256]{2,1,0:T(8,128)S(1)} %add.27.total), channel_id=1, source_target_pairs={{0,16},{1,9},{2,18},{3,11},{4,20},{5,13},{6,22},{7,15},{8,24},{9,1... | collective-permute-start | bytes 393224 | tf_op jit(solution)/shard_map/ppermute | solution.py:232
  41.1 6.7 %collective-permute-start.11 = (f32[2,64,256]{2,1,0:T(8,128)S(1)}, f32[2,64,256]{2,1,0:T(8,128)S(1)}, u32[]{:S(2)}, u32[]{:S(2)}) collective-permute-start(f32[2,64,256]{2,1,0:T(8,128)S(1)} %add.25.total), channel_id=1, source_target_pairs={{0,16},{1,9},{2,18},{3,11},{4,20},{5,13},{6,22},{7,15},{8,24},{9,1... | collective-permute-start | bytes 393224 | tf_op jit(solution)/shard_map/ppermute | solution.py:232
  43.9 5.0 %collective-permute-start.9 = (f32[2,64,256]{2,1,0:T(8,128)S(1)}, f32[2,64,256]{2,1,0:T(8,128)S(1)}, u32[]{:S(2)}, u32[]{:S(2)}) collective-permute-start(f32[2,64,256]{2,1,0:T(8,128)S(1)} %add.24.total), channel_id=1, source_target_pairs={{0,16},{1,9},{2,18},{3,11},{4,20},{5,13},{6,22},{7,15},{8,24},{9,1... | collective-permute-start | bytes 393224 | tf_op jit(solution)/shard_map/ppermute | solution.py:232

commit v4 on v3

--- a/solution.py
+++ b/solution.py
@@ -12,7 +12,7 @@
 VMEM = pltpu.VMEM
 SMEM = pltpu.SMEM
 SUMS = 5
-CHUNKS = 4
+CHUNKS = 2
 
 
 def params():
@@ -99,36 +99,34 @@
     return jnp.sum(value.reshape(ROWS // 8, 8, value.shape[1]), axis=0)
 
 
-def sums_kernel(far, near, far_part, near_part, far_in, near_in, far_part_in, near_part_in, image, image_in, sums):
-    slab, _ = place()
-    count = lax.axis_size("slab")
+def sums_kernel(far, near, far_part, near_part, far_in, near_in, near_part_in, image, near_image_in, sums):
     total, columns = far.shape[1:]
-    beyond = jnp.where((slab > 0) & (slab < count - 1), 1.0, 0.0).astype(jnp.float32)
-    sides = ((far, far_part, far_in, far_part_in, beyond), (near, near_part, near_in, near_part_in, None))
+    sides = ((far, far_part, far_in), (near, near_part, near_in))
     nil = jnp.zeros((8, columns), jnp.float32)
     m0, m1 = nil, nil
-    for side, (own, part, halo, part_in, keep) in enumerate(sides):
+    for side, (own, part, halo) in enumerate(sides):
         for start in range(0, total, ROWS):
             rows = slice(start, start + ROWS)
             v = own[1, rows, :]
             flux = 0.5 * (own[0, rows, :] + halo[0, rows, :]) * (v - halo[1, rows, :])
             y = part[0, rows, :] + flux
-            outer = part_in[0, rows, :] - flux
             image[side, rows, :] = y
-            image_in[side, rows, :] = outer if keep is None else keep * outer
+            if own is near:
+                near_image_in[0, rows, :] = near_part_in[0, rows, :] - flux
             m0 = m0 + fold(v * v)
             m1 = m1 + fold(v * y)
     m0 = jnp.sum(m0, keepdims=True)
     m1 = jnp.sum(m1, keepdims=True)
     c = jnp.where(m0 > 0, m1 / m0, 0.0)
     q, s, t = nil, nil, nil
-    for side, (own, _, halo, _, _) in enumerate(sides):
+    for side, (own, _, halo) in enumerate(sides):
         for start in range(0, total, ROWS):
             rows = slice(start, start + ROWS)
             nu, y, total_flux = in_plane(own, 0, image, side, start)
             other = (near, far)[side]
             total_flux = total_flux + (nu + other[0, rows, :]) * (y - image[1 - side, rows, :])
-            total_flux = total_flux + (nu + halo[0, rows, :]) * (y - image_in[side, rows, :])
+            if own is near:
+                total_flux = total_flux + (nu + halo[0, rows, :]) * (y - near_image_in[0, rows, :])
             z = 0.5 * (y + total_flux)
             v = own[1, rows, :]
             w = y - c * v
@@ -136,16 +134,42 @@
             q = q + fold(w * w)
             s = s + fold(w * u)
             t = t + fold(v * u)
+    for index, value in enumerate((m0, m1, q, s, t, c)):
+        value = jnp.sum(value, keepdims=True) if value.shape[0] > 1 else value
+        sums[index : index + 1, :] = jnp.broadcast_to(value, (1, sums.shape[1]))
+
+
+def face_kernel(far, far_in, far_part_in, image, own_sums, far_image_in, sums):
+    slab, _ = place()
+    count = lax.axis_size("slab")
+    total, columns = far.shape[1:]
+    beyond = jnp.where((slab > 0) & (slab < count - 1), 1.0, 0.0).astype(jnp.float32)
+    c = own_sums[SUMS : SUMS + 1, 0:1]
+    s = jnp.zeros((8, columns), jnp.float32)
+    t = s
+    for start in range(0, total, ROWS):
+        rows = slice(start, start + ROWS)
+        v = far[1, rows, :]
+        y = image[0, rows, :]
+        weight = 0.5 * (far[0, rows, :] + far_in[0, rows, :])
+        outer = beyond * (far_part_in[0, rows, :] - weight * (v - far_in[1, rows, :]))
+        far_image_in[0, rows, :] = outer
+        flux = weight * (y - outer)
+        s = s + fold((y - c * v) * flux)
+        t = t + fold(v * flux)
     here = lax.broadcasted_iota(jnp.int32, sums.shape[1:], 0) == slab
-    for index, value in enumerate((m0, m1, q, s, t)):
-        value = jnp.sum(value, keepdims=True) if index > 1 else value
+    added = (None, None, None, s, t)
+    for index in range(SUMS):
+        value = own_sums[index : index + 1, :]
+        if added[index] is not None:
+            value = value + jnp.sum(added[index], keepdims=True)
         sums[index] = jnp.where(here, value, 0.0)
 
 
 def finish_kernel(
-    sums, far, near, far_in, near_in, image, image_in, potential, far_potential, mask, adjoint, *rest
+    sums, far, near, far_in, near_in, image, far_image_in, near_image_in, potential, far_potential, mask, adjoint, *rest
 ):
-    *terms, mixed, mixed_in = rest
+    *pieces, mixed, mixed_in, term = rest
     _, even = place()
     total = far.shape[1]
     m0_d, m1_d, q_d, s_d, t_d = (sums[i] for i in range(SUMS))
@@ -162,16 +186,16 @@
     a = (alpha0 + alpha1 * (1.0 + beta))[:, 0:1]
     b = (-alpha1 * alpha0)[:, 0:1]
     scale = 0.25 / lax.axis_size("pos")
-    sides = ((far, even, far_in, far_potential, 0), (near, 1 - even, near_in, near_in, 2))
-    for side, (own, layer, halo, halo_potential, at) in enumerate(sides):
+    sides = ((far, even, far_in, far_image_in, far_potential, 0), (near, 1 - even, near_in, near_image_in, near_in, 2))
+    for side, (own, layer, halo, image_in, halo_potential, at) in enumerate(sides):
         for start in range(0, total, ROWS):
             rows = slice(start, start + ROWS)
             out = a * own[1, rows, :] + b * image[side, rows, :]
             adjoint[layer, rows, :] = out
             mixed[side, rows, :] = out + 0.5 * potential[layer, rows, :]
-            outer = a * halo[1, rows, :] + b * image_in[side, rows, :]
+            outer = a * halo[1, rows, :] + b * image_in[0, rows, :]
             mixed_in[side, rows, :] = outer + 0.5 * halo_potential[at, rows, :]
-    for side, (own, layer, halo, halo_potential, at) in enumerate(sides):
+    for side, (own, layer, halo, image_in, halo_potential, at) in enumerate(sides):
         for start in range(0, total, ROWS):
             rows = slice(start, start + ROWS)
             g = potential[layer, rows, :]
@@ -184,20 +208,40 @@
                 shifted(potential, layer, start, 1) - shifted(potential, layer, start, -1)
             ) * (shifted(mixed, side, start, 1) - shifted(mixed, side, start, -1))
             weight = mask[layer, rows, :].astype(jnp.float32) * own[0, rows, :]
-            span = total // CHUNKS
-            terms[start // span][layer, start % span : start % span + ROWS, :] = weight * (scale * result)
+            term[layer, rows, :] = weight * (scale * result)
+    first = own_half()
+    span = pieces[0].shape[1]
+    for index, piece in enumerate(pieces):
+        half = first if index < CHUNKS else 1 - first
+        base = pl.multiple_of(half * (total // 2) + index % CHUNKS * span, 8)
+        for layer in range(2):
+            piece[layer] = term[layer, pl.ds(base, span), :]
 
 
 def in_hbm(x):
     return pltpu.with_memory_space_constraint(x, pltpu.HBM)
 
 
-def close_kernel(start, total, arrived, *rest):
-    gradient, held, sem = rest[-3:]
-    held[...] = total[...] + arrived[...]
-    copy = pltpu.make_async_copy(held, gradient.at[:, pl.ds(start, total.shape[1]), :], sem)
-    copy.start()
-    copy.wait()
+def own_half():
+    bits = lax.axis_size("pos").bit_length() - 1
+    position = lax.axis_index("pos")
+    _, even = place()
+    return jnp.where(even == 0, lax.rem(position, 2), lax.rem(lax.div(position, 2 ** (bits - 1)), 2))
+
+
+def close_kernel(given, first_chunk, *rest):
+    gradient, sems = rest[-2:]
+    count = sems.shape[0]
+    span = rest[0].shape[1]
+    half = 1 - own_half() if given else own_half()
+    copies = []
+    for index in range(count):
+        base = pl.multiple_of(half * (gradient.shape[1] // 2) + (first_chunk + index) * span, 8)
+        copies.append(pltpu.make_async_copy(rest[index], gradient.at[:, pl.ds(base, span), :], sems.at[index]))
+    for copy in copies:
+        copy.start()
+    for copy in copies:
+        copy.wait()
 
 
 def pairs(size, first):
@@ -217,26 +261,28 @@
     return sums
 
 
-def sum_positions(term, positions, slabs):
-    if positions & (positions - 1) or positions == 1:
-        return lax.psum(term, "pos"), jnp.zeros_like(term)
+def partners(step, positions, slabs):
     bits = positions.bit_length() - 1
-    arrived = None
-    for step in range(bits):
-        term = term if arrived is None else term + arrived
-        route = []
-        for p in range(positions):
-            for s in range(slabs):
-                bit = step if s % 2 == 0 else bits - 1 - step
-                route.append((p * slabs + s, (p ^ (1 << bit)) * slabs + s))
-        arrived = lax.ppermute(term, ("pos", "slab"), route)
-    return term, arrived
+    route = []
+    for p in range(positions):
+        for s in range(slabs):
+            bit = step if s % 2 == 0 else bits - 1 - step
+            route.append((p * slabs + s, (p ^ (1 << bit)) * slabs + s))
+    return route
+
+
+def sum_positions(keep, give, positions, slabs):
+    bits = positions.bit_length() - 1
+    total = keep + lax.ppermute(give, ("pos", "slab"), partners(0, positions, slabs))
+    for step in range(1, bits):
+        total = total + lax.ppermute(total, ("pos", "slab"), partners(step, positions, slabs))
+    return total, lax.ppermute(total, ("pos", "slab"), partners(0, positions, slabs))
 
 
 def local(labels, magnet_mask, reluctivity, rotor_shift, potential, adjoint_load):
     layers, radial, angular = labels.shape
     positions, slabs = lax.axis_size("pos"), lax.axis_size("slab")
-    if layers != 2 or slabs % 2 or radial % (2 * CHUNKS * ROWS):
+    if layers != 2 or slabs % 2 or radial % (2 * CHUNKS * ROWS) or positions < 2 or positions & (positions - 1):
         raise ValueError("unsupported sizes")
     potential, load = potential[0], adjoint_load[0]
     f32 = functools.partial(jax.ShapeDtypeStruct, dtype=jnp.float32)
@@ -270,38 +316,49 @@
     far_part_in = lax.ppermute(far_part, "slab", pairs(slabs, 1))
     near_part_in = lax.ppermute(near_part, "slab", pairs(slabs, 0))
     far_potential = lax.ppermute(far_potential, "slab", pairs(slabs, 1))
-    image, image_in, sums = pl.pallas_call(
+    image, near_image_in, own_sums = pl.pallas_call(
         sums_kernel,
-        out_shape=(f32((2,) + plane), f32((2,) + plane), f32((SUMS, slabs, 128))),
-        in_specs=[vmem] * 8,
+        out_shape=(f32((2,) + plane), f32((1,) + plane), f32((8, 128))),
+        in_specs=[vmem] * 7,
         out_specs=(vmem,) * 3,
         compiler_params=params(),
         name="sums",
-    )(far, near, far_part, near_part, far_in, near_in, far_part_in, near_part_in)
+    )(far, near, far_part, near_part, far_in, near_in, near_part_in)
+    far_image_in, sums = pl.pallas_call(
+        face_kernel,
+        out_shape=(f32((1,) + plane), f32((SUMS, slabs, 128))),
+        in_specs=[vmem] * 5,
+        out_specs=(vmem,) * 2,
+        compiler_params=params(),
+        name="face",
+    )(far, far_in, far_part_in, image, own_sums)
     sums = gather_sums(sums, "slab", slabs)
-    adjoint, *terms = pl.pallas_call(
+    span = radial // 2 // CHUNKS
+    adjoint, *pieces = pl.pallas_call(
         finish_kernel,
-        out_shape=(pltpu.VMEM((2,) + plane, jnp.float32),)
-        + (f32((2, radial // CHUNKS, angular)),) * CHUNKS,
-        in_specs=[vmem] * 10,
-        out_specs=(vmem,) * (1 + CHUNKS),
-        scratch_shapes=[VMEM((2,) + plane, jnp.float32)] * 2,
+        out_shape=(pltpu.VMEM((2,) + plane, jnp.float32),) + (f32((2, span, angular)),) * (2 * CHUNKS),
+        in_specs=[vmem] * 11,
+        out_specs=(vmem,) * (1 + 2 * CHUNKS),
+        scratch_shapes=[VMEM((2,) + plane, jnp.float32)] * 3,
         compiler_params=params(),
         name="finish",
-    )(sums, far, near, far_in, near_in, image, image_in, potential, far_potential, magnet_mask)
-    span = radial // CHUNKS
+    )(sums, far, near, far_in, near_in, image, far_image_in, near_image_in, potential, far_potential, magnet_mask)
+    halves = [sum_positions(pieces[i], pieces[CHUNKS + i], positions, slabs) for i in range(CHUNKS)]
     gradient = ()
-    for index, (total, arrived) in enumerate([sum_positions(term, positions, slabs) for term in terms]):
+    for given, first_chunk, chunks in (
+        (False, 0, [kept for kept, _ in halves]),
+        *((True, i, [given]) for i, (_, given) in enumerate(halves)),
+    ):
         gradient = pl.pallas_call(
-            functools.partial(close_kernel, index * span),
+            functools.partial(close_kernel, given, first_chunk),
             out_shape=pltpu.HBM((2,) + plane, jnp.float32),
-            in_specs=[vmem] * 2 + [hbm] * (index > 0),
+            in_specs=[vmem] * len(chunks) + [hbm] * given,
             out_specs=hbm,
-            scratch_shapes=[VMEM((2, span, angular), jnp.float32), pltpu.SemaphoreType.DMA(())],
-            input_output_aliases={2: 0} if index else {},
+            scratch_shapes=[pltpu.SemaphoreType.DMA((len(chunks),))],
+            input_output_aliases={len(chunks): 0} if given else {},
             compiler_params=params(),
             name="close",
-        )(total, arrived, *((gradient,) if index else ()))
+        )(*chunks, *((gradient,) if given else ()))
     return gradient, adjoint[None]
 
 

time: 49.8 us -> 48.9 us (0.982)
  starting transfers between devices: 28.6 us -> 24.9 us
  waiting for transfers between devices: 9.77 us -> 12.9 us
    ppermute x8 -> x6, waiting for transfers between devices: 4.92 us -> 8.52 us  [the longest x2 4.2 us: sum_positions(): lax.ppermute(give, ('pos', 'slab'), partners(0, positions, slabs))]
    ppermute x8 -> x6, starting transfers between devices: 10.8 us -> 8.66 us  [the longest x2 3.3 us: sum_positions(): lax.ppermute(total, ('pos', 'slab'), partners(step, positions, slabs))]
    ppermute x1, starting transfers between devices: 5.23 us -> 3.99 us  [local(): near_part_in = lax.ppermute(near_part, 'slab', pairs(slabs, 0))]
  transfers between devices with their start and end apart: 16 -> 14, of which waited for: 9 -> 8; matrix products, arithmetic and copies ran while one was open for 2% -> 2% of each run, Pallas kernels for 12% -> 11%
where the time goes in v4:
time: 48.9 us; the launch traced here: 48.7 us
  starting transfers between devices  24.9 us (51%)
  waiting for transfers between devices  12.9 us (26%)
  Pallas kernels  8.57 us (18%)
  between operations  1.45 us (3%)
  local copies, waits for them, and re-layouts  0.81 us (2%)
    ppermute x3, starting transfers between devices, gather_sums(): sums = sums + lax.ppermute(sums, axis, [(i, i ^ step) for i in range(size)])  9.74 us
    ppermute x3, waiting for transfers between devices, gather_sums(): sums = sums + lax.ppermute(sums, axis, [(i, i ^ step) for i in range(size)])  4.36 us
    ppermute x2, waiting for transfers between devices, sum_positions(): lax.ppermute(give, ('pos', 'slab'), partners(0, positions, slabs))  4.2 us
    ppermute x1, starting transfers between devices, local(): near_part_in = lax.ppermute(near_part, 'slab', pairs(slabs, 0))  3.99 us
    ppermute x2, starting transfers between devices, sum_positions(): lax.ppermute(total, ('pos', 'slab'), partners(step, positions, slabs))  3.3 us
    ppermute x2, starting transfers between devices, sum_positions(): lax.ppermute(total, ('pos', 'slab'), partners(0, positions, slabs))  3.27 us
    ppermute x2, waiting for transfers between devices, sum_positions(): lax.ppermute(total, ('pos', 'slab'), partners(step, positions, slabs))  3.14 us
    ppermute x2, starting transfers between devices, sum_positions(): lax.ppermute(give, ('pos', 'slab'), partners(0, positions, slabs))  2.09 us
  transfers between devices with their start and end apart: 14, of which 8 were waited for; matrix products, arithmetic and copies ran while one was open for 2% of the time, Pallas kernels for 11%

profile of v4, /device:TPU:0, one launch (start us, length us, event | category | flops | bytes accessed | tf_op | source)
XLA Modules:
  0.0 48.7 jit_solution(10335829961671425604)
XLA Ops:
  1.3 1.4 %open.1 = (f32[2,256,256]{2,1,0:T(8,128)S(1)}, f32[3,256,256]{2,1,0:T(8,128)S(1)}, f32[1,256,256]{2,1,0:T(8,128)S(1)}) custom-call(f32[4]{0:T(128)} %reluctivity.1, s32[1]{0:T(128)S(6)} %copy.13.shift, s32[2,256,256]{2,1,0:T(8,128)} %labels.1, f32[2,256,256]{2,1,0:T(8,128)} %bitcast.6, f32[2,256,256]{2,1,0:T(8,128)} %bitcast.4), custom_call_target="tpu_custom_call" | custom-call | tf_op jit(solution)/shard_map/open/pallas_call | solution.py:293
  3.2 0.7 %collective-permute-start = (f32[2,256,256]{2,1,0:T(8,128)S(1)}, f32[2,256,256]{2,1,0:T(8,128)S(1)}, u32[]{:S(2)}, u32[]{:S(2)}) collective-permute-start(f32[2,256,256]{2,1,0:T(8,128)S(1)} %get-tuple-element.17.far), channel_id=1, source_target_pairs={{1,2},{2,1},{3,4},{4,3},{5,6},{6,5},{9,10},{10,9},{11,12},{12,11},... | collective-permute-start | bytes 1572872 | tf_op jit(solution)/shard_map/ppermute | solution.py:306
  3.9 1.9 %part.1 = (f32[1,256,256]{2,1,0:T(8,128)S(1)}, f32[1,256,256]{2,1,0:T(8,128)S(1)}) custom-call(f32[2,256,256]{2,1,0:T(8,128)S(1)} %get-tuple-element.17.far, f32[3,256,256]{2,1,0:T(8,128)S(1)} %get-tuple-element.18.near), custom_call_target="tpu_custom_call" | custom-call | tf_op jit(solution)/shard_map/part/pallas_call | solution.py:308
  5.9 4.0 %collective-permute-start.3 = (f32[1,256,256]{2,1,0:T(8,128)S(1)}, f32[1,256,256]{2,1,0:T(8,128)S(1)}, u32[]{:S(2)}, u32[]{:S(2)}) collective-permute-start(f32[1,256,256]{2,1,0:T(8,128)S(1)} %get-tuple-element.20.near_part), channel_id=1, source_target_pairs={{0,1},{1,0},{2,3},{3,2},{4,5},{5,4},{6,7},{7,6},{8,9},{9,8},{10,11... | collective-permute-start | bytes 786440 | tf_op jit(solution)/shard_map/ppermute | solution.py:317
  11.2 2.0 %sums.1 = (f32[2,256,256]{2,1,0:T(8,128)S(1)}, f32[1,256,256]{2,1,0:T(8,128)S(1)}, f32[8,128]{1,0:T(8,128)S(1)}) custom-call(f32[2,256,256]{2,1,0:T(8,128)S(1)} %get-tuple-element.17.far, f32[3,256,256]{2,1,0:T(8,128)S(1)} %get-tuple-element.18.near, f32[1,256,256]{2,1,0:T(8,128)S(1)} %get-tuple-element.19.far_part, ...), custom_call_target="tpu_custom_call" | custom-call | tf_op jit(solution)/shard_map/sums/pallas_call | solution.py:319
  13.5 4.4 %collective-permute-start.4 = (f32[5,8,128]{2,1,0:T(8,128)S(1)}, f32[5,8,128]{2,1,0:T(8,128)S(1)}, u32[]{:S(2)}, u32[]{:S(2)}) collective-permute-start(f32[5,8,128]{2,1,0:T(8,128)S(1)} %get-tuple-element.23), channel_id=1, source_target_pairs={{0,1},{1,0},{2,3},{3,2},{4,5},{5,4},{6,7},{7,6},{8,9},{9,8},{10,11... | collective-permute-start | bytes 61448 | tf_op jit(solution)/shard_map/ppermute | solution.py:259
  17.9 0.8 %collective-permute-done.4 = f32[5,8,128]{2,1,0:T(8,128)S(1)} collective-permute-done((f32[5,8,128]{2,1,0:T(8,128)S(1)}, f32[5,8,128]{2,1,0:T(8,128)S(1)}, u32[]{:S(2)}, u32[]{:S(2)}) %collective-permute-start.4) | collective-permute-done | bytes 20512 | tf_op jit(solution)/shard_map/ppermute | solution.py:259
  18.8 2.3 %collective-permute-start.5 = (f32[5,8,128]{2,1,0:T(8,128)S(1)}, f32[5,8,128]{2,1,0:T(8,128)S(1)}, u32[]{:S(2)}, u32[]{:S(2)}) collective-permute-start(f32[5,8,128]{2,1,0:T(8,128)S(1)} %add.21), channel_id=1, source_target_pairs={{0,2},{1,3},{2,0},{3,1},{4,6},{5,7},{6,4},{7,5},{8,10},{9,11},{10,... | collective-permute-start | bytes 61448 | tf_op jit(solution)/shard_map/ppermute | solution.py:259
  21.1 1.8 %collective-permute-done.5 = f32[5,8,128]{2,1,0:T(8,128)S(1)} collective-permute-done((f32[5,8,128]{2,1,0:T(8,128)S(1)}, f32[5,8,128]{2,1,0:T(8,128)S(1)}, u32[]{:S(2)}, u32[]{:S(2)}) %collective-permute-start.5) | collective-permute-done | bytes 20512 | tf_op jit(solution)/shard_map/ppermute | solution.py:259
  22.9 3.0 %collective-permute-start.6 = (f32[5,8,128]{2,1,0:T(8,128)S(1)}, f32[5,8,128]{2,1,0:T(8,128)S(1)}, u32[]{:S(2)}, u32[]{:S(2)}) collective-permute-start(f32[5,8,128]{2,1,0:T(8,128)S(1)} %add.22), channel_id=1, source_target_pairs={{0,4},{1,5},{2,6},{3,7},{4,0},{5,1},{6,2},{7,3},{8,12},{9,13},{10,... | collective-permute-start | bytes 61448 | tf_op jit(solution)/shard_map/ppermute | solution.py:259
  25.9 1.8 %collective-permute-done.6 = f32[5,8,128]{2,1,0:T(8,128)S(1)} collective-permute-done((f32[5,8,128]{2,1,0:T(8,128)S(1)}, f32[5,8,128]{2,1,0:T(8,128)S(1)}, u32[]{:S(2)}, u32[]{:S(2)}) %collective-permute-start.6) | collective-permute-done | bytes 20512 | tf_op jit(solution)/shard_map/ppermute | solution.py:259
  27.7 0.9 %finish.1 = (f32[2,256,256]{2,1,0:T(8,128)S(1)}, f32[2,64,256]{2,1,0:T(8,128)S(1)}, f32[2,64,256]{2,1,0:T(8,128)S(1)}, f32[2,64,256]{2,1,0:T(8,128)S(1)}, f32[2,64,256]{2,1,0:T(8,128)S(1)}) custom-call(f32[5,8,128]{2,1,0:T(8,128)S(1)} %add.23.sums, f32[2,256,256]{2,1,0:T(8,128)S(1)} %get-tuple-element.17.far, f32[3,256,256]{2,1,0:T(8,128)S(1)} %get-tuple-element.18.near, ...), custom_call_target="tpu_custom_call" | custom-call | tf_op jit(solution)/shard_map/finish/pallas_call | solution.py:337
  28.6 1.6 %collective-permute-start.11 = (f32[2,64,256]{2,1,0:T(8,128)S(1)}, f32[2,64,256]{2,1,0:T(8,128)S(1)}, u32[]{:S(2)}, u32[]{:S(2)}) collective-permute-start(f32[2,64,256]{2,1,0:T(8,128)S(1)} %get-tuple-element.30), channel_id=1, source_target_pairs={{0,8},{1,17},{2,10},{3,19},{4,12},{5,21},{6,14},{7,23},{8,0},{9,25... | collective-permute-start | bytes 393224 | tf_op jit(solution)/shard_map/ppermute | solution.py:276
  30.7 3.1 %collective-permute-done.11 = f32[2,64,256]{2,1,0:T(8,128)S(1)} collective-permute-done((f32[2,64,256]{2,1,0:T(8,128)S(1)}, f32[2,64,256]{2,1,0:T(8,128)S(1)}, u32[]{:S(2)}, u32[]{:S(2)}) %collective-permute-start.11) | collective-permute-done | bytes 131104 | tf_op jit(solution)/shard_map/ppermute | solution.py:276
  33.8 1.7 %collective-permute-start.12 = (f32[2,64,256]{2,1,0:T(8,128)S(1)}, f32[2,64,256]{2,1,0:T(8,128)S(1)}, u32[]{:S(2)}, u32[]{:S(2)}) collective-permute-start(f32[2,64,256]{2,1,0:T(8,128)S(1)} %add.26), channel_id=1, source_target_pairs={{0,16},{1,9},{2,18},{3,11},{4,20},{5,13},{6,22},{7,15},{8,24},{9,1... | collective-permute-start | bytes 393224 | tf_op jit(solution)/shard_map/ppermute | solution.py:278
  35.4 1.1 %collective-permute-done.8 = f32[2,64,256]{2,1,0:T(8,128)S(1)} collective-permute-done((f32[2,64,256]{2,1,0:T(8,128)S(1)}, f32[2,64,256]{2,1,0:T(8,128)S(1)}, u32[]{:S(2)}, u32[]{:S(2)}) %collective-permute-start.8) | collective-permute-done | bytes 131104 | tf_op jit(solution)/shard_map/ppermute | solution.py:276
  36.6 1.6 %collective-permute-start.9 = (f32[2,64,256]{2,1,0:T(8,128)S(1)}, f32[2,64,256]{2,1,0:T(8,128)S(1)}, u32[]{:S(2)}, u32[]{:S(2)}) collective-permute-start(f32[2,64,256]{2,1,0:T(8,128)S(1)} %add.24), channel_id=1, source_target_pairs={{0,16},{1,9},{2,18},{3,11},{4,20},{5,13},{6,22},{7,15},{8,24},{9,1... | collective-permute-start | bytes 393224 | tf_op jit(solution)/shard_map/ppermute | solution.py:278
  38.8 1.6 %collective-permute-start.13 = (f32[2,64,256]{2,1,0:T(8,128)S(1)}, f32[2,64,256]{2,1,0:T(8,128)S(1)}, u32[]{:S(2)}, u32[]{:S(2)}) collective-permute-start(f32[2,64,256]{2,1,0:T(8,128)S(1)} %add.27.rest_0_), channel_id=1, source_target_pairs={{0,8},{1,17},{2,10},{3,19},{4,12},{5,21},{6,14},{7,23},{8,0},{9,25... | collective-permute-start | bytes 393224 | tf_op jit(solution)/shard_map/ppermute | solution.py:279
  40.4 2.6 %collective-permute-done.9 = f32[2,64,256]{2,1,0:T(8,128)S(1)} collective-permute-done((f32[2,64,256]{2,1,0:T(8,128)S(1)}, f32[2,64,256]{2,1,0:T(8,128)S(1)}, u32[]{:S(2)}, u32[]{:S(2)}) %collective-permute-start.9) | collective-permute-done | bytes 131104 | tf_op jit(solution)/shard_map/ppermute | solution.py:278
  43.0 1.6 %collective-permute-start.10 = (f32[2,64,256]{2,1,0:T(8,128)S(1)}, f32[2,64,256]{2,1,0:T(8,128)S(1)}, u32[]{:S(2)}, u32[]{:S(2)}) collective-permute-start(f32[2,64,256]{2,1,0:T(8,128)S(1)} %add.25.rest_1_), channel_id=1, source_target_pairs={{0,8},{1,17},{2,10},{3,19},{4,12},{5,21},{6,14},{7,23},{8,0},{9,25... | collective-permute-start | bytes 393224 | tf_op jit(solution)/shard_map/ppermute | solution.py:279
  44.7 0.8 %copy.12 = f32[1,2,256,256]{3,2,1,0:T(8,128)} copy(f32[1,2,256,256]{3,2,1,0:T(8,128)S(1)} %bitcast.3) | data formatting | bytes 1048576
  45.5 0.7 %close.3.rest_1_ = f32[2,256,256]{2,1,0:T(8,128)} custom-call(f32[2,64,256]{2,1,0:T(8,128)S(1)} %add.27.rest_0_, f32[2,64,256]{2,1,0:T(8,128)S(1)} %add.25.rest_1_), custom_call_target="tpu_custom_call" | custom-call | tf_op jit(solution)/shard_map/close/pallas_call | solution.py:352
  46.2 0.7 %close.4.rest_1_ = f32[2,256,256]{2,1,0:T(8,128)} custom-call(f32[2,64,256]{2,1,0:T(8,128)S(1)} %collective-permute-done.13.rest_0_, f32[2,256,256]{2,1,0:T(8,128)} %close.3.rest_1_), custom_call_target="tpu_custom_call", output_to_operand_aliasing={{}: (1, {})} | custom-call | tf_op jit(solution)/shard_map/close/pallas_call | solution.py:352
  46.9 1.2 %collective-permute-done.10.rest_0_ = f32[2,64,256]{2,1,0:T(8,128)S(1)} collective-permute-done((f32[2,64,256]{2,1,0:T(8,128)S(1)}, f32[2,64,256]{2,1,0:T(8,128)S(1)}, u32[]{:S(2)}, u32[]{:S(2)}) %collective-permute-start.10) | collective-permute-done | bytes 131104 | tf_op jit(solution)/shard_map/ppermute | solution.py:279
  (24 shorter events, 4.0 us)
Async XLA Ops:
  2.7 8.5 %collective-permute-start.2 = (f32[3,256,256]{2,1,0:T(8,128)S(1)}, f32[3,256,256]{2,1,0:T(8,128)S(1)}, u32[]{:S(2)}, u32[]{:S(2)}) collective-permute-start(f32[3,256,256]{2,1,0:T(8,128)S(1)} %get-tuple-element.18.near), channel_id=1, source_target_pairs={{0,1},{1,0},{2,3},{3,2},{4,5},{5,4},{6,7},{7,6},{8,9},{9,8},{10,11... | collective-permute-start | bytes 2359304 | tf_op jit(solution)/shard_map/ppermute | solution.py:307
  3.2 8.0 %collective-permute-start = (f32[2,256,256]{2,1,0:T(8,128)S(1)}, f32[2,256,256]{2,1,0:T(8,128)S(1)}, u32[]{:S(2)}, u32[]{:S(2)}) collective-permute-start(f32[2,256,256]{2,1,0:T(8,128)S(1)} %get-tuple-element.17.far), channel_id=1, source_target_pairs={{1,2},{2,1},{3,4},{4,3},{5,6},{6,5},{9,10},{10,9},{11,12},{12,11},... | collective-permute-start | bytes 1572872 | tf_op jit(solution)/shard_map/ppermute | solution.py:306
  5.9 5.4 %collective-permute-start.3 = (f32[1,256,256]{2,1,0:T(8,128)S(1)}, f32[1,256,256]{2,1,0:T(8,128)S(1)}, u32[]{:S(2)}, u32[]{:S(2)}) collective-permute-start(f32[1,256,256]{2,1,0:T(8,128)S(1)} %get-tuple-element.20.near_part), channel_id=1, source_target_pairs={{0,1},{1,0},{2,3},{3,2},{4,5},{5,4},{6,7},{7,6},{8,9},{9,8},{10,11... | collective-permute-start | bytes 786440 | tf_op jit(solution)/shard_map/ppermute | solution.py:317
  9.9 3.4 %collective-permute-start.1 = (f32[1,256,256]{2,1,0:T(8,128)S(1)}, f32[1,256,256]{2,1,0:T(8,128)S(1)}, u32[]{:S(2)}, u32[]{:S(2)}) collective-permute-start(f32[1,256,256]{2,1,0:T(8,128)S(1)} %get-tuple-element.19.far_part), channel_id=1, source_target_pairs={{1,2},{2,1},{3,4},{4,3},{5,6},{6,5},{9,10},{10,9},{11,12},{12,11},... | collective-permute-start | bytes 786440 | tf_op jit(solution)/shard_map/ppermute | solution.py:316
  10.5 17.1 %collective-permute-start.7 = (f32[1,256,256]{2,1,0:T(8,128)S(1)}, f32[1,256,256]{2,1,0:T(8,128)S(1)}, u32[]{:S(2)}, u32[]{:S(2)}) collective-permute-start(f32[1,256,256]{2,1,0:T(8,128)S(1)} %get-tuple-element.26), channel_id=1, source_target_pairs={{1,2},{2,1},{3,4},{4,3},{5,6},{6,5},{9,10},{10,9},{11,12},{12,11},... | collective-permute-start | bytes 786440 | tf_op jit(solution)/shard_map/ppermute | solution.py:318
  13.2 14.4 %copy-start = (f32[1,2,256,256]{3,2,1,0:T(8,128)S(1)}, f32[1,2,256,256]{3,2,1,0:T(8,128)}, u32[]{:S(2)}) copy-start(f32[1,2,256,256]{3,2,1,0:T(8,128)} %param.10) | copy-start | bytes 1572868
  13.2 14.4 %copy-start.1 = (s32[2,256,256]{2,1,0:T(8,128)S(1)}, s32[2,256,256]{2,1,0:T(8,128)}, u32[]{:S(2)}) copy-start(s32[2,256,256]{2,1,0:T(8,128)} %mask.1) | copy-start | bytes 1572868
  13.5 5.2 %collective-permute-start.4 = (f32[5,8,128]{2,1,0:T(8,128)S(1)}, f32[5,8,128]{2,1,0:T(8,128)S(1)}, u32[]{:S(2)}, u32[]{:S(2)}) collective-permute-start(f32[5,8,128]{2,1,0:T(8,128)S(1)} %get-tuple-element.23), channel_id=1, source_target_pairs={{0,1},{1,0},{2,3},{3,2},{4,5},{5,4},{6,7},{7,6},{8,9},{9,8},{10,11... | collective-permute-start | bytes 61448 | tf_op jit(solution)/shard_map/ppermute | solution.py:259
  18.8 4.1 %collective-permute-start.5 = (f32[5,8,128]{2,1,0:T(8,128)S(1)}, f32[5,8,128]{2,1,0:T(8,128)S(1)}, u32[]{:S(2)}, u32[]{:S(2)}) collective-permute-start(f32[5,8,128]{2,1,0:T(8,128)S(1)} %add.21), channel_id=1, source_target_pairs={{0,2},{1,3},{2,0},{3,1},{4,6},{5,7},{6,4},{7,5},{8,10},{9,11},{10,... | collective-permute-start | bytes 61448 | tf_op jit(solution)/shard_map/ppermute | solution.py:259
  22.9 4.8 %collective-permute-start.6 = (f32[5,8,128]{2,1,0:T(8,128)S(1)}, f32[5,8,128]{2,1,0:T(8,128)S(1)}, u32[]{:S(2)}, u32[]{:S(2)}) collective-permute-start(f32[5,8,128]{2,1,0:T(8,128)S(1)} %add.22), channel_id=1, source_target_pairs={{0,4},{1,5},{2,6},{3,7},{4,0},{5,1},{6,2},{7,3},{8,12},{9,13},{10,... | collective-permute-start | bytes 61448 | tf_op jit(solution)/shard_map/ppermute | solution.py:259
  28.6 5.1 %collective-permute-start.11 = (f32[2,64,256]{2,1,0:T(8,128)S(1)}, f32[2,64,256]{2,1,0:T(8,128)S(1)}, u32[]{:S(2)}, u32[]{:S(2)}) collective-permute-start(f32[2,64,256]{2,1,0:T(8,128)S(1)} %get-tuple-element.30), channel_id=1, source_target_pairs={{0,8},{1,17},{2,10},{3,19},{4,12},{5,21},{6,14},{7,23},{8,0},{9,25... | collective-permute-start | bytes 393224 | tf_op jit(solution)/shard_map/ppermute | solution.py:276
  30.2 6.4 %collective-permute-start.8 = (f32[2,64,256]{2,1,0:T(8,128)S(1)}, f32[2,64,256]{2,1,0:T(8,128)S(1)}, u32[]{:S(2)}, u32[]{:S(2)}) collective-permute-start(f32[2,64,256]{2,1,0:T(8,128)S(1)} %get-tuple-element.28), channel_id=1, source_target_pairs={{0,8},{1,17},{2,10},{3,19},{4,12},{5,21},{6,14},{7,23},{8,0},{9,25... | collective-permute-start | bytes 393224 | tf_op jit(solution)/shard_map/ppermute | solution.py:276
  33.8 5.0 %collective-permute-start.12 = (f32[2,64,256]{2,1,0:T(8,128)S(1)}, f32[2,64,256]{2,1,0:T(8,128)S(1)}, u32[]{:S(2)}, u32[]{:S(2)}) collective-permute-start(f32[2,64,256]{2,1,0:T(8,128)S(1)} %add.26), channel_id=1, source_target_pairs={{0,16},{1,9},{2,18},{3,11},{4,20},{5,13},{6,22},{7,15},{8,24},{9,1... | collective-permute-start | bytes 393224 | tf_op jit(solution)/shard_map/ppermute | solution.py:278
  36.6 6.4 %collective-permute-start.9 = (f32[2,64,256]{2,1,0:T(8,128)S(1)}, f32[2,64,256]{2,1,0:T(8,128)S(1)}, u32[]{:S(2)}, u32[]{:S(2)}) collective-permute-start(f32[2,64,256]{2,1,0:T(8,128)S(1)} %add.24), channel_id=1, source_target_pairs={{0,16},{1,9},{2,18},{3,11},{4,20},{5,13},{6,22},{7,15},{8,24},{9,1... | collective-permute-start | bytes 393224 | tf_op jit(solution)/shard_map/ppermute | solution.py:278
  38.8 7.4 %collective-permute-start.13 = (f32[2,64,256]{2,1,0:T(8,128)S(1)}, f32[2,64,256]{2,1,0:T(8,128)S(1)}, u32[]{:S(2)}, u32[]{:S(2)}) collective-permute-start(f32[2,64,256]{2,1,0:T(8,128)S(1)} %add.27.rest_0_), channel_id=1, source_target_pairs={{0,8},{1,17},{2,10},{3,19},{4,12},{5,21},{6,14},{7,23},{8,0},{9,25... | collective-permute-start | bytes 393224 | tf_op jit(solution)/shard_map/ppermute | solution.py:279
  43.0 5.0 %collective-permute-start.10 = (f32[2,64,256]{2,1,0:T(8,128)S(1)}, f32[2,64,256]{2,1,0:T(8,128)S(1)}, u32[]{:S(2)}, u32[]{:S(2)}) collective-permute-start(f32[2,64,256]{2,1,0:T(8,128)S(1)} %add.25.rest_1_), channel_id=1, source_target_pairs={{0,8},{1,17},{2,10},{3,19},{4,12},{5,21},{6,14},{7,23},{8,0},{9,25... | collective-permute-start | bytes 393224 | tf_op jit(solution)/shard_map/ppermute | solution.py:279

commit v5 on v4

--- a/solution.py
+++ b/solution.py
@@ -12,7 +12,7 @@
 VMEM = pltpu.VMEM
 SMEM = pltpu.SMEM
 SUMS = 5
-CHUNKS = 2
+EIGHTHS = (3, 3, 2)
 
 
 def params():
@@ -167,12 +167,13 @@
 
 
 def finish_kernel(
-    sums, far, near, far_in, near_in, image, far_image_in, near_image_in, potential, far_potential, mask, adjoint, *rest
+    sums_odd, sums_in, far, near, far_in, near_in, image, far_image_in, near_image_in, potential, far_potential, mask, adjoint, *rest
 ):
-    *pieces, mixed, mixed_in, term = rest
+    *terms, mixed, mixed_in = rest
     _, even = place()
     total = far.shape[1]
-    m0_d, m1_d, q_d, s_d, t_d = (sums[i] for i in range(SUMS))
+    odd = even.astype(jnp.float32)
+    m0_d, m1_d, q_d, s_d, t_d = (odd * sums_odd[i] + sums_in[i] for i in range(SUMS))
     m0 = jnp.sum(m0_d, axis=0, keepdims=True)
     m1 = jnp.sum(m1_d, axis=0, keepdims=True)
     c = m1 / m0
@@ -186,6 +187,7 @@
     a = (alpha0 + alpha1 * (1.0 + beta))[:, 0:1]
     b = (-alpha1 * alpha0)[:, 0:1]
     scale = 0.25 / lax.axis_size("pos")
+    firsts = first_rows(total)
     sides = ((far, even, far_in, far_image_in, far_potential, 0), (near, 1 - even, near_in, near_image_in, near_in, 2))
     for side, (own, layer, halo, image_in, halo_potential, at) in enumerate(sides):
         for start in range(0, total, ROWS):
@@ -208,40 +210,25 @@
                 shifted(potential, layer, start, 1) - shifted(potential, layer, start, -1)
             ) * (shifted(mixed, side, start, 1) - shifted(mixed, side, start, -1))
             weight = mask[layer, rows, :].astype(jnp.float32) * own[0, rows, :]
-            term[layer, rows, :] = weight * (scale * result)
-    first = own_half()
-    span = pieces[0].shape[1]
-    for index, piece in enumerate(pieces):
-        half = first if index < CHUNKS else 1 - first
-        base = pl.multiple_of(half * (total // 2) + index % CHUNKS * span, 8)
-        for layer in range(2):
-            piece[layer] = term[layer, pl.ds(base, span), :]
+            index = max(i for i, first in enumerate(firsts) if first <= start)
+            at_row = start - firsts[index]
+            terms[index][layer, at_row : at_row + ROWS, :] = weight * (scale * result)
 
 
 def in_hbm(x):
     return pltpu.with_memory_space_constraint(x, pltpu.HBM)
 
 
-def own_half():
-    bits = lax.axis_size("pos").bit_length() - 1
-    position = lax.axis_index("pos")
-    _, even = place()
-    return jnp.where(even == 0, lax.rem(position, 2), lax.rem(lax.div(position, 2 ** (bits - 1)), 2))
-
-
-def close_kernel(given, first_chunk, *rest):
-    gradient, sems = rest[-2:]
-    count = sems.shape[0]
-    span = rest[0].shape[1]
-    half = 1 - own_half() if given else own_half()
-    copies = []
-    for index in range(count):
-        base = pl.multiple_of(half * (gradient.shape[1] // 2) + (first_chunk + index) * span, 8)
-        copies.append(pltpu.make_async_copy(rest[index], gradient.at[:, pl.ds(base, span), :], sems.at[index]))
-    for copy in copies:
-        copy.start()
-    for copy in copies:
-        copy.wait()
+def first_rows(total):
+    return [total // 8 * sum(EIGHTHS[:i]) for i in range(len(EIGHTHS))]
+
+
+def close_kernel(start, total, arrived, *rest):
+    gradient, held, sem = rest[-3:]
+    held[...] = total[...] + arrived[...]
+    copy = pltpu.make_async_copy(held, gradient.at[:, pl.ds(start, total.shape[1]), :], sem)
+    copy.start()
+    copy.wait()
 
 
 def pairs(size, first):
@@ -251,14 +238,14 @@
     return out
 
 
-def gather_sums(sums, axis, size):
-    if size & (size - 1):
-        return lax.psum(sums, axis)
-    step = 1
-    while step < size:
-        sums = sums + lax.ppermute(sums, axis, [(i, i ^ step) for i in range(size)])
+def gather_sums(sums, slabs):
+    chip = range(0, slabs, 2)
+    sums = sums + lax.ppermute(sums, "slab", [(i, i + 1) for i in chip])
+    step = 2
+    while step < slabs:
+        sums = sums + lax.ppermute(sums, "slab", [(i + 1, (i + 1) ^ step) for i in chip])
         step *= 2
-    return sums
+    return sums, lax.ppermute(sums, "slab", [(i + 1, i) for i in chip])
 
 
 def partners(step, positions, slabs):
@@ -271,18 +258,18 @@
     return route
 
 
-def sum_positions(keep, give, positions, slabs):
-    bits = positions.bit_length() - 1
-    total = keep + lax.ppermute(give, ("pos", "slab"), partners(0, positions, slabs))
-    for step in range(1, bits):
-        total = total + lax.ppermute(total, ("pos", "slab"), partners(step, positions, slabs))
-    return total, lax.ppermute(total, ("pos", "slab"), partners(0, positions, slabs))
+def sum_positions(term, positions, slabs):
+    arrived = lax.ppermute(term, ("pos", "slab"), partners(0, positions, slabs))
+    for step in range(1, positions.bit_length() - 1):
+        term = term + arrived
+        arrived = lax.ppermute(term, ("pos", "slab"), partners(step, positions, slabs))
+    return term, arrived
 
 
 def local(labels, magnet_mask, reluctivity, rotor_shift, potential, adjoint_load):
     layers, radial, angular = labels.shape
     positions, slabs = lax.axis_size("pos"), lax.axis_size("slab")
-    if layers != 2 or slabs % 2 or radial % (2 * CHUNKS * ROWS) or positions < 2 or positions & (positions - 1):
+    if layers != 2 or slabs % 2 or slabs & (slabs - 1) or radial % (8 * ROWS) or positions < 2 or positions & (positions - 1):
         raise ValueError("unsupported sizes")
     potential, load = potential[0], adjoint_load[0]
     f32 = functools.partial(jax.ShapeDtypeStruct, dtype=jnp.float32)
@@ -332,33 +319,30 @@
         compiler_params=params(),
         name="face",
     )(far, far_in, far_part_in, image, own_sums)
-    sums = gather_sums(sums, "slab", slabs)
-    span = radial // 2 // CHUNKS
-    adjoint, *pieces = pl.pallas_call(
+    sums_odd, sums_in = gather_sums(sums, slabs)
+    spans = [radial // 8 * k for k in EIGHTHS]
+    adjoint, *terms = pl.pallas_call(
         finish_kernel,
-        out_shape=(pltpu.VMEM((2,) + plane, jnp.float32),) + (f32((2, span, angular)),) * (2 * CHUNKS),
-        in_specs=[vmem] * 11,
-        out_specs=(vmem,) * (1 + 2 * CHUNKS),
-        scratch_shapes=[VMEM((2,) + plane, jnp.float32)] * 3,
+        out_shape=(pltpu.VMEM((2,) + plane, jnp.float32),) + tuple(f32((2, span, angular)) for span in spans),
+        in_specs=[vmem] * 12,
+        out_specs=(vmem,) * (1 + len(spans)),
+        scratch_shapes=[VMEM((2,) + plane, jnp.float32)] * 2,
         compiler_params=params(),
         name="finish",
-    )(sums, far, near, far_in, near_in, image, far_image_in, near_image_in, potential, far_potential, magnet_mask)
-    halves = [sum_positions(pieces[i], pieces[CHUNKS + i], positions, slabs) for i in range(CHUNKS)]
+    )(sums_odd, sums_in, far, near, far_in, near_in, image, far_image_in, near_image_in, potential, far_potential, magnet_mask)
     gradient = ()
-    for given, first_chunk, chunks in (
-        (False, 0, [kept for kept, _ in halves]),
-        *((True, i, [given]) for i, (_, given) in enumerate(halves)),
-    ):
+    for index, term in enumerate(terms):
+        total, arrived = sum_positions(term, positions, slabs)
         gradient = pl.pallas_call(
-            functools.partial(close_kernel, given, first_chunk),
+            functools.partial(close_kernel, first_rows(radial)[index]),
             out_shape=pltpu.HBM((2,) + plane, jnp.float32),
-            in_specs=[vmem] * len(chunks) + [hbm] * given,
+            in_specs=[vmem] * 2 + [hbm] * (index > 0),
             out_specs=hbm,
-            scratch_shapes=[pltpu.SemaphoreType.DMA((len(chunks),))],
-            input_output_aliases={len(chunks): 0} if given else {},
+            scratch_shapes=[VMEM(term.shape, jnp.float32), pltpu.SemaphoreType.DMA(())],
+            input_output_aliases={2: 0} if index else {},
             compiler_params=params(),
             name="close",
-        )(*chunks, *((gradient,) if given else ()))
+        )(total, arrived, *((gradient,) if index else ()))
     return gradient, adjoint[None]
 
 

time: 48.9 us -> 51.3 us (1.049)
  waiting for transfers between devices: 12.9 us -> 16.2 us
  starting transfers between devices: 24.9 us -> 23.8 us
    ppermute x9 -> x10, waiting for transfers between devices: 12.9 us -> 16.2 us  [the longest x1 10.3 us: gather_sums(): return (sums, lax.ppermute(sums, 'slab', [(i + 1, i) for i in chip]))]
    ppermute x9 -> x10, starting transfers between devices: 18.4 us -> 17.3 us  [the longest x1 6.31 us: gather_sums(): sums = sums + lax.ppermute(sums, 'slab', [(i, i + 1) for i in chip])]
  transfers between devices with their start and end apart: 14 -> 15, of which waited for: 8 -> 6; matrix products, arithmetic and copies ran while one was open for 2% -> 2% of each run, Pallas kernels for 11% -> 11%
where the time goes in v5:
time: 51.3 us; the launch traced here: 51 us
  starting transfers between devices  23.8 us (46%)
  waiting for transfers between devices  16.2 us (32%)
  Pallas kernels  8.61 us (17%)
  between operations  1.5 us (3%)
  local copies, waits for them, and re-layouts  0.81 us (2%)
    ppermute x1, waiting for transfers between devices, gather_sums(): return (sums, lax.ppermute(sums, 'slab', [(i + 1, i) for i in chip]))  10.3 us
    ppermute x1, starting transfers between devices, gather_sums(): sums = sums + lax.ppermute(sums, 'slab', [(i, i + 1) for i in chip])  6.31 us
    ppermute x3, starting transfers between devices, sum_positions(): lax.ppermute(term, ('pos', 'slab'), partners(step, positions, slabs))  4.75 us
    ppermute x1, starting transfers between devices, local(): near_part_in = lax.ppermute(near_part, 'slab', pairs(slabs, 0))  3.99 us
    ppermute x3, waiting for transfers between devices, sum_positions(): arrived = lax.ppermute(term, ('pos', 'slab'), partners(0, positions, slabs))  3.88 us
    ppermute x3, starting transfers between devices, sum_positions(): arrived = lax.ppermute(term, ('pos', 'slab'), partners(0, positions, slabs))  3.58 us
    pallas_call x3, Pallas kernels, local(): pl.pallas_call(functools.partial(close_kernel, first_rows(radial)[index])...  2.09 us
    pallas_call x1, Pallas kernels, local(): pl.pallas_call(sums_kernel, out_shape=(f32((2,) + plane), f32((1,) + plan...  2 us
  transfers between devices with their start and end apart: 15, of which 6 were waited for; matrix products, arithmetic and copies ran while one was open for 2% of the time, Pallas kernels for 11%

profile of v5, /device:TPU:0, one launch (start us, length us, event | category | flops | bytes accessed | tf_op | source)
XLA Modules:
  0.0 51.0 jit_solution(2636938528333188944)
XLA Ops:
  1.3 1.4 %open.1 = (f32[2,256,256]{2,1,0:T(8,128)S(1)}, f32[3,256,256]{2,1,0:T(8,128)S(1)}, f32[1,256,256]{2,1,0:T(8,128)S(1)}) custom-call(f32[4]{0:T(128)} %reluctivity.1, s32[1]{0:T(128)S(6)} %copy.13.shift, s32[2,256,256]{2,1,0:T(8,128)} %labels.1, f32[2,256,256]{2,1,0:T(8,128)} %bitcast.6, f32[2,256,256]{2,1,0:T(8,128)} %bitcast.4), custom_call_target="tpu_custom_call" | custom-call | tf_op jit(solution)/shard_map/open/pallas_call | solution.py:280
  3.2 0.7 %collective-permute-start = (f32[2,256,256]{2,1,0:T(8,128)S(1)}, f32[2,256,256]{2,1,0:T(8,128)S(1)}, u32[]{:S(2)}, u32[]{:S(2)}) collective-permute-start(f32[2,256,256]{2,1,0:T(8,128)S(1)} %get-tuple-element.16.far), channel_id=1, source_target_pairs={{1,2},{2,1},{3,4},{4,3},{5,6},{6,5},{9,10},{10,9},{11,12},{12,11},... | collective-permute-start | bytes 1572872 | tf_op jit(solution)/shard_map/ppermute | solution.py:293
  3.9 1.9 %part.1 = (f32[1,256,256]{2,1,0:T(8,128)S(1)}, f32[1,256,256]{2,1,0:T(8,128)S(1)}) custom-call(f32[2,256,256]{2,1,0:T(8,128)S(1)} %get-tuple-element.16.far, f32[3,256,256]{2,1,0:T(8,128)S(1)} %get-tuple-element.17.near), custom_call_target="tpu_custom_call" | custom-call | tf_op jit(solution)/shard_map/part/pallas_call | solution.py:295
  5.9 4.0 %collective-permute-start.3 = (f32[1,256,256]{2,1,0:T(8,128)S(1)}, f32[1,256,256]{2,1,0:T(8,128)S(1)}, u32[]{:S(2)}, u32[]{:S(2)}) collective-permute-start(f32[1,256,256]{2,1,0:T(8,128)S(1)} %get-tuple-element.19.near_part), channel_id=1, source_target_pairs={{0,1},{1,0},{2,3},{3,2},{4,5},{5,4},{6,7},{7,6},{8,9},{9,8},{10,11... | collective-permute-start | bytes 786440 | tf_op jit(solution)/shard_map/ppermute | solution.py:304
  9.9 0.7 %collective-permute-start.1 = (f32[1,256,256]{2,1,0:T(8,128)S(1)}, f32[1,256,256]{2,1,0:T(8,128)S(1)}, u32[]{:S(2)}, u32[]{:S(2)}) collective-permute-start(f32[1,256,256]{2,1,0:T(8,128)S(1)} %get-tuple-element.18.far_part), channel_id=1, source_target_pairs={{1,2},{2,1},{3,4},{4,3},{5,6},{6,5},{9,10},{10,9},{11,12},{12,11},... | collective-permute-start | bytes 786440 | tf_op jit(solution)/shard_map/ppermute | solution.py:303
  10.5 0.7 %collective-permute-start.8 = (f32[1,256,256]{2,1,0:T(8,128)S(1)}, f32[1,256,256]{2,1,0:T(8,128)S(1)}, u32[]{:S(2)}, u32[]{:S(2)}) collective-permute-start(f32[1,256,256]{2,1,0:T(8,128)S(1)} %get-tuple-element.25), channel_id=1, source_target_pairs={{1,2},{2,1},{3,4},{4,3},{5,6},{6,5},{9,10},{10,9},{11,12},{12,11},... | collective-permute-start | bytes 786440 | tf_op jit(solution)/shard_map/ppermute | solution.py:305
  11.2 2.0 %sums.1 = (f32[2,256,256]{2,1,0:T(8,128)S(1)}, f32[1,256,256]{2,1,0:T(8,128)S(1)}, f32[8,128]{1,0:T(8,128)S(1)}) custom-call(f32[2,256,256]{2,1,0:T(8,128)S(1)} %get-tuple-element.16.far, f32[3,256,256]{2,1,0:T(8,128)S(1)} %get-tuple-element.17.near, f32[1,256,256]{2,1,0:T(8,128)S(1)} %get-tuple-element.18.far_part, ...), custom_call_target="tpu_custom_call" | custom-call | tf_op jit(solution)/shard_map/sums/pallas_call | solution.py:306
  13.6 6.3 %collective-permute-start.4 = (f32[5,8,128]{2,1,0:T(8,128)S(1)}, f32[5,8,128]{2,1,0:T(8,128)S(1)}, u32[]{:S(2)}, u32[]{:S(2)}) collective-permute-start(f32[5,8,128]{2,1,0:T(8,128)S(1)} %get-tuple-element.22), channel_id=1, source_target_pairs={{0,1},{2,3},{4,5},{6,7},{8,9},{10,11},{12,13},{14,15},{16,17},{18,... | collective-permute-start | bytes 61448 | tf_op jit(solution)/shard_map/ppermute | solution.py:243
  19.9 0.8 %collective-permute-done.4 = f32[5,8,128]{2,1,0:T(8,128)S(1)} collective-permute-done((f32[5,8,128]{2,1,0:T(8,128)S(1)}, f32[5,8,128]{2,1,0:T(8,128)S(1)}, u32[]{:S(2)}, u32[]{:S(2)}) %collective-permute-start.4) | collective-permute-done | bytes 20512 | tf_op jit(solution)/shard_map/ppermute | solution.py:243
  22.1 1.3 %collective-permute-start.7 = (f32[5,8,128]{2,1,0:T(8,128)S(1)}, f32[5,8,128]{2,1,0:T(8,128)S(1)}, u32[]{:S(2)}, u32[]{:S(2)}) collective-permute-start(f32[5,8,128]{2,1,0:T(8,128)S(1)} %add.20.sums_odd), channel_id=1, source_target_pairs={{1,0},{3,2},{5,4},{7,6},{9,8},{11,10},{13,12},{15,14},{17,16},{19,... | collective-permute-start | bytes 61448 | tf_op jit(solution)/shard_map/ppermute | solution.py:248
  23.4 10.3 %collective-permute-done.7.sums_in = f32[5,8,128]{2,1,0:T(8,128)S(1)} collective-permute-done((f32[5,8,128]{2,1,0:T(8,128)S(1)}, f32[5,8,128]{2,1,0:T(8,128)S(1)}, u32[]{:S(2)}, u32[]{:S(2)}) %collective-permute-start.7) | collective-permute-done | bytes 20512 | tf_op jit(solution)/shard_map/ppermute | solution.py:248
  33.7 0.9 %finish.1 = (f32[2,256,256]{2,1,0:T(8,128)S(1)}, f32[2,96,256]{2,1,0:T(8,128)S(1)}, f32[2,96,256]{2,1,0:T(8,128)S(1)}, f32[2,64,256]{2,1,0:T(8,128)S(1)}) custom-call(f32[5,8,128]{2,1,0:T(8,128)S(1)} %add.20.sums_odd, f32[5,8,128]{2,1,0:T(8,128)S(1)} %collective-permute-done.7.sums_in, f32[2,256,256]{2,1,0:T(8,128)S(1)} %get-tuple-element.16.far, ...), custom_call_target="tpu_custom_call" | custom-call | tf_op jit(solution)/shard_map/finish/pallas_call | solution.py:324
  34.6 1.6 %collective-permute-start.13 = (f32[2,96,256]{2,1,0:T(8,128)S(1)}, f32[2,96,256]{2,1,0:T(8,128)S(1)}, u32[]{:S(2)}, u32[]{:S(2)}) collective-permute-start(f32[2,96,256]{2,1,0:T(8,128)S(1)} %get-tuple-element.28), channel_id=1, source_target_pairs={{0,8},{1,17},{2,10},{3,19},{4,12},{5,21},{6,14},{7,23},{8,0},{9,25... | collective-permute-start | bytes 589832 | tf_op jit(solution)/shard_map/ppermute | solution.py:262
  36.6 1.5 %collective-permute-start.9 = (f32[2,64,256]{2,1,0:T(8,128)S(1)}, f32[2,64,256]{2,1,0:T(8,128)S(1)}, u32[]{:S(2)}, u32[]{:S(2)}) collective-permute-start(f32[2,64,256]{2,1,0:T(8,128)S(1)} %get-tuple-element.26), channel_id=1, source_target_pairs={{0,8},{1,17},{2,10},{3,19},{4,12},{5,21},{6,14},{7,23},{8,0},{9,25... | collective-permute-start | bytes 393224 | tf_op jit(solution)/shard_map/ppermute | solution.py:262
  38.1 2.2 %collective-permute-done.13 = f32[2,96,256]{2,1,0:T(8,128)S(1)} collective-permute-done((f32[2,96,256]{2,1,0:T(8,128)S(1)}, f32[2,96,256]{2,1,0:T(8,128)S(1)}, u32[]{:S(2)}, u32[]{:S(2)}) %collective-permute-start.13) | collective-permute-done | bytes 196640 | tf_op jit(solution)/shard_map/ppermute | solution.py:262
  40.3 1.6 %collective-permute-start.14 = (f32[2,96,256]{2,1,0:T(8,128)S(1)}, f32[2,96,256]{2,1,0:T(8,128)S(1)}, u32[]{:S(2)}, u32[]{:S(2)}) collective-permute-start(f32[2,96,256]{2,1,0:T(8,128)S(1)} %add.23.total), channel_id=1, source_target_pairs={{0,16},{1,9},{2,18},{3,11},{4,20},{5,13},{6,22},{7,15},{8,24},{9,1... | collective-permute-start | bytes 589832 | tf_op jit(solution)/shard_map/ppermute | solution.py:265
  42.5 1.6 %collective-permute-start.12 = (f32[2,96,256]{2,1,0:T(8,128)S(1)}, f32[2,96,256]{2,1,0:T(8,128)S(1)}, u32[]{:S(2)}, u32[]{:S(2)}) collective-permute-start(f32[2,96,256]{2,1,0:T(8,128)S(1)} %add.22.total), channel_id=1, source_target_pairs={{0,16},{1,9},{2,18},{3,11},{4,20},{5,13},{6,22},{7,15},{8,24},{9,1... | collective-permute-start | bytes 589832 | tf_op jit(solution)/shard_map/ppermute | solution.py:265
  44.1 1.2 %collective-permute-done.9 = f32[2,64,256]{2,1,0:T(8,128)S(1)} collective-permute-done((f32[2,64,256]{2,1,0:T(8,128)S(1)}, f32[2,64,256]{2,1,0:T(8,128)S(1)}, u32[]{:S(2)}, u32[]{:S(2)}) %collective-permute-start.9) | collective-permute-done | bytes 131104 | tf_op jit(solution)/shard_map/ppermute | solution.py:262
  45.3 1.6 %collective-permute-start.10 = (f32[2,64,256]{2,1,0:T(8,128)S(1)}, f32[2,64,256]{2,1,0:T(8,128)S(1)}, u32[]{:S(2)}, u32[]{:S(2)}) collective-permute-start(f32[2,64,256]{2,1,0:T(8,128)S(1)} %add.21.total), channel_id=1, source_target_pairs={{0,16},{1,9},{2,18},{3,11},{4,20},{5,13},{6,22},{7,15},{8,24},{9,1... | collective-permute-start | bytes 393224 | tf_op jit(solution)/shard_map/ppermute | solution.py:265
  46.9 0.8 %copy.12 = f32[1,2,256,256]{3,2,1,0:T(8,128)} copy(f32[1,2,256,256]{3,2,1,0:T(8,128)S(1)} %bitcast.3) | data formatting | bytes 1048576
  47.6 0.7 %close.3.rest_0_ = f32[2,256,256]{2,1,0:T(8,128)} custom-call(f32[2,96,256]{2,1,0:T(8,128)S(1)} %add.23.total, f32[2,96,256]{2,1,0:T(8,128)S(1)} %collective-permute-done.14.arrived), custom_call_target="tpu_custom_call" | custom-call | tf_op jit(solution)/shard_map/close/pallas_call | solution.py:336
  48.4 0.7 %close.4.rest_0_ = f32[2,256,256]{2,1,0:T(8,128)} custom-call(f32[2,96,256]{2,1,0:T(8,128)S(1)} %add.22.total, f32[2,96,256]{2,1,0:T(8,128)S(1)} %collective-permute-done.12.arrived, f32[2,256,256]{2,1,0:T(8,128)} %close.3.rest_0_), custom_call_target="tpu_custom_call", output_to_operand_aliasing={{}: (2, {})} | custom-call | tf_op jit(solution)/shard_map/close/pallas_call | solution.py:336
  49.1 1.2 %collective-permute-done.10.arrived = f32[2,64,256]{2,1,0:T(8,128)S(1)} collective-permute-done((f32[2,64,256]{2,1,0:T(8,128)S(1)}, f32[2,64,256]{2,1,0:T(8,128)S(1)}, u32[]{:S(2)}, u32[]{:S(2)}) %collective-permute-start.10) | collective-permute-done | bytes 131104 | tf_op jit(solution)/shard_map/ppermute | solution.py:265
  50.3 0.7 %close.5 = f32[2,256,256]{2,1,0:T(8,128)} custom-call(f32[2,64,256]{2,1,0:T(8,128)S(1)} %add.21.total, f32[2,64,256]{2,1,0:T(8,128)S(1)} %collective-permute-done.10.arrived, f32[2,256,256]{2,1,0:T(8,128)} %close.4.rest_0_), custom_call_target="tpu_custom_call", output_to_operand_aliasing={{}: (2, {})} | custom-call | tf_op jit(solution)/shard_map/close/pallas_call | solution.py:336
  (25 shorter events, 3.3 us)
Async XLA Ops:
  2.7 8.5 %collective-permute-start.2 = (f32[3,256,256]{2,1,0:T(8,128)S(1)}, f32[3,256,256]{2,1,0:T(8,128)S(1)}, u32[]{:S(2)}, u32[]{:S(2)}) collective-permute-start(f32[3,256,256]{2,1,0:T(8,128)S(1)} %get-tuple-element.17.near), channel_id=1, source_target_pairs={{0,1},{1,0},{2,3},{3,2},{4,5},{5,4},{6,7},{7,6},{8,9},{9,8},{10,11... | collective-permute-start | bytes 2359304 | tf_op jit(solution)/shard_map/ppermute | solution.py:294
  3.2 8.0 %collective-permute-start = (f32[2,256,256]{2,1,0:T(8,128)S(1)}, f32[2,256,256]{2,1,0:T(8,128)S(1)}, u32[]{:S(2)}, u32[]{:S(2)}) collective-permute-start(f32[2,256,256]{2,1,0:T(8,128)S(1)} %get-tuple-element.16.far), channel_id=1, source_target_pairs={{1,2},{2,1},{3,4},{4,3},{5,6},{6,5},{9,10},{10,9},{11,12},{12,11},... | collective-permute-start | bytes 1572872 | tf_op jit(solution)/shard_map/ppermute | solution.py:293
  5.9 5.4 %collective-permute-start.3 = (f32[1,256,256]{2,1,0:T(8,128)S(1)}, f32[1,256,256]{2,1,0:T(8,128)S(1)}, u32[]{:S(2)}, u32[]{:S(2)}) collective-permute-start(f32[1,256,256]{2,1,0:T(8,128)S(1)} %get-tuple-element.19.near_part), channel_id=1, source_target_pairs={{0,1},{1,0},{2,3},{3,2},{4,5},{5,4},{6,7},{7,6},{8,9},{9,8},{10,11... | collective-permute-start | bytes 786440 | tf_op jit(solution)/shard_map/ppermute | solution.py:304
  9.9 3.4 %collective-permute-start.1 = (f32[1,256,256]{2,1,0:T(8,128)S(1)}, f32[1,256,256]{2,1,0:T(8,128)S(1)}, u32[]{:S(2)}, u32[]{:S(2)}) collective-permute-start(f32[1,256,256]{2,1,0:T(8,128)S(1)} %get-tuple-element.18.far_part), channel_id=1, source_target_pairs={{1,2},{2,1},{3,4},{4,3},{5,6},{6,5},{9,10},{10,9},{11,12},{12,11},... | collective-permute-start | bytes 786440 | tf_op jit(solution)/shard_map/ppermute | solution.py:303
  10.5 12.9 %collective-permute-start.8 = (f32[1,256,256]{2,1,0:T(8,128)S(1)}, f32[1,256,256]{2,1,0:T(8,128)S(1)}, u32[]{:S(2)}, u32[]{:S(2)}) collective-permute-start(f32[1,256,256]{2,1,0:T(8,128)S(1)} %get-tuple-element.25), channel_id=1, source_target_pairs={{1,2},{2,1},{3,4},{4,3},{5,6},{6,5},{9,10},{10,9},{11,12},{12,11},... | collective-permute-start | bytes 786440 | tf_op jit(solution)/shard_map/ppermute | solution.py:305
  13.3 20.4 %copy-start = (f32[1,2,256,256]{3,2,1,0:T(8,128)S(1)}, f32[1,2,256,256]{3,2,1,0:T(8,128)}, u32[]{:S(2)}) copy-start(f32[1,2,256,256]{3,2,1,0:T(8,128)} %param.10) | copy-start | bytes 1572868
  13.3 20.4 %copy-start.1 = (s32[2,256,256]{2,1,0:T(8,128)S(1)}, s32[2,256,256]{2,1,0:T(8,128)}, u32[]{:S(2)}) copy-start(s32[2,256,256]{2,1,0:T(8,128)} %mask.1) | copy-start | bytes 1572868
  13.6 7.1 %collective-permute-start.4 = (f32[5,8,128]{2,1,0:T(8,128)S(1)}, f32[5,8,128]{2,1,0:T(8,128)S(1)}, u32[]{:S(2)}, u32[]{:S(2)}) collective-permute-start(f32[5,8,128]{2,1,0:T(8,128)S(1)} %get-tuple-element.22), channel_id=1, source_target_pairs={{0,1},{2,3},{4,5},{6,7},{8,9},{10,11},{12,13},{14,15},{16,17},{18,... | collective-permute-start | bytes 61448 | tf_op jit(solution)/shard_map/ppermute | solution.py:243
  20.7 0.7 %collective-permute-start.5 = (f32[5,8,128]{2,1,0:T(8,128)S(1)}, f32[5,8,128]{2,1,0:T(8,128)S(1)}, u32[]{:S(2)}, u32[]{:S(2)}) collective-permute-start(f32[5,8,128]{2,1,0:T(8,128)S(1)} %add.18), channel_id=1, source_target_pairs={{1,3},{3,1},{5,7},{7,5},{9,11},{11,9},{13,15},{15,13},{17,19},{19,... | collective-permute-start | bytes 61448 | tf_op jit(solution)/shard_map/ppermute | solution.py:246
  21.4 0.7 %collective-permute-start.6 = (f32[5,8,128]{2,1,0:T(8,128)S(1)}, f32[5,8,128]{2,1,0:T(8,128)S(1)}, u32[]{:S(2)}, u32[]{:S(2)}) collective-permute-start(f32[5,8,128]{2,1,0:T(8,128)S(1)} %add.19), channel_id=1, source_target_pairs={{1,5},{3,7},{5,1},{7,3},{9,13},{11,15},{13,9},{15,11},{17,21},{19,... | collective-permute-start | bytes 61448 | tf_op jit(solution)/shard_map/ppermute | solution.py:246
  22.1 11.6 %collective-permute-start.7 = (f32[5,8,128]{2,1,0:T(8,128)S(1)}, f32[5,8,128]{2,1,0:T(8,128)S(1)}, u32[]{:S(2)}, u32[]{:S(2)}) collective-permute-start(f32[5,8,128]{2,1,0:T(8,128)S(1)} %add.20.sums_odd), channel_id=1, source_target_pairs={{1,0},{3,2},{5,4},{7,6},{9,8},{11,10},{13,12},{15,14},{17,16},{19,... | collective-permute-start | bytes 61448 | tf_op jit(solution)/shard_map/ppermute | solution.py:248
  34.6 5.7 %collective-permute-start.13 = (f32[2,96,256]{2,1,0:T(8,128)S(1)}, f32[2,96,256]{2,1,0:T(8,128)S(1)}, u32[]{:S(2)}, u32[]{:S(2)}) collective-permute-start(f32[2,96,256]{2,1,0:T(8,128)S(1)} %get-tuple-element.28), channel_id=1, source_target_pairs={{0,8},{1,17},{2,10},{3,19},{4,12},{5,21},{6,14},{7,23},{8,0},{9,25... | collective-permute-start | bytes 589832 | tf_op jit(solution)/shard_map/ppermute | solution.py:262
  36.1 6.3 %collective-permute-start.11 = (f32[2,96,256]{2,1,0:T(8,128)S(1)}, f32[2,96,256]{2,1,0:T(8,128)S(1)}, u32[]{:S(2)}, u32[]{:S(2)}) collective-permute-start(f32[2,96,256]{2,1,0:T(8,128)S(1)} %get-tuple-element.27), channel_id=1, source_target_pairs={{0,8},{1,17},{2,10},{3,19},{4,12},{5,21},{6,14},{7,23},{8,0},{9,25... | collective-permute-start | bytes 589832 | tf_op jit(solution)/shard_map/ppermute | solution.py:262
  36.6 8.6 %collective-permute-start.9 = (f32[2,64,256]{2,1,0:T(8,128)S(1)}, f32[2,64,256]{2,1,0:T(8,128)S(1)}, u32[]{:S(2)}, u32[]{:S(2)}) collective-permute-start(f32[2,64,256]{2,1,0:T(8,128)S(1)} %get-tuple-element.26), channel_id=1, source_target_pairs={{0,8},{1,17},{2,10},{3,19},{4,12},{5,21},{6,14},{7,23},{8,0},{9,25... | collective-permute-start | bytes 393224 | tf_op jit(solution)/shard_map/ppermute | solution.py:262
  40.3 7.3 %collective-permute-start.14 = (f32[2,96,256]{2,1,0:T(8,128)S(1)}, f32[2,96,256]{2,1,0:T(8,128)S(1)}, u32[]{:S(2)}, u32[]{:S(2)}) collective-permute-start(f32[2,96,256]{2,1,0:T(8,128)S(1)} %add.23.total), channel_id=1, source_target_pairs={{0,16},{1,9},{2,18},{3,11},{4,20},{5,13},{6,22},{7,15},{8,24},{9,1... | collective-permute-start | bytes 589832 | tf_op jit(solution)/shard_map/ppermute | solution.py:265
  42.5 5.9 %collective-permute-start.12 = (f32[2,96,256]{2,1,0:T(8,128)S(1)}, f32[2,96,256]{2,1,0:T(8,128)S(1)}, u32[]{:S(2)}, u32[]{:S(2)}) collective-permute-start(f32[2,96,256]{2,1,0:T(8,128)S(1)} %add.22.total), channel_id=1, source_target_pairs={{0,16},{1,9},{2,18},{3,11},{4,20},{5,13},{6,22},{7,15},{8,24},{9,1... | collective-permute-start | bytes 589832 | tf_op jit(solution)/shard_map/ppermute | solution.py:265
  45.3 5.0 %collective-permute-start.10 = (f32[2,64,256]{2,1,0:T(8,128)S(1)}, f32[2,64,256]{2,1,0:T(8,128)S(1)}, u32[]{:S(2)}, u32[]{:S(2)}) collective-permute-start(f32[2,64,256]{2,1,0:T(8,128)S(1)} %add.21.total), channel_id=1, source_target_pairs={{0,16},{1,9},{2,18},{3,11},{4,20},{5,13},{6,22},{7,15},{8,24},{9,1... | collective-permute-start | bytes 393224 | tf_op jit(solution)/shard_map/ppermute | solution.py:265

commit v6 on v5

--- a/solution.py
+++ b/solution.py
@@ -167,13 +167,12 @@
 
 
 def finish_kernel(
-    sums_odd, sums_in, far, near, far_in, near_in, image, far_image_in, near_image_in, potential, far_potential, mask, adjoint, *rest
+    sums, far, near, far_in, near_in, image, far_image_in, near_image_in, potential, far_potential, mask, adjoint, *rest
 ):
     *terms, mixed, mixed_in = rest
     _, even = place()
     total = far.shape[1]
-    odd = even.astype(jnp.float32)
-    m0_d, m1_d, q_d, s_d, t_d = (odd * sums_odd[i] + sums_in[i] for i in range(SUMS))
+    m0_d, m1_d, q_d, s_d, t_d = (sums[i] for i in range(SUMS))
     m0 = jnp.sum(m0_d, axis=0, keepdims=True)
     m1 = jnp.sum(m1_d, axis=0, keepdims=True)
     c = m1 / m0
@@ -239,13 +238,10 @@
 
 
 def gather_sums(sums, slabs):
-    chip = range(0, slabs, 2)
-    sums = sums + lax.ppermute(sums, "slab", [(i, i + 1) for i in chip])
-    step = 2
-    while step < slabs:
-        sums = sums + lax.ppermute(sums, "slab", [(i + 1, (i + 1) ^ step) for i in chip])
-        step *= 2
-    return sums, lax.ppermute(sums, "slab", [(i + 1, i) for i in chip])
+    steps = [2**k for k in range(1, slabs.bit_length() - 1)] + [1]
+    for step in steps:
+        sums = sums + lax.ppermute(sums, "slab", [(i, i ^ step) for i in range(slabs)])
+    return sums
 
 
 def partners(step, positions, slabs):
@@ -319,17 +315,17 @@
         compiler_params=params(),
         name="face",
     )(far, far_in, far_part_in, image, own_sums)
-    sums_odd, sums_in = gather_sums(sums, slabs)
+    sums = gather_sums(sums, slabs)
     spans = [radial // 8 * k for k in EIGHTHS]
     adjoint, *terms = pl.pallas_call(
         finish_kernel,
         out_shape=(pltpu.VMEM((2,) + plane, jnp.float32),) + tuple(f32((2, span, angular)) for span in spans),
-        in_specs=[vmem] * 12,
+        in_specs=[vmem] * 11,
         out_specs=(vmem,) * (1 + len(spans)),
         scratch_shapes=[VMEM((2,) + plane, jnp.float32)] * 2,
         compiler_params=params(),
         name="finish",
-    )(sums_odd, sums_in, far, near, far_in, near_in, image, far_image_in, near_image_in, potential, far_potential, magnet_mask)
+    )(sums, far, near, far_in, near_in, image, far_image_in, near_image_in, potential, far_potential, magnet_mask)
     gradient = ()
     for index, term in enumerate(terms):
         total, arrived = sum_positions(term, positions, slabs)

time: 51.3 us -> 45.3 us (0.88)
  waiting for transfers between devices: 16.2 us -> 10.9 us
    ppermute x4 -> x3, waiting for transfers between devices: 11.1 us -> 5.76 us  [gather_sums(): lax.ppermute(sums, 'slab', [(i, i ^ step) for i in range(slabs)])]
    ppermute x4 -> x3, starting transfers between devices: 8.92 us -> 8.44 us  [gather_sums(): lax.ppermute(sums, 'slab', [(i, i ^ step) for i in range(slabs)])]
  transfers between devices with their start and end apart: 15 -> 14, of which waited for: 6 -> 7; matrix products, arithmetic and copies ran while one was open for 2% -> 2% of each run, Pallas kernels for 11% -> 12%
where the time goes in v6:
time: 45.3 us; the launch traced here: 45.1 us
  starting transfers between devices  23.3 us (51%)
  waiting for transfers between devices  10.9 us (24%)
  Pallas kernels  8.57 us (19%)
  between operations  1.45 us (3%)
  local copies, waits for them, and re-layouts  0.81 us (2%)
    ppermute x3, starting transfers between devices, gather_sums(): lax.ppermute(sums, 'slab', [(i, i ^ step) for i in range(slabs)])  8.44 us
    ppermute x3, waiting for transfers between devices, gather_sums(): lax.ppermute(sums, 'slab', [(i, i ^ step) for i in range(slabs)])  5.76 us
    ppermute x3, starting transfers between devices, sum_positions(): lax.ppermute(term, ('pos', 'slab'), partners(step, positions, slabs))  4.75 us
    ppermute x1, starting transfers between devices, local(): near_part_in = lax.ppermute(near_part, 'slab', pairs(slabs, 0))  3.99 us
    ppermute x3, waiting for transfers between devices, sum_positions(): arrived = lax.ppermute(term, ('pos', 'slab'), partners(0, positions, slabs))  3.89 us
    ppermute x3, starting transfers between devices, sum_positions(): arrived = lax.ppermute(term, ('pos', 'slab'), partners(0, positions, slabs))  3.58 us
    pallas_call x3, Pallas kernels, local(): pl.pallas_call(functools.partial(close_kernel, first_rows(radial)[index])...  2.09 us
    pallas_call x1, Pallas kernels, local(): pl.pallas_call(sums_kernel, out_shape=(f32((2,) + plane), f32((1,) + plan...  1.97 us
  transfers between devices with their start and end apart: 14, of which 7 were waited for; matrix products, arithmetic and copies ran while one was open for 2% of the time, Pallas kernels for 12%

profile of v6, /device:TPU:0, one launch (start us, length us, event | category | flops | bytes accessed | tf_op | source)
XLA Modules:
  0.0 45.1 jit_solution(2140430051640292375)
XLA Ops:
  1.3 1.4 %open.1 = (f32[2,256,256]{2,1,0:T(8,128)S(1)}, f32[3,256,256]{2,1,0:T(8,128)S(1)}, f32[1,256,256]{2,1,0:T(8,128)S(1)}) custom-call(f32[4]{0:T(128)} %reluctivity.1, s32[1]{0:T(128)S(6)} %copy.13.shift, s32[2,256,256]{2,1,0:T(8,128)} %labels.1, f32[2,256,256]{2,1,0:T(8,128)} %bitcast.6, f32[2,256,256]{2,1,0:T(8,128)} %bitcast.4), custom_call_target="tpu_custom_call" | custom-call | tf_op jit(solution)/shard_map/open/pallas_call | solution.py:276
  3.2 0.7 %collective-permute-start = (f32[2,256,256]{2,1,0:T(8,128)S(1)}, f32[2,256,256]{2,1,0:T(8,128)S(1)}, u32[]{:S(2)}, u32[]{:S(2)}) collective-permute-start(f32[2,256,256]{2,1,0:T(8,128)S(1)} %get-tuple-element.16.far), channel_id=1, source_target_pairs={{1,2},{2,1},{3,4},{4,3},{5,6},{6,5},{9,10},{10,9},{11,12},{12,11},... | collective-permute-start | bytes 1572872 | tf_op jit(solution)/shard_map/ppermute | solution.py:289
  3.9 1.9 %part.1 = (f32[1,256,256]{2,1,0:T(8,128)S(1)}, f32[1,256,256]{2,1,0:T(8,128)S(1)}) custom-call(f32[2,256,256]{2,1,0:T(8,128)S(1)} %get-tuple-element.16.far, f32[3,256,256]{2,1,0:T(8,128)S(1)} %get-tuple-element.17.near), custom_call_target="tpu_custom_call" | custom-call | tf_op jit(solution)/shard_map/part/pallas_call | solution.py:291
  5.9 4.0 %collective-permute-start.3 = (f32[1,256,256]{2,1,0:T(8,128)S(1)}, f32[1,256,256]{2,1,0:T(8,128)S(1)}, u32[]{:S(2)}, u32[]{:S(2)}) collective-permute-start(f32[1,256,256]{2,1,0:T(8,128)S(1)} %get-tuple-element.19.near_part), channel_id=1, source_target_pairs={{0,1},{1,0},{2,3},{3,2},{4,5},{5,4},{6,7},{7,6},{8,9},{9,8},{10,11... | collective-permute-start | bytes 786440 | tf_op jit(solution)/shard_map/ppermute | solution.py:300
  10.5 0.7 %collective-permute-start.7 = (f32[1,256,256]{2,1,0:T(8,128)S(1)}, f32[1,256,256]{2,1,0:T(8,128)S(1)}, u32[]{:S(2)}, u32[]{:S(2)}) collective-permute-start(f32[1,256,256]{2,1,0:T(8,128)S(1)} %get-tuple-element.25), channel_id=1, source_target_pairs={{1,2},{2,1},{3,4},{4,3},{5,6},{6,5},{9,10},{10,9},{11,12},{12,11},... | collective-permute-start | bytes 786440 | tf_op jit(solution)/shard_map/ppermute | solution.py:301
  11.2 2.0 %sums.1 = (f32[2,256,256]{2,1,0:T(8,128)S(1)}, f32[1,256,256]{2,1,0:T(8,128)S(1)}, f32[8,128]{1,0:T(8,128)S(1)}) custom-call(f32[2,256,256]{2,1,0:T(8,128)S(1)} %get-tuple-element.16.far, f32[3,256,256]{2,1,0:T(8,128)S(1)} %get-tuple-element.17.near, f32[1,256,256]{2,1,0:T(8,128)S(1)} %get-tuple-element.18.far_part, ...), custom_call_target="tpu_custom_call" | custom-call | tf_op jit(solution)/shard_map/sums/pallas_call | solution.py:302
  13.5 5.9 %collective-permute-start.4 = (f32[5,8,128]{2,1,0:T(8,128)S(1)}, f32[5,8,128]{2,1,0:T(8,128)S(1)}, u32[]{:S(2)}, u32[]{:S(2)}) collective-permute-start(f32[5,8,128]{2,1,0:T(8,128)S(1)} %get-tuple-element.22), channel_id=1, source_target_pairs={{0,2},{1,3},{2,0},{3,1},{4,6},{5,7},{6,4},{7,5},{8,10},{9,11},{10,... | collective-permute-start | bytes 61448 | tf_op jit(solution)/shard_map/ppermute | solution.py:243
  19.5 2.3 %collective-permute-done.4 = f32[5,8,128]{2,1,0:T(8,128)S(1)} collective-permute-done((f32[5,8,128]{2,1,0:T(8,128)S(1)}, f32[5,8,128]{2,1,0:T(8,128)S(1)}, u32[]{:S(2)}, u32[]{:S(2)}) %collective-permute-start.4) | collective-permute-done | bytes 20512 | tf_op jit(solution)/shard_map/ppermute | solution.py:243
  21.8 2.5 %collective-permute-start.5 = (f32[5,8,128]{2,1,0:T(8,128)S(1)}, f32[5,8,128]{2,1,0:T(8,128)S(1)}, u32[]{:S(2)}, u32[]{:S(2)}) collective-permute-start(f32[5,8,128]{2,1,0:T(8,128)S(1)} %add.18), channel_id=1, source_target_pairs={{0,4},{1,5},{2,6},{3,7},{4,0},{5,1},{6,2},{7,3},{8,12},{9,13},{10,... | collective-permute-start | bytes 61448 | tf_op jit(solution)/shard_map/ppermute | solution.py:243
  24.3 2.3 %collective-permute-done.5 = f32[5,8,128]{2,1,0:T(8,128)S(1)} collective-permute-done((f32[5,8,128]{2,1,0:T(8,128)S(1)}, f32[5,8,128]{2,1,0:T(8,128)S(1)}, u32[]{:S(2)}, u32[]{:S(2)}) %collective-permute-start.5) | collective-permute-done | bytes 20512 | tf_op jit(solution)/shard_map/ppermute | solution.py:243
  26.6 1.2 %collective-permute-done.6 = f32[5,8,128]{2,1,0:T(8,128)S(1)} collective-permute-done((f32[5,8,128]{2,1,0:T(8,128)S(1)}, f32[5,8,128]{2,1,0:T(8,128)S(1)}, u32[]{:S(2)}, u32[]{:S(2)}) %collective-permute-start.6) | collective-permute-done | bytes 20512 | tf_op jit(solution)/shard_map/ppermute | solution.py:243
  27.8 0.9 %finish.1 = (f32[2,256,256]{2,1,0:T(8,128)S(1)}, f32[2,96,256]{2,1,0:T(8,128)S(1)}, f32[2,96,256]{2,1,0:T(8,128)S(1)}, f32[2,64,256]{2,1,0:T(8,128)S(1)}) custom-call(f32[5,8,128]{2,1,0:T(8,128)S(1)} %add.20.sums, f32[2,256,256]{2,1,0:T(8,128)S(1)} %get-tuple-element.16.far, f32[3,256,256]{2,1,0:T(8,128)S(1)} %get-tuple-element.17.near, ...), custom_call_target="tpu_custom_call" | custom-call | tf_op jit(solution)/shard_map/finish/pallas_call | solution.py:320
  28.7 1.6 %collective-permute-start.12 = (f32[2,96,256]{2,1,0:T(8,128)S(1)}, f32[2,96,256]{2,1,0:T(8,128)S(1)}, u32[]{:S(2)}, u32[]{:S(2)}) collective-permute-start(f32[2,96,256]{2,1,0:T(8,128)S(1)} %get-tuple-element.28), channel_id=1, source_target_pairs={{0,8},{1,17},{2,10},{3,19},{4,12},{5,21},{6,14},{7,23},{8,0},{9,25... | collective-permute-start | bytes 589832 | tf_op jit(solution)/shard_map/ppermute | solution.py:258
  30.8 1.5 %collective-permute-start.8 = (f32[2,64,256]{2,1,0:T(8,128)S(1)}, f32[2,64,256]{2,1,0:T(8,128)S(1)}, u32[]{:S(2)}, u32[]{:S(2)}) collective-permute-start(f32[2,64,256]{2,1,0:T(8,128)S(1)} %get-tuple-element.26), channel_id=1, source_target_pairs={{0,8},{1,17},{2,10},{3,19},{4,12},{5,21},{6,14},{7,23},{8,0},{9,25... | collective-permute-start | bytes 393224 | tf_op jit(solution)/shard_map/ppermute | solution.py:258
  32.3 2.2 %collective-permute-done.12 = f32[2,96,256]{2,1,0:T(8,128)S(1)} collective-permute-done((f32[2,96,256]{2,1,0:T(8,128)S(1)}, f32[2,96,256]{2,1,0:T(8,128)S(1)}, u32[]{:S(2)}, u32[]{:S(2)}) %collective-permute-start.12) | collective-permute-done | bytes 196640 | tf_op jit(solution)/shard_map/ppermute | solution.py:258
  34.4 1.6 %collective-permute-start.13 = (f32[2,96,256]{2,1,0:T(8,128)S(1)}, f32[2,96,256]{2,1,0:T(8,128)S(1)}, u32[]{:S(2)}, u32[]{:S(2)}) collective-permute-start(f32[2,96,256]{2,1,0:T(8,128)S(1)} %add.23.total), channel_id=1, source_target_pairs={{0,16},{1,9},{2,18},{3,11},{4,20},{5,13},{6,22},{7,15},{8,24},{9,1... | collective-permute-start | bytes 589832 | tf_op jit(solution)/shard_map/ppermute | solution.py:261
  36.6 1.6 %collective-permute-start.11 = (f32[2,96,256]{2,1,0:T(8,128)S(1)}, f32[2,96,256]{2,1,0:T(8,128)S(1)}, u32[]{:S(2)}, u32[]{:S(2)}) collective-permute-start(f32[2,96,256]{2,1,0:T(8,128)S(1)} %add.22.total), channel_id=1, source_target_pairs={{0,16},{1,9},{2,18},{3,11},{4,20},{5,13},{6,22},{7,15},{8,24},{9,1... | collective-permute-start | bytes 589832 | tf_op jit(solution)/shard_map/ppermute | solution.py:261
  38.2 1.2 %collective-permute-done.8 = f32[2,64,256]{2,1,0:T(8,128)S(1)} collective-permute-done((f32[2,64,256]{2,1,0:T(8,128)S(1)}, f32[2,64,256]{2,1,0:T(8,128)S(1)}, u32[]{:S(2)}, u32[]{:S(2)}) %collective-permute-start.8) | collective-permute-done | bytes 131104 | tf_op jit(solution)/shard_map/ppermute | solution.py:258
  39.4 1.6 %collective-permute-start.9 = (f32[2,64,256]{2,1,0:T(8,128)S(1)}, f32[2,64,256]{2,1,0:T(8,128)S(1)}, u32[]{:S(2)}, u32[]{:S(2)}) collective-permute-start(f32[2,64,256]{2,1,0:T(8,128)S(1)} %add.21.total), channel_id=1, source_target_pairs={{0,16},{1,9},{2,18},{3,11},{4,20},{5,13},{6,22},{7,15},{8,24},{9,1... | collective-permute-start | bytes 393224 | tf_op jit(solution)/shard_map/ppermute | solution.py:261
  41.0 0.8 %copy.12 = f32[1,2,256,256]{3,2,1,0:T(8,128)} copy(f32[1,2,256,256]{3,2,1,0:T(8,128)S(1)} %bitcast.3) | data formatting | bytes 1048576
  41.8 0.7 %close.3.rest_0_ = f32[2,256,256]{2,1,0:T(8,128)} custom-call(f32[2,96,256]{2,1,0:T(8,128)S(1)} %add.23.total, f32[2,96,256]{2,1,0:T(8,128)S(1)} %collective-permute-done.13.arrived), custom_call_target="tpu_custom_call" | custom-call | tf_op jit(solution)/shard_map/close/pallas_call | solution.py:332
  42.5 0.7 %close.4.rest_0_ = f32[2,256,256]{2,1,0:T(8,128)} custom-call(f32[2,96,256]{2,1,0:T(8,128)S(1)} %add.22.total, f32[2,96,256]{2,1,0:T(8,128)S(1)} %collective-permute-done.11.arrived, f32[2,256,256]{2,1,0:T(8,128)} %close.3.rest_0_), custom_call_target="tpu_custom_call", output_to_operand_aliasing={{}: (2, {})} | custom-call | tf_op jit(solution)/shard_map/close/pallas_call | solution.py:332
  43.2 1.2 %collective-permute-done.9.arrived = f32[2,64,256]{2,1,0:T(8,128)S(1)} collective-permute-done((f32[2,64,256]{2,1,0:T(8,128)S(1)}, f32[2,64,256]{2,1,0:T(8,128)S(1)}, u32[]{:S(2)}, u32[]{:S(2)}) %collective-permute-start.9) | collective-permute-done | bytes 131104 | tf_op jit(solution)/shard_map/ppermute | solution.py:261
  44.4 0.7 %close.5 = f32[2,256,256]{2,1,0:T(8,128)} custom-call(f32[2,64,256]{2,1,0:T(8,128)S(1)} %add.21.total, f32[2,64,256]{2,1,0:T(8,128)S(1)} %collective-permute-done.9.arrived, f32[2,256,256]{2,1,0:T(8,128)} %close.4.rest_0_), custom_call_target="tpu_custom_call", output_to_operand_aliasing={{}: (2, {})} | custom-call | tf_op jit(solution)/shard_map/close/pallas_call | solution.py:332
  (23 shorter events, 2.7 us)
Async XLA Ops:
  2.7 8.5 %collective-permute-start.2 = (f32[3,256,256]{2,1,0:T(8,128)S(1)}, f32[3,256,256]{2,1,0:T(8,128)S(1)}, u32[]{:S(2)}, u32[]{:S(2)}) collective-permute-start(f32[3,256,256]{2,1,0:T(8,128)S(1)} %get-tuple-element.17.near), channel_id=1, source_target_pairs={{0,1},{1,0},{2,3},{3,2},{4,5},{5,4},{6,7},{7,6},{8,9},{9,8},{10,11... | collective-permute-start | bytes 2359304 | tf_op jit(solution)/shard_map/ppermute | solution.py:290
  3.2 8.0 %collective-permute-start = (f32[2,256,256]{2,1,0:T(8,128)S(1)}, f32[2,256,256]{2,1,0:T(8,128)S(1)}, u32[]{:S(2)}, u32[]{:S(2)}) collective-permute-start(f32[2,256,256]{2,1,0:T(8,128)S(1)} %get-tuple-element.16.far), channel_id=1, source_target_pairs={{1,2},{2,1},{3,4},{4,3},{5,6},{6,5},{9,10},{10,9},{11,12},{12,11},... | collective-permute-start | bytes 1572872 | tf_op jit(solution)/shard_map/ppermute | solution.py:289
  5.9 5.4 %collective-permute-start.3 = (f32[1,256,256]{2,1,0:T(8,128)S(1)}, f32[1,256,256]{2,1,0:T(8,128)S(1)}, u32[]{:S(2)}, u32[]{:S(2)}) collective-permute-start(f32[1,256,256]{2,1,0:T(8,128)S(1)} %get-tuple-element.19.near_part), channel_id=1, source_target_pairs={{0,1},{1,0},{2,3},{3,2},{4,5},{5,4},{6,7},{7,6},{8,9},{9,8},{10,11... | collective-permute-start | bytes 786440 | tf_op jit(solution)/shard_map/ppermute | solution.py:300
  9.9 3.4 %collective-permute-start.1 = (f32[1,256,256]{2,1,0:T(8,128)S(1)}, f32[1,256,256]{2,1,0:T(8,128)S(1)}, u32[]{:S(2)}, u32[]{:S(2)}) collective-permute-start(f32[1,256,256]{2,1,0:T(8,128)S(1)} %get-tuple-element.18.far_part), channel_id=1, source_target_pairs={{1,2},{2,1},{3,4},{4,3},{5,6},{6,5},{9,10},{10,9},{11,12},{12,11},... | collective-permute-start | bytes 786440 | tf_op jit(solution)/shard_map/ppermute | solution.py:299
  10.5 17.2 %collective-permute-start.7 = (f32[1,256,256]{2,1,0:T(8,128)S(1)}, f32[1,256,256]{2,1,0:T(8,128)S(1)}, u32[]{:S(2)}, u32[]{:S(2)}) collective-permute-start(f32[1,256,256]{2,1,0:T(8,128)S(1)} %get-tuple-element.25), channel_id=1, source_target_pairs={{1,2},{2,1},{3,4},{4,3},{5,6},{6,5},{9,10},{10,9},{11,12},{12,11},... | collective-permute-start | bytes 786440 | tf_op jit(solution)/shard_map/ppermute | solution.py:301
  13.2 14.5 %copy-start = (f32[1,2,256,256]{3,2,1,0:T(8,128)S(1)}, f32[1,2,256,256]{3,2,1,0:T(8,128)}, u32[]{:S(2)}) copy-start(f32[1,2,256,256]{3,2,1,0:T(8,128)} %param.10) | copy-start | bytes 1572868
  13.2 14.5 %copy-start.1 = (s32[2,256,256]{2,1,0:T(8,128)S(1)}, s32[2,256,256]{2,1,0:T(8,128)}, u32[]{:S(2)}) copy-start(s32[2,256,256]{2,1,0:T(8,128)} %mask.1) | copy-start | bytes 1572868
  13.5 8.2 %collective-permute-start.4 = (f32[5,8,128]{2,1,0:T(8,128)S(1)}, f32[5,8,128]{2,1,0:T(8,128)S(1)}, u32[]{:S(2)}, u32[]{:S(2)}) collective-permute-start(f32[5,8,128]{2,1,0:T(8,128)S(1)} %get-tuple-element.22), channel_id=1, source_target_pairs={{0,2},{1,3},{2,0},{3,1},{4,6},{5,7},{6,4},{7,5},{8,10},{9,11},{10,... | collective-permute-start | bytes 61448 | tf_op jit(solution)/shard_map/ppermute | solution.py:243
  21.8 4.8 %collective-permute-start.5 = (f32[5,8,128]{2,1,0:T(8,128)S(1)}, f32[5,8,128]{2,1,0:T(8,128)S(1)}, u32[]{:S(2)}, u32[]{:S(2)}) collective-permute-start(f32[5,8,128]{2,1,0:T(8,128)S(1)} %add.18), channel_id=1, source_target_pairs={{0,4},{1,5},{2,6},{3,7},{4,0},{5,1},{6,2},{7,3},{8,12},{9,13},{10,... | collective-permute-start | bytes 61448 | tf_op jit(solution)/shard_map/ppermute | solution.py:243
  26.6 1.2 %collective-permute-start.6 = (f32[5,8,128]{2,1,0:T(8,128)S(1)}, f32[5,8,128]{2,1,0:T(8,128)S(1)}, u32[]{:S(2)}, u32[]{:S(2)}) collective-permute-start(f32[5,8,128]{2,1,0:T(8,128)S(1)} %add.19), channel_id=1, source_target_pairs={{0,1},{1,0},{2,3},{3,2},{4,5},{5,4},{6,7},{7,6},{8,9},{9,8},{10,11... | collective-permute-start | bytes 61448 | tf_op jit(solution)/shard_map/ppermute | solution.py:243
  28.7 5.7 %collective-permute-start.12 = (f32[2,96,256]{2,1,0:T(8,128)S(1)}, f32[2,96,256]{2,1,0:T(8,128)S(1)}, u32[]{:S(2)}, u32[]{:S(2)}) collective-permute-start(f32[2,96,256]{2,1,0:T(8,128)S(1)} %get-tuple-element.28), channel_id=1, source_target_pairs={{0,8},{1,17},{2,10},{3,19},{4,12},{5,21},{6,14},{7,23},{8,0},{9,25... | collective-permute-start | bytes 589832 | tf_op jit(solution)/shard_map/ppermute | solution.py:258
  30.2 6.3 %collective-permute-start.10 = (f32[2,96,256]{2,1,0:T(8,128)S(1)}, f32[2,96,256]{2,1,0:T(8,128)S(1)}, u32[]{:S(2)}, u32[]{:S(2)}) collective-permute-start(f32[2,96,256]{2,1,0:T(8,128)S(1)} %get-tuple-element.27), channel_id=1, source_target_pairs={{0,8},{1,17},{2,10},{3,19},{4,12},{5,21},{6,14},{7,23},{8,0},{9,25... | collective-permute-start | bytes 589832 | tf_op jit(solution)/shard_map/ppermute | solution.py:258
  30.8 8.6 %collective-permute-start.8 = (f32[2,64,256]{2,1,0:T(8,128)S(1)}, f32[2,64,256]{2,1,0:T(8,128)S(1)}, u32[]{:S(2)}, u32[]{:S(2)}) collective-permute-start(f32[2,64,256]{2,1,0:T(8,128)S(1)} %get-tuple-element.26), channel_id=1, source_target_pairs={{0,8},{1,17},{2,10},{3,19},{4,12},{5,21},{6,14},{7,23},{8,0},{9,25... | collective-permute-start | bytes 393224 | tf_op jit(solution)/shard_map/ppermute | solution.py:258
  34.4 7.3 %collective-permute-start.13 = (f32[2,96,256]{2,1,0:T(8,128)S(1)}, f32[2,96,256]{2,1,0:T(8,128)S(1)}, u32[]{:S(2)}, u32[]{:S(2)}) collective-permute-start(f32[2,96,256]{2,1,0:T(8,128)S(1)} %add.23.total), channel_id=1, source_target_pairs={{0,16},{1,9},{2,18},{3,11},{4,20},{5,13},{6,22},{7,15},{8,24},{9,1... | collective-permute-start | bytes 589832 | tf_op jit(solution)/shard_map/ppermute | solution.py:261
  36.6 5.9 %collective-permute-start.11 = (f32[2,96,256]{2,1,0:T(8,128)S(1)}, f32[2,96,256]{2,1,0:T(8,128)S(1)}, u32[]{:S(2)}, u32[]{:S(2)}) collective-permute-start(f32[2,96,256]{2,1,0:T(8,128)S(1)} %add.22.total), channel_id=1, source_target_pairs={{0,16},{1,9},{2,18},{3,11},{4,20},{5,13},{6,22},{7,15},{8,24},{9,1... | collective-permute-start | bytes 589832 | tf_op jit(solution)/shard_map/ppermute | solution.py:261
  39.4 5.0 %collective-permute-start.9 = (f32[2,64,256]{2,1,0:T(8,128)S(1)}, f32[2,64,256]{2,1,0:T(8,128)S(1)}, u32[]{:S(2)}, u32[]{:S(2)}) collective-permute-start(f32[2,64,256]{2,1,0:T(8,128)S(1)} %add.21.total), channel_id=1, source_target_pairs={{0,16},{1,9},{2,18},{3,11},{4,20},{5,13},{6,22},{7,15},{8,24},{9,1... | collective-permute-start | bytes 393224 | tf_op jit(solution)/shard_map/ppermute | solution.py:261

commit v7 on v6

--- a/solution.py
+++ b/solution.py
@@ -166,12 +166,38 @@
         sums[index] = jnp.where(here, value, 0.0)
 
 
-def finish_kernel(
-    sums, far, near, far_in, near_in, image, far_image_in, near_image_in, potential, far_potential, mask, adjoint, *rest
+def fields_kernel(
+    far, near, far_in, near_in, image, far_image_in, near_image_in, potential, far_potential, mask, u1, u2, u3
 ):
-    *terms, mixed, mixed_in = rest
     _, even = place()
     total = far.shape[1]
+    scale = 0.25 / lax.axis_size("pos")
+    sides = ((far, even, far_in, far_image_in, far_potential, 0), (near, 1 - even, near_in, near_image_in, near_in, 2))
+    for side, (own, layer, halo, image_in, halo_potential, at) in enumerate(sides):
+        other = (near, far)[side]
+        for start in range(0, total, ROWS):
+            rows = slice(start, start + ROWS)
+            slopes = []
+            for ref, index, beyond, inner in (
+                (potential, layer, halo_potential[at, rows, :], potential[1 - layer, rows, :]),
+                (own, 1, halo[1, rows, :], other[1, rows, :]),
+                (image, side, image_in[0, rows, :], image[1 - side, rows, :]),
+            ):
+                field = ref[index, rows, :]
+                slopes.append(
+                    (
+                        beyond - inner,
+                        turn(field, -1) - turn(field, 1),
+                        shifted(ref, index, start, 1) - shifted(ref, index, start, -1),
+                    )
+                )
+            weight = scale * (mask[layer, rows, :].astype(jnp.float32) * own[0, rows, :])
+            g = [weight * slope for slope in slopes[0]]
+            for out, factor, slope in ((u1, 1.0, slopes[1]), (u2, 1.0, slopes[2]), (u3, 0.5, slopes[0])):
+                out[layer, rows, :] = factor * (g[0] * slope[0] + g[1] * slope[1] + g[2] * slope[2])
+
+
+def coefficients(sums):
     m0_d, m1_d, q_d, s_d, t_d = (sums[i] for i in range(SUMS))
     m0 = jnp.sum(m0_d, axis=0, keepdims=True)
     m1 = jnp.sum(m1_d, axis=0, keepdims=True)
@@ -183,35 +209,30 @@
     beta = alpha0 * (ww * alpha0 / m0)
     divisor = waw - ww * (ww / m1)
     alpha1 = jnp.where(divisor == 0, 0.0, ww / divisor)
-    a = (alpha0 + alpha1 * (1.0 + beta))[:, 0:1]
-    b = (-alpha1 * alpha0)[:, 0:1]
-    scale = 0.25 / lax.axis_size("pos")
-    firsts = first_rows(total)
-    sides = ((far, even, far_in, far_image_in, far_potential, 0), (near, 1 - even, near_in, near_image_in, near_in, 2))
-    for side, (own, layer, halo, image_in, halo_potential, at) in enumerate(sides):
-        for start in range(0, total, ROWS):
-            rows = slice(start, start + ROWS)
-            out = a * own[1, rows, :] + b * image[side, rows, :]
-            adjoint[layer, rows, :] = out
-            mixed[side, rows, :] = out + 0.5 * potential[layer, rows, :]
-            outer = a * halo[1, rows, :] + b * image_in[0, rows, :]
-            mixed_in[side, rows, :] = outer + 0.5 * halo_potential[at, rows, :]
-    for side, (own, layer, halo, image_in, halo_potential, at) in enumerate(sides):
-        for start in range(0, total, ROWS):
-            rows = slice(start, start + ROWS)
-            g = potential[layer, rows, :]
-            f = mixed[side, rows, :]
-            result = (halo_potential[at, rows, :] - potential[1 - layer, rows, :]) * (
-                mixed_in[side, rows, :] - mixed[1 - side, rows, :]
-            )
-            result = result + (turn(g, -1) - turn(g, 1)) * (turn(f, -1) - turn(f, 1))
-            result = result + (
-                shifted(potential, layer, start, 1) - shifted(potential, layer, start, -1)
-            ) * (shifted(mixed, side, start, 1) - shifted(mixed, side, start, -1))
-            weight = mask[layer, rows, :].astype(jnp.float32) * own[0, rows, :]
-            index = max(i for i, first in enumerate(firsts) if first <= start)
-            at_row = start - firsts[index]
-            terms[index][layer, at_row : at_row + ROWS, :] = weight * (scale * result)
+    return (alpha0 + alpha1 * (1.0 + beta))[:, 0:1], (-alpha1 * alpha0)[:, 0:1]
+
+
+def term_kernel(sums, u1, u2, u3, *terms):
+    a, b = coefficients(sums)
+    for term, first in zip(terms, first_rows(u1.shape[1])):
+        for layer in range(2):
+            for start in range(0, term.shape[1], ROWS):
+                rows = slice(first + start, first + start + ROWS)
+                term[layer, start : start + ROWS, :] = (
+                    a * u1[layer, rows, :] + b * u2[layer, rows, :] + u3[layer, rows, :]
+                )
+
+
+def adjoint_kernel(sums, far, near, image, adjoint, held, sem):
+    _, even = place()
+    a, b = coefficients(sums)
+    for side, (own, layer) in enumerate(((far, even), (near, 1 - even))):
+        for start in range(0, far.shape[1], ROWS):
+            rows = slice(start, start + ROWS)
+            held[layer, rows, :] = a * own[1, rows, :] + b * image[side, rows, :]
+    copy = pltpu.make_async_copy(held, adjoint, sem)
+    copy.start()
+    copy.wait()
 
 
 def in_hbm(x):
@@ -237,11 +258,14 @@
     return out
 
 
-def gather_sums(sums, slabs):
+def gather_sums(sums, fields, slabs):
     steps = [2**k for k in range(1, slabs.bit_length() - 1)] + [1]
     for step in steps:
-        sums = sums + lax.ppermute(sums, "slab", [(i, i ^ step) for i in range(slabs)])
-    return sums
+        arrived = lax.ppermute(sums, "slab", [(i, i ^ step) for i in range(slabs)])
+        if step == steps[-2]:
+            arrived, *fields = lax.optimization_barrier((arrived, *fields))
+        sums = sums + arrived
+    return sums, fields
 
 
 def partners(step, positions, slabs):
@@ -265,7 +289,7 @@
 def local(labels, magnet_mask, reluctivity, rotor_shift, potential, adjoint_load):
     layers, radial, angular = labels.shape
     positions, slabs = lax.axis_size("pos"), lax.axis_size("slab")
-    if layers != 2 or slabs % 2 or slabs & (slabs - 1) or radial % (8 * ROWS) or positions < 2 or positions & (positions - 1):
+    if layers != 2 or slabs < 4 or slabs & (slabs - 1) or radial % (8 * ROWS) or positions < 2 or positions & (positions - 1):
         raise ValueError("unsupported sizes")
     potential, load = potential[0], adjoint_load[0]
     f32 = functools.partial(jax.ShapeDtypeStruct, dtype=jnp.float32)
@@ -315,17 +339,33 @@
         compiler_params=params(),
         name="face",
     )(far, far_in, far_part_in, image, own_sums)
-    sums = gather_sums(sums, slabs)
+    fields = pl.pallas_call(
+        fields_kernel,
+        out_shape=(f32((2,) + plane),) * 3,
+        in_specs=[vmem] * 10,
+        out_specs=(vmem,) * 3,
+        compiler_params=params(),
+        name="fields",
+    )(far, near, far_in, near_in, image, far_image_in, near_image_in, potential, far_potential, magnet_mask)
+    sums, fields = gather_sums(sums, fields, slabs)
     spans = [radial // 8 * k for k in EIGHTHS]
-    adjoint, *terms = pl.pallas_call(
-        finish_kernel,
-        out_shape=(pltpu.VMEM((2,) + plane, jnp.float32),) + tuple(f32((2, span, angular)) for span in spans),
-        in_specs=[vmem] * 11,
-        out_specs=(vmem,) * (1 + len(spans)),
-        scratch_shapes=[VMEM((2,) + plane, jnp.float32)] * 2,
-        compiler_params=params(),
-        name="finish",
-    )(sums, far, near, far_in, near_in, image, far_image_in, near_image_in, potential, far_potential, magnet_mask)
+    terms = pl.pallas_call(
+        term_kernel,
+        out_shape=tuple(f32((2, span, angular)) for span in spans),
+        in_specs=[vmem] * 4,
+        out_specs=(vmem,) * len(spans),
+        compiler_params=params(),
+        name="term",
+    )(sums, *fields)
+    adjoint = pl.pallas_call(
+        adjoint_kernel,
+        out_shape=pltpu.HBM((2,) + plane, jnp.float32),
+        in_specs=[vmem] * 4,
+        out_specs=hbm,
+        scratch_shapes=[VMEM((2,) + plane, jnp.float32), pltpu.SemaphoreType.DMA(())],
+        compiler_params=params(),
+        name="adjoint",
+    )(sums, far, near, image)
     gradient = ()
     for index, term in enumerate(terms):
         total, arrived = sum_positions(term, positions, slabs)

time: 45.3 us -> 44.6 us (0.985)
  waiting for transfers between devices: 10.9 us -> 9.69 us
  Pallas kernels: 8.57 us -> 9.69 us
  local copies, waits for them, and re-layouts: 0.81 us -> 0.01 us
    pallas_call x1 -> x3, Pallas kernels: 0.87 us -> 2.11 us  [the longest x1 0.97 us: local(): pl.pallas_call(fields_kernel, out_shape=(f32((2,) + plane),) * 3, in_spec...]
    ppermute x3, waiting for transfers between devices: 5.76 us -> 4.77 us  [gather_sums(): arrived = lax.ppermute(sums, 'slab', [(i, i ^ step) for i in range(slabs)])]
    unnamed x5 -> x4, local copies, waits for them, and re-layouts: 0.81 us -> 0.01 us
  transfers between devices with their start and end apart: 14 -> 14, of which waited for: 7 -> 7; matrix products, arithmetic and copies ran while one was open for 2% -> 0% of each run, Pallas kernels for 12% -> 17%
where the time goes in v7:
time: 44.6 us; the launch traced here: 44.4 us
  starting transfers between devices  23.4 us (52%)
  Pallas kernels  9.69 us (22%)
  waiting for transfers between devices  9.69 us (22%)
  between operations  1.46 us (3%)
    ppermute x3, starting transfers between devices, gather_sums(): arrived = lax.ppermute(sums, 'slab', [(i, i ^ step) for i in range(slabs)])  8.57 us
    ppermute x3, waiting for transfers between devices, gather_sums(): arrived = lax.ppermute(sums, 'slab', [(i, i ^ step) for i in range(slabs)])  4.77 us
    ppermute x3, starting transfers between devices, sum_positions(): lax.ppermute(term, ('pos', 'slab'), partners(step, positions, slabs))  4.75 us
    ppermute x1, starting transfers between devices, local(): near_part_in = lax.ppermute(near_part, 'slab', pairs(slabs, 0))  3.99 us
    ppermute x3, waiting for transfers between devices, sum_positions(): arrived = lax.ppermute(term, ('pos', 'slab'), partners(0, positions, slabs))  3.88 us
    ppermute x3, starting transfers between devices, sum_positions(): arrived = lax.ppermute(term, ('pos', 'slab'), partners(0, positions, slabs))  3.58 us
    pallas_call x3, Pallas kernels, local(): pl.pallas_call(functools.partial(close_kernel, first_rows(radial)[index])...  2.09 us
    pallas_call x1, Pallas kernels, local(): pl.pallas_call(part_kernel, out_shape=(pltpu.VMEM((1,) + plane, jnp.float...  1.94 us
  transfers between devices with their start and end apart: 14, of which 7 were waited for; matrix products, arithmetic and copies ran while one was open for 0% of the time, Pallas kernels for 17%

profile of v7, /device:TPU:0, one launch (start us, length us, event | category | flops | bytes accessed | tf_op | source)
XLA Modules:
  0.0 44.4 jit_solution(1847917368593830981)
XLA Ops:
  1.3 1.4 %open.1 = (f32[2,256,256]{2,1,0:T(8,128)S(1)}, f32[3,256,256]{2,1,0:T(8,128)S(1)}, f32[1,256,256]{2,1,0:T(8,128)S(1)}) custom-call(f32[4]{0:T(128)} %reluctivity.1, s32[1]{0:T(128)S(6)} %copy.12.shift, s32[2,256,256]{2,1,0:T(8,128)} %labels.1, f32[2,256,256]{2,1,0:T(8,128)} %bitcast.5, f32[2,256,256]{2,1,0:T(8,128)} %bitcast.3), custom_call_target="tpu_custom_call" | custom-call | tf_op jit(solution)/shard_map/open/pallas_call | solution.py:300
  3.2 0.7 %collective-permute-start = (f32[2,256,256]{2,1,0:T(8,128)S(1)}, f32[2,256,256]{2,1,0:T(8,128)S(1)}, u32[]{:S(2)}, u32[]{:S(2)}) collective-permute-start(f32[2,256,256]{2,1,0:T(8,128)S(1)} %get-tuple-element.22.far), channel_id=1, source_target_pairs={{1,2},{2,1},{3,4},{4,3},{5,6},{6,5},{9,10},{10,9},{11,12},{12,11},... | collective-permute-start | bytes 1572872 | tf_op jit(solution)/shard_map/ppermute | solution.py:313
  3.9 1.9 %part.1 = (f32[1,256,256]{2,1,0:T(8,128)S(1)}, f32[1,256,256]{2,1,0:T(8,128)S(1)}) custom-call(f32[2,256,256]{2,1,0:T(8,128)S(1)} %get-tuple-element.22.far, f32[3,256,256]{2,1,0:T(8,128)S(1)} %get-tuple-element.23.near), custom_call_target="tpu_custom_call" | custom-call | tf_op jit(solution)/shard_map/part/pallas_call | solution.py:315
  5.9 4.0 %collective-permute-start.3 = (f32[1,256,256]{2,1,0:T(8,128)S(1)}, f32[1,256,256]{2,1,0:T(8,128)S(1)}, u32[]{:S(2)}, u32[]{:S(2)}) collective-permute-start(f32[1,256,256]{2,1,0:T(8,128)S(1)} %get-tuple-element.25.near_part), channel_id=1, source_target_pairs={{0,1},{1,0},{2,3},{3,2},{4,5},{5,4},{6,7},{7,6},{8,9},{9,8},{10,11... | collective-permute-start | bytes 786440 | tf_op jit(solution)/shard_map/ppermute | solution.py:324
  10.5 0.7 %collective-permute-start.6 = (f32[1,256,256]{2,1,0:T(8,128)S(1)}, f32[1,256,256]{2,1,0:T(8,128)S(1)}, u32[]{:S(2)}, u32[]{:S(2)}) collective-permute-start(f32[1,256,256]{2,1,0:T(8,128)S(1)} %get-tuple-element.31), channel_id=1, source_target_pairs={{1,2},{2,1},{3,4},{4,3},{5,6},{6,5},{9,10},{10,9},{11,12},{12,11},... | collective-permute-start | bytes 786440 | tf_op jit(solution)/shard_map/ppermute | solution.py:325
  11.2 1.9 %sums.1 = (f32[2,256,256]{2,1,0:T(8,128)S(1)}, f32[1,256,256]{2,1,0:T(8,128)S(1)}, f32[8,128]{1,0:T(8,128)S(1)}) custom-call(f32[2,256,256]{2,1,0:T(8,128)S(1)} %get-tuple-element.22.far, f32[3,256,256]{2,1,0:T(8,128)S(1)} %get-tuple-element.23.near, f32[1,256,256]{2,1,0:T(8,128)S(1)} %get-tuple-element.24.far_part, ...), custom_call_target="tpu_custom_call" | custom-call | tf_op jit(solution)/shard_map/sums/pallas_call | solution.py:326
  13.4 6.0 %collective-permute-start.4 = (f32[5,8,128]{2,1,0:T(8,128)S(1)}, f32[5,8,128]{2,1,0:T(8,128)S(1)}, u32[]{:S(2)}, u32[]{:S(2)}) collective-permute-start(f32[5,8,128]{2,1,0:T(8,128)S(1)} %get-tuple-element.28), channel_id=1, source_target_pairs={{0,2},{1,3},{2,0},{3,1},{4,6},{5,7},{6,4},{7,5},{8,10},{9,11},{10,... | collective-permute-start | bytes 61448 | tf_op jit(solution)/shard_map/ppermute | solution.py:264
  19.5 2.3 %collective-permute-done.4 = f32[5,8,128]{2,1,0:T(8,128)S(1)} collective-permute-done((f32[5,8,128]{2,1,0:T(8,128)S(1)}, f32[5,8,128]{2,1,0:T(8,128)S(1)}, u32[]{:S(2)}, u32[]{:S(2)}) %collective-permute-start.4) | collective-permute-done | bytes 20512 | tf_op jit(solution)/shard_map/ppermute | solution.py:264
  21.8 2.5 %collective-permute-start.5 = (f32[5,8,128]{2,1,0:T(8,128)S(1)}, f32[5,8,128]{2,1,0:T(8,128)S(1)}, u32[]{:S(2)}, u32[]{:S(2)}) collective-permute-start(f32[5,8,128]{2,1,0:T(8,128)S(1)} %add.18), channel_id=1, source_target_pairs={{0,4},{1,5},{2,6},{3,7},{4,0},{5,1},{6,2},{7,3},{8,12},{9,13},{10,... | collective-permute-start | bytes 61448 | tf_op jit(solution)/shard_map/ppermute | solution.py:264
  24.3 1.0 %fields.1 = (f32[2,256,256]{2,1,0:T(8,128)S(1)}, f32[2,256,256]{2,1,0:T(8,128)S(1)}, f32[2,256,256]{2,1,0:T(8,128)S(1)}) custom-call(f32[2,256,256]{2,1,0:T(8,128)S(1)} %get-tuple-element.22.far, f32[3,256,256]{2,1,0:T(8,128)S(1)} %get-tuple-element.23.near, f32[2,256,256]{2,1,0:T(8,128)S(1)} %collective-permute-done.far_in, ...), custom_call_target="tpu_custom_call" | custom-call | tf_op jit(solution)/shard_map/fields/pallas_call | solution.py:342
  25.3 1.3 %collective-permute-done.5 = f32[5,8,128]{2,1,0:T(8,128)S(1)} collective-permute-done((f32[5,8,128]{2,1,0:T(8,128)S(1)}, f32[5,8,128]{2,1,0:T(8,128)S(1)}, u32[]{:S(2)}, u32[]{:S(2)}) %collective-permute-start.5) | collective-permute-done | bytes 20512 | tf_op jit(solution)/shard_map/ppermute | solution.py:264
  26.6 1.2 %collective-permute-done.7 = f32[5,8,128]{2,1,0:T(8,128)S(1)} collective-permute-done((f32[5,8,128]{2,1,0:T(8,128)S(1)}, f32[5,8,128]{2,1,0:T(8,128)S(1)}, u32[]{:S(2)}, u32[]{:S(2)}) %collective-permute-start.7) | collective-permute-done | bytes 20512 | tf_op jit(solution)/shard_map/ppermute | solution.py:264
  28.0 1.6 %collective-permute-start.12 = (f32[2,96,256]{2,1,0:T(8,128)S(1)}, f32[2,96,256]{2,1,0:T(8,128)S(1)}, u32[]{:S(2)}, u32[]{:S(2)}) collective-permute-start(f32[2,96,256]{2,1,0:T(8,128)S(1)} %get-tuple-element.41), channel_id=1, source_target_pairs={{0,8},{1,17},{2,10},{3,19},{4,12},{5,21},{6,14},{7,23},{8,0},{9,25... | collective-permute-start | bytes 589832 | tf_op jit(solution)/shard_map/ppermute | solution.py:282
  30.0 1.5 %collective-permute-start.8 = (f32[2,64,256]{2,1,0:T(8,128)S(1)}, f32[2,64,256]{2,1,0:T(8,128)S(1)}, u32[]{:S(2)}, u32[]{:S(2)}) collective-permute-start(f32[2,64,256]{2,1,0:T(8,128)S(1)} %get-tuple-element.39), channel_id=1, source_target_pairs={{0,8},{1,17},{2,10},{3,19},{4,12},{5,21},{6,14},{7,23},{8,0},{9,25... | collective-permute-start | bytes 393224 | tf_op jit(solution)/shard_map/ppermute | solution.py:282
  31.5 2.2 %collective-permute-done.12 = f32[2,96,256]{2,1,0:T(8,128)S(1)} collective-permute-done((f32[2,96,256]{2,1,0:T(8,128)S(1)}, f32[2,96,256]{2,1,0:T(8,128)S(1)}, u32[]{:S(2)}, u32[]{:S(2)}) %collective-permute-start.12) | collective-permute-done | bytes 196640 | tf_op jit(solution)/shard_map/ppermute | solution.py:282
  33.7 1.6 %collective-permute-start.13 = (f32[2,96,256]{2,1,0:T(8,128)S(1)}, f32[2,96,256]{2,1,0:T(8,128)S(1)}, u32[]{:S(2)}, u32[]{:S(2)}) collective-permute-start(f32[2,96,256]{2,1,0:T(8,128)S(1)} %add.23.total), channel_id=1, source_target_pairs={{0,16},{1,9},{2,18},{3,11},{4,20},{5,13},{6,22},{7,15},{8,24},{9,1... | collective-permute-start | bytes 589832 | tf_op jit(solution)/shard_map/ppermute | solution.py:285
  35.9 1.6 %collective-permute-start.11 = (f32[2,96,256]{2,1,0:T(8,128)S(1)}, f32[2,96,256]{2,1,0:T(8,128)S(1)}, u32[]{:S(2)}, u32[]{:S(2)}) collective-permute-start(f32[2,96,256]{2,1,0:T(8,128)S(1)} %add.22.total), channel_id=1, source_target_pairs={{0,16},{1,9},{2,18},{3,11},{4,20},{5,13},{6,22},{7,15},{8,24},{9,1... | collective-permute-start | bytes 589832 | tf_op jit(solution)/shard_map/ppermute | solution.py:285
  37.4 1.2 %collective-permute-done.8 = f32[2,64,256]{2,1,0:T(8,128)S(1)} collective-permute-done((f32[2,64,256]{2,1,0:T(8,128)S(1)}, f32[2,64,256]{2,1,0:T(8,128)S(1)}, u32[]{:S(2)}, u32[]{:S(2)}) %collective-permute-start.8) | collective-permute-done | bytes 131104 | tf_op jit(solution)/shard_map/ppermute | solution.py:282
  38.7 1.6 %collective-permute-start.9 = (f32[2,64,256]{2,1,0:T(8,128)S(1)}, f32[2,64,256]{2,1,0:T(8,128)S(1)}, u32[]{:S(2)}, u32[]{:S(2)}) collective-permute-start(f32[2,64,256]{2,1,0:T(8,128)S(1)} %add.21.total), channel_id=1, source_target_pairs={{0,16},{1,9},{2,18},{3,11},{4,20},{5,13},{6,22},{7,15},{8,24},{9,1... | collective-permute-start | bytes 393224 | tf_op jit(solution)/shard_map/ppermute | solution.py:285
  40.2 1.0 %adjoint.1 = f32[2,256,256]{2,1,0:T(8,128)} custom-call(f32[5,8,128]{2,1,0:T(8,128)S(1)} %add.20.sums, f32[2,256,256]{2,1,0:T(8,128)S(1)} %get-tuple-element.22.far, f32[3,256,256]{2,1,0:T(8,128)S(1)} %get-tuple-element.23.near, f32[2,256,256]{2,1,0:T(8,128)S(1)} %get-tuple-element.26.image), custom_call_target="tpu_custom_call" | custom-call | tf_op jit(solution)/shard_map/adjoint/pallas_call | solution.py:360
  41.2 0.7 %close.3.rest_0_ = f32[2,256,256]{2,1,0:T(8,128)} custom-call(f32[2,96,256]{2,1,0:T(8,128)S(1)} %add.23.total, f32[2,96,256]{2,1,0:T(8,128)S(1)} %collective-permute-done.13.arrived), custom_call_target="tpu_custom_call" | custom-call | tf_op jit(solution)/shard_map/close/pallas_call | solution.py:372
  42.0 0.7 %close.4.rest_0_ = f32[2,256,256]{2,1,0:T(8,128)} custom-call(f32[2,96,256]{2,1,0:T(8,128)S(1)} %add.22.total, f32[2,96,256]{2,1,0:T(8,128)S(1)} %collective-permute-done.11.arrived, f32[2,256,256]{2,1,0:T(8,128)} %close.3.rest_0_), custom_call_target="tpu_custom_call", output_to_operand_aliasing={{}: (2, {})} | custom-call | tf_op jit(solution)/shard_map/close/pallas_call | solution.py:372
  42.7 1.0 %collective-permute-done.9.arrived = f32[2,64,256]{2,1,0:T(8,128)S(1)} collective-permute-done((f32[2,64,256]{2,1,0:T(8,128)S(1)}, f32[2,64,256]{2,1,0:T(8,128)S(1)}, u32[]{:S(2)}, u32[]{:S(2)}) %collective-permute-start.9) | collective-permute-done | bytes 131104 | tf_op jit(solution)/shard_map/ppermute | solution.py:285
  43.7 0.7 %close.5 = f32[2,256,256]{2,1,0:T(8,128)} custom-call(f32[2,64,256]{2,1,0:T(8,128)S(1)} %add.21.total, f32[2,64,256]{2,1,0:T(8,128)S(1)} %collective-permute-done.9.arrived, f32[2,256,256]{2,1,0:T(8,128)} %close.4.rest_0_), custom_call_target="tpu_custom_call", output_to_operand_aliasing={{}: (2, {})} | custom-call | tf_op jit(solution)/shard_map/close/pallas_call | solution.py:372
  (24 shorter events, 2.8 us)
Async XLA Ops:
  2.7 8.5 %collective-permute-start.2 = (f32[3,256,256]{2,1,0:T(8,128)S(1)}, f32[3,256,256]{2,1,0:T(8,128)S(1)}, u32[]{:S(2)}, u32[]{:S(2)}) collective-permute-start(f32[3,256,256]{2,1,0:T(8,128)S(1)} %get-tuple-element.23.near), channel_id=1, source_target_pairs={{0,1},{1,0},{2,3},{3,2},{4,5},{5,4},{6,7},{7,6},{8,9},{9,8},{10,11... | collective-permute-start | bytes 2359304 | tf_op jit(solution)/shard_map/ppermute | solution.py:314
  3.2 8.0 %collective-permute-start = (f32[2,256,256]{2,1,0:T(8,128)S(1)}, f32[2,256,256]{2,1,0:T(8,128)S(1)}, u32[]{:S(2)}, u32[]{:S(2)}) collective-permute-start(f32[2,256,256]{2,1,0:T(8,128)S(1)} %get-tuple-element.22.far), channel_id=1, source_target_pairs={{1,2},{2,1},{3,4},{4,3},{5,6},{6,5},{9,10},{10,9},{11,12},{12,11},... | collective-permute-start | bytes 1572872 | tf_op jit(solution)/shard_map/ppermute | solution.py:313
  5.9 5.4 %collective-permute-start.3 = (f32[1,256,256]{2,1,0:T(8,128)S(1)}, f32[1,256,256]{2,1,0:T(8,128)S(1)}, u32[]{:S(2)}, u32[]{:S(2)}) collective-permute-start(f32[1,256,256]{2,1,0:T(8,128)S(1)} %get-tuple-element.25.near_part), channel_id=1, source_target_pairs={{0,1},{1,0},{2,3},{3,2},{4,5},{5,4},{6,7},{7,6},{8,9},{9,8},{10,11... | collective-permute-start | bytes 786440 | tf_op jit(solution)/shard_map/ppermute | solution.py:324
  9.8 3.3 %collective-permute-start.1 = (f32[1,256,256]{2,1,0:T(8,128)S(1)}, f32[1,256,256]{2,1,0:T(8,128)S(1)}, u32[]{:S(2)}, u32[]{:S(2)}) collective-permute-start(f32[1,256,256]{2,1,0:T(8,128)S(1)} %get-tuple-element.24.far_part), channel_id=1, source_target_pairs={{1,2},{2,1},{3,4},{4,3},{5,6},{6,5},{9,10},{10,9},{11,12},{12,11},... | collective-permute-start | bytes 786440 | tf_op jit(solution)/shard_map/ppermute | solution.py:323
  10.5 13.8 %collective-permute-start.6 = (f32[1,256,256]{2,1,0:T(8,128)S(1)}, f32[1,256,256]{2,1,0:T(8,128)S(1)}, u32[]{:S(2)}, u32[]{:S(2)}) collective-permute-start(f32[1,256,256]{2,1,0:T(8,128)S(1)} %get-tuple-element.31), channel_id=1, source_target_pairs={{1,2},{2,1},{3,4},{4,3},{5,6},{6,5},{9,10},{10,9},{11,12},{12,11},... | collective-permute-start | bytes 786440 | tf_op jit(solution)/shard_map/ppermute | solution.py:325
  13.1 11.2 %copy-start = (f32[1,2,256,256]{3,2,1,0:T(8,128)S(1)}, f32[1,2,256,256]{3,2,1,0:T(8,128)}, u32[]{:S(2)}) copy-start(f32[1,2,256,256]{3,2,1,0:T(8,128)} %param.10) | copy-start | bytes 1572868
  13.1 11.2 %copy-start.1 = (s32[2,256,256]{2,1,0:T(8,128)S(1)}, s32[2,256,256]{2,1,0:T(8,128)}, u32[]{:S(2)}) copy-start(s32[2,256,256]{2,1,0:T(8,128)} %mask.1) | copy-start | bytes 1572868
  13.4 8.3 %collective-permute-start.4 = (f32[5,8,128]{2,1,0:T(8,128)S(1)}, f32[5,8,128]{2,1,0:T(8,128)S(1)}, u32[]{:S(2)}, u32[]{:S(2)}) collective-permute-start(f32[5,8,128]{2,1,0:T(8,128)S(1)} %get-tuple-element.28), channel_id=1, source_target_pairs={{0,2},{1,3},{2,0},{3,1},{4,6},{5,7},{6,4},{7,5},{8,10},{9,11},{10,... | collective-permute-start | bytes 61448 | tf_op jit(solution)/shard_map/ppermute | solution.py:264
  21.8 4.8 %collective-permute-start.5 = (f32[5,8,128]{2,1,0:T(8,128)S(1)}, f32[5,8,128]{2,1,0:T(8,128)S(1)}, u32[]{:S(2)}, u32[]{:S(2)}) collective-permute-start(f32[5,8,128]{2,1,0:T(8,128)S(1)} %add.18), channel_id=1, source_target_pairs={{0,4},{1,5},{2,6},{3,7},{4,0},{5,1},{6,2},{7,3},{8,12},{9,13},{10,... | collective-permute-start | bytes 61448 | tf_op jit(solution)/shard_map/ppermute | solution.py:264
  26.6 1.2 %collective-permute-start.7 = (f32[5,8,128]{2,1,0:T(8,128)S(1)}, f32[5,8,128]{2,1,0:T(8,128)S(1)}, u32[]{:S(2)}, u32[]{:S(2)}) collective-permute-start(f32[5,8,128]{2,1,0:T(8,128)S(1)} %add.19), channel_id=1, source_target_pairs={{0,1},{1,0},{2,3},{3,2},{4,5},{5,4},{6,7},{7,6},{8,9},{9,8},{10,11... | collective-permute-start | bytes 61448 | tf_op jit(solution)/shard_map/ppermute | solution.py:264
  28.0 5.7 %collective-permute-start.12 = (f32[2,96,256]{2,1,0:T(8,128)S(1)}, f32[2,96,256]{2,1,0:T(8,128)S(1)}, u32[]{:S(2)}, u32[]{:S(2)}) collective-permute-start(f32[2,96,256]{2,1,0:T(8,128)S(1)} %get-tuple-element.41), channel_id=1, source_target_pairs={{0,8},{1,17},{2,10},{3,19},{4,12},{5,21},{6,14},{7,23},{8,0},{9,25... | collective-permute-start | bytes 589832 | tf_op jit(solution)/shard_map/ppermute | solution.py:282
  29.5 6.3 %collective-permute-start.10 = (f32[2,96,256]{2,1,0:T(8,128)S(1)}, f32[2,96,256]{2,1,0:T(8,128)S(1)}, u32[]{:S(2)}, u32[]{:S(2)}) collective-permute-start(f32[2,96,256]{2,1,0:T(8,128)S(1)} %get-tuple-element.40), channel_id=1, source_target_pairs={{0,8},{1,17},{2,10},{3,19},{4,12},{5,21},{6,14},{7,23},{8,0},{9,25... | collective-permute-start | bytes 589832 | tf_op jit(solution)/shard_map/ppermute | solution.py:282
  30.0 8.6 %collective-permute-start.8 = (f32[2,64,256]{2,1,0:T(8,128)S(1)}, f32[2,64,256]{2,1,0:T(8,128)S(1)}, u32[]{:S(2)}, u32[]{:S(2)}) collective-permute-start(f32[2,64,256]{2,1,0:T(8,128)S(1)} %get-tuple-element.39), channel_id=1, source_target_pairs={{0,8},{1,17},{2,10},{3,19},{4,12},{5,21},{6,14},{7,23},{8,0},{9,25... | collective-permute-start | bytes 393224 | tf_op jit(solution)/shard_map/ppermute | solution.py:282
  33.7 7.5 %collective-permute-start.13 = (f32[2,96,256]{2,1,0:T(8,128)S(1)}, f32[2,96,256]{2,1,0:T(8,128)S(1)}, u32[]{:S(2)}, u32[]{:S(2)}) collective-permute-start(f32[2,96,256]{2,1,0:T(8,128)S(1)} %add.23.total), channel_id=1, source_target_pairs={{0,16},{1,9},{2,18},{3,11},{4,20},{5,13},{6,22},{7,15},{8,24},{9,1... | collective-permute-start | bytes 589832 | tf_op jit(solution)/shard_map/ppermute | solution.py:285
  35.9 6.1 %collective-permute-start.11 = (f32[2,96,256]{2,1,0:T(8,128)S(1)}, f32[2,96,256]{2,1,0:T(8,128)S(1)}, u32[]{:S(2)}, u32[]{:S(2)}) collective-permute-start(f32[2,96,256]{2,1,0:T(8,128)S(1)} %add.22.total), channel_id=1, source_target_pairs={{0,16},{1,9},{2,18},{3,11},{4,20},{5,13},{6,22},{7,15},{8,24},{9,1... | collective-permute-start | bytes 589832 | tf_op jit(solution)/shard_map/ppermute | solution.py:285
  38.7 5.0 %collective-permute-start.9 = (f32[2,64,256]{2,1,0:T(8,128)S(1)}, f32[2,64,256]{2,1,0:T(8,128)S(1)}, u32[]{:S(2)}, u32[]{:S(2)}) collective-permute-start(f32[2,64,256]{2,1,0:T(8,128)S(1)} %add.21.total), channel_id=1, source_target_pairs={{0,16},{1,9},{2,18},{3,11},{4,20},{5,13},{6,22},{7,15},{8,24},{9,1... | collective-permute-start | bytes 393224 | tf_op jit(solution)/shard_map/ppermute | solution.py:285

commit v8 on v7

--- a/solution.py
+++ b/solution.py
@@ -36,21 +36,28 @@
 def in_plane(nu_ref, nu_index, ref, index, start):
     nu = nu_ref[nu_index, start : start + ROWS, :]
     v = ref[index, start : start + ROWS, :]
-    flux = (nu + turn(nu, -1)) * (v - turn(v, -1))
-    total = flux - turn(flux, 1)
+    total = None
     for offset in (-1, 1):
+        across = (nu + turn(nu, offset)) * (v - turn(v, offset))
+        total = across if total is None else total + across
         total = total + (nu + shifted(nu_ref, nu_index, start, offset)) * (
             v - shifted(ref, index, start, offset)
         )
     return nu, v, total
 
 
+def beyond_far():
+    slab, _ = place()
+    inside = (slab > 0) & (slab < lax.axis_size("slab") - 1)
+    return jnp.where(inside, 1.0, 0.0).astype(jnp.float32)
+
+
 def place():
     slab = lax.axis_index("slab")
     return slab, lax.rem(slab, 2)
 
 
-def open_kernel(reluctivity, shift, labels, load, potential, far, near, far_potential, held, table, sems):
+def open_kernel(reluctivity, shift, labels, load, potential, far, near, far_potential, near_potential, held, table, sems):
     _, even = place()
     odd = 1 - even
     total = labels.shape[1]
@@ -60,7 +67,7 @@
         (load.at[even], far.at[1]),
         (load.at[odd], near.at[1]),
         (potential.at[even], far_potential.at[0]),
-        (potential.at[odd], near.at[2]),
+        (potential.at[odd], near_potential.at[0]),
         (reluctivity, table),
     )
     copies = [pltpu.make_async_copy(src, dst, sems.at[i]) for i, (src, dst) in enumerate(moves)]
@@ -85,14 +92,19 @@
         copy.wait()
 
 
-def part_kernel(far, near, far_part, near_part):
+def part_kernel(far, near, far_potential, far_part, near_part, far_early, far_late):
+    _, even = place()
     total = far.shape[1]
+    half = total // 2
     for own, other, out in ((far, near, far_part), (near, far, near_part)):
         for start in range(0, total, ROWS):
             rows = slice(start, start + ROWS)
             nu, v, total_flux = in_plane(own, 0, own, 1, start)
             total_flux = total_flux + (nu + other[0, rows, :]) * (v - other[1, rows, :])
             out[0, rows, :] = 0.5 * (v + total_flux)
+    far_early[0] = far_part[0, pl.ds(pl.multiple_of((1 - even) * half, 8), half), :]
+    far_late[0, 0:half, :] = far_part[0, pl.ds(pl.multiple_of(even * half, 8), half), :]
+    far_late[0, half : half + total, :] = far_potential[0]
 
 
 def fold(value):
@@ -102,6 +114,7 @@
 def sums_kernel(far, near, far_part, near_part, far_in, near_in, near_part_in, image, near_image_in, sums):
     total, columns = far.shape[1:]
     sides = ((far, far_part, far_in), (near, near_part, near_in))
+    end = 1.0 - beyond_far()
     nil = jnp.zeros((8, columns), jnp.float32)
     m0, m1 = nil, nil
     for side, (own, part, halo) in enumerate(sides):
@@ -127,6 +140,8 @@
             total_flux = total_flux + (nu + other[0, rows, :]) * (y - image[1 - side, rows, :])
             if own is near:
                 total_flux = total_flux + (nu + halo[0, rows, :]) * (y - near_image_in[0, rows, :])
+            else:
+                total_flux = total_flux + end * (nu * y)
             z = 0.5 * (y + total_flux)
             v = own[1, rows, :]
             w = y - c * v
@@ -139,24 +154,25 @@
         sums[index : index + 1, :] = jnp.broadcast_to(value, (1, sums.shape[1]))
 
 
-def face_kernel(far, far_in, far_part_in, image, own_sums, far_image_in, sums):
-    slab, _ = place()
-    count = lax.axis_size("slab")
+def face_kernel(far, far_in, far_early_in, image, own_sums, sums):
+    slab, even = place()
     total, columns = far.shape[1:]
-    beyond = jnp.where((slab > 0) & (slab < count - 1), 1.0, 0.0).astype(jnp.float32)
+    half = total // 2
+    beyond = beyond_far()
     c = own_sums[SUMS : SUMS + 1, 0:1]
     s = jnp.zeros((8, columns), jnp.float32)
     t = s
-    for start in range(0, total, ROWS):
-        rows = slice(start, start + ROWS)
+    for start in range(0, half, ROWS):
+        rows = pl.ds(pl.multiple_of(even * half + start, 8), ROWS)
         v = far[1, rows, :]
         y = image[0, rows, :]
+        outer_v = far_in[1, rows, :]
+        step = v - outer_v
         weight = 0.5 * (far[0, rows, :] + far_in[0, rows, :])
-        outer = beyond * (far_part_in[0, rows, :] - weight * (v - far_in[1, rows, :]))
-        far_image_in[0, rows, :] = outer
-        flux = weight * (y - outer)
-        s = s + fold((y - c * v) * flux)
-        t = t + fold(v * flux)
+        outer = far_early_in[0, start : start + ROWS, :] - weight * step
+        flux = beyond * (weight * (y - outer))
+        s = s + fold(((y - c * v) - (outer - c * outer_v)) * flux)
+        t = t + fold(step * flux)
     here = lax.broadcasted_iota(jnp.int32, sums.shape[1:], 0) == slab
     added = (None, None, None, s, t)
     for index in range(SUMS):
@@ -167,21 +183,33 @@
 
 
 def fields_kernel(
-    far, near, far_in, near_in, image, far_image_in, near_image_in, potential, far_potential, mask, u1, u2, u3
+    far, near, far_in, near_in, image, far_early_in, far_late_in, near_image_in, potential, near_potential, mask, u1, u2, u3
 ):
     _, even = place()
     total = far.shape[1]
     scale = 0.25 / lax.axis_size("pos")
-    sides = ((far, even, far_in, far_image_in, far_potential, 0), (near, 1 - even, near_in, near_image_in, near_in, 2))
-    for side, (own, layer, halo, image_in, halo_potential, at) in enumerate(sides):
+    half = total // 2
+    beyond_end = beyond_far()
+    sides = ((far, even, far_in), (near, 1 - even, near_in))
+    for side, (own, layer, halo) in enumerate(sides):
         other = (near, far)[side]
         for start in range(0, total, ROWS):
             rows = slice(start, start + ROWS)
+            if own is far:
+                piece = slice(start % half, start % half + ROWS)
+                early = even == start // half
+                part = jnp.where(early, far_early_in[0, piece, :], far_late_in[0, piece, :])
+                weight = 0.5 * (far[0, rows, :] + far_in[0, rows, :])
+                image_in = beyond_end * (part - weight * (far[1, rows, :] - far_in[1, rows, :]))
+                potential_in = far_late_in[0, half + start : half + start + ROWS, :]
+            else:
+                image_in = near_image_in[0, rows, :]
+                potential_in = near_potential[0, rows, :]
             slopes = []
             for ref, index, beyond, inner in (
-                (potential, layer, halo_potential[at, rows, :], potential[1 - layer, rows, :]),
+                (potential, layer, potential_in, potential[1 - layer, rows, :]),
                 (own, 1, halo[1, rows, :], other[1, rows, :]),
-                (image, side, image_in[0, rows, :], image[1 - side, rows, :]),
+                (image, side, image_in, image[1 - side, rows, :]),
             ):
                 field = ref[index, rows, :]
                 slopes.append(
@@ -297,11 +325,11 @@
     vmem = pl.BlockSpec(memory_space=VMEM)
     smem = pl.BlockSpec(memory_space=SMEM)
     hbm = pl.BlockSpec(memory_space=pltpu.HBM)
-    far, near, far_potential = pl.pallas_call(
+    far, near, far_potential, near_potential = pl.pallas_call(
         open_kernel,
-        out_shape=tuple(pltpu.VMEM((k,) + plane, jnp.float32) for k in (2, 3, 1)),
+        out_shape=tuple(pltpu.VMEM((k,) + plane, jnp.float32) for k in (2, 2, 1, 1)),
         in_specs=[hbm, smem, hbm, hbm, hbm],
-        out_specs=(vmem,) * 3,
+        out_specs=(vmem,) * 4,
         scratch_shapes=[
             VMEM((2,) + plane, jnp.int32),
             SMEM(reluctivity.shape, jnp.float32),
@@ -312,17 +340,18 @@
     )(in_hbm(reluctivity), rotor_shift, in_hbm(labels), in_hbm(load), in_hbm(potential))
     far_in = lax.ppermute(far, "slab", pairs(slabs, 1))
     near_in = lax.ppermute(near, "slab", pairs(slabs, 0))
-    far_part, near_part = pl.pallas_call(
+    half = radial // 2
+    far_part, near_part, far_early, far_late = pl.pallas_call(
         part_kernel,
-        out_shape=(pltpu.VMEM((1,) + plane, jnp.float32),) * 2,
-        in_specs=[vmem] * 2,
-        out_specs=(vmem,) * 2,
+        out_shape=tuple(pltpu.VMEM((1, rows, angular), jnp.float32) for rows in (radial, radial, half, half + radial)),
+        in_specs=[vmem] * 3,
+        out_specs=(vmem,) * 4,
         compiler_params=params(),
         name="part",
-    )(far, near)
-    far_part_in = lax.ppermute(far_part, "slab", pairs(slabs, 1))
+    )(far, near, far_potential)
+    far_early_in = lax.ppermute(far_early, "slab", pairs(slabs, 1))
     near_part_in = lax.ppermute(near_part, "slab", pairs(slabs, 0))
-    far_potential = lax.ppermute(far_potential, "slab", pairs(slabs, 1))
+    far_late_in = lax.ppermute(far_late, "slab", pairs(slabs, 1))
     image, near_image_in, own_sums = pl.pallas_call(
         sums_kernel,
         out_shape=(f32((2,) + plane), f32((1,) + plane), f32((8, 128))),
@@ -331,22 +360,24 @@
         compiler_params=params(),
         name="sums",
     )(far, near, far_part, near_part, far_in, near_in, near_part_in)
-    far_image_in, sums = pl.pallas_call(
+    sums = pl.pallas_call(
         face_kernel,
-        out_shape=(f32((1,) + plane), f32((SUMS, slabs, 128))),
+        out_shape=f32((SUMS, slabs, 128)),
         in_specs=[vmem] * 5,
-        out_specs=(vmem,) * 2,
+        out_specs=vmem,
         compiler_params=params(),
         name="face",
-    )(far, far_in, far_part_in, image, own_sums)
+    )(far, far_in, far_early_in, image, own_sums)
+    near_potential, sums = lax.optimization_barrier((near_potential, sums))
+    near_potential = lax.ppermute(near_potential, "slab", pairs(slabs, 0))
     fields = pl.pallas_call(
         fields_kernel,
         out_shape=(f32((2,) + plane),) * 3,
-        in_specs=[vmem] * 10,
+        in_specs=[vmem] * 11,
         out_specs=(vmem,) * 3,
         compiler_params=params(),
         name="fields",
-    )(far, near, far_in, near_in, image, far_image_in, near_image_in, potential, far_potential, magnet_mask)
+    )(far, near, far_in, near_in, image, far_early_in, far_late_in, near_image_in, potential, near_potential, magnet_mask)
     sums, fields = gather_sums(sums, fields, slabs)
     spans = [radial // 8 * k for k in EIGHTHS]
     terms = pl.pallas_call(

time: 44.6 us -> 44.6 us (level)
  waiting for transfers between devices: 9.69 us -> 12 us
  Pallas kernels: 9.69 us -> 7.88 us
    ppermute x3, starting transfers between devices: 8.57 us -> 3.42 us  [gather_sums(): arrived = lax.ppermute(sums, 'slab', [(i, i ^ step) for i in range(slabs)])]
    ppermute x2 -> x3, starting transfers between devices: 1.34 us -> 6.07 us  [the longest x1 4.72 us: local(): near_potential = lax.ppermute(near_potential, 'slab', pairs(slabs, 0))]
    ppermute x1, starting transfers between devices: 3.99 us -> 0.08 us  [local(): near_part_in = lax.ppermute(near_part, 'slab', pairs(slabs, 0))]
    ppermute x1, starting transfers between devices: 0.52 us -> 4.42 us  [local(): near_in = lax.ppermute(near, 'slab', pairs(slabs, 0))]
    ppermute x3, waiting for transfers between devices: 4.77 us -> 6.9 us  [gather_sums(): arrived = lax.ppermute(sums, 'slab', [(i, i ^ step) for i in range(slabs)])]
    pallas_call x2, Pallas kernels: 2.2 us -> 0.88 us  [the longest x1 0.66 us: local(): pl.pallas_call(part_kernel, out_shape=tuple((pltpu.VMEM((1, rows, angular...]
    pallas_call x1, Pallas kernels: 1.86 us -> 1.22 us  [local(): pl.pallas_call(sums_kernel, out_shape=(f32((2,) + plane), f32((1,) + plan...]
  transfers between devices with their start and end apart: 14 -> 15, of which waited for: 7 -> 8; matrix products, arithmetic and copies ran while one was open for 0% -> 0% of each run, Pallas kernels for 17% -> 13%
where the time goes in v8:
time: 44.6 us; the launch traced here: 44.4 us
  starting transfers between devices  23 us (52%)
  waiting for transfers between devices  12 us (27%)
  Pallas kernels  7.88 us (18%)
  between operations  1.44 us (3%)
    ppermute x3, waiting for transfers between devices, gather_sums(): arrived = lax.ppermute(sums, 'slab', [(i, i ^ step) for i in range(slabs)])  6.9 us
    ppermute x3, starting transfers between devices, sum_positions(): lax.ppermute(term, ('pos', 'slab'), partners(step, positions, slabs))  4.75 us
    ppermute x1, starting transfers between devices, local(): near_potential = lax.ppermute(near_potential, 'slab', pairs(slabs, 0))  4.72 us
    ppermute x1, starting transfers between devices, local(): near_in = lax.ppermute(near, 'slab', pairs(slabs, 0))  4.42 us
    ppermute x3, waiting for transfers between devices, sum_positions(): arrived = lax.ppermute(term, ('pos', 'slab'), partners(0, positions, slabs))  3.88 us
    ppermute x3, starting transfers between devices, sum_positions(): arrived = lax.ppermute(term, ('pos', 'slab'), partners(0, positions, slabs))  3.58 us
    ppermute x3, starting transfers between devices, gather_sums(): arrived = lax.ppermute(sums, 'slab', [(i, i ^ step) for i in range(slabs)])  3.42 us
    pallas_call x3, Pallas kernels, local(): pl.pallas_call(functools.partial(close_kernel, first_rows(radial)[index])...  2.09 us
  transfers between devices with their start and end apart: 15, of which 8 were waited for; matrix products, arithmetic and copies ran while one was open for 0% of the time, Pallas kernels for 13%

profile of v8, /device:TPU:0, one launch (start us, length us, event | category | flops | bytes accessed | tf_op | source)
XLA Modules:
  0.0 44.4 jit_solution(4436443470850587930)
XLA Ops:
  1.3 1.4 %open.1 = (f32[2,256,256]{2,1,0:T(8,128)S(1)}, f32[2,256,256]{2,1,0:T(8,128)S(1)}, f32[1,256,256]{2,1,0:T(8,128)S(1)}, f32[1,256,256]{2,1,0:T(8,128)S(1)}) custom-call(f32[4]{0:T(128)} %reluctivity.1, s32[1]{0:T(128)S(6)} %copy.12.shift, s32[2,256,256]{2,1,0:T(8,128)} %labels.1, f32[2,256,256]{2,1,0:T(8,128)} %bitcast.5, f32[2,256,256]{2,1,0:T(8,128)} %bitcast.3), custom_call_target="tpu_custom_call" | custom-call | tf_op jit(solution)/shard_map/open/pallas_call | solution.py:328
  2.7 0.7 %collective-permute-start = (f32[2,256,256]{2,1,0:T(8,128)S(1)}, f32[2,256,256]{2,1,0:T(8,128)S(1)}, u32[]{:S(2)}, u32[]{:S(2)}) collective-permute-start(f32[2,256,256]{2,1,0:T(8,128)S(1)} %get-tuple-element.26.far), channel_id=1, source_target_pairs={{1,2},{2,1},{3,4},{4,3},{5,6},{6,5},{9,10},{10,9},{11,12},{12,11},... | collective-permute-start | bytes 1572872 | tf_op jit(solution)/shard_map/ppermute | solution.py:341
  3.4 4.4 %collective-permute-start.2 = (f32[2,256,256]{2,1,0:T(8,128)S(1)}, f32[2,256,256]{2,1,0:T(8,128)S(1)}, u32[]{:S(2)}, u32[]{:S(2)}) collective-permute-start(f32[2,256,256]{2,1,0:T(8,128)S(1)} %get-tuple-element.27.near), channel_id=1, source_target_pairs={{0,1},{1,0},{2,3},{3,2},{4,5},{5,4},{6,7},{7,6},{8,9},{9,8},{10,11... | collective-permute-start | bytes 1572872 | tf_op jit(solution)/shard_map/ppermute | solution.py:342
  9.2 0.7 %collective-permute-start.6 = (f32[1,384,256]{2,1,0:T(8,128)S(1)}, f32[1,384,256]{2,1,0:T(8,128)S(1)}, u32[]{:S(2)}, u32[]{:S(2)}) collective-permute-start(f32[1,384,256]{2,1,0:T(8,128)S(1)} %get-tuple-element.35), channel_id=1, source_target_pairs={{1,2},{2,1},{3,4},{4,3},{5,6},{6,5},{9,10},{10,9},{11,12},{12,11},... | collective-permute-start | bytes 1179656 | tf_op jit(solution)/shard_map/ppermute | solution.py:354
  10.1 1.2 %sums.1 = (f32[2,256,256]{2,1,0:T(8,128)S(1)}, f32[1,256,256]{2,1,0:T(8,128)S(1)}, f32[8,128]{1,0:T(8,128)S(1)}) custom-call(f32[2,256,256]{2,1,0:T(8,128)S(1)} %get-tuple-element.26.far, f32[2,256,256]{2,1,0:T(8,128)S(1)} %get-tuple-element.27.near, f32[1,256,256]{2,1,0:T(8,128)S(1)} %get-tuple-element.30.far_part, ...), custom_call_target="tpu_custom_call" | custom-call | tf_op jit(solution)/shard_map/sums/pallas_call | solution.py:355
  11.6 4.7 %collective-permute-start.7 = (f32[1,256,256]{2,1,0:T(8,128)S(1)}, f32[1,256,256]{2,1,0:T(8,128)S(1)}, u32[]{:S(2)}, u32[]{:S(2)}) collective-permute-start(f32[1,256,256]{2,1,0:T(8,128)S(1)} %get-tuple-element.37), channel_id=1, source_target_pairs={{0,1},{1,0},{2,3},{3,2},{4,5},{5,4},{6,7},{7,6},{8,9},{9,8},{10,11... | collective-permute-start | bytes 786440 | tf_op jit(solution)/shard_map/ppermute | solution.py:372
  16.3 1.9 %collective-permute-start.4 = (f32[5,8,128]{2,1,0:T(8,128)S(1)}, f32[5,8,128]{2,1,0:T(8,128)S(1)}, u32[]{:S(2)}, u32[]{:S(2)}) collective-permute-start(f32[5,8,128]{2,1,0:T(8,128)S(1)} %face.1), channel_id=1, source_target_pairs={{0,2},{1,3},{2,0},{3,1},{4,6},{5,7},{6,4},{7,5},{8,10},{9,11},{10,... | collective-permute-start | bytes 61448 | tf_op jit(solution)/shard_map/ppermute | solution.py:292
  18.2 3.7 %collective-permute-done.4 = f32[5,8,128]{2,1,0:T(8,128)S(1)} collective-permute-done((f32[5,8,128]{2,1,0:T(8,128)S(1)}, f32[5,8,128]{2,1,0:T(8,128)S(1)}, u32[]{:S(2)}, u32[]{:S(2)}) %collective-permute-start.4) | collective-permute-done | bytes 20512 | tf_op jit(solution)/shard_map/ppermute | solution.py:292
  21.9 1.5 %collective-permute-start.5 = (f32[5,8,128]{2,1,0:T(8,128)S(1)}, f32[5,8,128]{2,1,0:T(8,128)S(1)}, u32[]{:S(2)}, u32[]{:S(2)}) collective-permute-start(f32[5,8,128]{2,1,0:T(8,128)S(1)} %add.18), channel_id=1, source_target_pairs={{0,4},{1,5},{2,6},{3,7},{4,0},{5,1},{6,2},{7,3},{8,12},{9,13},{10,... | collective-permute-start | bytes 61448 | tf_op jit(solution)/shard_map/ppermute | solution.py:292
  23.5 1.1 %fields.1 = (f32[2,256,256]{2,1,0:T(8,128)S(1)}, f32[2,256,256]{2,1,0:T(8,128)S(1)}, f32[2,256,256]{2,1,0:T(8,128)S(1)}) custom-call(f32[2,256,256]{2,1,0:T(8,128)S(1)} %get-tuple-element.26.far, f32[2,256,256]{2,1,0:T(8,128)S(1)} %get-tuple-element.27.near, f32[2,256,256]{2,1,0:T(8,128)S(1)} %collective-permute-done.far_in, ...), custom_call_target="tpu_custom_call" | custom-call | tf_op jit(solution)/shard_map/fields/pallas_call | solution.py:373
  24.6 2.0 %collective-permute-done.5 = f32[5,8,128]{2,1,0:T(8,128)S(1)} collective-permute-done((f32[5,8,128]{2,1,0:T(8,128)S(1)}, f32[5,8,128]{2,1,0:T(8,128)S(1)}, u32[]{:S(2)}, u32[]{:S(2)}) %collective-permute-start.5) | collective-permute-done | bytes 20512 | tf_op jit(solution)/shard_map/ppermute | solution.py:292
  26.6 1.2 %collective-permute-done.8 = f32[5,8,128]{2,1,0:T(8,128)S(1)} collective-permute-done((f32[5,8,128]{2,1,0:T(8,128)S(1)}, f32[5,8,128]{2,1,0:T(8,128)S(1)}, u32[]{:S(2)}, u32[]{:S(2)}) %collective-permute-start.8) | collective-permute-done | bytes 20512 | tf_op jit(solution)/shard_map/ppermute | solution.py:292
  28.0 1.6 %collective-permute-start.13 = (f32[2,96,256]{2,1,0:T(8,128)S(1)}, f32[2,96,256]{2,1,0:T(8,128)S(1)}, u32[]{:S(2)}, u32[]{:S(2)}) collective-permute-start(f32[2,96,256]{2,1,0:T(8,128)S(1)} %get-tuple-element.47), channel_id=1, source_target_pairs={{0,8},{1,17},{2,10},{3,19},{4,12},{5,21},{6,14},{7,23},{8,0},{9,25... | collective-permute-start | bytes 589832 | tf_op jit(solution)/shard_map/ppermute | solution.py:310
  30.1 1.5 %collective-permute-start.9 = (f32[2,64,256]{2,1,0:T(8,128)S(1)}, f32[2,64,256]{2,1,0:T(8,128)S(1)}, u32[]{:S(2)}, u32[]{:S(2)}) collective-permute-start(f32[2,64,256]{2,1,0:T(8,128)S(1)} %get-tuple-element.45), channel_id=1, source_target_pairs={{0,8},{1,17},{2,10},{3,19},{4,12},{5,21},{6,14},{7,23},{8,0},{9,25... | collective-permute-start | bytes 393224 | tf_op jit(solution)/shard_map/ppermute | solution.py:310
  31.6 2.2 %collective-permute-done.13 = f32[2,96,256]{2,1,0:T(8,128)S(1)} collective-permute-done((f32[2,96,256]{2,1,0:T(8,128)S(1)}, f32[2,96,256]{2,1,0:T(8,128)S(1)}, u32[]{:S(2)}, u32[]{:S(2)}) %collective-permute-start.13) | collective-permute-done | bytes 196640 | tf_op jit(solution)/shard_map/ppermute | solution.py:310
  33.7 1.6 %collective-permute-start.14 = (f32[2,96,256]{2,1,0:T(8,128)S(1)}, f32[2,96,256]{2,1,0:T(8,128)S(1)}, u32[]{:S(2)}, u32[]{:S(2)}) collective-permute-start(f32[2,96,256]{2,1,0:T(8,128)S(1)} %add.23.total), channel_id=1, source_target_pairs={{0,16},{1,9},{2,18},{3,11},{4,20},{5,13},{6,22},{7,15},{8,24},{9,1... | collective-permute-start | bytes 589832 | tf_op jit(solution)/shard_map/ppermute | solution.py:313
  35.9 1.6 %collective-permute-start.12 = (f32[2,96,256]{2,1,0:T(8,128)S(1)}, f32[2,96,256]{2,1,0:T(8,128)S(1)}, u32[]{:S(2)}, u32[]{:S(2)}) collective-permute-start(f32[2,96,256]{2,1,0:T(8,128)S(1)} %add.22.total), channel_id=1, source_target_pairs={{0,16},{1,9},{2,18},{3,11},{4,20},{5,13},{6,22},{7,15},{8,24},{9,1... | collective-permute-start | bytes 589832 | tf_op jit(solution)/shard_map/ppermute | solution.py:313
  37.5 1.2 %collective-permute-done.9 = f32[2,64,256]{2,1,0:T(8,128)S(1)} collective-permute-done((f32[2,64,256]{2,1,0:T(8,128)S(1)}, f32[2,64,256]{2,1,0:T(8,128)S(1)}, u32[]{:S(2)}, u32[]{:S(2)}) %collective-permute-start.9) | collective-permute-done | bytes 131104 | tf_op jit(solution)/shard_map/ppermute | solution.py:310
  38.7 1.6 %collective-permute-start.10 = (f32[2,64,256]{2,1,0:T(8,128)S(1)}, f32[2,64,256]{2,1,0:T(8,128)S(1)}, u32[]{:S(2)}, u32[]{:S(2)}) collective-permute-start(f32[2,64,256]{2,1,0:T(8,128)S(1)} %add.21.total), channel_id=1, source_target_pairs={{0,16},{1,9},{2,18},{3,11},{4,20},{5,13},{6,22},{7,15},{8,24},{9,1... | collective-permute-start | bytes 393224 | tf_op jit(solution)/shard_map/ppermute | solution.py:313
  40.3 1.0 %adjoint.1 = f32[2,256,256]{2,1,0:T(8,128)} custom-call(f32[5,8,128]{2,1,0:T(8,128)S(1)} %add.20.sums, f32[2,256,256]{2,1,0:T(8,128)S(1)} %get-tuple-element.26.far, f32[2,256,256]{2,1,0:T(8,128)S(1)} %get-tuple-element.27.near, f32[2,256,256]{2,1,0:T(8,128)S(1)} %get-tuple-element.32.image), custom_call_target="tpu_custom_call" | custom-call | tf_op jit(solution)/shard_map/adjoint/pallas_call | solution.py:391
  41.3 0.7 %close.3.rest_0_ = f32[2,256,256]{2,1,0:T(8,128)} custom-call(f32[2,96,256]{2,1,0:T(8,128)S(1)} %add.23.total, f32[2,96,256]{2,1,0:T(8,128)S(1)} %collective-permute-done.14.arrived), custom_call_target="tpu_custom_call" | custom-call | tf_op jit(solution)/shard_map/close/pallas_call | solution.py:403
  42.0 0.7 %close.4.rest_0_ = f32[2,256,256]{2,1,0:T(8,128)} custom-call(f32[2,96,256]{2,1,0:T(8,128)S(1)} %add.22.total, f32[2,96,256]{2,1,0:T(8,128)S(1)} %collective-permute-done.12.arrived, f32[2,256,256]{2,1,0:T(8,128)} %close.3.rest_0_), custom_call_target="tpu_custom_call", output_to_operand_aliasing={{}: (2, {})} | custom-call | tf_op jit(solution)/shard_map/close/pallas_call | solution.py:403
  42.7 1.0 %collective-permute-done.10.arrived = f32[2,64,256]{2,1,0:T(8,128)S(1)} collective-permute-done((f32[2,64,256]{2,1,0:T(8,128)S(1)}, f32[2,64,256]{2,1,0:T(8,128)S(1)}, u32[]{:S(2)}, u32[]{:S(2)}) %collective-permute-start.10) | collective-permute-done | bytes 131104 | tf_op jit(solution)/shard_map/ppermute | solution.py:313
  43.7 0.7 %close.5 = f32[2,256,256]{2,1,0:T(8,128)} custom-call(f32[2,64,256]{2,1,0:T(8,128)S(1)} %add.21.total, f32[2,64,256]{2,1,0:T(8,128)S(1)} %collective-permute-done.10.arrived, f32[2,256,256]{2,1,0:T(8,128)} %close.4.rest_0_), custom_call_target="tpu_custom_call", output_to_operand_aliasing={{}: (2, {})} | custom-call | tf_op jit(solution)/shard_map/close/pallas_call | solution.py:403
  (26 shorter events, 3.1 us)
Async XLA Ops:
  2.7 7.4 %collective-permute-start = (f32[2,256,256]{2,1,0:T(8,128)S(1)}, f32[2,256,256]{2,1,0:T(8,128)S(1)}, u32[]{:S(2)}, u32[]{:S(2)}) collective-permute-start(f32[2,256,256]{2,1,0:T(8,128)S(1)} %get-tuple-element.26.far), channel_id=1, source_target_pairs={{1,2},{2,1},{3,4},{4,3},{5,6},{6,5},{9,10},{10,9},{11,12},{12,11},... | collective-permute-start | bytes 1572872 | tf_op jit(solution)/shard_map/ppermute | solution.py:341
  3.4 6.7 %collective-permute-start.2 = (f32[2,256,256]{2,1,0:T(8,128)S(1)}, f32[2,256,256]{2,1,0:T(8,128)S(1)}, u32[]{:S(2)}, u32[]{:S(2)}) collective-permute-start(f32[2,256,256]{2,1,0:T(8,128)S(1)} %get-tuple-element.27.near), channel_id=1, source_target_pairs={{0,1},{1,0},{2,3},{3,2},{4,5},{5,4},{6,7},{7,6},{8,9},{9,8},{10,11... | collective-permute-start | bytes 1572872 | tf_op jit(solution)/shard_map/ppermute | solution.py:342
  8.5 1.6 %collective-permute-start.3 = (f32[1,256,256]{2,1,0:T(8,128)S(1)}, f32[1,256,256]{2,1,0:T(8,128)S(1)}, u32[]{:S(2)}, u32[]{:S(2)}) collective-permute-start(f32[1,256,256]{2,1,0:T(8,128)S(1)} %get-tuple-element.31.near_part), channel_id=1, source_target_pairs={{0,1},{1,0},{2,3},{3,2},{4,5},{5,4},{6,7},{7,6},{8,9},{9,8},{10,11... | collective-permute-start | bytes 786440 | tf_op jit(solution)/shard_map/ppermute | solution.py:353
  8.6 2.8 %collective-permute-start.1 = (f32[1,128,256]{2,1,0:T(8,128)S(1)}, f32[1,128,256]{2,1,0:T(8,128)S(1)}, u32[]{:S(2)}, u32[]{:S(2)}) collective-permute-start(f32[1,128,256]{2,1,0:T(8,128)S(1)} %get-tuple-element.29), channel_id=1, source_target_pairs={{1,2},{2,1},{3,4},{4,3},{5,6},{6,5},{9,10},{10,9},{11,12},{12,11},... | collective-permute-start | bytes 393224 | tf_op jit(solution)/shard_map/ppermute | solution.py:352
  9.2 14.2 %collective-permute-start.6 = (f32[1,384,256]{2,1,0:T(8,128)S(1)}, f32[1,384,256]{2,1,0:T(8,128)S(1)}, u32[]{:S(2)}, u32[]{:S(2)}) collective-permute-start(f32[1,384,256]{2,1,0:T(8,128)S(1)} %get-tuple-element.35), channel_id=1, source_target_pairs={{1,2},{2,1},{3,4},{4,3},{5,6},{6,5},{9,10},{10,9},{11,12},{12,11},... | collective-permute-start | bytes 1179656 | tf_op jit(solution)/shard_map/ppermute | solution.py:354
  11.3 12.1 %copy-start = (f32[1,2,256,256]{3,2,1,0:T(8,128)S(1)}, f32[1,2,256,256]{3,2,1,0:T(8,128)}, u32[]{:S(2)}) copy-start(f32[1,2,256,256]{3,2,1,0:T(8,128)} %param.10) | copy-start | bytes 1572868
  11.4 12.1 %copy-start.1 = (s32[2,256,256]{2,1,0:T(8,128)S(1)}, s32[2,256,256]{2,1,0:T(8,128)}, u32[]{:S(2)}) copy-start(s32[2,256,256]{2,1,0:T(8,128)} %mask.1) | copy-start | bytes 1572868
  11.6 11.9 %collective-permute-start.7 = (f32[1,256,256]{2,1,0:T(8,128)S(1)}, f32[1,256,256]{2,1,0:T(8,128)S(1)}, u32[]{:S(2)}, u32[]{:S(2)}) collective-permute-start(f32[1,256,256]{2,1,0:T(8,128)S(1)} %get-tuple-element.37), channel_id=1, source_target_pairs={{0,1},{1,0},{2,3},{3,2},{4,5},{5,4},{6,7},{7,6},{8,9},{9,8},{10,11... | collective-permute-start | bytes 786440 | tf_op jit(solution)/shard_map/ppermute | solution.py:372
  16.3 5.6 %collective-permute-start.4 = (f32[5,8,128]{2,1,0:T(8,128)S(1)}, f32[5,8,128]{2,1,0:T(8,128)S(1)}, u32[]{:S(2)}, u32[]{:S(2)}) collective-permute-start(f32[5,8,128]{2,1,0:T(8,128)S(1)} %face.1), channel_id=1, source_target_pairs={{0,2},{1,3},{2,0},{3,1},{4,6},{5,7},{6,4},{7,5},{8,10},{9,11},{10,... | collective-permute-start | bytes 61448 | tf_op jit(solution)/shard_map/ppermute | solution.py:292
  21.9 4.7 %collective-permute-start.5 = (f32[5,8,128]{2,1,0:T(8,128)S(1)}, f32[5,8,128]{2,1,0:T(8,128)S(1)}, u32[]{:S(2)}, u32[]{:S(2)}) collective-permute-start(f32[5,8,128]{2,1,0:T(8,128)S(1)} %add.18), channel_id=1, source_target_pairs={{0,4},{1,5},{2,6},{3,7},{4,0},{5,1},{6,2},{7,3},{8,12},{9,13},{10,... | collective-permute-start | bytes 61448 | tf_op jit(solution)/shard_map/ppermute | solution.py:292
  26.6 1.2 %collective-permute-start.8 = (f32[5,8,128]{2,1,0:T(8,128)S(1)}, f32[5,8,128]{2,1,0:T(8,128)S(1)}, u32[]{:S(2)}, u32[]{:S(2)}) collective-permute-start(f32[5,8,128]{2,1,0:T(8,128)S(1)} %add.19), channel_id=1, source_target_pairs={{0,1},{1,0},{2,3},{3,2},{4,5},{5,4},{6,7},{7,6},{8,9},{9,8},{10,11... | collective-permute-start | bytes 61448 | tf_op jit(solution)/shard_map/ppermute | solution.py:292
  28.0 5.7 %collective-permute-start.13 = (f32[2,96,256]{2,1,0:T(8,128)S(1)}, f32[2,96,256]{2,1,0:T(8,128)S(1)}, u32[]{:S(2)}, u32[]{:S(2)}) collective-permute-start(f32[2,96,256]{2,1,0:T(8,128)S(1)} %get-tuple-element.47), channel_id=1, source_target_pairs={{0,8},{1,17},{2,10},{3,19},{4,12},{5,21},{6,14},{7,23},{8,0},{9,25... | collective-permute-start | bytes 589832 | tf_op jit(solution)/shard_map/ppermute | solution.py:310
  29.5 6.3 %collective-permute-start.11 = (f32[2,96,256]{2,1,0:T(8,128)S(1)}, f32[2,96,256]{2,1,0:T(8,128)S(1)}, u32[]{:S(2)}, u32[]{:S(2)}) collective-permute-start(f32[2,96,256]{2,1,0:T(8,128)S(1)} %get-tuple-element.46), channel_id=1, source_target_pairs={{0,8},{1,17},{2,10},{3,19},{4,12},{5,21},{6,14},{7,23},{8,0},{9,25... | collective-permute-start | bytes 589832 | tf_op jit(solution)/shard_map/ppermute | solution.py:310
  30.1 8.6 %collective-permute-start.9 = (f32[2,64,256]{2,1,0:T(8,128)S(1)}, f32[2,64,256]{2,1,0:T(8,128)S(1)}, u32[]{:S(2)}, u32[]{:S(2)}) collective-permute-start(f32[2,64,256]{2,1,0:T(8,128)S(1)} %get-tuple-element.45), channel_id=1, source_target_pairs={{0,8},{1,17},{2,10},{3,19},{4,12},{5,21},{6,14},{7,23},{8,0},{9,25... | collective-permute-start | bytes 393224 | tf_op jit(solution)/shard_map/ppermute | solution.py:310
  33.7 7.5 %collective-permute-start.14 = (f32[2,96,256]{2,1,0:T(8,128)S(1)}, f32[2,96,256]{2,1,0:T(8,128)S(1)}, u32[]{:S(2)}, u32[]{:S(2)}) collective-permute-start(f32[2,96,256]{2,1,0:T(8,128)S(1)} %add.23.total), channel_id=1, source_target_pairs={{0,16},{1,9},{2,18},{3,11},{4,20},{5,13},{6,22},{7,15},{8,24},{9,1... | collective-permute-start | bytes 589832 | tf_op jit(solution)/shard_map/ppermute | solution.py:313
  35.9 6.1 %collective-permute-start.12 = (f32[2,96,256]{2,1,0:T(8,128)S(1)}, f32[2,96,256]{2,1,0:T(8,128)S(1)}, u32[]{:S(2)}, u32[]{:S(2)}) collective-permute-start(f32[2,96,256]{2,1,0:T(8,128)S(1)} %add.22.total), channel_id=1, source_target_pairs={{0,16},{1,9},{2,18},{3,11},{4,20},{5,13},{6,22},{7,15},{8,24},{9,1... | collective-permute-start | bytes 589832 | tf_op jit(solution)/shard_map/ppermute | solution.py:313
  38.7 5.0 %collective-permute-start.10 = (f32[2,64,256]{2,1,0:T(8,128)S(1)}, f32[2,64,256]{2,1,0:T(8,128)S(1)}, u32[]{:S(2)}, u32[]{:S(2)}) collective-permute-start(f32[2,64,256]{2,1,0:T(8,128)S(1)} %add.21.total), channel_id=1, source_target_pairs={{0,16},{1,9},{2,18},{3,11},{4,20},{5,13},{6,22},{7,15},{8,24},{9,1... | collective-permute-start | bytes 393224 | tf_op jit(solution)/shard_map/ppermute | solution.py:313

commit v9 on v8

--- a/solution.py
+++ b/solution.py
@@ -287,7 +287,7 @@
 
 
 def gather_sums(sums, fields, slabs):
-    steps = [2**k for k in range(1, slabs.bit_length() - 1)] + [1]
+    steps = [2**k for k in range(2, slabs.bit_length() - 1)] + [1]
     for step in steps:
         arrived = lax.ppermute(sums, "slab", [(i, i ^ step) for i in range(slabs)])
         if step == steps[-2]:
@@ -317,7 +317,7 @@
 def local(labels, magnet_mask, reluctivity, rotor_shift, potential, adjoint_load):
     layers, radial, angular = labels.shape
     positions, slabs = lax.axis_size("pos"), lax.axis_size("slab")
-    if layers != 2 or slabs < 4 or slabs & (slabs - 1) or radial % (8 * ROWS) or positions < 2 or positions & (positions - 1):
+    if layers != 2 or slabs < 8 or slabs & (slabs - 1) or radial % (8 * ROWS) or positions < 2 or positions & (positions - 1):
         raise ValueError("unsupported sizes")
     potential, load = potential[0], adjoint_load[0]
     f32 = functools.partial(jax.ShapeDtypeStruct, dtype=jnp.float32)
@@ -368,8 +368,10 @@
         compiler_params=params(),
         name="face",
     )(far, far_in, far_early_in, image, own_sums)
-    near_potential, sums = lax.optimization_barrier((near_potential, sums))
+    arrived = lax.ppermute(sums, "slab", [(i, i ^ 2) for i in range(slabs)])
+    near_potential, arrived = lax.optimization_barrier((near_potential, arrived))
     near_potential = lax.ppermute(near_potential, "slab", pairs(slabs, 0))
+    sums = sums + arrived
     fields = pl.pallas_call(
         fields_kernel,
         out_shape=(f32((2,) + plane),) * 3,

time: 44.6 us -> 44.6 us (level)
  starting transfers between devices: 23 us -> 23.7 us
  waiting for transfers between devices: 12 us -> 11.3 us
    ppermute x0 -> x1, starting transfers between devices: none -> 6.55 us  [local(): arrived = lax.ppermute(sums, 'slab', [(i, i ^ 2) for i in range(slabs)])]
    ppermute x1, starting transfers between devices: 4.72 us -> 0.01 us  [local(): near_potential = lax.ppermute(near_potential, 'slab', pairs(slabs, 0))]
    ppermute x3 -> x2, waiting for transfers between devices: 6.9 us -> 2.56 us  [gather_sums(): arrived = lax.ppermute(sums, 'slab', [(i, i ^ step) for i in range(slabs)])]
    ppermute x1, starting transfers between devices: 0.08 us -> 3.99 us  [local(): near_part_in = lax.ppermute(near_part, 'slab', pairs(slabs, 0))]
    ppermute x1, starting transfers between devices: 4.42 us -> 0.52 us  [local(): near_in = lax.ppermute(near, 'slab', pairs(slabs, 0))]
    ppermute x0 -> x1, waiting for transfers between devices: none -> 3.87 us  [local(): arrived = lax.ppermute(sums, 'slab', [(i, i ^ 2) for i in range(slabs)])]
    ppermute x3 -> x2, starting transfers between devices: 3.42 us -> 2.23 us  [gather_sums(): arrived = lax.ppermute(sums, 'slab', [(i, i ^ step) for i in range(slabs)])]
  transfers between devices with their start and end apart: 15 -> 15, of which waited for: 8 -> 7; matrix products, arithmetic and copies ran while one was open for 0% -> 0% of each run, Pallas kernels for 13% -> 13%
where the time goes in v9:
time: 44.6 us; the launch traced here: 44.4 us
  starting transfers between devices  23.7 us (53%)
  waiting for transfers between devices  11.3 us (25%)
  Pallas kernels  7.89 us (18%)
  between operations  1.47 us (3%)
    ppermute x1, starting transfers between devices, local(): arrived = lax.ppermute(sums, 'slab', [(i, i ^ 2) for i in range(slabs)])  6.55 us
    ppermute x3, starting transfers between devices, sum_positions(): lax.ppermute(term, ('pos', 'slab'), partners(step, positions, slabs))  4.75 us
    ppermute x1, starting transfers between devices, local(): near_part_in = lax.ppermute(near_part, 'slab', pairs(slabs, 0))  3.99 us
    ppermute x3, waiting for transfers between devices, sum_positions(): arrived = lax.ppermute(term, ('pos', 'slab'), partners(0, positions, slabs))  3.88 us
    ppermute x1, waiting for transfers between devices, local(): arrived = lax.ppermute(sums, 'slab', [(i, i ^ 2) for i in range(slabs)])  3.87 us
    ppermute x3, starting transfers between devices, sum_positions(): arrived = lax.ppermute(term, ('pos', 'slab'), partners(0, positions, slabs))  3.58 us
    ppermute x2, waiting for transfers between devices, gather_sums(): arrived = lax.ppermute(sums, 'slab', [(i, i ^ step) for i in range(slabs)])  2.56 us
    ppermute x2, starting transfers between devices, gather_sums(): arrived = lax.ppermute(sums, 'slab', [(i, i ^ step) for i in range(slabs)])  2.23 us
  transfers between devices with their start and end apart: 15, of which 7 were waited for; matrix products, arithmetic and copies ran while one was open for 0% of the time, Pallas kernels for 13%

profile of v9, /device:TPU:0, one launch (start us, length us, event | category | flops | bytes accessed | tf_op | source)
XLA Modules:
  0.0 44.4 jit_solution(11624512393192449696)
XLA Ops:
  1.3 1.4 %open.1 = (f32[2,256,256]{2,1,0:T(8,128)S(1)}, f32[2,256,256]{2,1,0:T(8,128)S(1)}, f32[1,256,256]{2,1,0:T(8,128)S(1)}, f32[1,256,256]{2,1,0:T(8,128)S(1)}) custom-call(f32[4]{0:T(128)} %reluctivity.1, s32[1]{0:T(128)S(6)} %copy.12.shift, s32[2,256,256]{2,1,0:T(8,128)} %labels.1, f32[2,256,256]{2,1,0:T(8,128)} %bitcast.5, f32[2,256,256]{2,1,0:T(8,128)} %bitcast.3), custom_call_target="tpu_custom_call" | custom-call | tf_op jit(solution)/shard_map/open/pallas_call | solution.py:328
  3.2 0.7 %collective-permute-start = (f32[2,256,256]{2,1,0:T(8,128)S(1)}, f32[2,256,256]{2,1,0:T(8,128)S(1)}, u32[]{:S(2)}, u32[]{:S(2)}) collective-permute-start(f32[2,256,256]{2,1,0:T(8,128)S(1)} %get-tuple-element.25.far), channel_id=1, source_target_pairs={{1,2},{2,1},{3,4},{4,3},{5,6},{6,5},{9,10},{10,9},{11,12},{12,11},... | collective-permute-start | bytes 1572872 | tf_op jit(solution)/shard_map/ppermute | solution.py:341
  3.9 0.7 %part.1 = (f32[1,256,256]{2,1,0:T(8,128)S(1)}, f32[1,256,256]{2,1,0:T(8,128)S(1)}, f32[1,128,256]{2,1,0:T(8,128)S(1)}, f32[1,384,256]{2,1,0:T(8,128)S(1)}) custom-call(f32[2,256,256]{2,1,0:T(8,128)S(1)} %get-tuple-element.25.far, f32[2,256,256]{2,1,0:T(8,128)S(1)} %get-tuple-element.26.near, f32[1,256,256]{2,1,0:T(8,128)S(1)} %get-tuple-element.27.far_potential), custom_call_target="tpu_custom_call" | custom-call | tf_op jit(solution)/shard_map/part/pallas_call | solution.py:344
  4.6 4.0 %collective-permute-start.3 = (f32[1,256,256]{2,1,0:T(8,128)S(1)}, f32[1,256,256]{2,1,0:T(8,128)S(1)}, u32[]{:S(2)}, u32[]{:S(2)}) collective-permute-start(f32[1,256,256]{2,1,0:T(8,128)S(1)} %get-tuple-element.30.near_part), channel_id=1, source_target_pairs={{0,1},{1,0},{2,3},{3,2},{4,5},{5,4},{6,7},{7,6},{8,9},{9,8},{10,11... | collective-permute-start | bytes 786440 | tf_op jit(solution)/shard_map/ppermute | solution.py:353
  9.2 0.7 %collective-permute-start.6 = (f32[1,384,256]{2,1,0:T(8,128)S(1)}, f32[1,384,256]{2,1,0:T(8,128)S(1)}, u32[]{:S(2)}, u32[]{:S(2)}) collective-permute-start(f32[1,384,256]{2,1,0:T(8,128)S(1)} %get-tuple-element.35), channel_id=1, source_target_pairs={{1,2},{2,1},{3,4},{4,3},{5,6},{6,5},{9,10},{10,9},{11,12},{12,11},... | collective-permute-start | bytes 1179656 | tf_op jit(solution)/shard_map/ppermute | solution.py:354
  10.0 1.2 %sums.1 = (f32[2,256,256]{2,1,0:T(8,128)S(1)}, f32[1,256,256]{2,1,0:T(8,128)S(1)}, f32[8,128]{1,0:T(8,128)S(1)}) custom-call(f32[2,256,256]{2,1,0:T(8,128)S(1)} %get-tuple-element.25.far, f32[2,256,256]{2,1,0:T(8,128)S(1)} %get-tuple-element.26.near, f32[1,256,256]{2,1,0:T(8,128)S(1)} %get-tuple-element.29.far_part, ...), custom_call_target="tpu_custom_call" | custom-call | tf_op jit(solution)/shard_map/sums/pallas_call | solution.py:355
  11.5 6.6 %collective-permute-start.4 = (f32[5,8,128]{2,1,0:T(8,128)S(1)}, f32[5,8,128]{2,1,0:T(8,128)S(1)}, u32[]{:S(2)}, u32[]{:S(2)}) collective-permute-start(f32[5,8,128]{2,1,0:T(8,128)S(1)} %face.1), channel_id=1, source_target_pairs={{0,2},{1,3},{2,0},{3,1},{4,6},{5,7},{6,4},{7,5},{8,10},{9,11},{10,... | collective-permute-start | bytes 61448 | tf_op jit(solution)/shard_map/ppermute | solution.py:371
  18.0 3.9 %collective-permute-done.4 = f32[5,8,128]{2,1,0:T(8,128)S(1)} collective-permute-done((f32[5,8,128]{2,1,0:T(8,128)S(1)}, f32[5,8,128]{2,1,0:T(8,128)S(1)}, u32[]{:S(2)}, u32[]{:S(2)}) %collective-permute-start.4) | collective-permute-done | bytes 20512 | tf_op jit(solution)/shard_map/ppermute | solution.py:371
  21.9 2.2 %collective-permute-start.5 = (f32[5,8,128]{2,1,0:T(8,128)S(1)}, f32[5,8,128]{2,1,0:T(8,128)S(1)}, u32[]{:S(2)}, u32[]{:S(2)}) collective-permute-start(f32[5,8,128]{2,1,0:T(8,128)S(1)} %add.18), channel_id=1, source_target_pairs={{0,4},{1,5},{2,6},{3,7},{4,0},{5,1},{6,2},{7,3},{8,12},{9,13},{10,... | collective-permute-start | bytes 61448 | tf_op jit(solution)/shard_map/ppermute | solution.py:292
  24.1 1.1 %fields.1 = (f32[2,256,256]{2,1,0:T(8,128)S(1)}, f32[2,256,256]{2,1,0:T(8,128)S(1)}, f32[2,256,256]{2,1,0:T(8,128)S(1)}) custom-call(f32[2,256,256]{2,1,0:T(8,128)S(1)} %get-tuple-element.25.far, f32[2,256,256]{2,1,0:T(8,128)S(1)} %get-tuple-element.26.near, f32[2,256,256]{2,1,0:T(8,128)S(1)} %collective-permute-done.far_in, ...), custom_call_target="tpu_custom_call" | custom-call | tf_op jit(solution)/shard_map/fields/pallas_call | solution.py:375
  25.3 1.4 %collective-permute-done.5 = f32[5,8,128]{2,1,0:T(8,128)S(1)} collective-permute-done((f32[5,8,128]{2,1,0:T(8,128)S(1)}, f32[5,8,128]{2,1,0:T(8,128)S(1)}, u32[]{:S(2)}, u32[]{:S(2)}) %collective-permute-start.5) | collective-permute-done | bytes 20512 | tf_op jit(solution)/shard_map/ppermute | solution.py:292
  26.6 1.2 %collective-permute-done.8 = f32[5,8,128]{2,1,0:T(8,128)S(1)} collective-permute-done((f32[5,8,128]{2,1,0:T(8,128)S(1)}, f32[5,8,128]{2,1,0:T(8,128)S(1)}, u32[]{:S(2)}, u32[]{:S(2)}) %collective-permute-start.8) | collective-permute-done | bytes 20512 | tf_op jit(solution)/shard_map/ppermute | solution.py:292
  28.0 1.6 %collective-permute-start.13 = (f32[2,96,256]{2,1,0:T(8,128)S(1)}, f32[2,96,256]{2,1,0:T(8,128)S(1)}, u32[]{:S(2)}, u32[]{:S(2)}) collective-permute-start(f32[2,96,256]{2,1,0:T(8,128)S(1)} %get-tuple-element.47), channel_id=1, source_target_pairs={{0,8},{1,17},{2,10},{3,19},{4,12},{5,21},{6,14},{7,23},{8,0},{9,25... | collective-permute-start | bytes 589832 | tf_op jit(solution)/shard_map/ppermute | solution.py:310
  30.1 1.5 %collective-permute-start.9 = (f32[2,64,256]{2,1,0:T(8,128)S(1)}, f32[2,64,256]{2,1,0:T(8,128)S(1)}, u32[]{:S(2)}, u32[]{:S(2)}) collective-permute-start(f32[2,64,256]{2,1,0:T(8,128)S(1)} %get-tuple-element.45), channel_id=1, source_target_pairs={{0,8},{1,17},{2,10},{3,19},{4,12},{5,21},{6,14},{7,23},{8,0},{9,25... | collective-permute-start | bytes 393224 | tf_op jit(solution)/shard_map/ppermute | solution.py:310
  31.6 2.2 %collective-permute-done.13 = f32[2,96,256]{2,1,0:T(8,128)S(1)} collective-permute-done((f32[2,96,256]{2,1,0:T(8,128)S(1)}, f32[2,96,256]{2,1,0:T(8,128)S(1)}, u32[]{:S(2)}, u32[]{:S(2)}) %collective-permute-start.13) | collective-permute-done | bytes 196640 | tf_op jit(solution)/shard_map/ppermute | solution.py:310
  33.8 1.6 %collective-permute-start.14 = (f32[2,96,256]{2,1,0:T(8,128)S(1)}, f32[2,96,256]{2,1,0:T(8,128)S(1)}, u32[]{:S(2)}, u32[]{:S(2)}) collective-permute-start(f32[2,96,256]{2,1,0:T(8,128)S(1)} %add.23.total), channel_id=1, source_target_pairs={{0,16},{1,9},{2,18},{3,11},{4,20},{5,13},{6,22},{7,15},{8,24},{9,1... | collective-permute-start | bytes 589832 | tf_op jit(solution)/shard_map/ppermute | solution.py:313
  35.9 1.6 %collective-permute-start.12 = (f32[2,96,256]{2,1,0:T(8,128)S(1)}, f32[2,96,256]{2,1,0:T(8,128)S(1)}, u32[]{:S(2)}, u32[]{:S(2)}) collective-permute-start(f32[2,96,256]{2,1,0:T(8,128)S(1)} %add.22.total), channel_id=1, source_target_pairs={{0,16},{1,9},{2,18},{3,11},{4,20},{5,13},{6,22},{7,15},{8,24},{9,1... | collective-permute-start | bytes 589832 | tf_op jit(solution)/shard_map/ppermute | solution.py:313
  37.5 1.2 %collective-permute-done.9 = f32[2,64,256]{2,1,0:T(8,128)S(1)} collective-permute-done((f32[2,64,256]{2,1,0:T(8,128)S(1)}, f32[2,64,256]{2,1,0:T(8,128)S(1)}, u32[]{:S(2)}, u32[]{:S(2)}) %collective-permute-start.9) | collective-permute-done | bytes 131104 | tf_op jit(solution)/shard_map/ppermute | solution.py:310
  38.7 1.6 %collective-permute-start.10 = (f32[2,64,256]{2,1,0:T(8,128)S(1)}, f32[2,64,256]{2,1,0:T(8,128)S(1)}, u32[]{:S(2)}, u32[]{:S(2)}) collective-permute-start(f32[2,64,256]{2,1,0:T(8,128)S(1)} %add.21.total), channel_id=1, source_target_pairs={{0,16},{1,9},{2,18},{3,11},{4,20},{5,13},{6,22},{7,15},{8,24},{9,1... | collective-permute-start | bytes 393224 | tf_op jit(solution)/shard_map/ppermute | solution.py:313
  40.3 1.0 %adjoint.1 = f32[2,256,256]{2,1,0:T(8,128)} custom-call(f32[5,8,128]{2,1,0:T(8,128)S(1)} %add.20.sums, f32[2,256,256]{2,1,0:T(8,128)S(1)} %get-tuple-element.25.far, f32[2,256,256]{2,1,0:T(8,128)S(1)} %get-tuple-element.26.near, f32[2,256,256]{2,1,0:T(8,128)S(1)} %get-tuple-element.31.image), custom_call_target="tpu_custom_call" | custom-call | tf_op jit(solution)/shard_map/adjoint/pallas_call | solution.py:393
  41.3 0.7 %close.3.rest_0_ = f32[2,256,256]{2,1,0:T(8,128)} custom-call(f32[2,96,256]{2,1,0:T(8,128)S(1)} %add.23.total, f32[2,96,256]{2,1,0:T(8,128)S(1)} %collective-permute-done.14.arrived), custom_call_target="tpu_custom_call" | custom-call | tf_op jit(solution)/shard_map/close/pallas_call | solution.py:405
  42.0 0.7 %close.4.rest_0_ = f32[2,256,256]{2,1,0:T(8,128)} custom-call(f32[2,96,256]{2,1,0:T(8,128)S(1)} %add.22.total, f32[2,96,256]{2,1,0:T(8,128)S(1)} %collective-permute-done.12.arrived, f32[2,256,256]{2,1,0:T(8,128)} %close.3.rest_0_), custom_call_target="tpu_custom_call", output_to_operand_aliasing={{}: (2, {})} | custom-call | tf_op jit(solution)/shard_map/close/pallas_call | solution.py:405
  42.7 1.0 %collective-permute-done.10.arrived = f32[2,64,256]{2,1,0:T(8,128)S(1)} collective-permute-done((f32[2,64,256]{2,1,0:T(8,128)S(1)}, f32[2,64,256]{2,1,0:T(8,128)S(1)}, u32[]{:S(2)}, u32[]{:S(2)}) %collective-permute-start.10) | collective-permute-done | bytes 131104 | tf_op jit(solution)/shard_map/ppermute | solution.py:313
  43.8 0.7 %close.5 = f32[2,256,256]{2,1,0:T(8,128)} custom-call(f32[2,64,256]{2,1,0:T(8,128)S(1)} %add.21.total, f32[2,64,256]{2,1,0:T(8,128)S(1)} %collective-permute-done.10.arrived, f32[2,256,256]{2,1,0:T(8,128)} %close.4.rest_0_), custom_call_target="tpu_custom_call", output_to_operand_aliasing={{}: (2, {})} | custom-call | tf_op jit(solution)/shard_map/close/pallas_call | solution.py:405
  (26 shorter events, 2.8 us)
Async XLA Ops:
  2.7 7.2 %collective-permute-start.2 = (f32[2,256,256]{2,1,0:T(8,128)S(1)}, f32[2,256,256]{2,1,0:T(8,128)S(1)}, u32[]{:S(2)}, u32[]{:S(2)}) collective-permute-start(f32[2,256,256]{2,1,0:T(8,128)S(1)} %get-tuple-element.26.near), channel_id=1, source_target_pairs={{0,1},{1,0},{2,3},{3,2},{4,5},{5,4},{6,7},{7,6},{8,9},{9,8},{10,11... | collective-permute-start | bytes 1572872 | tf_op jit(solution)/shard_map/ppermute | solution.py:342
  3.2 6.7 %collective-permute-start = (f32[2,256,256]{2,1,0:T(8,128)S(1)}, f32[2,256,256]{2,1,0:T(8,128)S(1)}, u32[]{:S(2)}, u32[]{:S(2)}) collective-permute-start(f32[2,256,256]{2,1,0:T(8,128)S(1)} %get-tuple-element.25.far), channel_id=1, source_target_pairs={{1,2},{2,1},{3,4},{4,3},{5,6},{6,5},{9,10},{10,9},{11,12},{12,11},... | collective-permute-start | bytes 1572872 | tf_op jit(solution)/shard_map/ppermute | solution.py:341
  4.6 5.3 %collective-permute-start.3 = (f32[1,256,256]{2,1,0:T(8,128)S(1)}, f32[1,256,256]{2,1,0:T(8,128)S(1)}, u32[]{:S(2)}, u32[]{:S(2)}) collective-permute-start(f32[1,256,256]{2,1,0:T(8,128)S(1)} %get-tuple-element.30.near_part), channel_id=1, source_target_pairs={{0,1},{1,0},{2,3},{3,2},{4,5},{5,4},{6,7},{7,6},{8,9},{9,8},{10,11... | collective-permute-start | bytes 786440 | tf_op jit(solution)/shard_map/ppermute | solution.py:353
  8.6 2.6 %collective-permute-start.1 = (f32[1,128,256]{2,1,0:T(8,128)S(1)}, f32[1,128,256]{2,1,0:T(8,128)S(1)}, u32[]{:S(2)}, u32[]{:S(2)}) collective-permute-start(f32[1,128,256]{2,1,0:T(8,128)S(1)} %get-tuple-element.28), channel_id=1, source_target_pairs={{1,2},{2,1},{3,4},{4,3},{5,6},{6,5},{9,10},{10,9},{11,12},{12,11},... | collective-permute-start | bytes 393224 | tf_op jit(solution)/shard_map/ppermute | solution.py:352
  9.2 14.9 %collective-permute-start.6 = (f32[1,384,256]{2,1,0:T(8,128)S(1)}, f32[1,384,256]{2,1,0:T(8,128)S(1)}, u32[]{:S(2)}, u32[]{:S(2)}) collective-permute-start(f32[1,384,256]{2,1,0:T(8,128)S(1)} %get-tuple-element.35), channel_id=1, source_target_pairs={{1,2},{2,1},{3,4},{4,3},{5,6},{6,5},{9,10},{10,9},{11,12},{12,11},... | collective-permute-start | bytes 1179656 | tf_op jit(solution)/shard_map/ppermute | solution.py:354
  11.2 12.9 %copy-start = (f32[1,2,256,256]{3,2,1,0:T(8,128)S(1)}, f32[1,2,256,256]{3,2,1,0:T(8,128)}, u32[]{:S(2)}) copy-start(f32[1,2,256,256]{3,2,1,0:T(8,128)} %param.10) | copy-start | bytes 1572868
  11.2 12.9 %copy-start.1 = (s32[2,256,256]{2,1,0:T(8,128)S(1)}, s32[2,256,256]{2,1,0:T(8,128)}, u32[]{:S(2)}) copy-start(s32[2,256,256]{2,1,0:T(8,128)} %mask.1) | copy-start | bytes 1572868
  11.5 10.4 %collective-permute-start.4 = (f32[5,8,128]{2,1,0:T(8,128)S(1)}, f32[5,8,128]{2,1,0:T(8,128)S(1)}, u32[]{:S(2)}, u32[]{:S(2)}) collective-permute-start(f32[5,8,128]{2,1,0:T(8,128)S(1)} %face.1), channel_id=1, source_target_pairs={{0,2},{1,3},{2,0},{3,1},{4,6},{5,7},{6,4},{7,5},{8,10},{9,11},{10,... | collective-permute-start | bytes 61448 | tf_op jit(solution)/shard_map/ppermute | solution.py:371
  21.9 2.2 %collective-permute-start.7 = (f32[1,256,256]{2,1,0:T(8,128)S(1)}, f32[1,256,256]{2,1,0:T(8,128)S(1)}, u32[]{:S(2)}, u32[]{:S(2)}) collective-permute-start(f32[1,256,256]{2,1,0:T(8,128)S(1)} %get-tuple-element.37), channel_id=1, source_target_pairs={{0,1},{1,0},{2,3},{3,2},{4,5},{5,4},{6,7},{7,6},{8,9},{9,8},{10,11... | collective-permute-start | bytes 786440 | tf_op jit(solution)/shard_map/ppermute | solution.py:373
  21.9 4.7 %collective-permute-start.5 = (f32[5,8,128]{2,1,0:T(8,128)S(1)}, f32[5,8,128]{2,1,0:T(8,128)S(1)}, u32[]{:S(2)}, u32[]{:S(2)}) collective-permute-start(f32[5,8,128]{2,1,0:T(8,128)S(1)} %add.18), channel_id=1, source_target_pairs={{0,4},{1,5},{2,6},{3,7},{4,0},{5,1},{6,2},{7,3},{8,12},{9,13},{10,... | collective-permute-start | bytes 61448 | tf_op jit(solution)/shard_map/ppermute | solution.py:292
  26.6 1.2 %collective-permute-start.8 = (f32[5,8,128]{2,1,0:T(8,128)S(1)}, f32[5,8,128]{2,1,0:T(8,128)S(1)}, u32[]{:S(2)}, u32[]{:S(2)}) collective-permute-start(f32[5,8,128]{2,1,0:T(8,128)S(1)} %add.19), channel_id=1, source_target_pairs={{0,1},{1,0},{2,3},{3,2},{4,5},{5,4},{6,7},{7,6},{8,9},{9,8},{10,11... | collective-permute-start | bytes 61448 | tf_op jit(solution)/shard_map/ppermute | solution.py:292
  28.0 5.7 %collective-permute-start.13 = (f32[2,96,256]{2,1,0:T(8,128)S(1)}, f32[2,96,256]{2,1,0:T(8,128)S(1)}, u32[]{:S(2)}, u32[]{:S(2)}) collective-permute-start(f32[2,96,256]{2,1,0:T(8,128)S(1)} %get-tuple-element.47), channel_id=1, source_target_pairs={{0,8},{1,17},{2,10},{3,19},{4,12},{5,21},{6,14},{7,23},{8,0},{9,25... | collective-permute-start | bytes 589832 | tf_op jit(solution)/shard_map/ppermute | solution.py:310
  29.6 6.3 %collective-permute-start.11 = (f32[2,96,256]{2,1,0:T(8,128)S(1)}, f32[2,96,256]{2,1,0:T(8,128)S(1)}, u32[]{:S(2)}, u32[]{:S(2)}) collective-permute-start(f32[2,96,256]{2,1,0:T(8,128)S(1)} %get-tuple-element.46), channel_id=1, source_target_pairs={{0,8},{1,17},{2,10},{3,19},{4,12},{5,21},{6,14},{7,23},{8,0},{9,25... | collective-permute-start | bytes 589832 | tf_op jit(solution)/shard_map/ppermute | solution.py:310
  30.1 8.6 %collective-permute-start.9 = (f32[2,64,256]{2,1,0:T(8,128)S(1)}, f32[2,64,256]{2,1,0:T(8,128)S(1)}, u32[]{:S(2)}, u32[]{:S(2)}) collective-permute-start(f32[2,64,256]{2,1,0:T(8,128)S(1)} %get-tuple-element.45), channel_id=1, source_target_pairs={{0,8},{1,17},{2,10},{3,19},{4,12},{5,21},{6,14},{7,23},{8,0},{9,25... | collective-permute-start | bytes 393224 | tf_op jit(solution)/shard_map/ppermute | solution.py:310
  33.8 7.5 %collective-permute-start.14 = (f32[2,96,256]{2,1,0:T(8,128)S(1)}, f32[2,96,256]{2,1,0:T(8,128)S(1)}, u32[]{:S(2)}, u32[]{:S(2)}) collective-permute-start(f32[2,96,256]{2,1,0:T(8,128)S(1)} %add.23.total), channel_id=1, source_target_pairs={{0,16},{1,9},{2,18},{3,11},{4,20},{5,13},{6,22},{7,15},{8,24},{9,1... | collective-permute-start | bytes 589832 | tf_op jit(solution)/shard_map/ppermute | solution.py:313
  35.9 6.1 %collective-permute-start.12 = (f32[2,96,256]{2,1,0:T(8,128)S(1)}, f32[2,96,256]{2,1,0:T(8,128)S(1)}, u32[]{:S(2)}, u32[]{:S(2)}) collective-permute-start(f32[2,96,256]{2,1,0:T(8,128)S(1)} %add.22.total), channel_id=1, source_target_pairs={{0,16},{1,9},{2,18},{3,11},{4,20},{5,13},{6,22},{7,15},{8,24},{9,1... | collective-permute-start | bytes 589832 | tf_op jit(solution)/shard_map/ppermute | solution.py:313
  38.7 5.0 %collective-permute-start.10 = (f32[2,64,256]{2,1,0:T(8,128)S(1)}, f32[2,64,256]{2,1,0:T(8,128)S(1)}, u32[]{:S(2)}, u32[]{:S(2)}) collective-permute-start(f32[2,64,256]{2,1,0:T(8,128)S(1)} %add.21.total), channel_id=1, source_target_pairs={{0,16},{1,9},{2,18},{3,11},{4,20},{5,13},{6,22},{7,15},{8,24},{9,1... | collective-permute-start | bytes 393224 | tf_op jit(solution)/shard_map/ppermute | solution.py:313

commit v10 on v9

--- a/solution.py
+++ b/solution.py
@@ -57,7 +57,7 @@
     return slab, lax.rem(slab, 2)
 
 
-def open_kernel(reluctivity, shift, labels, load, potential, far, near, far_potential, near_potential, held, table, sems):
+def open_kernel(reluctivity, shift, labels, load, far, near, held, table, sems):
     _, even = place()
     odd = 1 - even
     total = labels.shape[1]
@@ -66,8 +66,6 @@
         (labels.at[odd], held.at[1]),
         (load.at[even], far.at[1]),
         (load.at[odd], near.at[1]),
-        (potential.at[even], far_potential.at[0]),
-        (potential.at[odd], near_potential.at[0]),
         (reluctivity, table),
     )
     copies = [pltpu.make_async_copy(src, dst, sems.at[i]) for i, (src, dst) in enumerate(moves)]
@@ -92,10 +90,16 @@
         copy.wait()
 
 
-def part_kernel(far, near, far_potential, far_part, near_part, far_early, far_late):
+def part_kernel(far, near, potential, far_part, near_part, far_early, far_late, near_potential, sems):
     _, even = place()
     total = far.shape[1]
     half = total // 2
+    copies = (
+        pltpu.make_async_copy(potential.at[even], far_late.at[0, pl.ds(half, total), :], sems.at[0]),
+        pltpu.make_async_copy(potential.at[1 - even], near_potential.at[0], sems.at[1]),
+    )
+    for copy in copies:
+        copy.start()
     for own, other, out in ((far, near, far_part), (near, far, near_part)):
         for start in range(0, total, ROWS):
             rows = slice(start, start + ROWS)
@@ -104,7 +108,8 @@
             out[0, rows, :] = 0.5 * (v + total_flux)
     far_early[0] = far_part[0, pl.ds(pl.multiple_of((1 - even) * half, 8), half), :]
     far_late[0, 0:half, :] = far_part[0, pl.ds(pl.multiple_of(even * half, 8), half), :]
-    far_late[0, half : half + total, :] = far_potential[0]
+    for copy in copies:
+        copy.wait()
 
 
 def fold(value):
@@ -325,30 +330,31 @@
     vmem = pl.BlockSpec(memory_space=VMEM)
     smem = pl.BlockSpec(memory_space=SMEM)
     hbm = pl.BlockSpec(memory_space=pltpu.HBM)
-    far, near, far_potential, near_potential = pl.pallas_call(
+    far, near = pl.pallas_call(
         open_kernel,
-        out_shape=tuple(pltpu.VMEM((k,) + plane, jnp.float32) for k in (2, 2, 1, 1)),
-        in_specs=[hbm, smem, hbm, hbm, hbm],
-        out_specs=(vmem,) * 4,
+        out_shape=tuple(pltpu.VMEM((k,) + plane, jnp.float32) for k in (2, 2)),
+        in_specs=[hbm, smem, hbm, hbm],
+        out_specs=(vmem,) * 2,
         scratch_shapes=[
             VMEM((2,) + plane, jnp.int32),
             SMEM(reluctivity.shape, jnp.float32),
-            pltpu.SemaphoreType.DMA((7,)),
+            pltpu.SemaphoreType.DMA((5,)),
         ],
         compiler_params=params(),
         name="open",
-    )(in_hbm(reluctivity), rotor_shift, in_hbm(labels), in_hbm(load), in_hbm(potential))
+    )(in_hbm(reluctivity), rotor_shift, in_hbm(labels), in_hbm(load))
     far_in = lax.ppermute(far, "slab", pairs(slabs, 1))
     near_in = lax.ppermute(near, "slab", pairs(slabs, 0))
     half = radial // 2
-    far_part, near_part, far_early, far_late = pl.pallas_call(
+    far_part, near_part, far_early, far_late, near_potential = pl.pallas_call(
         part_kernel,
-        out_shape=tuple(pltpu.VMEM((1, rows, angular), jnp.float32) for rows in (radial, radial, half, half + radial)),
-        in_specs=[vmem] * 3,
-        out_specs=(vmem,) * 4,
+        out_shape=tuple(pltpu.VMEM((1, rows, angular), jnp.float32) for rows in (radial, radial, half, half + radial, radial)),
+        in_specs=[vmem, vmem, hbm],
+        out_specs=(vmem,) * 5,
+        scratch_shapes=[pltpu.SemaphoreType.DMA((2,))],
         compiler_params=params(),
         name="part",
-    )(far, near, far_potential)
+    )(far, near, in_hbm(potential))
     far_early_in = lax.ppermute(far_early, "slab", pairs(slabs, 1))
     near_part_in = lax.ppermute(near_part, "slab", pairs(slabs, 0))
     far_late_in = lax.ppermute(far_late, "slab", pairs(slabs, 1))
@@ -402,6 +408,9 @@
     gradient = ()
     for index, term in enumerate(terms):
         total, arrived = sum_positions(term, positions, slabs)
+        if index == len(terms) - 1:
+            gradient = lax.dynamic_update_slice(gradient, total + arrived, (0, first_rows(radial)[index], 0))
+            break
         gradient = pl.pallas_call(
             functools.partial(close_kernel, first_rows(radial)[index]),
             out_shape=pltpu.HBM((2,) + plane, jnp.float32),

time: 44.6 us -> 45.2 us (1.013)
  waiting for transfers between devices: 11.3 us -> 12.8 us
  starting transfers between devices: 23.7 us -> 22.3 us
  other arithmetic: 0.08 us -> 0.75 us
    ppermute x2, waiting for transfers between devices: 2.56 us -> 3.32 us  [gather_sums(): arrived = lax.ppermute(sums, 'slab', [(i, i ^ step) for i in range(slabs)])]
    ppermute x1, waiting for transfers between devices: 3.87 us -> 4.58 us  [local(): arrived = lax.ppermute(sums, 'slab', [(i, i ^ 2) for i in range(slabs)])]
    ppermute x2, starting transfers between devices: 2.23 us -> 1.52 us  [gather_sums(): arrived = lax.ppermute(sums, 'slab', [(i, i ^ step) for i in range(slabs)])]
    ppermute x1, starting transfers between devices: 6.55 us -> 5.85 us  [local(): arrived = lax.ppermute(sums, 'slab', [(i, i ^ 2) for i in range(slabs)])]
    pallas_call x1, Pallas kernels: 0.66 us -> 1.36 us  [local(): pl.pallas_call(part_kernel, out_shape=tuple((pltpu.VMEM((1, rows, angular...]
    pallas_call x3 -> x2, Pallas kernels: 2.09 us -> 1.42 us  [local(): pl.pallas_call(functools.partial(close_kernel, first_rows(radial)[index])...]
    dynamic_update_slice x0 -> x1, other arithmetic: none -> 0.67 us  [local(): lax.dynamic_update_slice(gradient, total + arrived, (0, first_rows(radial...]
  transfers between devices with their start and end apart: 15 -> 15, of which waited for: 7 -> 7; matrix products, arithmetic and copies ran while one was open for 0% -> 0% of each run, Pallas kernels for 13% -> 14%
where the time goes in v10:
time: 45.2 us; the launch traced here: 45 us
  starting transfers between devices  22.3 us (49%)
  waiting for transfers between devices  12.8 us (28%)
  Pallas kernels  7.67 us (17%)
  between operations  1.47 us (3%)
  other arithmetic  0.75 us (2%)
    ppermute x1, starting transfers between devices, local(): arrived = lax.ppermute(sums, 'slab', [(i, i ^ 2) for i in range(slabs)])  5.85 us
    ppermute x3, starting transfers between devices, sum_positions(): lax.ppermute(term, ('pos', 'slab'), partners(step, positions, slabs))  4.75 us
    ppermute x1, waiting for transfers between devices, local(): arrived = lax.ppermute(sums, 'slab', [(i, i ^ 2) for i in range(slabs)])  4.58 us
    ppermute x1, starting transfers between devices, local(): near_part_in = lax.ppermute(near_part, 'slab', pairs(slabs, 0))  4 us
    ppermute x3, waiting for transfers between devices, sum_positions(): arrived = lax.ppermute(term, ('pos', 'slab'), partners(0, positions, slabs))  3.88 us
    ppermute x3, starting transfers between devices, sum_positions(): arrived = lax.ppermute(term, ('pos', 'slab'), partners(0, positions, slabs))  3.58 us
    ppermute x2, waiting for transfers between devices, gather_sums(): arrived = lax.ppermute(sums, 'slab', [(i, i ^ step) for i in range(slabs)])  3.32 us
    ppermute x2, starting transfers between devices, gather_sums(): arrived = lax.ppermute(sums, 'slab', [(i, i ^ step) for i in range(slabs)])  1.52 us
  transfers between devices with their start and end apart: 15, of which 7 were waited for; matrix products, arithmetic and copies ran while one was open for 0% of the time, Pallas kernels for 14%

profile of v10, /device:TPU:0, one launch (start us, length us, event | category | flops | bytes accessed | tf_op | source)
XLA Modules:
  0.0 45.0 jit_solution(535263887123989520)
XLA Ops:
  1.3 1.2 %open.1 = (f32[2,256,256]{2,1,0:T(8,128)S(1)}, f32[2,256,256]{2,1,0:T(8,128)S(1)}) custom-call(f32[4]{0:T(128)} %reluctivity.1, s32[1]{0:T(128)S(6)} %copy.11.shift, s32[2,256,256]{2,1,0:T(8,128)} %labels.1, f32[2,256,256]{2,1,0:T(8,128)} %bitcast.5), custom_call_target="tpu_custom_call" | custom-call | tf_op jit(solution)/shard_map/open/pallas_call | solution.py:333
  3.0 0.7 %collective-permute-start = (f32[2,256,256]{2,1,0:T(8,128)S(1)}, f32[2,256,256]{2,1,0:T(8,128)S(1)}, u32[]{:S(2)}, u32[]{:S(2)}) collective-permute-start(f32[2,256,256]{2,1,0:T(8,128)S(1)} %get-tuple-element.24.far), channel_id=1, source_target_pairs={{1,2},{2,1},{3,4},{4,3},{5,6},{6,5},{9,10},{10,9},{11,12},{12,11},... | collective-permute-start | bytes 1572872 | tf_op jit(solution)/shard_map/ppermute | solution.py:346
  3.7 1.4 %part.1 = (f32[1,256,256]{2,1,0:T(8,128)S(1)}, f32[1,256,256]{2,1,0:T(8,128)S(1)}, f32[1,128,256]{2,1,0:T(8,128)S(1)}, f32[1,384,256]{2,1,0:T(8,128)S(1)}, f32[1,256,256]{2,1,0:T(8,128)S(1)}) custom-call(f32[2,256,256]{2,1,0:T(8,128)S(1)} %get-tuple-element.24.far, f32[2,256,256]{2,1,0:T(8,128)S(1)} %get-tuple-element.25.near, f32[2,256,256]{2,1,0:T(8,128)} %bitcast.3), custom_call_target="tpu_custom_call" | custom-call | tf_op jit(solution)/shard_map/part/pallas_call | solution.py:349
  5.1 4.0 %collective-permute-start.3 = (f32[1,256,256]{2,1,0:T(8,128)S(1)}, f32[1,256,256]{2,1,0:T(8,128)S(1)}, u32[]{:S(2)}, u32[]{:S(2)}) collective-permute-start(f32[1,256,256]{2,1,0:T(8,128)S(1)} %get-tuple-element.28.near_part), channel_id=1, source_target_pairs={{0,1},{1,0},{2,3},{3,2},{4,5},{5,4},{6,7},{7,6},{8,9},{9,8},{10,11... | collective-permute-start | bytes 786440 | tf_op jit(solution)/shard_map/ppermute | solution.py:359
  9.8 0.7 %collective-permute-start.6 = (f32[1,384,256]{2,1,0:T(8,128)S(1)}, f32[1,384,256]{2,1,0:T(8,128)S(1)}, u32[]{:S(2)}, u32[]{:S(2)}) collective-permute-start(f32[1,384,256]{2,1,0:T(8,128)S(1)} %get-tuple-element.33), channel_id=1, source_target_pairs={{1,2},{2,1},{3,4},{4,3},{5,6},{6,5},{9,10},{10,9},{11,12},{12,11},... | collective-permute-start | bytes 1179656 | tf_op jit(solution)/shard_map/ppermute | solution.py:360
  10.5 1.2 %sums.1 = (f32[2,256,256]{2,1,0:T(8,128)S(1)}, f32[1,256,256]{2,1,0:T(8,128)S(1)}, f32[8,128]{1,0:T(8,128)S(1)}) custom-call(f32[2,256,256]{2,1,0:T(8,128)S(1)} %get-tuple-element.24.far, f32[2,256,256]{2,1,0:T(8,128)S(1)} %get-tuple-element.25.near, f32[1,256,256]{2,1,0:T(8,128)S(1)} %get-tuple-element.27.far_part, ...), custom_call_target="tpu_custom_call" | custom-call | tf_op jit(solution)/shard_map/sums/pallas_call | solution.py:361
  12.0 5.8 %collective-permute-start.4 = (f32[5,8,128]{2,1,0:T(8,128)S(1)}, f32[5,8,128]{2,1,0:T(8,128)S(1)}, u32[]{:S(2)}, u32[]{:S(2)}) collective-permute-start(f32[5,8,128]{2,1,0:T(8,128)S(1)} %face.1), channel_id=1, source_target_pairs={{0,2},{1,3},{2,0},{3,1},{4,6},{5,7},{6,4},{7,5},{8,10},{9,11},{10,... | collective-permute-start | bytes 61448 | tf_op jit(solution)/shard_map/ppermute | solution.py:377
  17.8 4.6 %collective-permute-done.4 = f32[5,8,128]{2,1,0:T(8,128)S(1)} collective-permute-done((f32[5,8,128]{2,1,0:T(8,128)S(1)}, f32[5,8,128]{2,1,0:T(8,128)S(1)}, u32[]{:S(2)}, u32[]{:S(2)}) %collective-permute-start.4) | collective-permute-done | bytes 20512 | tf_op jit(solution)/shard_map/ppermute | solution.py:377
  22.4 1.5 %collective-permute-start.5 = (f32[5,8,128]{2,1,0:T(8,128)S(1)}, f32[5,8,128]{2,1,0:T(8,128)S(1)}, u32[]{:S(2)}, u32[]{:S(2)}) collective-permute-start(f32[5,8,128]{2,1,0:T(8,128)S(1)} %add.21), channel_id=1, source_target_pairs={{0,4},{1,5},{2,6},{3,7},{4,0},{5,1},{6,2},{7,3},{8,12},{9,13},{10,... | collective-permute-start | bytes 61448 | tf_op jit(solution)/shard_map/ppermute | solution.py:297
  24.0 1.1 %fields.1 = (f32[2,256,256]{2,1,0:T(8,128)S(1)}, f32[2,256,256]{2,1,0:T(8,128)S(1)}, f32[2,256,256]{2,1,0:T(8,128)S(1)}) custom-call(f32[2,256,256]{2,1,0:T(8,128)S(1)} %get-tuple-element.24.far, f32[2,256,256]{2,1,0:T(8,128)S(1)} %get-tuple-element.25.near, f32[2,256,256]{2,1,0:T(8,128)S(1)} %collective-permute-done.far_in, ...), custom_call_target="tpu_custom_call" | custom-call | tf_op jit(solution)/shard_map/fields/pallas_call | solution.py:381
  25.0 2.1 %collective-permute-done.5 = f32[5,8,128]{2,1,0:T(8,128)S(1)} collective-permute-done((f32[5,8,128]{2,1,0:T(8,128)S(1)}, f32[5,8,128]{2,1,0:T(8,128)S(1)}, u32[]{:S(2)}, u32[]{:S(2)}) %collective-permute-start.5) | collective-permute-done | bytes 20512 | tf_op jit(solution)/shard_map/ppermute | solution.py:297
  27.2 1.2 %collective-permute-done.8 = f32[5,8,128]{2,1,0:T(8,128)S(1)} collective-permute-done((f32[5,8,128]{2,1,0:T(8,128)S(1)}, f32[5,8,128]{2,1,0:T(8,128)S(1)}, u32[]{:S(2)}, u32[]{:S(2)}) %collective-permute-start.8) | collective-permute-done | bytes 20512 | tf_op jit(solution)/shard_map/ppermute | solution.py:297
  28.6 1.6 %collective-permute-start.11 = (f32[2,96,256]{2,1,0:T(8,128)S(1)}, f32[2,96,256]{2,1,0:T(8,128)S(1)}, u32[]{:S(2)}, u32[]{:S(2)}) collective-permute-start(f32[2,96,256]{2,1,0:T(8,128)S(1)} %get-tuple-element.44), channel_id=1, source_target_pairs={{0,8},{1,17},{2,10},{3,19},{4,12},{5,21},{6,14},{7,23},{8,0},{9,25... | collective-permute-start | bytes 589832 | tf_op jit(solution)/shard_map/ppermute | solution.py:315
  30.7 1.5 %collective-permute-start.13 = (f32[2,64,256]{2,1,0:T(8,128)S(1)}, f32[2,64,256]{2,1,0:T(8,128)S(1)}, u32[]{:S(2)}, u32[]{:S(2)}) collective-permute-start(f32[2,64,256]{2,1,0:T(8,128)S(1)} %get-tuple-element.45), channel_id=1, source_target_pairs={{0,8},{1,17},{2,10},{3,19},{4,12},{5,21},{6,14},{7,23},{8,0},{9,25... | collective-permute-start | bytes 393224 | tf_op jit(solution)/shard_map/ppermute | solution.py:315
  32.1 2.2 %collective-permute-done.11 = f32[2,96,256]{2,1,0:T(8,128)S(1)} collective-permute-done((f32[2,96,256]{2,1,0:T(8,128)S(1)}, f32[2,96,256]{2,1,0:T(8,128)S(1)}, u32[]{:S(2)}, u32[]{:S(2)}) %collective-permute-start.11) | collective-permute-done | bytes 196640 | tf_op jit(solution)/shard_map/ppermute | solution.py:315
  34.3 1.6 %collective-permute-start.12 = (f32[2,96,256]{2,1,0:T(8,128)S(1)}, f32[2,96,256]{2,1,0:T(8,128)S(1)}, u32[]{:S(2)}, u32[]{:S(2)}) collective-permute-start(f32[2,96,256]{2,1,0:T(8,128)S(1)} %add.25.total), channel_id=1, source_target_pairs={{0,16},{1,9},{2,18},{3,11},{4,20},{5,13},{6,22},{7,15},{8,24},{9,1... | collective-permute-start | bytes 589832 | tf_op jit(solution)/shard_map/ppermute | solution.py:318
  36.5 1.6 %collective-permute-start.10 = (f32[2,96,256]{2,1,0:T(8,128)S(1)}, f32[2,96,256]{2,1,0:T(8,128)S(1)}, u32[]{:S(2)}, u32[]{:S(2)}) collective-permute-start(f32[2,96,256]{2,1,0:T(8,128)S(1)} %add.24.total), channel_id=1, source_target_pairs={{0,16},{1,9},{2,18},{3,11},{4,20},{5,13},{6,22},{7,15},{8,24},{9,1... | collective-permute-start | bytes 589832 | tf_op jit(solution)/shard_map/ppermute | solution.py:318
  38.1 1.2 %collective-permute-done.13 = f32[2,64,256]{2,1,0:T(8,128)S(1)} collective-permute-done((f32[2,64,256]{2,1,0:T(8,128)S(1)}, f32[2,64,256]{2,1,0:T(8,128)S(1)}, u32[]{:S(2)}, u32[]{:S(2)}) %collective-permute-start.13) | collective-permute-done | bytes 131104 | tf_op jit(solution)/shard_map/ppermute | solution.py:315
  39.3 1.6 %collective-permute-start.14 = (f32[2,64,256]{2,1,0:T(8,128)S(1)}, f32[2,64,256]{2,1,0:T(8,128)S(1)}, u32[]{:S(2)}, u32[]{:S(2)}) collective-permute-start(f32[2,64,256]{2,1,0:T(8,128)S(1)} %add.26), channel_id=1, source_target_pairs={{0,16},{1,9},{2,18},{3,11},{4,20},{5,13},{6,22},{7,15},{8,24},{9,1... | collective-permute-start | bytes 393224 | tf_op jit(solution)/shard_map/ppermute | solution.py:318
  40.9 1.0 %adjoint.1 = f32[2,256,256]{2,1,0:T(8,128)} custom-call(f32[5,8,128]{2,1,0:T(8,128)S(1)} %add.23.sums, f32[2,256,256]{2,1,0:T(8,128)S(1)} %get-tuple-element.24.far, f32[2,256,256]{2,1,0:T(8,128)S(1)} %get-tuple-element.25.near, f32[2,256,256]{2,1,0:T(8,128)S(1)} %get-tuple-element.29.image), custom_call_target="tpu_custom_call" | custom-call | tf_op jit(solution)/shard_map/adjoint/pallas_call | solution.py:399
  41.8 0.7 %close.2.rest_0_ = f32[2,256,256]{2,1,0:T(8,128)} custom-call(f32[2,96,256]{2,1,0:T(8,128)S(1)} %add.25.total, f32[2,96,256]{2,1,0:T(8,128)S(1)} %collective-permute-done.12.arrived), custom_call_target="tpu_custom_call" | custom-call | tf_op jit(solution)/shard_map/close/pallas_call | solution.py:414
  42.6 0.7 %close.3 = f32[2,256,256]{2,1,0:T(8,128)} custom-call(f32[2,96,256]{2,1,0:T(8,128)S(1)} %add.24.total, f32[2,96,256]{2,1,0:T(8,128)S(1)} %collective-permute-done.10.arrived, f32[2,256,256]{2,1,0:T(8,128)} %close.2.rest_0_), custom_call_target="tpu_custom_call", output_to_operand_aliasing={{}: (2, {})} | custom-call | tf_op jit(solution)/shard_map/close/pallas_call | solution.py:414
  43.3 1.0 %collective-permute-done.14 = f32[2,64,256]{2,1,0:T(8,128)S(1)} collective-permute-done((f32[2,64,256]{2,1,0:T(8,128)S(1)}, f32[2,64,256]{2,1,0:T(8,128)S(1)}, u32[]{:S(2)}, u32[]{:S(2)}) %collective-permute-start.14) | collective-permute-done | bytes 131104 | tf_op jit(solution)/shard_map/ppermute | solution.py:318
  44.3 0.7 %add_dynamic-update-slice_fusion = f32[2,256,256]{2,1,0:T(8,128)} fusion(f32[2,256,256]{2,1,0:T(8,128)} %close.3, f32[2,64,256]{2,1,0:T(8,128)S(1)} %add.26, f32[2,64,256]{2,1,0:T(8,128)S(1)} %collective-permute-done.14), kind=kLoop, calls=%fused_computation | loop fusion | flops 32768 | bytes 393216 | tf_op jit(solution)/shard_map/dynamic_update_slice | solution.py:412
  (26 shorter events, 2.8 us)
Async XLA Ops:
  2.5 7.9 %collective-permute-start.2 = (f32[2,256,256]{2,1,0:T(8,128)S(1)}, f32[2,256,256]{2,1,0:T(8,128)S(1)}, u32[]{:S(2)}, u32[]{:S(2)}) collective-permute-start(f32[2,256,256]{2,1,0:T(8,128)S(1)} %get-tuple-element.25.near), channel_id=1, source_target_pairs={{0,1},{1,0},{2,3},{3,2},{4,5},{5,4},{6,7},{7,6},{8,9},{9,8},{10,11... | collective-permute-start | bytes 1572872 | tf_op jit(solution)/shard_map/ppermute | solution.py:347
  3.0 7.4 %collective-permute-start = (f32[2,256,256]{2,1,0:T(8,128)S(1)}, f32[2,256,256]{2,1,0:T(8,128)S(1)}, u32[]{:S(2)}, u32[]{:S(2)}) collective-permute-start(f32[2,256,256]{2,1,0:T(8,128)S(1)} %get-tuple-element.24.far), channel_id=1, source_target_pairs={{1,2},{2,1},{3,4},{4,3},{5,6},{6,5},{9,10},{10,9},{11,12},{12,11},... | collective-permute-start | bytes 1572872 | tf_op jit(solution)/shard_map/ppermute | solution.py:346
  5.1 5.4 %collective-permute-start.3 = (f32[1,256,256]{2,1,0:T(8,128)S(1)}, f32[1,256,256]{2,1,0:T(8,128)S(1)}, u32[]{:S(2)}, u32[]{:S(2)}) collective-permute-start(f32[1,256,256]{2,1,0:T(8,128)S(1)} %get-tuple-element.28.near_part), channel_id=1, source_target_pairs={{0,1},{1,0},{2,3},{3,2},{4,5},{5,4},{6,7},{7,6},{8,9},{9,8},{10,11... | collective-permute-start | bytes 786440 | tf_op jit(solution)/shard_map/ppermute | solution.py:359
  9.1 2.6 %collective-permute-start.1 = (f32[1,128,256]{2,1,0:T(8,128)S(1)}, f32[1,128,256]{2,1,0:T(8,128)S(1)}, u32[]{:S(2)}, u32[]{:S(2)}) collective-permute-start(f32[1,128,256]{2,1,0:T(8,128)S(1)} %get-tuple-element.26), channel_id=1, source_target_pairs={{1,2},{2,1},{3,4},{4,3},{5,6},{6,5},{9,10},{10,9},{11,12},{12,11},... | collective-permute-start | bytes 393224 | tf_op jit(solution)/shard_map/ppermute | solution.py:358
  9.8 14.2 %collective-permute-start.6 = (f32[1,384,256]{2,1,0:T(8,128)S(1)}, f32[1,384,256]{2,1,0:T(8,128)S(1)}, u32[]{:S(2)}, u32[]{:S(2)}) collective-permute-start(f32[1,384,256]{2,1,0:T(8,128)S(1)} %get-tuple-element.33), channel_id=1, source_target_pairs={{1,2},{2,1},{3,4},{4,3},{5,6},{6,5},{9,10},{10,9},{11,12},{12,11},... | collective-permute-start | bytes 1179656 | tf_op jit(solution)/shard_map/ppermute | solution.py:360
  11.7 12.2 %copy-start = (f32[1,2,256,256]{3,2,1,0:T(8,128)S(1)}, f32[1,2,256,256]{3,2,1,0:T(8,128)}, u32[]{:S(2)}) copy-start(f32[1,2,256,256]{3,2,1,0:T(8,128)} %param.10) | copy-start | bytes 1572868
  11.7 12.2 %copy-start.1 = (s32[2,256,256]{2,1,0:T(8,128)S(1)}, s32[2,256,256]{2,1,0:T(8,128)}, u32[]{:S(2)}) copy-start(s32[2,256,256]{2,1,0:T(8,128)} %mask.1) | copy-start | bytes 1572868
  12.0 10.4 %collective-permute-start.4 = (f32[5,8,128]{2,1,0:T(8,128)S(1)}, f32[5,8,128]{2,1,0:T(8,128)S(1)}, u32[]{:S(2)}, u32[]{:S(2)}) collective-permute-start(f32[5,8,128]{2,1,0:T(8,128)S(1)} %face.1), channel_id=1, source_target_pairs={{0,2},{1,3},{2,0},{3,1},{4,6},{5,7},{6,4},{7,5},{8,10},{9,11},{10,... | collective-permute-start | bytes 61448 | tf_op jit(solution)/shard_map/ppermute | solution.py:377
  22.4 1.5 %collective-permute-start.7 = (f32[1,256,256]{2,1,0:T(8,128)S(1)}, f32[1,256,256]{2,1,0:T(8,128)S(1)}, u32[]{:S(2)}, u32[]{:S(2)}) collective-permute-start(f32[1,256,256]{2,1,0:T(8,128)S(1)} %get-tuple-element.35), channel_id=1, source_target_pairs={{0,1},{1,0},{2,3},{3,2},{4,5},{5,4},{6,7},{7,6},{8,9},{9,8},{10,11... | collective-permute-start | bytes 786440 | tf_op jit(solution)/shard_map/ppermute | solution.py:379
  22.4 4.7 %collective-permute-start.5 = (f32[5,8,128]{2,1,0:T(8,128)S(1)}, f32[5,8,128]{2,1,0:T(8,128)S(1)}, u32[]{:S(2)}, u32[]{:S(2)}) collective-permute-start(f32[5,8,128]{2,1,0:T(8,128)S(1)} %add.21), channel_id=1, source_target_pairs={{0,4},{1,5},{2,6},{3,7},{4,0},{5,1},{6,2},{7,3},{8,12},{9,13},{10,... | collective-permute-start | bytes 61448 | tf_op jit(solution)/shard_map/ppermute | solution.py:297
  27.2 1.2 %collective-permute-start.8 = (f32[5,8,128]{2,1,0:T(8,128)S(1)}, f32[5,8,128]{2,1,0:T(8,128)S(1)}, u32[]{:S(2)}, u32[]{:S(2)}) collective-permute-start(f32[5,8,128]{2,1,0:T(8,128)S(1)} %add.22), channel_id=1, source_target_pairs={{0,1},{1,0},{2,3},{3,2},{4,5},{5,4},{6,7},{7,6},{8,9},{9,8},{10,11... | collective-permute-start | bytes 61448 | tf_op jit(solution)/shard_map/ppermute | solution.py:297
  28.6 5.7 %collective-permute-start.11 = (f32[2,96,256]{2,1,0:T(8,128)S(1)}, f32[2,96,256]{2,1,0:T(8,128)S(1)}, u32[]{:S(2)}, u32[]{:S(2)}) collective-permute-start(f32[2,96,256]{2,1,0:T(8,128)S(1)} %get-tuple-element.44), channel_id=1, source_target_pairs={{0,8},{1,17},{2,10},{3,19},{4,12},{5,21},{6,14},{7,23},{8,0},{9,25... | collective-permute-start | bytes 589832 | tf_op jit(solution)/shard_map/ppermute | solution.py:315
  30.1 6.3 %collective-permute-start.9 = (f32[2,96,256]{2,1,0:T(8,128)S(1)}, f32[2,96,256]{2,1,0:T(8,128)S(1)}, u32[]{:S(2)}, u32[]{:S(2)}) collective-permute-start(f32[2,96,256]{2,1,0:T(8,128)S(1)} %get-tuple-element.43), channel_id=1, source_target_pairs={{0,8},{1,17},{2,10},{3,19},{4,12},{5,21},{6,14},{7,23},{8,0},{9,25... | collective-permute-start | bytes 589832 | tf_op jit(solution)/shard_map/ppermute | solution.py:315
  30.7 8.6 %collective-permute-start.13 = (f32[2,64,256]{2,1,0:T(8,128)S(1)}, f32[2,64,256]{2,1,0:T(8,128)S(1)}, u32[]{:S(2)}, u32[]{:S(2)}) collective-permute-start(f32[2,64,256]{2,1,0:T(8,128)S(1)} %get-tuple-element.45), channel_id=1, source_target_pairs={{0,8},{1,17},{2,10},{3,19},{4,12},{5,21},{6,14},{7,23},{8,0},{9,25... | collective-permute-start | bytes 393224 | tf_op jit(solution)/shard_map/ppermute | solution.py:315
  34.3 7.5 %collective-permute-start.12 = (f32[2,96,256]{2,1,0:T(8,128)S(1)}, f32[2,96,256]{2,1,0:T(8,128)S(1)}, u32[]{:S(2)}, u32[]{:S(2)}) collective-permute-start(f32[2,96,256]{2,1,0:T(8,128)S(1)} %add.25.total), channel_id=1, source_target_pairs={{0,16},{1,9},{2,18},{3,11},{4,20},{5,13},{6,22},{7,15},{8,24},{9,1... | collective-permute-start | bytes 589832 | tf_op jit(solution)/shard_map/ppermute | solution.py:318
  36.5 6.1 %collective-permute-start.10 = (f32[2,96,256]{2,1,0:T(8,128)S(1)}, f32[2,96,256]{2,1,0:T(8,128)S(1)}, u32[]{:S(2)}, u32[]{:S(2)}) collective-permute-start(f32[2,96,256]{2,1,0:T(8,128)S(1)} %add.24.total), channel_id=1, source_target_pairs={{0,16},{1,9},{2,18},{3,11},{4,20},{5,13},{6,22},{7,15},{8,24},{9,1... | collective-permute-start | bytes 589832 | tf_op jit(solution)/shard_map/ppermute | solution.py:318
  39.3 5.0 %collective-permute-start.14 = (f32[2,64,256]{2,1,0:T(8,128)S(1)}, f32[2,64,256]{2,1,0:T(8,128)S(1)}, u32[]{:S(2)}, u32[]{:S(2)}) collective-permute-start(f32[2,64,256]{2,1,0:T(8,128)S(1)} %add.26), channel_id=1, source_target_pairs={{0,16},{1,9},{2,18},{3,11},{4,20},{5,13},{6,22},{7,15},{8,24},{9,1... | collective-permute-start | bytes 393224 | tf_op jit(solution)/shard_map/ppermute | solution.py:318

commit v11 on v9

--- a/solution.py
+++ b/solution.py
@@ -301,7 +301,7 @@
     route = []
     for p in range(positions):
         for s in range(slabs):
-            bit = step if s % 2 == 0 else bits - 1 - step
+            bit = step if s % 2 == 1 else bits - 1 - step
             route.append((p * slabs + s, (p ^ (1 << bit)) * slabs + s))
     return route
 

time: 44.6 us -> 44.6 us (level)
  no operation moved by 1% of the time
where the time goes in v11:
time: 44.6 us; the launch traced here: 44.4 us
  starting transfers between devices  23.6 us (53%)
  waiting for transfers between devices  11.4 us (26%)
  Pallas kernels  7.89 us (18%)
  between operations  1.47 us (3%)
    ppermute x1, starting transfers between devices, local(): arrived = lax.ppermute(sums, 'slab', [(i, i ^ 2) for i in range(slabs)])  6.55 us
    ppermute x3, starting transfers between devices, sum_positions(): lax.ppermute(term, ('pos', 'slab'), partners(step, positions, slabs))  4.67 us
    ppermute x1, starting transfers between devices, local(): near_part_in = lax.ppermute(near_part, 'slab', pairs(slabs, 0))  3.99 us
    ppermute x3, waiting for transfers between devices, sum_positions(): arrived = lax.ppermute(term, ('pos', 'slab'), partners(0, positions, slabs))  3.91 us
    ppermute x1, waiting for transfers between devices, local(): arrived = lax.ppermute(sums, 'slab', [(i, i ^ 2) for i in range(slabs)])  3.87 us
    ppermute x3, starting transfers between devices, sum_positions(): arrived = lax.ppermute(term, ('pos', 'slab'), partners(0, positions, slabs))  3.61 us
    ppermute x2, waiting for transfers between devices, gather_sums(): arrived = lax.ppermute(sums, 'slab', [(i, i ^ step) for i in range(slabs)])  2.56 us
    ppermute x2, starting transfers between devices, gather_sums(): arrived = lax.ppermute(sums, 'slab', [(i, i ^ step) for i in range(slabs)])  2.23 us
  transfers between devices with their start and end apart: 15, of which 7 were waited for; matrix products, arithmetic and copies ran while one was open for 0% of the time, Pallas kernels for 13%

profile of v11, /device:TPU:0, one launch (start us, length us, event | category | flops | bytes accessed | tf_op | source)
XLA Modules:
  0.0 44.4 jit_solution(12765447496377087610)
XLA Ops:
  1.3 1.4 %open.1 = (f32[2,256,256]{2,1,0:T(8,128)S(1)}, f32[2,256,256]{2,1,0:T(8,128)S(1)}, f32[1,256,256]{2,1,0:T(8,128)S(1)}, f32[1,256,256]{2,1,0:T(8,128)S(1)}) custom-call(f32[4]{0:T(128)} %reluctivity.1, s32[1]{0:T(128)S(6)} %copy.12.shift, s32[2,256,256]{2,1,0:T(8,128)} %labels.1, f32[2,256,256]{2,1,0:T(8,128)} %bitcast.5, f32[2,256,256]{2,1,0:T(8,128)} %bitcast.3), custom_call_target="tpu_custom_call" | custom-call | tf_op jit(solution)/shard_map/open/pallas_call | solution.py:328
  3.2 0.7 %collective-permute-start = (f32[2,256,256]{2,1,0:T(8,128)S(1)}, f32[2,256,256]{2,1,0:T(8,128)S(1)}, u32[]{:S(2)}, u32[]{:S(2)}) collective-permute-start(f32[2,256,256]{2,1,0:T(8,128)S(1)} %get-tuple-element.25.far), channel_id=1, source_target_pairs={{1,2},{2,1},{3,4},{4,3},{5,6},{6,5},{9,10},{10,9},{11,12},{12,11},... | collective-permute-start | bytes 1572872 | tf_op jit(solution)/shard_map/ppermute | solution.py:341
  3.9 0.7 %part.1 = (f32[1,256,256]{2,1,0:T(8,128)S(1)}, f32[1,256,256]{2,1,0:T(8,128)S(1)}, f32[1,128,256]{2,1,0:T(8,128)S(1)}, f32[1,384,256]{2,1,0:T(8,128)S(1)}) custom-call(f32[2,256,256]{2,1,0:T(8,128)S(1)} %get-tuple-element.25.far, f32[2,256,256]{2,1,0:T(8,128)S(1)} %get-tuple-element.26.near, f32[1,256,256]{2,1,0:T(8,128)S(1)} %get-tuple-element.27.far_potential), custom_call_target="tpu_custom_call" | custom-call | tf_op jit(solution)/shard_map/part/pallas_call | solution.py:344
  4.6 4.0 %collective-permute-start.3 = (f32[1,256,256]{2,1,0:T(8,128)S(1)}, f32[1,256,256]{2,1,0:T(8,128)S(1)}, u32[]{:S(2)}, u32[]{:S(2)}) collective-permute-start(f32[1,256,256]{2,1,0:T(8,128)S(1)} %get-tuple-element.30.near_part), channel_id=1, source_target_pairs={{0,1},{1,0},{2,3},{3,2},{4,5},{5,4},{6,7},{7,6},{8,9},{9,8},{10,11... | collective-permute-start | bytes 786440 | tf_op jit(solution)/shard_map/ppermute | solution.py:353
  9.2 0.7 %collective-permute-start.6 = (f32[1,384,256]{2,1,0:T(8,128)S(1)}, f32[1,384,256]{2,1,0:T(8,128)S(1)}, u32[]{:S(2)}, u32[]{:S(2)}) collective-permute-start(f32[1,384,256]{2,1,0:T(8,128)S(1)} %get-tuple-element.35), channel_id=1, source_target_pairs={{1,2},{2,1},{3,4},{4,3},{5,6},{6,5},{9,10},{10,9},{11,12},{12,11},... | collective-permute-start | bytes 1179656 | tf_op jit(solution)/shard_map/ppermute | solution.py:354
  10.0 1.2 %sums.1 = (f32[2,256,256]{2,1,0:T(8,128)S(1)}, f32[1,256,256]{2,1,0:T(8,128)S(1)}, f32[8,128]{1,0:T(8,128)S(1)}) custom-call(f32[2,256,256]{2,1,0:T(8,128)S(1)} %get-tuple-element.25.far, f32[2,256,256]{2,1,0:T(8,128)S(1)} %get-tuple-element.26.near, f32[1,256,256]{2,1,0:T(8,128)S(1)} %get-tuple-element.29.far_part, ...), custom_call_target="tpu_custom_call" | custom-call | tf_op jit(solution)/shard_map/sums/pallas_call | solution.py:355
  11.5 6.6 %collective-permute-start.4 = (f32[5,8,128]{2,1,0:T(8,128)S(1)}, f32[5,8,128]{2,1,0:T(8,128)S(1)}, u32[]{:S(2)}, u32[]{:S(2)}) collective-permute-start(f32[5,8,128]{2,1,0:T(8,128)S(1)} %face.1), channel_id=1, source_target_pairs={{0,2},{1,3},{2,0},{3,1},{4,6},{5,7},{6,4},{7,5},{8,10},{9,11},{10,... | collective-permute-start | bytes 61448 | tf_op jit(solution)/shard_map/ppermute | solution.py:371
  18.0 3.9 %collective-permute-done.4 = f32[5,8,128]{2,1,0:T(8,128)S(1)} collective-permute-done((f32[5,8,128]{2,1,0:T(8,128)S(1)}, f32[5,8,128]{2,1,0:T(8,128)S(1)}, u32[]{:S(2)}, u32[]{:S(2)}) %collective-permute-start.4) | collective-permute-done | bytes 20512 | tf_op jit(solution)/shard_map/ppermute | solution.py:371
  21.9 2.2 %collective-permute-start.5 = (f32[5,8,128]{2,1,0:T(8,128)S(1)}, f32[5,8,128]{2,1,0:T(8,128)S(1)}, u32[]{:S(2)}, u32[]{:S(2)}) collective-permute-start(f32[5,8,128]{2,1,0:T(8,128)S(1)} %add.18), channel_id=1, source_target_pairs={{0,4},{1,5},{2,6},{3,7},{4,0},{5,1},{6,2},{7,3},{8,12},{9,13},{10,... | collective-permute-start | bytes 61448 | tf_op jit(solution)/shard_map/ppermute | solution.py:292
  24.1 1.1 %fields.1 = (f32[2,256,256]{2,1,0:T(8,128)S(1)}, f32[2,256,256]{2,1,0:T(8,128)S(1)}, f32[2,256,256]{2,1,0:T(8,128)S(1)}) custom-call(f32[2,256,256]{2,1,0:T(8,128)S(1)} %get-tuple-element.25.far, f32[2,256,256]{2,1,0:T(8,128)S(1)} %get-tuple-element.26.near, f32[2,256,256]{2,1,0:T(8,128)S(1)} %collective-permute-done.far_in, ...), custom_call_target="tpu_custom_call" | custom-call | tf_op jit(solution)/shard_map/fields/pallas_call | solution.py:375
  25.3 1.4 %collective-permute-done.5 = f32[5,8,128]{2,1,0:T(8,128)S(1)} collective-permute-done((f32[5,8,128]{2,1,0:T(8,128)S(1)}, f32[5,8,128]{2,1,0:T(8,128)S(1)}, u32[]{:S(2)}, u32[]{:S(2)}) %collective-permute-start.5) | collective-permute-done | bytes 20512 | tf_op jit(solution)/shard_map/ppermute | solution.py:292
  26.6 1.2 %collective-permute-done.8 = f32[5,8,128]{2,1,0:T(8,128)S(1)} collective-permute-done((f32[5,8,128]{2,1,0:T(8,128)S(1)}, f32[5,8,128]{2,1,0:T(8,128)S(1)}, u32[]{:S(2)}, u32[]{:S(2)}) %collective-permute-start.8) | collective-permute-done | bytes 20512 | tf_op jit(solution)/shard_map/ppermute | solution.py:292
  28.0 1.6 %collective-permute-start.13 = (f32[2,96,256]{2,1,0:T(8,128)S(1)}, f32[2,96,256]{2,1,0:T(8,128)S(1)}, u32[]{:S(2)}, u32[]{:S(2)}) collective-permute-start(f32[2,96,256]{2,1,0:T(8,128)S(1)} %get-tuple-element.47), channel_id=1, source_target_pairs={{0,16},{1,9},{2,18},{3,11},{4,20},{5,13},{6,22},{7,15},{8,24},{9,1... | collective-permute-start | bytes 589832 | tf_op jit(solution)/shard_map/ppermute | solution.py:310
  30.1 1.5 %collective-permute-start.9 = (f32[2,64,256]{2,1,0:T(8,128)S(1)}, f32[2,64,256]{2,1,0:T(8,128)S(1)}, u32[]{:S(2)}, u32[]{:S(2)}) collective-permute-start(f32[2,64,256]{2,1,0:T(8,128)S(1)} %get-tuple-element.45), channel_id=1, source_target_pairs={{0,16},{1,9},{2,18},{3,11},{4,20},{5,13},{6,22},{7,15},{8,24},{9,1... | collective-permute-start | bytes 393224 | tf_op jit(solution)/shard_map/ppermute | solution.py:310
  31.6 2.1 %collective-permute-done.13 = f32[2,96,256]{2,1,0:T(8,128)S(1)} collective-permute-done((f32[2,96,256]{2,1,0:T(8,128)S(1)}, f32[2,96,256]{2,1,0:T(8,128)S(1)}, u32[]{:S(2)}, u32[]{:S(2)}) %collective-permute-start.13) | collective-permute-done | bytes 196640 | tf_op jit(solution)/shard_map/ppermute | solution.py:310
  33.8 1.6 %collective-permute-start.14 = (f32[2,96,256]{2,1,0:T(8,128)S(1)}, f32[2,96,256]{2,1,0:T(8,128)S(1)}, u32[]{:S(2)}, u32[]{:S(2)}) collective-permute-start(f32[2,96,256]{2,1,0:T(8,128)S(1)} %add.23.total), channel_id=1, source_target_pairs={{0,8},{1,17},{2,10},{3,19},{4,12},{5,21},{6,14},{7,23},{8,0},{9,25... | collective-permute-start | bytes 589832 | tf_op jit(solution)/shard_map/ppermute | solution.py:313
  35.9 1.6 %collective-permute-start.12 = (f32[2,96,256]{2,1,0:T(8,128)S(1)}, f32[2,96,256]{2,1,0:T(8,128)S(1)}, u32[]{:S(2)}, u32[]{:S(2)}) collective-permute-start(f32[2,96,256]{2,1,0:T(8,128)S(1)} %add.22.total), channel_id=1, source_target_pairs={{0,8},{1,17},{2,10},{3,19},{4,12},{5,21},{6,14},{7,23},{8,0},{9,25... | collective-permute-start | bytes 589832 | tf_op jit(solution)/shard_map/ppermute | solution.py:313
  37.5 1.2 %collective-permute-done.9 = f32[2,64,256]{2,1,0:T(8,128)S(1)} collective-permute-done((f32[2,64,256]{2,1,0:T(8,128)S(1)}, f32[2,64,256]{2,1,0:T(8,128)S(1)}, u32[]{:S(2)}, u32[]{:S(2)}) %collective-permute-start.9) | collective-permute-done | bytes 131104 | tf_op jit(solution)/shard_map/ppermute | solution.py:310
  38.7 1.6 %collective-permute-start.10 = (f32[2,64,256]{2,1,0:T(8,128)S(1)}, f32[2,64,256]{2,1,0:T(8,128)S(1)}, u32[]{:S(2)}, u32[]{:S(2)}) collective-permute-start(f32[2,64,256]{2,1,0:T(8,128)S(1)} %add.21.total), channel_id=1, source_target_pairs={{0,8},{1,17},{2,10},{3,19},{4,12},{5,21},{6,14},{7,23},{8,0},{9,25... | collective-permute-start | bytes 393224 | tf_op jit(solution)/shard_map/ppermute | solution.py:313
  40.3 1.0 %adjoint.1 = f32[2,256,256]{2,1,0:T(8,128)} custom-call(f32[5,8,128]{2,1,0:T(8,128)S(1)} %add.20.sums, f32[2,256,256]{2,1,0:T(8,128)S(1)} %get-tuple-element.25.far, f32[2,256,256]{2,1,0:T(8,128)S(1)} %get-tuple-element.26.near, f32[2,256,256]{2,1,0:T(8,128)S(1)} %get-tuple-element.31.image), custom_call_target="tpu_custom_call" | custom-call | tf_op jit(solution)/shard_map/adjoint/pallas_call | solution.py:393
  41.3 0.7 %close.3.rest_0_ = f32[2,256,256]{2,1,0:T(8,128)} custom-call(f32[2,96,256]{2,1,0:T(8,128)S(1)} %add.23.total, f32[2,96,256]{2,1,0:T(8,128)S(1)} %collective-permute-done.14.arrived), custom_call_target="tpu_custom_call" | custom-call | tf_op jit(solution)/shard_map/close/pallas_call | solution.py:405
  42.0 0.7 %close.4.rest_0_ = f32[2,256,256]{2,1,0:T(8,128)} custom-call(f32[2,96,256]{2,1,0:T(8,128)S(1)} %add.22.total, f32[2,96,256]{2,1,0:T(8,128)S(1)} %collective-permute-done.12.arrived, f32[2,256,256]{2,1,0:T(8,128)} %close.3.rest_0_), custom_call_target="tpu_custom_call", output_to_operand_aliasing={{}: (2, {})} | custom-call | tf_op jit(solution)/shard_map/close/pallas_call | solution.py:405
  42.7 1.1 %collective-permute-done.10.arrived = f32[2,64,256]{2,1,0:T(8,128)S(1)} collective-permute-done((f32[2,64,256]{2,1,0:T(8,128)S(1)}, f32[2,64,256]{2,1,0:T(8,128)S(1)}, u32[]{:S(2)}, u32[]{:S(2)}) %collective-permute-start.10) | collective-permute-done | bytes 131104 | tf_op jit(solution)/shard_map/ppermute | solution.py:313
  43.8 0.7 %close.5 = f32[2,256,256]{2,1,0:T(8,128)} custom-call(f32[2,64,256]{2,1,0:T(8,128)S(1)} %add.21.total, f32[2,64,256]{2,1,0:T(8,128)S(1)} %collective-permute-done.10.arrived, f32[2,256,256]{2,1,0:T(8,128)} %close.4.rest_0_), custom_call_target="tpu_custom_call", output_to_operand_aliasing={{}: (2, {})} | custom-call | tf_op jit(solution)/shard_map/close/pallas_call | solution.py:405
  (26 shorter events, 2.8 us)
Async XLA Ops:
  2.7 7.2 %collective-permute-start.2 = (f32[2,256,256]{2,1,0:T(8,128)S(1)}, f32[2,256,256]{2,1,0:T(8,128)S(1)}, u32[]{:S(2)}, u32[]{:S(2)}) collective-permute-start(f32[2,256,256]{2,1,0:T(8,128)S(1)} %get-tuple-element.26.near), channel_id=1, source_target_pairs={{0,1},{1,0},{2,3},{3,2},{4,5},{5,4},{6,7},{7,6},{8,9},{9,8},{10,11... | collective-permute-start | bytes 1572872 | tf_op jit(solution)/shard_map/ppermute | solution.py:342
  3.2 6.7 %collective-permute-start = (f32[2,256,256]{2,1,0:T(8,128)S(1)}, f32[2,256,256]{2,1,0:T(8,128)S(1)}, u32[]{:S(2)}, u32[]{:S(2)}) collective-permute-start(f32[2,256,256]{2,1,0:T(8,128)S(1)} %get-tuple-element.25.far), channel_id=1, source_target_pairs={{1,2},{2,1},{3,4},{4,3},{5,6},{6,5},{9,10},{10,9},{11,12},{12,11},... | collective-permute-start | bytes 1572872 | tf_op jit(solution)/shard_map/ppermute | solution.py:341
  4.6 5.3 %collective-permute-start.3 = (f32[1,256,256]{2,1,0:T(8,128)S(1)}, f32[1,256,256]{2,1,0:T(8,128)S(1)}, u32[]{:S(2)}, u32[]{:S(2)}) collective-permute-start(f32[1,256,256]{2,1,0:T(8,128)S(1)} %get-tuple-element.30.near_part), channel_id=1, source_target_pairs={{0,1},{1,0},{2,3},{3,2},{4,5},{5,4},{6,7},{7,6},{8,9},{9,8},{10,11... | collective-permute-start | bytes 786440 | tf_op jit(solution)/shard_map/ppermute | solution.py:353
  8.6 2.6 %collective-permute-start.1 = (f32[1,128,256]{2,1,0:T(8,128)S(1)}, f32[1,128,256]{2,1,0:T(8,128)S(1)}, u32[]{:S(2)}, u32[]{:S(2)}) collective-permute-start(f32[1,128,256]{2,1,0:T(8,128)S(1)} %get-tuple-element.28), channel_id=1, source_target_pairs={{1,2},{2,1},{3,4},{4,3},{5,6},{6,5},{9,10},{10,9},{11,12},{12,11},... | collective-permute-start | bytes 393224 | tf_op jit(solution)/shard_map/ppermute | solution.py:352
  9.2 14.9 %collective-permute-start.6 = (f32[1,384,256]{2,1,0:T(8,128)S(1)}, f32[1,384,256]{2,1,0:T(8,128)S(1)}, u32[]{:S(2)}, u32[]{:S(2)}) collective-permute-start(f32[1,384,256]{2,1,0:T(8,128)S(1)} %get-tuple-element.35), channel_id=1, source_target_pairs={{1,2},{2,1},{3,4},{4,3},{5,6},{6,5},{9,10},{10,9},{11,12},{12,11},... | collective-permute-start | bytes 1179656 | tf_op jit(solution)/shard_map/ppermute | solution.py:354
  11.2 12.9 %copy-start = (f32[1,2,256,256]{3,2,1,0:T(8,128)S(1)}, f32[1,2,256,256]{3,2,1,0:T(8,128)}, u32[]{:S(2)}) copy-start(f32[1,2,256,256]{3,2,1,0:T(8,128)} %param.10) | copy-start | bytes 1572868
  11.2 12.9 %copy-start.1 = (s32[2,256,256]{2,1,0:T(8,128)S(1)}, s32[2,256,256]{2,1,0:T(8,128)}, u32[]{:S(2)}) copy-start(s32[2,256,256]{2,1,0:T(8,128)} %mask.1) | copy-start | bytes 1572868
  11.5 10.4 %collective-permute-start.4 = (f32[5,8,128]{2,1,0:T(8,128)S(1)}, f32[5,8,128]{2,1,0:T(8,128)S(1)}, u32[]{:S(2)}, u32[]{:S(2)}) collective-permute-start(f32[5,8,128]{2,1,0:T(8,128)S(1)} %face.1), channel_id=1, source_target_pairs={{0,2},{1,3},{2,0},{3,1},{4,6},{5,7},{6,4},{7,5},{8,10},{9,11},{10,... | collective-permute-start | bytes 61448 | tf_op jit(solution)/shard_map/ppermute | solution.py:371
  21.9 2.2 %collective-permute-start.7 = (f32[1,256,256]{2,1,0:T(8,128)S(1)}, f32[1,256,256]{2,1,0:T(8,128)S(1)}, u32[]{:S(2)}, u32[]{:S(2)}) collective-permute-start(f32[1,256,256]{2,1,0:T(8,128)S(1)} %get-tuple-element.37), channel_id=1, source_target_pairs={{0,1},{1,0},{2,3},{3,2},{4,5},{5,4},{6,7},{7,6},{8,9},{9,8},{10,11... | collective-permute-start | bytes 786440 | tf_op jit(solution)/shard_map/ppermute | solution.py:373
  21.9 4.7 %collective-permute-start.5 = (f32[5,8,128]{2,1,0:T(8,128)S(1)}, f32[5,8,128]{2,1,0:T(8,128)S(1)}, u32[]{:S(2)}, u32[]{:S(2)}) collective-permute-start(f32[5,8,128]{2,1,0:T(8,128)S(1)} %add.18), channel_id=1, source_target_pairs={{0,4},{1,5},{2,6},{3,7},{4,0},{5,1},{6,2},{7,3},{8,12},{9,13},{10,... | collective-permute-start | bytes 61448 | tf_op jit(solution)/shard_map/ppermute | solution.py:292
  26.6 1.2 %collective-permute-start.8 = (f32[5,8,128]{2,1,0:T(8,128)S(1)}, f32[5,8,128]{2,1,0:T(8,128)S(1)}, u32[]{:S(2)}, u32[]{:S(2)}) collective-permute-start(f32[5,8,128]{2,1,0:T(8,128)S(1)} %add.19), channel_id=1, source_target_pairs={{0,1},{1,0},{2,3},{3,2},{4,5},{5,4},{6,7},{7,6},{8,9},{9,8},{10,11... | collective-permute-start | bytes 61448 | tf_op jit(solution)/shard_map/ppermute | solution.py:292
  28.0 5.7 %collective-permute-start.13 = (f32[2,96,256]{2,1,0:T(8,128)S(1)}, f32[2,96,256]{2,1,0:T(8,128)S(1)}, u32[]{:S(2)}, u32[]{:S(2)}) collective-permute-start(f32[2,96,256]{2,1,0:T(8,128)S(1)} %get-tuple-element.47), channel_id=1, source_target_pairs={{0,16},{1,9},{2,18},{3,11},{4,20},{5,13},{6,22},{7,15},{8,24},{9,1... | collective-permute-start | bytes 589832 | tf_op jit(solution)/shard_map/ppermute | solution.py:310
  29.6 6.3 %collective-permute-start.11 = (f32[2,96,256]{2,1,0:T(8,128)S(1)}, f32[2,96,256]{2,1,0:T(8,128)S(1)}, u32[]{:S(2)}, u32[]{:S(2)}) collective-permute-start(f32[2,96,256]{2,1,0:T(8,128)S(1)} %get-tuple-element.46), channel_id=1, source_target_pairs={{0,16},{1,9},{2,18},{3,11},{4,20},{5,13},{6,22},{7,15},{8,24},{9,1... | collective-permute-start | bytes 589832 | tf_op jit(solution)/shard_map/ppermute | solution.py:310
  30.1 8.6 %collective-permute-start.9 = (f32[2,64,256]{2,1,0:T(8,128)S(1)}, f32[2,64,256]{2,1,0:T(8,128)S(1)}, u32[]{:S(2)}, u32[]{:S(2)}) collective-permute-start(f32[2,64,256]{2,1,0:T(8,128)S(1)} %get-tuple-element.45), channel_id=1, source_target_pairs={{0,16},{1,9},{2,18},{3,11},{4,20},{5,13},{6,22},{7,15},{8,24},{9,1... | collective-permute-start | bytes 393224 | tf_op jit(solution)/shard_map/ppermute | solution.py:310
  33.8 7.5 %collective-permute-start.14 = (f32[2,96,256]{2,1,0:T(8,128)S(1)}, f32[2,96,256]{2,1,0:T(8,128)S(1)}, u32[]{:S(2)}, u32[]{:S(2)}) collective-permute-start(f32[2,96,256]{2,1,0:T(8,128)S(1)} %add.23.total), channel_id=1, source_target_pairs={{0,8},{1,17},{2,10},{3,19},{4,12},{5,21},{6,14},{7,23},{8,0},{9,25... | collective-permute-start | bytes 589832 | tf_op jit(solution)/shard_map/ppermute | solution.py:313
  35.9 6.1 %collective-permute-start.12 = (f32[2,96,256]{2,1,0:T(8,128)S(1)}, f32[2,96,256]{2,1,0:T(8,128)S(1)}, u32[]{:S(2)}, u32[]{:S(2)}) collective-permute-start(f32[2,96,256]{2,1,0:T(8,128)S(1)} %add.22.total), channel_id=1, source_target_pairs={{0,8},{1,17},{2,10},{3,19},{4,12},{5,21},{6,14},{7,23},{8,0},{9,25... | collective-permute-start | bytes 589832 | tf_op jit(solution)/shard_map/ppermute | solution.py:313
  38.7 5.0 %collective-permute-start.10 = (f32[2,64,256]{2,1,0:T(8,128)S(1)}, f32[2,64,256]{2,1,0:T(8,128)S(1)}, u32[]{:S(2)}, u32[]{:S(2)}) collective-permute-start(f32[2,64,256]{2,1,0:T(8,128)S(1)} %add.21.total), channel_id=1, source_target_pairs={{0,8},{1,17},{2,10},{3,19},{4,12},{5,21},{6,14},{7,23},{8,0},{9,25... | collective-permute-start | bytes 393224 | tf_op jit(solution)/shard_map/ppermute | solution.py:313

commit v12 on v9

--- a/solution.py
+++ b/solution.py
@@ -12,7 +12,7 @@
 VMEM = pltpu.VMEM
 SMEM = pltpu.SMEM
 SUMS = 5
-EIGHTHS = (3, 3, 2)
+EIGHTHS = (2, 2, 2, 2)
 
 
 def params():

time: 44.6 us -> 45.5 us (1.020)
  starting transfers between devices: 23.7 us -> 25.7 us
  waiting for transfers between devices: 11.3 us -> 9.58 us
  Pallas kernels: 7.89 us -> 8.51 us
    ppermute x3 -> x4, starting transfers between devices: 4.75 us -> 6.22 us  [sum_positions(): lax.ppermute(term, ('pos', 'slab'), partners(step, positions, slabs))]
    ppermute x3 -> x4, waiting for transfers between devices: 3.88 us -> 2.76 us  [sum_positions(): arrived = lax.ppermute(term, ('pos', 'slab'), partners(0, positions, slabs))]
    ppermute x3 -> x4, waiting for transfers between devices: 1.03 us -> 0.38 us  [sum_positions(): lax.ppermute(term, ('pos', 'slab'), partners(step, positions, slabs))]
    pallas_call x3 -> x4, Pallas kernels: 2.09 us -> 2.72 us  [local(): pl.pallas_call(functools.partial(close_kernel, first_rows(radial)[index])...]
    ppermute x3 -> x4, starting transfers between devices: 3.58 us -> 4.12 us  [sum_positions(): arrived = lax.ppermute(term, ('pos', 'slab'), partners(0, positions, slabs))]
  transfers between devices with their start and end apart: 15 -> 17, of which waited for: 7 -> 7; matrix products, arithmetic and copies ran while one was open for 0% -> 0% of each run, Pallas kernels for 13% -> 14%
where the time goes in v12:
time: 45.5 us; the launch traced here: 45.3 us
  starting transfers between devices  25.7 us (56%)
  waiting for transfers between devices  9.58 us (21%)
  Pallas kernels  8.51 us (19%)
  between operations  1.49 us (3%)
    ppermute x1, starting transfers between devices, local(): arrived = lax.ppermute(sums, 'slab', [(i, i ^ 2) for i in range(slabs)])  6.55 us
    ppermute x4, starting transfers between devices, sum_positions(): lax.ppermute(term, ('pos', 'slab'), partners(step, positions, slabs))  6.22 us
    ppermute x4, starting transfers between devices, sum_positions(): arrived = lax.ppermute(term, ('pos', 'slab'), partners(0, positions, slabs))  4.12 us
    ppermute x1, starting transfers between devices, local(): near_part_in = lax.ppermute(near_part, 'slab', pairs(slabs, 0))  3.99 us
    ppermute x1, waiting for transfers between devices, local(): arrived = lax.ppermute(sums, 'slab', [(i, i ^ 2) for i in range(slabs)])  3.87 us
    ppermute x4, waiting for transfers between devices, sum_positions(): arrived = lax.ppermute(term, ('pos', 'slab'), partners(0, positions, slabs))  2.76 us
    pallas_call x4, Pallas kernels, local(): pl.pallas_call(functools.partial(close_kernel, first_rows(radial)[index])...  2.72 us
    ppermute x2, waiting for transfers between devices, gather_sums(): arrived = lax.ppermute(sums, 'slab', [(i, i ^ step) for i in range(slabs)])  2.56 us
  transfers between devices with their start and end apart: 17, of which 7 were waited for; matrix products, arithmetic and copies ran while one was open for 0% of the time, Pallas kernels for 14%

profile of v12, /device:TPU:0, one launch (start us, length us, event | category | flops | bytes accessed | tf_op | source)
XLA Modules:
  0.0 45.3 jit_solution(256374177639337244)
XLA Ops:
  1.3 1.4 %open.1 = (f32[2,256,256]{2,1,0:T(8,128)S(1)}, f32[2,256,256]{2,1,0:T(8,128)S(1)}, f32[1,256,256]{2,1,0:T(8,128)S(1)}, f32[1,256,256]{2,1,0:T(8,128)S(1)}) custom-call(f32[4]{0:T(128)} %reluctivity.1, s32[1]{0:T(128)S(6)} %copy.14.shift, s32[2,256,256]{2,1,0:T(8,128)} %labels.1, f32[2,256,256]{2,1,0:T(8,128)} %bitcast.5, f32[2,256,256]{2,1,0:T(8,128)} %bitcast.3), custom_call_target="tpu_custom_call" | custom-call | tf_op jit(solution)/shard_map/open/pallas_call | solution.py:328
  3.2 0.7 %collective-permute-start = (f32[2,256,256]{2,1,0:T(8,128)S(1)}, f32[2,256,256]{2,1,0:T(8,128)S(1)}, u32[]{:S(2)}, u32[]{:S(2)}) collective-permute-start(f32[2,256,256]{2,1,0:T(8,128)S(1)} %get-tuple-element.26.far), channel_id=1, source_target_pairs={{1,2},{2,1},{3,4},{4,3},{5,6},{6,5},{9,10},{10,9},{11,12},{12,11},... | collective-permute-start | bytes 1572872 | tf_op jit(solution)/shard_map/ppermute | solution.py:341
  4.6 4.0 %collective-permute-start.3 = (f32[1,256,256]{2,1,0:T(8,128)S(1)}, f32[1,256,256]{2,1,0:T(8,128)S(1)}, u32[]{:S(2)}, u32[]{:S(2)}) collective-permute-start(f32[1,256,256]{2,1,0:T(8,128)S(1)} %get-tuple-element.31.near_part), channel_id=1, source_target_pairs={{0,1},{1,0},{2,3},{3,2},{4,5},{5,4},{6,7},{7,6},{8,9},{9,8},{10,11... | collective-permute-start | bytes 786440 | tf_op jit(solution)/shard_map/ppermute | solution.py:353
  9.2 0.7 %collective-permute-start.6 = (f32[1,384,256]{2,1,0:T(8,128)S(1)}, f32[1,384,256]{2,1,0:T(8,128)S(1)}, u32[]{:S(2)}, u32[]{:S(2)}) collective-permute-start(f32[1,384,256]{2,1,0:T(8,128)S(1)} %get-tuple-element.36), channel_id=1, source_target_pairs={{1,2},{2,1},{3,4},{4,3},{5,6},{6,5},{9,10},{10,9},{11,12},{12,11},... | collective-permute-start | bytes 1179656 | tf_op jit(solution)/shard_map/ppermute | solution.py:354
  10.0 1.2 %sums.1 = (f32[2,256,256]{2,1,0:T(8,128)S(1)}, f32[1,256,256]{2,1,0:T(8,128)S(1)}, f32[8,128]{1,0:T(8,128)S(1)}) custom-call(f32[2,256,256]{2,1,0:T(8,128)S(1)} %get-tuple-element.26.far, f32[2,256,256]{2,1,0:T(8,128)S(1)} %get-tuple-element.27.near, f32[1,256,256]{2,1,0:T(8,128)S(1)} %get-tuple-element.30.far_part, ...), custom_call_target="tpu_custom_call" | custom-call | tf_op jit(solution)/shard_map/sums/pallas_call | solution.py:355
  11.5 6.6 %collective-permute-start.4 = (f32[5,8,128]{2,1,0:T(8,128)S(1)}, f32[5,8,128]{2,1,0:T(8,128)S(1)}, u32[]{:S(2)}, u32[]{:S(2)}) collective-permute-start(f32[5,8,128]{2,1,0:T(8,128)S(1)} %face.1), channel_id=1, source_target_pairs={{0,2},{1,3},{2,0},{3,1},{4,6},{5,7},{6,4},{7,5},{8,10},{9,11},{10,... | collective-permute-start | bytes 61448 | tf_op jit(solution)/shard_map/ppermute | solution.py:371
  18.0 3.9 %collective-permute-done.4 = f32[5,8,128]{2,1,0:T(8,128)S(1)} collective-permute-done((f32[5,8,128]{2,1,0:T(8,128)S(1)}, f32[5,8,128]{2,1,0:T(8,128)S(1)}, u32[]{:S(2)}, u32[]{:S(2)}) %collective-permute-start.4) | collective-permute-done | bytes 20512 | tf_op jit(solution)/shard_map/ppermute | solution.py:371
  21.9 2.2 %collective-permute-start.5 = (f32[5,8,128]{2,1,0:T(8,128)S(1)}, f32[5,8,128]{2,1,0:T(8,128)S(1)}, u32[]{:S(2)}, u32[]{:S(2)}) collective-permute-start(f32[5,8,128]{2,1,0:T(8,128)S(1)} %add.21), channel_id=1, source_target_pairs={{0,4},{1,5},{2,6},{3,7},{4,0},{5,1},{6,2},{7,3},{8,12},{9,13},{10,... | collective-permute-start | bytes 61448 | tf_op jit(solution)/shard_map/ppermute | solution.py:292
  24.1 1.1 %fields.1 = (f32[2,256,256]{2,1,0:T(8,128)S(1)}, f32[2,256,256]{2,1,0:T(8,128)S(1)}, f32[2,256,256]{2,1,0:T(8,128)S(1)}) custom-call(f32[2,256,256]{2,1,0:T(8,128)S(1)} %get-tuple-element.26.far, f32[2,256,256]{2,1,0:T(8,128)S(1)} %get-tuple-element.27.near, f32[2,256,256]{2,1,0:T(8,128)S(1)} %collective-permute-done.far_in, ...), custom_call_target="tpu_custom_call" | custom-call | tf_op jit(solution)/shard_map/fields/pallas_call | solution.py:375
  25.3 1.4 %collective-permute-done.5 = f32[5,8,128]{2,1,0:T(8,128)S(1)} collective-permute-done((f32[5,8,128]{2,1,0:T(8,128)S(1)}, f32[5,8,128]{2,1,0:T(8,128)S(1)}, u32[]{:S(2)}, u32[]{:S(2)}) %collective-permute-start.5) | collective-permute-done | bytes 20512 | tf_op jit(solution)/shard_map/ppermute | solution.py:292
  26.6 1.2 %collective-permute-done.8 = f32[5,8,128]{2,1,0:T(8,128)S(1)} collective-permute-done((f32[5,8,128]{2,1,0:T(8,128)S(1)}, f32[5,8,128]{2,1,0:T(8,128)S(1)}, u32[]{:S(2)}, u32[]{:S(2)}) %collective-permute-start.8) | collective-permute-done | bytes 20512 | tf_op jit(solution)/shard_map/ppermute | solution.py:292
  28.0 1.6 %collective-permute-start.13 = (f32[2,64,256]{2,1,0:T(8,128)S(1)}, f32[2,64,256]{2,1,0:T(8,128)S(1)}, u32[]{:S(2)}, u32[]{:S(2)}) collective-permute-start(f32[2,64,256]{2,1,0:T(8,128)S(1)} %get-tuple-element.48), channel_id=1, source_target_pairs={{0,8},{1,17},{2,10},{3,19},{4,12},{5,21},{6,14},{7,23},{8,0},{9,25... | collective-permute-start | bytes 393224 | tf_op jit(solution)/shard_map/ppermute | solution.py:310
  30.1 1.5 %collective-permute-start.11 = (f32[2,64,256]{2,1,0:T(8,128)S(1)}, f32[2,64,256]{2,1,0:T(8,128)S(1)}, u32[]{:S(2)}, u32[]{:S(2)}) collective-permute-start(f32[2,64,256]{2,1,0:T(8,128)S(1)} %get-tuple-element.47), channel_id=1, source_target_pairs={{0,8},{1,17},{2,10},{3,19},{4,12},{5,21},{6,14},{7,23},{8,0},{9,25... | collective-permute-start | bytes 393224 | tf_op jit(solution)/shard_map/ppermute | solution.py:310
  32.1 0.9 %collective-permute-done.13 = f32[2,64,256]{2,1,0:T(8,128)S(1)} collective-permute-done((f32[2,64,256]{2,1,0:T(8,128)S(1)}, f32[2,64,256]{2,1,0:T(8,128)S(1)}, u32[]{:S(2)}, u32[]{:S(2)}) %collective-permute-start.13) | collective-permute-done | bytes 131104 | tf_op jit(solution)/shard_map/ppermute | solution.py:310
  33.1 1.6 %collective-permute-start.14 = (f32[2,64,256]{2,1,0:T(8,128)S(1)}, f32[2,64,256]{2,1,0:T(8,128)S(1)}, u32[]{:S(2)}, u32[]{:S(2)}) collective-permute-start(f32[2,64,256]{2,1,0:T(8,128)S(1)} %add.26.total), channel_id=1, source_target_pairs={{0,16},{1,9},{2,18},{3,11},{4,20},{5,13},{6,22},{7,15},{8,24},{9,1... | collective-permute-start | bytes 393224 | tf_op jit(solution)/shard_map/ppermute | solution.py:313
  34.7 1.5 %collective-permute-start.16 = (f32[2,64,256]{2,1,0:T(8,128)S(1)}, f32[2,64,256]{2,1,0:T(8,128)S(1)}, u32[]{:S(2)}, u32[]{:S(2)}) collective-permute-start(f32[2,64,256]{2,1,0:T(8,128)S(1)} %add.27.total), channel_id=1, source_target_pairs={{0,16},{1,9},{2,18},{3,11},{4,20},{5,13},{6,22},{7,15},{8,24},{9,1... | collective-permute-start | bytes 393224 | tf_op jit(solution)/shard_map/ppermute | solution.py:313
  36.8 1.6 %collective-permute-start.12 = (f32[2,64,256]{2,1,0:T(8,128)S(1)}, f32[2,64,256]{2,1,0:T(8,128)S(1)}, u32[]{:S(2)}, u32[]{:S(2)}) collective-permute-start(f32[2,64,256]{2,1,0:T(8,128)S(1)} %add.25.total), channel_id=1, source_target_pairs={{0,16},{1,9},{2,18},{3,11},{4,20},{5,13},{6,22},{7,15},{8,24},{9,1... | collective-permute-start | bytes 393224 | tf_op jit(solution)/shard_map/ppermute | solution.py:313
  38.4 1.2 %collective-permute-done.9 = f32[2,64,256]{2,1,0:T(8,128)S(1)} collective-permute-done((f32[2,64,256]{2,1,0:T(8,128)S(1)}, f32[2,64,256]{2,1,0:T(8,128)S(1)}, u32[]{:S(2)}, u32[]{:S(2)}) %collective-permute-start.9) | collective-permute-done | bytes 131104 | tf_op jit(solution)/shard_map/ppermute | solution.py:310
  39.6 1.6 %collective-permute-start.10 = (f32[2,64,256]{2,1,0:T(8,128)S(1)}, f32[2,64,256]{2,1,0:T(8,128)S(1)}, u32[]{:S(2)}, u32[]{:S(2)}) collective-permute-start(f32[2,64,256]{2,1,0:T(8,128)S(1)} %add.24.total), channel_id=1, source_target_pairs={{0,16},{1,9},{2,18},{3,11},{4,20},{5,13},{6,22},{7,15},{8,24},{9,1... | collective-permute-start | bytes 393224 | tf_op jit(solution)/shard_map/ppermute | solution.py:313
  41.2 1.0 %adjoint.1 = f32[2,256,256]{2,1,0:T(8,128)} custom-call(f32[5,8,128]{2,1,0:T(8,128)S(1)} %add.23.sums, f32[2,256,256]{2,1,0:T(8,128)S(1)} %get-tuple-element.26.far, f32[2,256,256]{2,1,0:T(8,128)S(1)} %get-tuple-element.27.near, f32[2,256,256]{2,1,0:T(8,128)S(1)} %get-tuple-element.32.image), custom_call_target="tpu_custom_call" | custom-call | tf_op jit(solution)/shard_map/adjoint/pallas_call | solution.py:393
  42.2 0.7 %close.4.rest_0_ = f32[2,256,256]{2,1,0:T(8,128)} custom-call(f32[2,64,256]{2,1,0:T(8,128)S(1)} %add.27.total, f32[2,64,256]{2,1,0:T(8,128)S(1)} %collective-permute-done.16.arrived), custom_call_target="tpu_custom_call" | custom-call | tf_op jit(solution)/shard_map/close/pallas_call | solution.py:405
  42.9 0.7 %close.5.rest_0_ = f32[2,256,256]{2,1,0:T(8,128)} custom-call(f32[2,64,256]{2,1,0:T(8,128)S(1)} %add.26.total, f32[2,64,256]{2,1,0:T(8,128)S(1)} %collective-permute-done.14.arrived, f32[2,256,256]{2,1,0:T(8,128)} %close.4.rest_0_), custom_call_target="tpu_custom_call", output_to_operand_aliasing={{}: (2, {})} | custom-call | tf_op jit(solution)/shard_map/close/pallas_call | solution.py:405
  43.6 0.7 %close.6.rest_0_ = f32[2,256,256]{2,1,0:T(8,128)} custom-call(f32[2,64,256]{2,1,0:T(8,128)S(1)} %add.25.total, f32[2,64,256]{2,1,0:T(8,128)S(1)} %collective-permute-done.12.arrived, f32[2,256,256]{2,1,0:T(8,128)} %close.5.rest_0_), custom_call_target="tpu_custom_call", output_to_operand_aliasing={{}: (2, {})} | custom-call | tf_op jit(solution)/shard_map/close/pallas_call | solution.py:405
  44.7 0.7 %close.7 = f32[2,256,256]{2,1,0:T(8,128)} custom-call(f32[2,64,256]{2,1,0:T(8,128)S(1)} %add.24.total, f32[2,64,256]{2,1,0:T(8,128)S(1)} %collective-permute-done.10.arrived, f32[2,256,256]{2,1,0:T(8,128)} %close.6.rest_0_), custom_call_target="tpu_custom_call", output_to_operand_aliasing={{}: (2, {})} | custom-call | tf_op jit(solution)/shard_map/close/pallas_call | solution.py:405
  (32 shorter events, 4.4 us)
Async XLA Ops:
  2.7 7.2 %collective-permute-start.2 = (f32[2,256,256]{2,1,0:T(8,128)S(1)}, f32[2,256,256]{2,1,0:T(8,128)S(1)}, u32[]{:S(2)}, u32[]{:S(2)}) collective-permute-start(f32[2,256,256]{2,1,0:T(8,128)S(1)} %get-tuple-element.27.near), channel_id=1, source_target_pairs={{0,1},{1,0},{2,3},{3,2},{4,5},{5,4},{6,7},{7,6},{8,9},{9,8},{10,11... | collective-permute-start | bytes 1572872 | tf_op jit(solution)/shard_map/ppermute | solution.py:342
  3.2 6.7 %collective-permute-start = (f32[2,256,256]{2,1,0:T(8,128)S(1)}, f32[2,256,256]{2,1,0:T(8,128)S(1)}, u32[]{:S(2)}, u32[]{:S(2)}) collective-permute-start(f32[2,256,256]{2,1,0:T(8,128)S(1)} %get-tuple-element.26.far), channel_id=1, source_target_pairs={{1,2},{2,1},{3,4},{4,3},{5,6},{6,5},{9,10},{10,9},{11,12},{12,11},... | collective-permute-start | bytes 1572872 | tf_op jit(solution)/shard_map/ppermute | solution.py:341
  4.6 5.3 %collective-permute-start.3 = (f32[1,256,256]{2,1,0:T(8,128)S(1)}, f32[1,256,256]{2,1,0:T(8,128)S(1)}, u32[]{:S(2)}, u32[]{:S(2)}) collective-permute-start(f32[1,256,256]{2,1,0:T(8,128)S(1)} %get-tuple-element.31.near_part), channel_id=1, source_target_pairs={{0,1},{1,0},{2,3},{3,2},{4,5},{5,4},{6,7},{7,6},{8,9},{9,8},{10,11... | collective-permute-start | bytes 786440 | tf_op jit(solution)/shard_map/ppermute | solution.py:353
  8.6 2.6 %collective-permute-start.1 = (f32[1,128,256]{2,1,0:T(8,128)S(1)}, f32[1,128,256]{2,1,0:T(8,128)S(1)}, u32[]{:S(2)}, u32[]{:S(2)}) collective-permute-start(f32[1,128,256]{2,1,0:T(8,128)S(1)} %get-tuple-element.29), channel_id=1, source_target_pairs={{1,2},{2,1},{3,4},{4,3},{5,6},{6,5},{9,10},{10,9},{11,12},{12,11},... | collective-permute-start | bytes 393224 | tf_op jit(solution)/shard_map/ppermute | solution.py:352
  9.2 14.9 %collective-permute-start.6 = (f32[1,384,256]{2,1,0:T(8,128)S(1)}, f32[1,384,256]{2,1,0:T(8,128)S(1)}, u32[]{:S(2)}, u32[]{:S(2)}) collective-permute-start(f32[1,384,256]{2,1,0:T(8,128)S(1)} %get-tuple-element.36), channel_id=1, source_target_pairs={{1,2},{2,1},{3,4},{4,3},{5,6},{6,5},{9,10},{10,9},{11,12},{12,11},... | collective-permute-start | bytes 1179656 | tf_op jit(solution)/shard_map/ppermute | solution.py:354
  11.2 12.9 %copy-start = (f32[1,2,256,256]{3,2,1,0:T(8,128)S(1)}, f32[1,2,256,256]{3,2,1,0:T(8,128)}, u32[]{:S(2)}) copy-start(f32[1,2,256,256]{3,2,1,0:T(8,128)} %param.10) | copy-start | bytes 1572868
  11.2 12.9 %copy-start.1 = (s32[2,256,256]{2,1,0:T(8,128)S(1)}, s32[2,256,256]{2,1,0:T(8,128)}, u32[]{:S(2)}) copy-start(s32[2,256,256]{2,1,0:T(8,128)} %mask.1) | copy-start | bytes 1572868
  11.5 10.4 %collective-permute-start.4 = (f32[5,8,128]{2,1,0:T(8,128)S(1)}, f32[5,8,128]{2,1,0:T(8,128)S(1)}, u32[]{:S(2)}, u32[]{:S(2)}) collective-permute-start(f32[5,8,128]{2,1,0:T(8,128)S(1)} %face.1), channel_id=1, source_target_pairs={{0,2},{1,3},{2,0},{3,1},{4,6},{5,7},{6,4},{7,5},{8,10},{9,11},{10,... | collective-permute-start | bytes 61448 | tf_op jit(solution)/shard_map/ppermute | solution.py:371
  21.9 2.2 %collective-permute-start.7 = (f32[1,256,256]{2,1,0:T(8,128)S(1)}, f32[1,256,256]{2,1,0:T(8,128)S(1)}, u32[]{:S(2)}, u32[]{:S(2)}) collective-permute-start(f32[1,256,256]{2,1,0:T(8,128)S(1)} %get-tuple-element.38), channel_id=1, source_target_pairs={{0,1},{1,0},{2,3},{3,2},{4,5},{5,4},{6,7},{7,6},{8,9},{9,8},{10,11... | collective-permute-start | bytes 786440 | tf_op jit(solution)/shard_map/ppermute | solution.py:373
  21.9 4.7 %collective-permute-start.5 = (f32[5,8,128]{2,1,0:T(8,128)S(1)}, f32[5,8,128]{2,1,0:T(8,128)S(1)}, u32[]{:S(2)}, u32[]{:S(2)}) collective-permute-start(f32[5,8,128]{2,1,0:T(8,128)S(1)} %add.21), channel_id=1, source_target_pairs={{0,4},{1,5},{2,6},{3,7},{4,0},{5,1},{6,2},{7,3},{8,12},{9,13},{10,... | collective-permute-start | bytes 61448 | tf_op jit(solution)/shard_map/ppermute | solution.py:292
  26.6 1.2 %collective-permute-start.8 = (f32[5,8,128]{2,1,0:T(8,128)S(1)}, f32[5,8,128]{2,1,0:T(8,128)S(1)}, u32[]{:S(2)}, u32[]{:S(2)}) collective-permute-start(f32[5,8,128]{2,1,0:T(8,128)S(1)} %add.22), channel_id=1, source_target_pairs={{0,1},{1,0},{2,3},{3,2},{4,5},{5,4},{6,7},{7,6},{8,9},{9,8},{10,11... | collective-permute-start | bytes 61448 | tf_op jit(solution)/shard_map/ppermute | solution.py:292
  28.0 5.0 %collective-permute-start.13 = (f32[2,64,256]{2,1,0:T(8,128)S(1)}, f32[2,64,256]{2,1,0:T(8,128)S(1)}, u32[]{:S(2)}, u32[]{:S(2)}) collective-permute-start(f32[2,64,256]{2,1,0:T(8,128)S(1)} %get-tuple-element.48), channel_id=1, source_target_pairs={{0,8},{1,17},{2,10},{3,19},{4,12},{5,21},{6,14},{7,23},{8,0},{9,25... | collective-permute-start | bytes 393224 | tf_op jit(solution)/shard_map/ppermute | solution.py:310
  29.6 5.1 %collective-permute-start.15 = (f32[2,64,256]{2,1,0:T(8,128)S(1)}, f32[2,64,256]{2,1,0:T(8,128)S(1)}, u32[]{:S(2)}, u32[]{:S(2)}) collective-permute-start(f32[2,64,256]{2,1,0:T(8,128)S(1)} %get-tuple-element.49), channel_id=1, source_target_pairs={{0,8},{1,17},{2,10},{3,19},{4,12},{5,21},{6,14},{7,23},{8,0},{9,25... | collective-permute-start | bytes 393224 | tf_op jit(solution)/shard_map/ppermute | solution.py:310
  30.1 6.7 %collective-permute-start.11 = (f32[2,64,256]{2,1,0:T(8,128)S(1)}, f32[2,64,256]{2,1,0:T(8,128)S(1)}, u32[]{:S(2)}, u32[]{:S(2)}) collective-permute-start(f32[2,64,256]{2,1,0:T(8,128)S(1)} %get-tuple-element.47), channel_id=1, source_target_pairs={{0,8},{1,17},{2,10},{3,19},{4,12},{5,21},{6,14},{7,23},{8,0},{9,25... | collective-permute-start | bytes 393224 | tf_op jit(solution)/shard_map/ppermute | solution.py:310
  31.6 8.0 %collective-permute-start.9 = (f32[2,64,256]{2,1,0:T(8,128)S(1)}, f32[2,64,256]{2,1,0:T(8,128)S(1)}, u32[]{:S(2)}, u32[]{:S(2)}) collective-permute-start(f32[2,64,256]{2,1,0:T(8,128)S(1)} %get-tuple-element.46), channel_id=1, source_target_pairs={{0,8},{1,17},{2,10},{3,19},{4,12},{5,21},{6,14},{7,23},{8,0},{9,25... | collective-permute-start | bytes 393224 | tf_op jit(solution)/shard_map/ppermute | solution.py:310
  33.1 9.8 %collective-permute-start.14 = (f32[2,64,256]{2,1,0:T(8,128)S(1)}, f32[2,64,256]{2,1,0:T(8,128)S(1)}, u32[]{:S(2)}, u32[]{:S(2)}) collective-permute-start(f32[2,64,256]{2,1,0:T(8,128)S(1)} %add.26.total), channel_id=1, source_target_pairs={{0,16},{1,9},{2,18},{3,11},{4,20},{5,13},{6,22},{7,15},{8,24},{9,1... | collective-permute-start | bytes 393224 | tf_op jit(solution)/shard_map/ppermute | solution.py:313
  34.7 7.5 %collective-permute-start.16 = (f32[2,64,256]{2,1,0:T(8,128)S(1)}, f32[2,64,256]{2,1,0:T(8,128)S(1)}, u32[]{:S(2)}, u32[]{:S(2)}) collective-permute-start(f32[2,64,256]{2,1,0:T(8,128)S(1)} %add.27.total), channel_id=1, source_target_pairs={{0,16},{1,9},{2,18},{3,11},{4,20},{5,13},{6,22},{7,15},{8,24},{9,1... | collective-permute-start | bytes 393224 | tf_op jit(solution)/shard_map/ppermute | solution.py:313
  36.8 6.8 %collective-permute-start.12 = (f32[2,64,256]{2,1,0:T(8,128)S(1)}, f32[2,64,256]{2,1,0:T(8,128)S(1)}, u32[]{:S(2)}, u32[]{:S(2)}) collective-permute-start(f32[2,64,256]{2,1,0:T(8,128)S(1)} %add.25.total), channel_id=1, source_target_pairs={{0,16},{1,9},{2,18},{3,11},{4,20},{5,13},{6,22},{7,15},{8,24},{9,1... | collective-permute-start | bytes 393224 | tf_op jit(solution)/shard_map/ppermute | solution.py:313
  39.6 5.0 %collective-permute-start.10 = (f32[2,64,256]{2,1,0:T(8,128)S(1)}, f32[2,64,256]{2,1,0:T(8,128)S(1)}, u32[]{:S(2)}, u32[]{:S(2)}) collective-permute-start(f32[2,64,256]{2,1,0:T(8,128)S(1)} %add.24.total), channel_id=1, source_target_pairs={{0,16},{1,9},{2,18},{3,11},{4,20},{5,13},{6,22},{7,15},{8,24},{9,1... | collective-permute-start | bytes 393224 | tf_op jit(solution)/shard_map/ppermute | solution.py:313

commit v13 on v12

--- a/solution.py
+++ b/solution.py
@@ -12,7 +12,7 @@
 VMEM = pltpu.VMEM
 SMEM = pltpu.SMEM
 SUMS = 5
-EIGHTHS = (2, 2, 2, 2)
+EIGHTHS = (4, 4)
 
 
 def params():

time: 45.5 us -> 45.4 us (level)
  waiting for transfers between devices: 9.58 us -> 15.8 us
  starting transfers between devices: 25.7 us -> 20.6 us
  Pallas kernels: 8.51 us -> 7.27 us
    ppermute x4 -> x2, waiting for transfers between devices: 2.76 us -> 6.26 us  [sum_positions(): arrived = lax.ppermute(term, ('pos', 'slab'), partners(0, positions, slabs))]
    ppermute x4 -> x2, starting transfers between devices: 6.22 us -> 3.17 us  [sum_positions(): lax.ppermute(term, ('pos', 'slab'), partners(step, positions, slabs))]
    ppermute x4 -> x2, waiting for transfers between devices: 0.38 us -> 3.13 us  [sum_positions(): lax.ppermute(term, ('pos', 'slab'), partners(step, positions, slabs))]
    ppermute x4 -> x2, starting transfers between devices: 4.12 us -> 2.09 us  [sum_positions(): arrived = lax.ppermute(term, ('pos', 'slab'), partners(0, positions, slabs))]
    pallas_call x4 -> x2, Pallas kernels: 2.72 us -> 1.48 us  [local(): pl.pallas_call(functools.partial(close_kernel, first_rows(radial)[index])...]
  transfers between devices with their start and end apart: 17 -> 13, of which waited for: 7 -> 7; matrix products, arithmetic and copies ran while one was open for 0% -> 0% of each run, Pallas kernels for 14% -> 11%
where the time goes in v13:
time: 45.4 us; the launch traced here: 45.2 us
  starting transfers between devices  20.6 us (45%)
  waiting for transfers between devices  15.8 us (35%)
  Pallas kernels  7.27 us (16%)
  between operations  1.44 us (3%)
    ppermute x1, starting transfers between devices, local(): arrived = lax.ppermute(sums, 'slab', [(i, i ^ 2) for i in range(slabs)])  6.55 us
    ppermute x2, waiting for transfers between devices, sum_positions(): arrived = lax.ppermute(term, ('pos', 'slab'), partners(0, positions, slabs))  6.26 us
    ppermute x1, starting transfers between devices, local(): near_part_in = lax.ppermute(near_part, 'slab', pairs(slabs, 0))  3.99 us
    ppermute x1, waiting for transfers between devices, local(): arrived = lax.ppermute(sums, 'slab', [(i, i ^ 2) for i in range(slabs)])  3.87 us
    ppermute x2, starting transfers between devices, sum_positions(): lax.ppermute(term, ('pos', 'slab'), partners(step, positions, slabs))  3.17 us
    ppermute x2, waiting for transfers between devices, sum_positions(): lax.ppermute(term, ('pos', 'slab'), partners(step, positions, slabs))  3.13 us
    ppermute x2, waiting for transfers between devices, gather_sums(): arrived = lax.ppermute(sums, 'slab', [(i, i ^ step) for i in range(slabs)])  2.56 us
    ppermute x2, starting transfers between devices, gather_sums(): arrived = lax.ppermute(sums, 'slab', [(i, i ^ step) for i in range(slabs)])  2.23 us
  transfers between devices with their start and end apart: 13, of which 7 were waited for; matrix products, arithmetic and copies ran while one was open for 0% of the time, Pallas kernels for 11%

profile of v13, /device:TPU:0, one launch (start us, length us, event | category | flops | bytes accessed | tf_op | source)
XLA Modules:
  0.0 45.2 jit_solution(2707140272584697218)
XLA Ops:
  1.3 1.4 %open.1 = (f32[2,256,256]{2,1,0:T(8,128)S(1)}, f32[2,256,256]{2,1,0:T(8,128)S(1)}, f32[1,256,256]{2,1,0:T(8,128)S(1)}, f32[1,256,256]{2,1,0:T(8,128)S(1)}) custom-call(f32[4]{0:T(128)} %reluctivity.1, s32[1]{0:T(128)S(6)} %copy.10.shift, s32[2,256,256]{2,1,0:T(8,128)} %labels.1, f32[2,256,256]{2,1,0:T(8,128)} %bitcast.5, f32[2,256,256]{2,1,0:T(8,128)} %bitcast.3), custom_call_target="tpu_custom_call" | custom-call | tf_op jit(solution)/shard_map/open/pallas_call | solution.py:328
  2.7 0.5 %collective-permute-start.2 = (f32[2,256,256]{2,1,0:T(8,128)S(1)}, f32[2,256,256]{2,1,0:T(8,128)S(1)}, u32[]{:S(2)}, u32[]{:S(2)}) collective-permute-start(f32[2,256,256]{2,1,0:T(8,128)S(1)} %get-tuple-element.25.near), channel_id=1, source_target_pairs={{0,1},{1,0},{2,3},{3,2},{4,5},{5,4},{6,7},{7,6},{8,9},{9,8},{10,11... | collective-permute-start | bytes 1572872 | tf_op jit(solution)/shard_map/ppermute | solution.py:342
  3.2 0.7 %collective-permute-start = (f32[2,256,256]{2,1,0:T(8,128)S(1)}, f32[2,256,256]{2,1,0:T(8,128)S(1)}, u32[]{:S(2)}, u32[]{:S(2)}) collective-permute-start(f32[2,256,256]{2,1,0:T(8,128)S(1)} %get-tuple-element.24.far), channel_id=1, source_target_pairs={{1,2},{2,1},{3,4},{4,3},{5,6},{6,5},{9,10},{10,9},{11,12},{12,11},... | collective-permute-start | bytes 1572872 | tf_op jit(solution)/shard_map/ppermute | solution.py:341
  3.9 0.7 %part.1 = (f32[1,256,256]{2,1,0:T(8,128)S(1)}, f32[1,256,256]{2,1,0:T(8,128)S(1)}, f32[1,128,256]{2,1,0:T(8,128)S(1)}, f32[1,384,256]{2,1,0:T(8,128)S(1)}) custom-call(f32[2,256,256]{2,1,0:T(8,128)S(1)} %get-tuple-element.24.far, f32[2,256,256]{2,1,0:T(8,128)S(1)} %get-tuple-element.25.near, f32[1,256,256]{2,1,0:T(8,128)S(1)} %get-tuple-element.26.far_potential), custom_call_target="tpu_custom_call" | custom-call | tf_op jit(solution)/shard_map/part/pallas_call | solution.py:344
  4.6 4.0 %collective-permute-start.3 = (f32[1,256,256]{2,1,0:T(8,128)S(1)}, f32[1,256,256]{2,1,0:T(8,128)S(1)}, u32[]{:S(2)}, u32[]{:S(2)}) collective-permute-start(f32[1,256,256]{2,1,0:T(8,128)S(1)} %get-tuple-element.29.near_part), channel_id=1, source_target_pairs={{0,1},{1,0},{2,3},{3,2},{4,5},{5,4},{6,7},{7,6},{8,9},{9,8},{10,11... | collective-permute-start | bytes 786440 | tf_op jit(solution)/shard_map/ppermute | solution.py:353
  8.6 0.7 %collective-permute-start.1 = (f32[1,128,256]{2,1,0:T(8,128)S(1)}, f32[1,128,256]{2,1,0:T(8,128)S(1)}, u32[]{:S(2)}, u32[]{:S(2)}) collective-permute-start(f32[1,128,256]{2,1,0:T(8,128)S(1)} %get-tuple-element.27), channel_id=1, source_target_pairs={{1,2},{2,1},{3,4},{4,3},{5,6},{6,5},{9,10},{10,9},{11,12},{12,11},... | collective-permute-start | bytes 393224 | tf_op jit(solution)/shard_map/ppermute | solution.py:352
  9.2 0.7 %collective-permute-start.6 = (f32[1,384,256]{2,1,0:T(8,128)S(1)}, f32[1,384,256]{2,1,0:T(8,128)S(1)}, u32[]{:S(2)}, u32[]{:S(2)}) collective-permute-start(f32[1,384,256]{2,1,0:T(8,128)S(1)} %get-tuple-element.34), channel_id=1, source_target_pairs={{1,2},{2,1},{3,4},{4,3},{5,6},{6,5},{9,10},{10,9},{11,12},{12,11},... | collective-permute-start | bytes 1179656 | tf_op jit(solution)/shard_map/ppermute | solution.py:354
  10.0 1.2 %sums.1 = (f32[2,256,256]{2,1,0:T(8,128)S(1)}, f32[1,256,256]{2,1,0:T(8,128)S(1)}, f32[8,128]{1,0:T(8,128)S(1)}) custom-call(f32[2,256,256]{2,1,0:T(8,128)S(1)} %get-tuple-element.24.far, f32[2,256,256]{2,1,0:T(8,128)S(1)} %get-tuple-element.25.near, f32[1,256,256]{2,1,0:T(8,128)S(1)} %get-tuple-element.28.far_part, ...), custom_call_target="tpu_custom_call" | custom-call | tf_op jit(solution)/shard_map/sums/pallas_call | solution.py:355
  11.5 6.6 %collective-permute-start.4 = (f32[5,8,128]{2,1,0:T(8,128)S(1)}, f32[5,8,128]{2,1,0:T(8,128)S(1)}, u32[]{:S(2)}, u32[]{:S(2)}) collective-permute-start(f32[5,8,128]{2,1,0:T(8,128)S(1)} %face.1), channel_id=1, source_target_pairs={{0,2},{1,3},{2,0},{3,1},{4,6},{5,7},{6,4},{7,5},{8,10},{9,11},{10,... | collective-permute-start | bytes 61448 | tf_op jit(solution)/shard_map/ppermute | solution.py:371
  18.0 3.9 %collective-permute-done.4 = f32[5,8,128]{2,1,0:T(8,128)S(1)} collective-permute-done((f32[5,8,128]{2,1,0:T(8,128)S(1)}, f32[5,8,128]{2,1,0:T(8,128)S(1)}, u32[]{:S(2)}, u32[]{:S(2)}) %collective-permute-start.4) | collective-permute-done | bytes 20512 | tf_op jit(solution)/shard_map/ppermute | solution.py:371
  21.9 2.2 %collective-permute-start.5 = (f32[5,8,128]{2,1,0:T(8,128)S(1)}, f32[5,8,128]{2,1,0:T(8,128)S(1)}, u32[]{:S(2)}, u32[]{:S(2)}) collective-permute-start(f32[5,8,128]{2,1,0:T(8,128)S(1)} %add.15), channel_id=1, source_target_pairs={{0,4},{1,5},{2,6},{3,7},{4,0},{5,1},{6,2},{7,3},{8,12},{9,13},{10,... | collective-permute-start | bytes 61448 | tf_op jit(solution)/shard_map/ppermute | solution.py:292
  24.1 1.1 %fields.1 = (f32[2,256,256]{2,1,0:T(8,128)S(1)}, f32[2,256,256]{2,1,0:T(8,128)S(1)}, f32[2,256,256]{2,1,0:T(8,128)S(1)}) custom-call(f32[2,256,256]{2,1,0:T(8,128)S(1)} %get-tuple-element.24.far, f32[2,256,256]{2,1,0:T(8,128)S(1)} %get-tuple-element.25.near, f32[2,256,256]{2,1,0:T(8,128)S(1)} %collective-permute-done.far_in, ...), custom_call_target="tpu_custom_call" | custom-call | tf_op jit(solution)/shard_map/fields/pallas_call | solution.py:375
  25.3 1.4 %collective-permute-done.5 = f32[5,8,128]{2,1,0:T(8,128)S(1)} collective-permute-done((f32[5,8,128]{2,1,0:T(8,128)S(1)}, f32[5,8,128]{2,1,0:T(8,128)S(1)}, u32[]{:S(2)}, u32[]{:S(2)}) %collective-permute-start.5) | collective-permute-done | bytes 20512 | tf_op jit(solution)/shard_map/ppermute | solution.py:292
  26.6 1.2 %collective-permute-done.8 = f32[5,8,128]{2,1,0:T(8,128)S(1)} collective-permute-done((f32[5,8,128]{2,1,0:T(8,128)S(1)}, f32[5,8,128]{2,1,0:T(8,128)S(1)}, u32[]{:S(2)}, u32[]{:S(2)}) %collective-permute-start.8) | collective-permute-done | bytes 20512 | tf_op jit(solution)/shard_map/ppermute | solution.py:292
  28.0 1.6 %collective-permute-start.11 = (f32[2,128,256]{2,1,0:T(8,128)S(1)}, f32[2,128,256]{2,1,0:T(8,128)S(1)}, u32[]{:S(2)}, u32[]{:S(2)}) collective-permute-start(f32[2,128,256]{2,1,0:T(8,128)S(1)} %get-tuple-element.45), channel_id=1, source_target_pairs={{0,8},{1,17},{2,10},{3,19},{4,12},{5,21},{6,14},{7,23},{8,0},{9,25... | collective-permute-start | bytes 786440 | tf_op jit(solution)/shard_map/ppermute | solution.py:310
  29.6 0.5 %collective-permute-start.9 = (f32[2,128,256]{2,1,0:T(8,128)S(1)}, f32[2,128,256]{2,1,0:T(8,128)S(1)}, u32[]{:S(2)}, u32[]{:S(2)}) collective-permute-start(f32[2,128,256]{2,1,0:T(8,128)S(1)} %get-tuple-element.44), channel_id=1, source_target_pairs={{0,8},{1,17},{2,10},{3,19},{4,12},{5,21},{6,14},{7,23},{8,0},{9,25... | collective-permute-start | bytes 786440 | tf_op jit(solution)/shard_map/ppermute | solution.py:310
  30.1 4.3 %collective-permute-done.11 = f32[2,128,256]{2,1,0:T(8,128)S(1)} collective-permute-done((f32[2,128,256]{2,1,0:T(8,128)S(1)}, f32[2,128,256]{2,1,0:T(8,128)S(1)}, u32[]{:S(2)}, u32[]{:S(2)}) %collective-permute-start.11) | collective-permute-done | bytes 262176 | tf_op jit(solution)/shard_map/ppermute | solution.py:310
  34.5 1.6 %collective-permute-start.12 = (f32[2,128,256]{2,1,0:T(8,128)S(1)}, f32[2,128,256]{2,1,0:T(8,128)S(1)}, u32[]{:S(2)}, u32[]{:S(2)}) collective-permute-start(f32[2,128,256]{2,1,0:T(8,128)S(1)} %add.19.total), channel_id=1, source_target_pairs={{0,16},{1,9},{2,18},{3,11},{4,20},{5,13},{6,22},{7,15},{8,24},{9,1... | collective-permute-start | bytes 786440 | tf_op jit(solution)/shard_map/ppermute | solution.py:313
  36.1 1.9 %collective-permute-done.9 = f32[2,128,256]{2,1,0:T(8,128)S(1)} collective-permute-done((f32[2,128,256]{2,1,0:T(8,128)S(1)}, f32[2,128,256]{2,1,0:T(8,128)S(1)}, u32[]{:S(2)}, u32[]{:S(2)}) %collective-permute-start.9) | collective-permute-done | bytes 262176 | tf_op jit(solution)/shard_map/ppermute | solution.py:310
  38.0 1.6 %collective-permute-start.10 = (f32[2,128,256]{2,1,0:T(8,128)S(1)}, f32[2,128,256]{2,1,0:T(8,128)S(1)}, u32[]{:S(2)}, u32[]{:S(2)}) collective-permute-start(f32[2,128,256]{2,1,0:T(8,128)S(1)} %add.18.total), channel_id=1, source_target_pairs={{0,16},{1,9},{2,18},{3,11},{4,20},{5,13},{6,22},{7,15},{8,24},{9,1... | collective-permute-start | bytes 786440 | tf_op jit(solution)/shard_map/ppermute | solution.py:313
  39.6 1.0 %adjoint.1 = f32[2,256,256]{2,1,0:T(8,128)} custom-call(f32[5,8,128]{2,1,0:T(8,128)S(1)} %add.17.sums, f32[2,256,256]{2,1,0:T(8,128)S(1)} %get-tuple-element.24.far, f32[2,256,256]{2,1,0:T(8,128)S(1)} %get-tuple-element.25.near, f32[2,256,256]{2,1,0:T(8,128)S(1)} %get-tuple-element.30.image), custom_call_target="tpu_custom_call" | custom-call | tf_op jit(solution)/shard_map/adjoint/pallas_call | solution.py:393
  40.9 0.7 %close.2.rest_0_ = f32[2,256,256]{2,1,0:T(8,128)} custom-call(f32[2,128,256]{2,1,0:T(8,128)S(1)} %add.19.total, f32[2,128,256]{2,1,0:T(8,128)S(1)} %collective-permute-done.12.arrived), custom_call_target="tpu_custom_call" | custom-call | tf_op jit(solution)/shard_map/close/pallas_call | solution.py:405
  41.7 2.8 %collective-permute-done.10.arrived = f32[2,128,256]{2,1,0:T(8,128)S(1)} collective-permute-done((f32[2,128,256]{2,1,0:T(8,128)S(1)}, f32[2,128,256]{2,1,0:T(8,128)S(1)}, u32[]{:S(2)}, u32[]{:S(2)}) %collective-permute-start.10) | collective-permute-done | bytes 262176 | tf_op jit(solution)/shard_map/ppermute | solution.py:313
  44.5 0.7 %close.3 = f32[2,256,256]{2,1,0:T(8,128)} custom-call(f32[2,128,256]{2,1,0:T(8,128)S(1)} %add.18.total, f32[2,128,256]{2,1,0:T(8,128)S(1)} %collective-permute-done.10.arrived, f32[2,256,256]{2,1,0:T(8,128)} %close.2.rest_0_), custom_call_target="tpu_custom_call", output_to_operand_aliasing={{}: (2, {})} | custom-call | tf_op jit(solution)/shard_map/close/pallas_call | solution.py:405
  (20 shorter events, 0.9 us)
Async XLA Ops:
  2.7 7.2 %collective-permute-start.2 = (f32[2,256,256]{2,1,0:T(8,128)S(1)}, f32[2,256,256]{2,1,0:T(8,128)S(1)}, u32[]{:S(2)}, u32[]{:S(2)}) collective-permute-start(f32[2,256,256]{2,1,0:T(8,128)S(1)} %get-tuple-element.25.near), channel_id=1, source_target_pairs={{0,1},{1,0},{2,3},{3,2},{4,5},{5,4},{6,7},{7,6},{8,9},{9,8},{10,11... | collective-permute-start | bytes 1572872 | tf_op jit(solution)/shard_map/ppermute | solution.py:342
  3.2 6.7 %collective-permute-start = (f32[2,256,256]{2,1,0:T(8,128)S(1)}, f32[2,256,256]{2,1,0:T(8,128)S(1)}, u32[]{:S(2)}, u32[]{:S(2)}) collective-permute-start(f32[2,256,256]{2,1,0:T(8,128)S(1)} %get-tuple-element.24.far), channel_id=1, source_target_pairs={{1,2},{2,1},{3,4},{4,3},{5,6},{6,5},{9,10},{10,9},{11,12},{12,11},... | collective-permute-start | bytes 1572872 | tf_op jit(solution)/shard_map/ppermute | solution.py:341
  4.6 5.3 %collective-permute-start.3 = (f32[1,256,256]{2,1,0:T(8,128)S(1)}, f32[1,256,256]{2,1,0:T(8,128)S(1)}, u32[]{:S(2)}, u32[]{:S(2)}) collective-permute-start(f32[1,256,256]{2,1,0:T(8,128)S(1)} %get-tuple-element.29.near_part), channel_id=1, source_target_pairs={{0,1},{1,0},{2,3},{3,2},{4,5},{5,4},{6,7},{7,6},{8,9},{9,8},{10,11... | collective-permute-start | bytes 786440 | tf_op jit(solution)/shard_map/ppermute | solution.py:353
  8.6 2.6 %collective-permute-start.1 = (f32[1,128,256]{2,1,0:T(8,128)S(1)}, f32[1,128,256]{2,1,0:T(8,128)S(1)}, u32[]{:S(2)}, u32[]{:S(2)}) collective-permute-start(f32[1,128,256]{2,1,0:T(8,128)S(1)} %get-tuple-element.27), channel_id=1, source_target_pairs={{1,2},{2,1},{3,4},{4,3},{5,6},{6,5},{9,10},{10,9},{11,12},{12,11},... | collective-permute-start | bytes 393224 | tf_op jit(solution)/shard_map/ppermute | solution.py:352
  9.2 14.9 %collective-permute-start.6 = (f32[1,384,256]{2,1,0:T(8,128)S(1)}, f32[1,384,256]{2,1,0:T(8,128)S(1)}, u32[]{:S(2)}, u32[]{:S(2)}) collective-permute-start(f32[1,384,256]{2,1,0:T(8,128)S(1)} %get-tuple-element.34), channel_id=1, source_target_pairs={{1,2},{2,1},{3,4},{4,3},{5,6},{6,5},{9,10},{10,9},{11,12},{12,11},... | collective-permute-start | bytes 1179656 | tf_op jit(solution)/shard_map/ppermute | solution.py:354
  11.2 12.9 %copy-start = (f32[1,2,256,256]{3,2,1,0:T(8,128)S(1)}, f32[1,2,256,256]{3,2,1,0:T(8,128)}, u32[]{:S(2)}) copy-start(f32[1,2,256,256]{3,2,1,0:T(8,128)} %param.10) | copy-start | bytes 1572868
  11.2 12.9 %copy-start.1 = (s32[2,256,256]{2,1,0:T(8,128)S(1)}, s32[2,256,256]{2,1,0:T(8,128)}, u32[]{:S(2)}) copy-start(s32[2,256,256]{2,1,0:T(8,128)} %mask.1) | copy-start | bytes 1572868
  11.5 10.4 %collective-permute-start.4 = (f32[5,8,128]{2,1,0:T(8,128)S(1)}, f32[5,8,128]{2,1,0:T(8,128)S(1)}, u32[]{:S(2)}, u32[]{:S(2)}) collective-permute-start(f32[5,8,128]{2,1,0:T(8,128)S(1)} %face.1), channel_id=1, source_target_pairs={{0,2},{1,3},{2,0},{3,1},{4,6},{5,7},{6,4},{7,5},{8,10},{9,11},{10,... | collective-permute-start | bytes 61448 | tf_op jit(solution)/shard_map/ppermute | solution.py:371
  21.9 2.2 %collective-permute-start.7 = (f32[1,256,256]{2,1,0:T(8,128)S(1)}, f32[1,256,256]{2,1,0:T(8,128)S(1)}, u32[]{:S(2)}, u32[]{:S(2)}) collective-permute-start(f32[1,256,256]{2,1,0:T(8,128)S(1)} %get-tuple-element.36), channel_id=1, source_target_pairs={{0,1},{1,0},{2,3},{3,2},{4,5},{5,4},{6,7},{7,6},{8,9},{9,8},{10,11... | collective-permute-start | bytes 786440 | tf_op jit(solution)/shard_map/ppermute | solution.py:373
  21.9 4.7 %collective-permute-start.5 = (f32[5,8,128]{2,1,0:T(8,128)S(1)}, f32[5,8,128]{2,1,0:T(8,128)S(1)}, u32[]{:S(2)}, u32[]{:S(2)}) collective-permute-start(f32[5,8,128]{2,1,0:T(8,128)S(1)} %add.15), channel_id=1, source_target_pairs={{0,4},{1,5},{2,6},{3,7},{4,0},{5,1},{6,2},{7,3},{8,12},{9,13},{10,... | collective-permute-start | bytes 61448 | tf_op jit(solution)/shard_map/ppermute | solution.py:292
  26.6 1.2 %collective-permute-start.8 = (f32[5,8,128]{2,1,0:T(8,128)S(1)}, f32[5,8,128]{2,1,0:T(8,128)S(1)}, u32[]{:S(2)}, u32[]{:S(2)}) collective-permute-start(f32[5,8,128]{2,1,0:T(8,128)S(1)} %add.16), channel_id=1, source_target_pairs={{0,1},{1,0},{2,3},{3,2},{4,5},{5,4},{6,7},{7,6},{8,9},{9,8},{10,11... | collective-permute-start | bytes 61448 | tf_op jit(solution)/shard_map/ppermute | solution.py:292
  28.0 6.4 %collective-permute-start.11 = (f32[2,128,256]{2,1,0:T(8,128)S(1)}, f32[2,128,256]{2,1,0:T(8,128)S(1)}, u32[]{:S(2)}, u32[]{:S(2)}) collective-permute-start(f32[2,128,256]{2,1,0:T(8,128)S(1)} %get-tuple-element.45), channel_id=1, source_target_pairs={{0,8},{1,17},{2,10},{3,19},{4,12},{5,21},{6,14},{7,23},{8,0},{9,25... | collective-permute-start | bytes 786440 | tf_op jit(solution)/shard_map/ppermute | solution.py:310
  29.6 8.4 %collective-permute-start.9 = (f32[2,128,256]{2,1,0:T(8,128)S(1)}, f32[2,128,256]{2,1,0:T(8,128)S(1)}, u32[]{:S(2)}, u32[]{:S(2)}) collective-permute-start(f32[2,128,256]{2,1,0:T(8,128)S(1)} %get-tuple-element.44), channel_id=1, source_target_pairs={{0,8},{1,17},{2,10},{3,19},{4,12},{5,21},{6,14},{7,23},{8,0},{9,25... | collective-permute-start | bytes 786440 | tf_op jit(solution)/shard_map/ppermute | solution.py:310
  34.5 6.4 %collective-permute-start.12 = (f32[2,128,256]{2,1,0:T(8,128)S(1)}, f32[2,128,256]{2,1,0:T(8,128)S(1)}, u32[]{:S(2)}, u32[]{:S(2)}) collective-permute-start(f32[2,128,256]{2,1,0:T(8,128)S(1)} %add.19.total), channel_id=1, source_target_pairs={{0,16},{1,9},{2,18},{3,11},{4,20},{5,13},{6,22},{7,15},{8,24},{9,1... | collective-permute-start | bytes 786440 | tf_op jit(solution)/shard_map/ppermute | solution.py:313
  38.0 6.4 %collective-permute-start.10 = (f32[2,128,256]{2,1,0:T(8,128)S(1)}, f32[2,128,256]{2,1,0:T(8,128)S(1)}, u32[]{:S(2)}, u32[]{:S(2)}) collective-permute-start(f32[2,128,256]{2,1,0:T(8,128)S(1)} %add.18.total), channel_id=1, source_target_pairs={{0,16},{1,9},{2,18},{3,11},{4,20},{5,13},{6,22},{7,15},{8,24},{9,1... | collective-permute-start | bytes 786440 | tf_op jit(solution)/shard_map/ppermute | solution.py:313

commit v14 on v9

--- a/solution.py
+++ b/solution.py
@@ -287,7 +287,7 @@
 
 
 def gather_sums(sums, fields, slabs):
-    steps = [2**k for k in range(2, slabs.bit_length() - 1)] + [1]
+    steps = [2**k for k in range(1, slabs.bit_length() - 2)] + [1]
     for step in steps:
         arrived = lax.ppermute(sums, "slab", [(i, i ^ step) for i in range(slabs)])
         if step == steps[-2]:
@@ -368,7 +368,7 @@
         compiler_params=params(),
         name="face",
     )(far, far_in, far_early_in, image, own_sums)
-    arrived = lax.ppermute(sums, "slab", [(i, i ^ 2) for i in range(slabs)])
+    arrived = lax.ppermute(sums, "slab", [(i, i ^ (slabs // 2)) for i in range(slabs)])
     near_potential, arrived = lax.optimization_barrier((near_potential, arrived))
     near_potential = lax.ppermute(near_potential, "slab", pairs(slabs, 0))
     sums = sums + arrived

time: 44.6 us -> 45 us (level)
  waiting for transfers between devices: 11.3 us -> 11.9 us
    ppermute x2, starting transfers between devices: 2.23 us -> 1 us  [gather_sums(): arrived = lax.ppermute(sums, 'slab', [(i, i ^ step) for i in range(slabs)])]
    ppermute x1, starting transfers between devices: 6.55 us -> 7.57 us  [local(): lax.ppermute(sums, 'slab', [(i, i ^ slabs // 2) for i in range(slabs)])]
    ppermute x1, waiting for transfers between devices: 0.01 us -> 0.52 us  [local(): near_potential = lax.ppermute(near_potential, 'slab', pairs(slabs, 0))]
  transfers between devices with their start and end apart: 15 -> 15, of which waited for: 7 -> 8; matrix products, arithmetic and copies ran while one was open for 0% -> 0% of each run, Pallas kernels for 13% -> 13%
where the time goes in v14:
time: 45 us; the launch traced here: 44.8 us
  starting transfers between devices  23.4 us (52%)
  waiting for transfers between devices  11.9 us (26%)
  Pallas kernels  7.88 us (18%)
  between operations  1.46 us (3%)
    ppermute x1, starting transfers between devices, local(): lax.ppermute(sums, 'slab', [(i, i ^ slabs // 2) for i in range(slabs)])  7.57 us
    ppermute x3, starting transfers between devices, sum_positions(): lax.ppermute(term, ('pos', 'slab'), partners(step, positions, slabs))  4.75 us
    ppermute x1, waiting for transfers between devices, local(): lax.ppermute(sums, 'slab', [(i, i ^ slabs // 2) for i in range(slabs)])  4.09 us
    ppermute x1, starting transfers between devices, local(): near_part_in = lax.ppermute(near_part, 'slab', pairs(slabs, 0))  3.99 us
    ppermute x3, waiting for transfers between devices, sum_positions(): arrived = lax.ppermute(term, ('pos', 'slab'), partners(0, positions, slabs))  3.88 us
    ppermute x3, starting transfers between devices, sum_positions(): arrived = lax.ppermute(term, ('pos', 'slab'), partners(0, positions, slabs))  3.58 us
    ppermute x2, waiting for transfers between devices, gather_sums(): arrived = lax.ppermute(sums, 'slab', [(i, i ^ step) for i in range(slabs)])  2.38 us
    pallas_call x3, Pallas kernels, local(): pl.pallas_call(functools.partial(close_kernel, first_rows(radial)[index])...  2.09 us
  transfers between devices with their start and end apart: 15, of which 8 were waited for; matrix products, arithmetic and copies ran while one was open for 0% of the time, Pallas kernels for 13%

profile of v14, /device:TPU:0, one launch (start us, length us, event | category | flops | bytes accessed | tf_op | source)
XLA Modules:
  0.0 44.8 jit_solution(5320213977587202633)
XLA Ops:
  1.3 1.4 %open.1 = (f32[2,256,256]{2,1,0:T(8,128)S(1)}, f32[2,256,256]{2,1,0:T(8,128)S(1)}, f32[1,256,256]{2,1,0:T(8,128)S(1)}, f32[1,256,256]{2,1,0:T(8,128)S(1)}) custom-call(f32[4]{0:T(128)} %reluctivity.1, s32[1]{0:T(128)S(6)} %copy.12.shift, s32[2,256,256]{2,1,0:T(8,128)} %labels.1, f32[2,256,256]{2,1,0:T(8,128)} %bitcast.5, f32[2,256,256]{2,1,0:T(8,128)} %bitcast.3), custom_call_target="tpu_custom_call" | custom-call | tf_op jit(solution)/shard_map/open/pallas_call | solution.py:328
  3.2 0.7 %collective-permute-start = (f32[2,256,256]{2,1,0:T(8,128)S(1)}, f32[2,256,256]{2,1,0:T(8,128)S(1)}, u32[]{:S(2)}, u32[]{:S(2)}) collective-permute-start(f32[2,256,256]{2,1,0:T(8,128)S(1)} %get-tuple-element.25.far), channel_id=1, source_target_pairs={{1,2},{2,1},{3,4},{4,3},{5,6},{6,5},{9,10},{10,9},{11,12},{12,11},... | collective-permute-start | bytes 1572872 | tf_op jit(solution)/shard_map/ppermute | solution.py:341
  3.9 0.7 %part.1 = (f32[1,256,256]{2,1,0:T(8,128)S(1)}, f32[1,256,256]{2,1,0:T(8,128)S(1)}, f32[1,128,256]{2,1,0:T(8,128)S(1)}, f32[1,384,256]{2,1,0:T(8,128)S(1)}) custom-call(f32[2,256,256]{2,1,0:T(8,128)S(1)} %get-tuple-element.25.far, f32[2,256,256]{2,1,0:T(8,128)S(1)} %get-tuple-element.26.near, f32[1,256,256]{2,1,0:T(8,128)S(1)} %get-tuple-element.27.far_potential), custom_call_target="tpu_custom_call" | custom-call | tf_op jit(solution)/shard_map/part/pallas_call | solution.py:344
  4.6 4.0 %collective-permute-start.3 = (f32[1,256,256]{2,1,0:T(8,128)S(1)}, f32[1,256,256]{2,1,0:T(8,128)S(1)}, u32[]{:S(2)}, u32[]{:S(2)}) collective-permute-start(f32[1,256,256]{2,1,0:T(8,128)S(1)} %get-tuple-element.30.near_part), channel_id=1, source_target_pairs={{0,1},{1,0},{2,3},{3,2},{4,5},{5,4},{6,7},{7,6},{8,9},{9,8},{10,11... | collective-permute-start | bytes 786440 | tf_op jit(solution)/shard_map/ppermute | solution.py:353
  9.2 0.7 %collective-permute-start.6 = (f32[1,384,256]{2,1,0:T(8,128)S(1)}, f32[1,384,256]{2,1,0:T(8,128)S(1)}, u32[]{:S(2)}, u32[]{:S(2)}) collective-permute-start(f32[1,384,256]{2,1,0:T(8,128)S(1)} %get-tuple-element.35), channel_id=1, source_target_pairs={{1,2},{2,1},{3,4},{4,3},{5,6},{6,5},{9,10},{10,9},{11,12},{12,11},... | collective-permute-start | bytes 1179656 | tf_op jit(solution)/shard_map/ppermute | solution.py:354
  10.0 1.2 %sums.1 = (f32[2,256,256]{2,1,0:T(8,128)S(1)}, f32[1,256,256]{2,1,0:T(8,128)S(1)}, f32[8,128]{1,0:T(8,128)S(1)}) custom-call(f32[2,256,256]{2,1,0:T(8,128)S(1)} %get-tuple-element.25.far, f32[2,256,256]{2,1,0:T(8,128)S(1)} %get-tuple-element.26.near, f32[1,256,256]{2,1,0:T(8,128)S(1)} %get-tuple-element.29.far_part, ...), custom_call_target="tpu_custom_call" | custom-call | tf_op jit(solution)/shard_map/sums/pallas_call | solution.py:355
  11.5 7.6 %collective-permute-start.4 = (f32[5,8,128]{2,1,0:T(8,128)S(1)}, f32[5,8,128]{2,1,0:T(8,128)S(1)}, u32[]{:S(2)}, u32[]{:S(2)}) collective-permute-start(f32[5,8,128]{2,1,0:T(8,128)S(1)} %face.1), channel_id=1, source_target_pairs={{0,4},{1,5},{2,6},{3,7},{4,0},{5,1},{6,2},{7,3},{8,12},{9,13},{10,... | collective-permute-start | bytes 61448 | tf_op jit(solution)/shard_map/ppermute | solution.py:371
  19.0 4.1 %collective-permute-done.4 = f32[5,8,128]{2,1,0:T(8,128)S(1)} collective-permute-done((f32[5,8,128]{2,1,0:T(8,128)S(1)}, f32[5,8,128]{2,1,0:T(8,128)S(1)}, u32[]{:S(2)}, u32[]{:S(2)}) %collective-permute-start.4) | collective-permute-done | bytes 20512 | tf_op jit(solution)/shard_map/ppermute | solution.py:371
  23.1 1.0 %collective-permute-start.5 = (f32[5,8,128]{2,1,0:T(8,128)S(1)}, f32[5,8,128]{2,1,0:T(8,128)S(1)}, u32[]{:S(2)}, u32[]{:S(2)}) collective-permute-start(f32[5,8,128]{2,1,0:T(8,128)S(1)} %add.18), channel_id=1, source_target_pairs={{0,2},{1,3},{2,0},{3,1},{4,6},{5,7},{6,4},{7,5},{8,10},{9,11},{10,... | collective-permute-start | bytes 61448 | tf_op jit(solution)/shard_map/ppermute | solution.py:292
  24.6 1.1 %fields.1 = (f32[2,256,256]{2,1,0:T(8,128)S(1)}, f32[2,256,256]{2,1,0:T(8,128)S(1)}, f32[2,256,256]{2,1,0:T(8,128)S(1)}) custom-call(f32[2,256,256]{2,1,0:T(8,128)S(1)} %get-tuple-element.25.far, f32[2,256,256]{2,1,0:T(8,128)S(1)} %get-tuple-element.26.near, f32[2,256,256]{2,1,0:T(8,128)S(1)} %collective-permute-done.far_in, ...), custom_call_target="tpu_custom_call" | custom-call | tf_op jit(solution)/shard_map/fields/pallas_call | solution.py:375
  25.8 1.2 %collective-permute-done.5 = f32[5,8,128]{2,1,0:T(8,128)S(1)} collective-permute-done((f32[5,8,128]{2,1,0:T(8,128)S(1)}, f32[5,8,128]{2,1,0:T(8,128)S(1)}, u32[]{:S(2)}, u32[]{:S(2)}) %collective-permute-start.5) | collective-permute-done | bytes 20512 | tf_op jit(solution)/shard_map/ppermute | solution.py:292
  27.0 1.2 %collective-permute-done.8 = f32[5,8,128]{2,1,0:T(8,128)S(1)} collective-permute-done((f32[5,8,128]{2,1,0:T(8,128)S(1)}, f32[5,8,128]{2,1,0:T(8,128)S(1)}, u32[]{:S(2)}, u32[]{:S(2)}) %collective-permute-start.8) | collective-permute-done | bytes 20512 | tf_op jit(solution)/shard_map/ppermute | solution.py:292
  28.4 1.6 %collective-permute-start.13 = (f32[2,96,256]{2,1,0:T(8,128)S(1)}, f32[2,96,256]{2,1,0:T(8,128)S(1)}, u32[]{:S(2)}, u32[]{:S(2)}) collective-permute-start(f32[2,96,256]{2,1,0:T(8,128)S(1)} %get-tuple-element.47), channel_id=1, source_target_pairs={{0,8},{1,17},{2,10},{3,19},{4,12},{5,21},{6,14},{7,23},{8,0},{9,25... | collective-permute-start | bytes 589832 | tf_op jit(solution)/shard_map/ppermute | solution.py:310
  30.4 1.5 %collective-permute-start.9 = (f32[2,64,256]{2,1,0:T(8,128)S(1)}, f32[2,64,256]{2,1,0:T(8,128)S(1)}, u32[]{:S(2)}, u32[]{:S(2)}) collective-permute-start(f32[2,64,256]{2,1,0:T(8,128)S(1)} %get-tuple-element.45), channel_id=1, source_target_pairs={{0,8},{1,17},{2,10},{3,19},{4,12},{5,21},{6,14},{7,23},{8,0},{9,25... | collective-permute-start | bytes 393224 | tf_op jit(solution)/shard_map/ppermute | solution.py:310
  31.9 2.2 %collective-permute-done.13 = f32[2,96,256]{2,1,0:T(8,128)S(1)} collective-permute-done((f32[2,96,256]{2,1,0:T(8,128)S(1)}, f32[2,96,256]{2,1,0:T(8,128)S(1)}, u32[]{:S(2)}, u32[]{:S(2)}) %collective-permute-start.13) | collective-permute-done | bytes 196640 | tf_op jit(solution)/shard_map/ppermute | solution.py:310
  34.1 1.6 %collective-permute-start.14 = (f32[2,96,256]{2,1,0:T(8,128)S(1)}, f32[2,96,256]{2,1,0:T(8,128)S(1)}, u32[]{:S(2)}, u32[]{:S(2)}) collective-permute-start(f32[2,96,256]{2,1,0:T(8,128)S(1)} %add.23.total), channel_id=1, source_target_pairs={{0,16},{1,9},{2,18},{3,11},{4,20},{5,13},{6,22},{7,15},{8,24},{9,1... | collective-permute-start | bytes 589832 | tf_op jit(solution)/shard_map/ppermute | solution.py:313
  36.3 1.6 %collective-permute-start.12 = (f32[2,96,256]{2,1,0:T(8,128)S(1)}, f32[2,96,256]{2,1,0:T(8,128)S(1)}, u32[]{:S(2)}, u32[]{:S(2)}) collective-permute-start(f32[2,96,256]{2,1,0:T(8,128)S(1)} %add.22.total), channel_id=1, source_target_pairs={{0,16},{1,9},{2,18},{3,11},{4,20},{5,13},{6,22},{7,15},{8,24},{9,1... | collective-permute-start | bytes 589832 | tf_op jit(solution)/shard_map/ppermute | solution.py:313
  37.8 1.2 %collective-permute-done.9 = f32[2,64,256]{2,1,0:T(8,128)S(1)} collective-permute-done((f32[2,64,256]{2,1,0:T(8,128)S(1)}, f32[2,64,256]{2,1,0:T(8,128)S(1)}, u32[]{:S(2)}, u32[]{:S(2)}) %collective-permute-start.9) | collective-permute-done | bytes 131104 | tf_op jit(solution)/shard_map/ppermute | solution.py:310
  39.1 1.6 %collective-permute-start.10 = (f32[2,64,256]{2,1,0:T(8,128)S(1)}, f32[2,64,256]{2,1,0:T(8,128)S(1)}, u32[]{:S(2)}, u32[]{:S(2)}) collective-permute-start(f32[2,64,256]{2,1,0:T(8,128)S(1)} %add.21.total), channel_id=1, source_target_pairs={{0,16},{1,9},{2,18},{3,11},{4,20},{5,13},{6,22},{7,15},{8,24},{9,1... | collective-permute-start | bytes 393224 | tf_op jit(solution)/shard_map/ppermute | solution.py:313
  40.6 1.0 %adjoint.1 = f32[2,256,256]{2,1,0:T(8,128)} custom-call(f32[5,8,128]{2,1,0:T(8,128)S(1)} %add.20.sums, f32[2,256,256]{2,1,0:T(8,128)S(1)} %get-tuple-element.25.far, f32[2,256,256]{2,1,0:T(8,128)S(1)} %get-tuple-element.26.near, f32[2,256,256]{2,1,0:T(8,128)S(1)} %get-tuple-element.31.image), custom_call_target="tpu_custom_call" | custom-call | tf_op jit(solution)/shard_map/adjoint/pallas_call | solution.py:393
  41.6 0.7 %close.3.rest_0_ = f32[2,256,256]{2,1,0:T(8,128)} custom-call(f32[2,96,256]{2,1,0:T(8,128)S(1)} %add.23.total, f32[2,96,256]{2,1,0:T(8,128)S(1)} %collective-permute-done.14.arrived), custom_call_target="tpu_custom_call" | custom-call | tf_op jit(solution)/shard_map/close/pallas_call | solution.py:405
  42.4 0.7 %close.4.rest_0_ = f32[2,256,256]{2,1,0:T(8,128)} custom-call(f32[2,96,256]{2,1,0:T(8,128)S(1)} %add.22.total, f32[2,96,256]{2,1,0:T(8,128)S(1)} %collective-permute-done.12.arrived, f32[2,256,256]{2,1,0:T(8,128)} %close.3.rest_0_), custom_call_target="tpu_custom_call", output_to_operand_aliasing={{}: (2, {})} | custom-call | tf_op jit(solution)/shard_map/close/pallas_call | solution.py:405
  43.1 1.0 %collective-permute-done.10.arrived = f32[2,64,256]{2,1,0:T(8,128)S(1)} collective-permute-done((f32[2,64,256]{2,1,0:T(8,128)S(1)}, f32[2,64,256]{2,1,0:T(8,128)S(1)}, u32[]{:S(2)}, u32[]{:S(2)}) %collective-permute-start.10) | collective-permute-done | bytes 131104 | tf_op jit(solution)/shard_map/ppermute | solution.py:313
  44.1 0.7 %close.5 = f32[2,256,256]{2,1,0:T(8,128)} custom-call(f32[2,64,256]{2,1,0:T(8,128)S(1)} %add.21.total, f32[2,64,256]{2,1,0:T(8,128)S(1)} %collective-permute-done.10.arrived, f32[2,256,256]{2,1,0:T(8,128)} %close.4.rest_0_), custom_call_target="tpu_custom_call", output_to_operand_aliasing={{}: (2, {})} | custom-call | tf_op jit(solution)/shard_map/close/pallas_call | solution.py:405
  (26 shorter events, 3.3 us)
Async XLA Ops:
  2.7 7.2 %collective-permute-start.2 = (f32[2,256,256]{2,1,0:T(8,128)S(1)}, f32[2,256,256]{2,1,0:T(8,128)S(1)}, u32[]{:S(2)}, u32[]{:S(2)}) collective-permute-start(f32[2,256,256]{2,1,0:T(8,128)S(1)} %get-tuple-element.26.near), channel_id=1, source_target_pairs={{0,1},{1,0},{2,3},{3,2},{4,5},{5,4},{6,7},{7,6},{8,9},{9,8},{10,11... | collective-permute-start | bytes 1572872 | tf_op jit(solution)/shard_map/ppermute | solution.py:342
  3.2 6.7 %collective-permute-start = (f32[2,256,256]{2,1,0:T(8,128)S(1)}, f32[2,256,256]{2,1,0:T(8,128)S(1)}, u32[]{:S(2)}, u32[]{:S(2)}) collective-permute-start(f32[2,256,256]{2,1,0:T(8,128)S(1)} %get-tuple-element.25.far), channel_id=1, source_target_pairs={{1,2},{2,1},{3,4},{4,3},{5,6},{6,5},{9,10},{10,9},{11,12},{12,11},... | collective-permute-start | bytes 1572872 | tf_op jit(solution)/shard_map/ppermute | solution.py:341
  4.6 5.3 %collective-permute-start.3 = (f32[1,256,256]{2,1,0:T(8,128)S(1)}, f32[1,256,256]{2,1,0:T(8,128)S(1)}, u32[]{:S(2)}, u32[]{:S(2)}) collective-permute-start(f32[1,256,256]{2,1,0:T(8,128)S(1)} %get-tuple-element.30.near_part), channel_id=1, source_target_pairs={{0,1},{1,0},{2,3},{3,2},{4,5},{5,4},{6,7},{7,6},{8,9},{9,8},{10,11... | collective-permute-start | bytes 786440 | tf_op jit(solution)/shard_map/ppermute | solution.py:353
  8.6 2.6 %collective-permute-start.1 = (f32[1,128,256]{2,1,0:T(8,128)S(1)}, f32[1,128,256]{2,1,0:T(8,128)S(1)}, u32[]{:S(2)}, u32[]{:S(2)}) collective-permute-start(f32[1,128,256]{2,1,0:T(8,128)S(1)} %get-tuple-element.28), channel_id=1, source_target_pairs={{1,2},{2,1},{3,4},{4,3},{5,6},{6,5},{9,10},{10,9},{11,12},{12,11},... | collective-permute-start | bytes 393224 | tf_op jit(solution)/shard_map/ppermute | solution.py:352
  9.2 14.9 %collective-permute-start.6 = (f32[1,384,256]{2,1,0:T(8,128)S(1)}, f32[1,384,256]{2,1,0:T(8,128)S(1)}, u32[]{:S(2)}, u32[]{:S(2)}) collective-permute-start(f32[1,384,256]{2,1,0:T(8,128)S(1)} %get-tuple-element.35), channel_id=1, source_target_pairs={{1,2},{2,1},{3,4},{4,3},{5,6},{6,5},{9,10},{10,9},{11,12},{12,11},... | collective-permute-start | bytes 1179656 | tf_op jit(solution)/shard_map/ppermute | solution.py:354
  11.2 13.4 %copy-start = (f32[1,2,256,256]{3,2,1,0:T(8,128)S(1)}, f32[1,2,256,256]{3,2,1,0:T(8,128)}, u32[]{:S(2)}) copy-start(f32[1,2,256,256]{3,2,1,0:T(8,128)} %param.10) | copy-start | bytes 1572868
  11.2 13.4 %copy-start.1 = (s32[2,256,256]{2,1,0:T(8,128)S(1)}, s32[2,256,256]{2,1,0:T(8,128)}, u32[]{:S(2)}) copy-start(s32[2,256,256]{2,1,0:T(8,128)} %mask.1) | copy-start | bytes 1572868
  11.5 11.7 %collective-permute-start.4 = (f32[5,8,128]{2,1,0:T(8,128)S(1)}, f32[5,8,128]{2,1,0:T(8,128)S(1)}, u32[]{:S(2)}, u32[]{:S(2)}) collective-permute-start(f32[5,8,128]{2,1,0:T(8,128)S(1)} %face.1), channel_id=1, source_target_pairs={{0,4},{1,5},{2,6},{3,7},{4,0},{5,1},{6,2},{7,3},{8,12},{9,13},{10,... | collective-permute-start | bytes 61448 | tf_op jit(solution)/shard_map/ppermute | solution.py:371
  23.1 1.5 %collective-permute-start.7 = (f32[1,256,256]{2,1,0:T(8,128)S(1)}, f32[1,256,256]{2,1,0:T(8,128)S(1)}, u32[]{:S(2)}, u32[]{:S(2)}) collective-permute-start(f32[1,256,256]{2,1,0:T(8,128)S(1)} %get-tuple-element.37), channel_id=1, source_target_pairs={{0,1},{1,0},{2,3},{3,2},{4,5},{5,4},{6,7},{7,6},{8,9},{9,8},{10,11... | collective-permute-start | bytes 786440 | tf_op jit(solution)/shard_map/ppermute | solution.py:373
  23.1 3.8 %collective-permute-start.5 = (f32[5,8,128]{2,1,0:T(8,128)S(1)}, f32[5,8,128]{2,1,0:T(8,128)S(1)}, u32[]{:S(2)}, u32[]{:S(2)}) collective-permute-start(f32[5,8,128]{2,1,0:T(8,128)S(1)} %add.18), channel_id=1, source_target_pairs={{0,2},{1,3},{2,0},{3,1},{4,6},{5,7},{6,4},{7,5},{8,10},{9,11},{10,... | collective-permute-start | bytes 61448 | tf_op jit(solution)/shard_map/ppermute | solution.py:292
  27.0 1.2 %collective-permute-start.8 = (f32[5,8,128]{2,1,0:T(8,128)S(1)}, f32[5,8,128]{2,1,0:T(8,128)S(1)}, u32[]{:S(2)}, u32[]{:S(2)}) collective-permute-start(f32[5,8,128]{2,1,0:T(8,128)S(1)} %add.19), channel_id=1, source_target_pairs={{0,1},{1,0},{2,3},{3,2},{4,5},{5,4},{6,7},{7,6},{8,9},{9,8},{10,11... | collective-permute-start | bytes 61448 | tf_op jit(solution)/shard_map/ppermute | solution.py:292
  28.4 5.7 %collective-permute-start.13 = (f32[2,96,256]{2,1,0:T(8,128)S(1)}, f32[2,96,256]{2,1,0:T(8,128)S(1)}, u32[]{:S(2)}, u32[]{:S(2)}) collective-permute-start(f32[2,96,256]{2,1,0:T(8,128)S(1)} %get-tuple-element.47), channel_id=1, source_target_pairs={{0,8},{1,17},{2,10},{3,19},{4,12},{5,21},{6,14},{7,23},{8,0},{9,25... | collective-permute-start | bytes 589832 | tf_op jit(solution)/shard_map/ppermute | solution.py:310
  29.9 6.3 %collective-permute-start.11 = (f32[2,96,256]{2,1,0:T(8,128)S(1)}, f32[2,96,256]{2,1,0:T(8,128)S(1)}, u32[]{:S(2)}, u32[]{:S(2)}) collective-permute-start(f32[2,96,256]{2,1,0:T(8,128)S(1)} %get-tuple-element.46), channel_id=1, source_target_pairs={{0,8},{1,17},{2,10},{3,19},{4,12},{5,21},{6,14},{7,23},{8,0},{9,25... | collective-permute-start | bytes 589832 | tf_op jit(solution)/shard_map/ppermute | solution.py:310
  30.4 8.6 %collective-permute-start.9 = (f32[2,64,256]{2,1,0:T(8,128)S(1)}, f32[2,64,256]{2,1,0:T(8,128)S(1)}, u32[]{:S(2)}, u32[]{:S(2)}) collective-permute-start(f32[2,64,256]{2,1,0:T(8,128)S(1)} %get-tuple-element.45), channel_id=1, source_target_pairs={{0,8},{1,17},{2,10},{3,19},{4,12},{5,21},{6,14},{7,23},{8,0},{9,25... | collective-permute-start | bytes 393224 | tf_op jit(solution)/shard_map/ppermute | solution.py:310
  34.1 7.5 %collective-permute-start.14 = (f32[2,96,256]{2,1,0:T(8,128)S(1)}, f32[2,96,256]{2,1,0:T(8,128)S(1)}, u32[]{:S(2)}, u32[]{:S(2)}) collective-permute-start(f32[2,96,256]{2,1,0:T(8,128)S(1)} %add.23.total), channel_id=1, source_target_pairs={{0,16},{1,9},{2,18},{3,11},{4,20},{5,13},{6,22},{7,15},{8,24},{9,1... | collective-permute-start | bytes 589832 | tf_op jit(solution)/shard_map/ppermute | solution.py:313
  36.3 6.1 %collective-permute-start.12 = (f32[2,96,256]{2,1,0:T(8,128)S(1)}, f32[2,96,256]{2,1,0:T(8,128)S(1)}, u32[]{:S(2)}, u32[]{:S(2)}) collective-permute-start(f32[2,96,256]{2,1,0:T(8,128)S(1)} %add.22.total), channel_id=1, source_target_pairs={{0,16},{1,9},{2,18},{3,11},{4,20},{5,13},{6,22},{7,15},{8,24},{9,1... | collective-permute-start | bytes 589832 | tf_op jit(solution)/shard_map/ppermute | solution.py:313
  39.1 5.0 %collective-permute-start.10 = (f32[2,64,256]{2,1,0:T(8,128)S(1)}, f32[2,64,256]{2,1,0:T(8,128)S(1)}, u32[]{:S(2)}, u32[]{:S(2)}) collective-permute-start(f32[2,64,256]{2,1,0:T(8,128)S(1)} %add.21.total), channel_id=1, source_target_pairs={{0,16},{1,9},{2,18},{3,11},{4,20},{5,13},{6,22},{7,15},{8,24},{9,1... | collective-permute-start | bytes 393224 | tf_op jit(solution)/shard_map/ppermute | solution.py:313

commit v15 on v13

--- a/solution.py
+++ b/solution.py
@@ -12,7 +12,7 @@
 VMEM = pltpu.VMEM
 SMEM = pltpu.SMEM
 SUMS = 5
-EIGHTHS = (4, 4)
+EIGHTHS = (4, 2, 2)
 
 
 def params():

time: 45.4 us -> 48 us (1.057)
  starting transfers between devices: 20.6 us -> 22.1 us
  Pallas kernels: 7.27 us -> 7.9 us
  waiting for transfers between devices: 15.8 us -> 16.3 us
    ppermute x2 -> x3, waiting for transfers between devices: 6.26 us -> 8.26 us  [sum_positions(): arrived = lax.ppermute(term, ('pos', 'slab'), partners(0, positions, slabs))]
    ppermute x2 -> x3, waiting for transfers between devices: 3.13 us -> 1.6 us  [sum_positions(): lax.ppermute(term, ('pos', 'slab'), partners(step, positions, slabs))]
    ppermute x2 -> x3, starting transfers between devices: 2.09 us -> 3.58 us  [sum_positions(): arrived = lax.ppermute(term, ('pos', 'slab'), partners(0, positions, slabs))]
    pallas_call x2 -> x3, Pallas kernels: 1.48 us -> 2.1 us  [local(): pl.pallas_call(functools.partial(close_kernel, first_rows(radial)[index])...]
    ppermute x2 -> x3, starting transfers between devices: 3.17 us -> 3.17 us  [sum_positions(): lax.ppermute(term, ('pos', 'slab'), partners(step, positions, slabs))]
  transfers between devices with their start and end apart: 13 -> 15, of which waited for: 7 -> 6; matrix products, arithmetic and copies ran while one was open for 0% -> 0% of each run, Pallas kernels for 11% -> 12%
where the time goes in v15:
time: 48 us; the launch traced here: 47.8 us
  starting transfers between devices  22.1 us (46%)
  waiting for transfers between devices  16.3 us (34%)
  Pallas kernels  7.9 us (16%)
  between operations  1.47 us (3%)
    ppermute x3, waiting for transfers between devices, sum_positions(): arrived = lax.ppermute(term, ('pos', 'slab'), partners(0, positions, slabs))  8.26 us
    ppermute x1, starting transfers between devices, local(): arrived = lax.ppermute(sums, 'slab', [(i, i ^ 2) for i in range(slabs)])  6.55 us
    ppermute x1, starting transfers between devices, local(): near_part_in = lax.ppermute(near_part, 'slab', pairs(slabs, 0))  3.99 us
    ppermute x1, waiting for transfers between devices, local(): arrived = lax.ppermute(sums, 'slab', [(i, i ^ 2) for i in range(slabs)])  3.87 us
    ppermute x3, starting transfers between devices, sum_positions(): arrived = lax.ppermute(term, ('pos', 'slab'), partners(0, positions, slabs))  3.58 us
    ppermute x3, starting transfers between devices, sum_positions(): lax.ppermute(term, ('pos', 'slab'), partners(step, positions, slabs))  3.17 us
    ppermute x2, waiting for transfers between devices, gather_sums(): arrived = lax.ppermute(sums, 'slab', [(i, i ^ step) for i in range(slabs)])  2.56 us
    ppermute x2, starting transfers between devices, gather_sums(): arrived = lax.ppermute(sums, 'slab', [(i, i ^ step) for i in range(slabs)])  2.23 us
  transfers between devices with their start and end apart: 15, of which 6 were waited for; matrix products, arithmetic and copies ran while one was open for 0% of the time, Pallas kernels for 12%

profile of v15, /device:TPU:0, one launch (start us, length us, event | category | flops | bytes accessed | tf_op | source)
XLA Modules:
  0.0 47.8 jit_solution(10419340760163645426)
XLA Ops:
  1.3 1.4 %open.1 = (f32[2,256,256]{2,1,0:T(8,128)S(1)}, f32[2,256,256]{2,1,0:T(8,128)S(1)}, f32[1,256,256]{2,1,0:T(8,128)S(1)}, f32[1,256,256]{2,1,0:T(8,128)S(1)}) custom-call(f32[4]{0:T(128)} %reluctivity.1, s32[1]{0:T(128)S(6)} %copy.12.shift, s32[2,256,256]{2,1,0:T(8,128)} %labels.1, f32[2,256,256]{2,1,0:T(8,128)} %bitcast.5, f32[2,256,256]{2,1,0:T(8,128)} %bitcast.3), custom_call_target="tpu_custom_call" | custom-call | tf_op jit(solution)/shard_map/open/pallas_call | solution.py:328
  3.2 0.7 %collective-permute-start = (f32[2,256,256]{2,1,0:T(8,128)S(1)}, f32[2,256,256]{2,1,0:T(8,128)S(1)}, u32[]{:S(2)}, u32[]{:S(2)}) collective-permute-start(f32[2,256,256]{2,1,0:T(8,128)S(1)} %get-tuple-element.25.far), channel_id=1, source_target_pairs={{1,2},{2,1},{3,4},{4,3},{5,6},{6,5},{9,10},{10,9},{11,12},{12,11},... | collective-permute-start | bytes 1572872 | tf_op jit(solution)/shard_map/ppermute | solution.py:341
  3.9 0.7 %part.1 = (f32[1,256,256]{2,1,0:T(8,128)S(1)}, f32[1,256,256]{2,1,0:T(8,128)S(1)}, f32[1,128,256]{2,1,0:T(8,128)S(1)}, f32[1,384,256]{2,1,0:T(8,128)S(1)}) custom-call(f32[2,256,256]{2,1,0:T(8,128)S(1)} %get-tuple-element.25.far, f32[2,256,256]{2,1,0:T(8,128)S(1)} %get-tuple-element.26.near, f32[1,256,256]{2,1,0:T(8,128)S(1)} %get-tuple-element.27.far_potential), custom_call_target="tpu_custom_call" | custom-call | tf_op jit(solution)/shard_map/part/pallas_call | solution.py:344
  4.6 4.0 %collective-permute-start.3 = (f32[1,256,256]{2,1,0:T(8,128)S(1)}, f32[1,256,256]{2,1,0:T(8,128)S(1)}, u32[]{:S(2)}, u32[]{:S(2)}) collective-permute-start(f32[1,256,256]{2,1,0:T(8,128)S(1)} %get-tuple-element.30.near_part), channel_id=1, source_target_pairs={{0,1},{1,0},{2,3},{3,2},{4,5},{5,4},{6,7},{7,6},{8,9},{9,8},{10,11... | collective-permute-start | bytes 786440 | tf_op jit(solution)/shard_map/ppermute | solution.py:353
  8.6 0.7 %collective-permute-start.1 = (f32[1,128,256]{2,1,0:T(8,128)S(1)}, f32[1,128,256]{2,1,0:T(8,128)S(1)}, u32[]{:S(2)}, u32[]{:S(2)}) collective-permute-start(f32[1,128,256]{2,1,0:T(8,128)S(1)} %get-tuple-element.28), channel_id=1, source_target_pairs={{1,2},{2,1},{3,4},{4,3},{5,6},{6,5},{9,10},{10,9},{11,12},{12,11},... | collective-permute-start | bytes 393224 | tf_op jit(solution)/shard_map/ppermute | solution.py:352
  9.2 0.7 %collective-permute-start.6 = (f32[1,384,256]{2,1,0:T(8,128)S(1)}, f32[1,384,256]{2,1,0:T(8,128)S(1)}, u32[]{:S(2)}, u32[]{:S(2)}) collective-permute-start(f32[1,384,256]{2,1,0:T(8,128)S(1)} %get-tuple-element.35), channel_id=1, source_target_pairs={{1,2},{2,1},{3,4},{4,3},{5,6},{6,5},{9,10},{10,9},{11,12},{12,11},... | collective-permute-start | bytes 1179656 | tf_op jit(solution)/shard_map/ppermute | solution.py:354
  10.0 1.2 %sums.1 = (f32[2,256,256]{2,1,0:T(8,128)S(1)}, f32[1,256,256]{2,1,0:T(8,128)S(1)}, f32[8,128]{1,0:T(8,128)S(1)}) custom-call(f32[2,256,256]{2,1,0:T(8,128)S(1)} %get-tuple-element.25.far, f32[2,256,256]{2,1,0:T(8,128)S(1)} %get-tuple-element.26.near, f32[1,256,256]{2,1,0:T(8,128)S(1)} %get-tuple-element.29.far_part, ...), custom_call_target="tpu_custom_call" | custom-call | tf_op jit(solution)/shard_map/sums/pallas_call | solution.py:355
  11.5 6.6 %collective-permute-start.4 = (f32[5,8,128]{2,1,0:T(8,128)S(1)}, f32[5,8,128]{2,1,0:T(8,128)S(1)}, u32[]{:S(2)}, u32[]{:S(2)}) collective-permute-start(f32[5,8,128]{2,1,0:T(8,128)S(1)} %face.1), channel_id=1, source_target_pairs={{0,2},{1,3},{2,0},{3,1},{4,6},{5,7},{6,4},{7,5},{8,10},{9,11},{10,... | collective-permute-start | bytes 61448 | tf_op jit(solution)/shard_map/ppermute | solution.py:371
  18.0 3.9 %collective-permute-done.4 = f32[5,8,128]{2,1,0:T(8,128)S(1)} collective-permute-done((f32[5,8,128]{2,1,0:T(8,128)S(1)}, f32[5,8,128]{2,1,0:T(8,128)S(1)}, u32[]{:S(2)}, u32[]{:S(2)}) %collective-permute-start.4) | collective-permute-done | bytes 20512 | tf_op jit(solution)/shard_map/ppermute | solution.py:371
  21.9 2.2 %collective-permute-start.5 = (f32[5,8,128]{2,1,0:T(8,128)S(1)}, f32[5,8,128]{2,1,0:T(8,128)S(1)}, u32[]{:S(2)}, u32[]{:S(2)}) collective-permute-start(f32[5,8,128]{2,1,0:T(8,128)S(1)} %add.18), channel_id=1, source_target_pairs={{0,4},{1,5},{2,6},{3,7},{4,0},{5,1},{6,2},{7,3},{8,12},{9,13},{10,... | collective-permute-start | bytes 61448 | tf_op jit(solution)/shard_map/ppermute | solution.py:292
  24.1 1.1 %fields.1 = (f32[2,256,256]{2,1,0:T(8,128)S(1)}, f32[2,256,256]{2,1,0:T(8,128)S(1)}, f32[2,256,256]{2,1,0:T(8,128)S(1)}) custom-call(f32[2,256,256]{2,1,0:T(8,128)S(1)} %get-tuple-element.25.far, f32[2,256,256]{2,1,0:T(8,128)S(1)} %get-tuple-element.26.near, f32[2,256,256]{2,1,0:T(8,128)S(1)} %collective-permute-done.far_in, ...), custom_call_target="tpu_custom_call" | custom-call | tf_op jit(solution)/shard_map/fields/pallas_call | solution.py:375
  25.3 1.4 %collective-permute-done.5 = f32[5,8,128]{2,1,0:T(8,128)S(1)} collective-permute-done((f32[5,8,128]{2,1,0:T(8,128)S(1)}, f32[5,8,128]{2,1,0:T(8,128)S(1)}, u32[]{:S(2)}, u32[]{:S(2)}) %collective-permute-start.5) | collective-permute-done | bytes 20512 | tf_op jit(solution)/shard_map/ppermute | solution.py:292
  26.6 1.2 %collective-permute-done.8 = f32[5,8,128]{2,1,0:T(8,128)S(1)} collective-permute-done((f32[5,8,128]{2,1,0:T(8,128)S(1)}, f32[5,8,128]{2,1,0:T(8,128)S(1)}, u32[]{:S(2)}, u32[]{:S(2)}) %collective-permute-start.8) | collective-permute-done | bytes 20512 | tf_op jit(solution)/shard_map/ppermute | solution.py:292
  28.0 1.6 %collective-permute-start.13 = (f32[2,128,256]{2,1,0:T(8,128)S(1)}, f32[2,128,256]{2,1,0:T(8,128)S(1)}, u32[]{:S(2)}, u32[]{:S(2)}) collective-permute-start(f32[2,128,256]{2,1,0:T(8,128)S(1)} %get-tuple-element.47), channel_id=1, source_target_pairs={{0,8},{1,17},{2,10},{3,19},{4,12},{5,21},{6,14},{7,23},{8,0},{9,25... | collective-permute-start | bytes 786440 | tf_op jit(solution)/shard_map/ppermute | solution.py:310
  30.1 4.3 %collective-permute-done.13 = f32[2,128,256]{2,1,0:T(8,128)S(1)} collective-permute-done((f32[2,128,256]{2,1,0:T(8,128)S(1)}, f32[2,128,256]{2,1,0:T(8,128)S(1)}, u32[]{:S(2)}, u32[]{:S(2)}) %collective-permute-start.13) | collective-permute-done | bytes 262176 | tf_op jit(solution)/shard_map/ppermute | solution.py:310
  34.5 1.6 %collective-permute-start.14 = (f32[2,128,256]{2,1,0:T(8,128)S(1)}, f32[2,128,256]{2,1,0:T(8,128)S(1)}, u32[]{:S(2)}, u32[]{:S(2)}) collective-permute-start(f32[2,128,256]{2,1,0:T(8,128)S(1)} %add.23.total), channel_id=1, source_target_pairs={{0,16},{1,9},{2,18},{3,11},{4,20},{5,13},{6,22},{7,15},{8,24},{9,1... | collective-permute-start | bytes 786440 | tf_op jit(solution)/shard_map/ppermute | solution.py:313
  36.1 1.5 %collective-permute-start.9 = (f32[2,64,256]{2,1,0:T(8,128)S(1)}, f32[2,64,256]{2,1,0:T(8,128)S(1)}, u32[]{:S(2)}, u32[]{:S(2)}) collective-permute-start(f32[2,64,256]{2,1,0:T(8,128)S(1)} %get-tuple-element.45), channel_id=1, source_target_pairs={{0,8},{1,17},{2,10},{3,19},{4,12},{5,21},{6,14},{7,23},{8,0},{9,25... | collective-permute-start | bytes 393224 | tf_op jit(solution)/shard_map/ppermute | solution.py:310
  38.2 3.9 %collective-permute-done.9 = f32[2,64,256]{2,1,0:T(8,128)S(1)} collective-permute-done((f32[2,64,256]{2,1,0:T(8,128)S(1)}, f32[2,64,256]{2,1,0:T(8,128)S(1)}, u32[]{:S(2)}, u32[]{:S(2)}) %collective-permute-start.9) | collective-permute-done | bytes 131104 | tf_op jit(solution)/shard_map/ppermute | solution.py:310
  42.1 1.0 %collective-permute-start.10 = (f32[2,64,256]{2,1,0:T(8,128)S(1)}, f32[2,64,256]{2,1,0:T(8,128)S(1)}, u32[]{:S(2)}, u32[]{:S(2)}) collective-permute-start(f32[2,64,256]{2,1,0:T(8,128)S(1)} %add.21.total), channel_id=1, source_target_pairs={{0,16},{1,9},{2,18},{3,11},{4,20},{5,13},{6,22},{7,15},{8,24},{9,1... | collective-permute-start | bytes 393224 | tf_op jit(solution)/shard_map/ppermute | solution.py:313
  43.1 1.0 %adjoint.1 = f32[2,256,256]{2,1,0:T(8,128)} custom-call(f32[5,8,128]{2,1,0:T(8,128)S(1)} %add.20.sums, f32[2,256,256]{2,1,0:T(8,128)S(1)} %get-tuple-element.25.far, f32[2,256,256]{2,1,0:T(8,128)S(1)} %get-tuple-element.26.near, f32[2,256,256]{2,1,0:T(8,128)S(1)} %get-tuple-element.31.image), custom_call_target="tpu_custom_call" | custom-call | tf_op jit(solution)/shard_map/adjoint/pallas_call | solution.py:393
  44.1 0.7 %close.3.rest_0_ = f32[2,256,256]{2,1,0:T(8,128)} custom-call(f32[2,128,256]{2,1,0:T(8,128)S(1)} %add.23.total, f32[2,128,256]{2,1,0:T(8,128)S(1)} %collective-permute-done.14.arrived), custom_call_target="tpu_custom_call" | custom-call | tf_op jit(solution)/shard_map/close/pallas_call | solution.py:405
  44.9 0.7 %close.4.rest_0_ = f32[2,256,256]{2,1,0:T(8,128)} custom-call(f32[2,64,256]{2,1,0:T(8,128)S(1)} %add.22.total, f32[2,64,256]{2,1,0:T(8,128)S(1)} %collective-permute-done.12.arrived, f32[2,256,256]{2,1,0:T(8,128)} %close.3.rest_0_), custom_call_target="tpu_custom_call", output_to_operand_aliasing={{}: (2, {})} | custom-call | tf_op jit(solution)/shard_map/close/pallas_call | solution.py:405
  45.5 1.6 %collective-permute-done.10.arrived = f32[2,64,256]{2,1,0:T(8,128)S(1)} collective-permute-done((f32[2,64,256]{2,1,0:T(8,128)S(1)}, f32[2,64,256]{2,1,0:T(8,128)S(1)}, u32[]{:S(2)}, u32[]{:S(2)}) %collective-permute-start.10) | collective-permute-done | bytes 131104 | tf_op jit(solution)/shard_map/ppermute | solution.py:313
  47.1 0.7 %close.5 = f32[2,256,256]{2,1,0:T(8,128)} custom-call(f32[2,64,256]{2,1,0:T(8,128)S(1)} %add.21.total, f32[2,64,256]{2,1,0:T(8,128)S(1)} %collective-permute-done.10.arrived, f32[2,256,256]{2,1,0:T(8,128)} %close.4.rest_0_), custom_call_target="tpu_custom_call", output_to_operand_aliasing={{}: (2, {})} | custom-call | tf_op jit(solution)/shard_map/close/pallas_call | solution.py:405
  (26 shorter events, 2.2 us)
Async XLA Ops:
  2.7 7.2 %collective-permute-start.2 = (f32[2,256,256]{2,1,0:T(8,128)S(1)}, f32[2,256,256]{2,1,0:T(8,128)S(1)}, u32[]{:S(2)}, u32[]{:S(2)}) collective-permute-start(f32[2,256,256]{2,1,0:T(8,128)S(1)} %get-tuple-element.26.near), channel_id=1, source_target_pairs={{0,1},{1,0},{2,3},{3,2},{4,5},{5,4},{6,7},{7,6},{8,9},{9,8},{10,11... | collective-permute-start | bytes 1572872 | tf_op jit(solution)/shard_map/ppermute | solution.py:342
  3.2 6.7 %collective-permute-start = (f32[2,256,256]{2,1,0:T(8,128)S(1)}, f32[2,256,256]{2,1,0:T(8,128)S(1)}, u32[]{:S(2)}, u32[]{:S(2)}) collective-permute-start(f32[2,256,256]{2,1,0:T(8,128)S(1)} %get-tuple-element.25.far), channel_id=1, source_target_pairs={{1,2},{2,1},{3,4},{4,3},{5,6},{6,5},{9,10},{10,9},{11,12},{12,11},... | collective-permute-start | bytes 1572872 | tf_op jit(solution)/shard_map/ppermute | solution.py:341
  4.6 5.3 %collective-permute-start.3 = (f32[1,256,256]{2,1,0:T(8,128)S(1)}, f32[1,256,256]{2,1,0:T(8,128)S(1)}, u32[]{:S(2)}, u32[]{:S(2)}) collective-permute-start(f32[1,256,256]{2,1,0:T(8,128)S(1)} %get-tuple-element.30.near_part), channel_id=1, source_target_pairs={{0,1},{1,0},{2,3},{3,2},{4,5},{5,4},{6,7},{7,6},{8,9},{9,8},{10,11... | collective-permute-start | bytes 786440 | tf_op jit(solution)/shard_map/ppermute | solution.py:353
  8.6 2.6 %collective-permute-start.1 = (f32[1,128,256]{2,1,0:T(8,128)S(1)}, f32[1,128,256]{2,1,0:T(8,128)S(1)}, u32[]{:S(2)}, u32[]{:S(2)}) collective-permute-start(f32[1,128,256]{2,1,0:T(8,128)S(1)} %get-tuple-element.28), channel_id=1, source_target_pairs={{1,2},{2,1},{3,4},{4,3},{5,6},{6,5},{9,10},{10,9},{11,12},{12,11},... | collective-permute-start | bytes 393224 | tf_op jit(solution)/shard_map/ppermute | solution.py:352
  9.2 14.9 %collective-permute-start.6 = (f32[1,384,256]{2,1,0:T(8,128)S(1)}, f32[1,384,256]{2,1,0:T(8,128)S(1)}, u32[]{:S(2)}, u32[]{:S(2)}) collective-permute-start(f32[1,384,256]{2,1,0:T(8,128)S(1)} %get-tuple-element.35), channel_id=1, source_target_pairs={{1,2},{2,1},{3,4},{4,3},{5,6},{6,5},{9,10},{10,9},{11,12},{12,11},... | collective-permute-start | bytes 1179656 | tf_op jit(solution)/shard_map/ppermute | solution.py:354
  11.2 12.9 %copy-start = (f32[1,2,256,256]{3,2,1,0:T(8,128)S(1)}, f32[1,2,256,256]{3,2,1,0:T(8,128)}, u32[]{:S(2)}) copy-start(f32[1,2,256,256]{3,2,1,0:T(8,128)} %param.10) | copy-start | bytes 1572868
  11.2 12.9 %copy-start.1 = (s32[2,256,256]{2,1,0:T(8,128)S(1)}, s32[2,256,256]{2,1,0:T(8,128)}, u32[]{:S(2)}) copy-start(s32[2,256,256]{2,1,0:T(8,128)} %mask.1) | copy-start | bytes 1572868
  11.5 10.4 %collective-permute-start.4 = (f32[5,8,128]{2,1,0:T(8,128)S(1)}, f32[5,8,128]{2,1,0:T(8,128)S(1)}, u32[]{:S(2)}, u32[]{:S(2)}) collective-permute-start(f32[5,8,128]{2,1,0:T(8,128)S(1)} %face.1), channel_id=1, source_target_pairs={{0,2},{1,3},{2,0},{3,1},{4,6},{5,7},{6,4},{7,5},{8,10},{9,11},{10,... | collective-permute-start | bytes 61448 | tf_op jit(solution)/shard_map/ppermute | solution.py:371
  21.9 2.2 %collective-permute-start.7 = (f32[1,256,256]{2,1,0:T(8,128)S(1)}, f32[1,256,256]{2,1,0:T(8,128)S(1)}, u32[]{:S(2)}, u32[]{:S(2)}) collective-permute-start(f32[1,256,256]{2,1,0:T(8,128)S(1)} %get-tuple-element.37), channel_id=1, source_target_pairs={{0,1},{1,0},{2,3},{3,2},{4,5},{5,4},{6,7},{7,6},{8,9},{9,8},{10,11... | collective-permute-start | bytes 786440 | tf_op jit(solution)/shard_map/ppermute | solution.py:373
  21.9 4.7 %collective-permute-start.5 = (f32[5,8,128]{2,1,0:T(8,128)S(1)}, f32[5,8,128]{2,1,0:T(8,128)S(1)}, u32[]{:S(2)}, u32[]{:S(2)}) collective-permute-start(f32[5,8,128]{2,1,0:T(8,128)S(1)} %add.18), channel_id=1, source_target_pairs={{0,4},{1,5},{2,6},{3,7},{4,0},{5,1},{6,2},{7,3},{8,12},{9,13},{10,... | collective-permute-start | bytes 61448 | tf_op jit(solution)/shard_map/ppermute | solution.py:292
  26.6 1.2 %collective-permute-start.8 = (f32[5,8,128]{2,1,0:T(8,128)S(1)}, f32[5,8,128]{2,1,0:T(8,128)S(1)}, u32[]{:S(2)}, u32[]{:S(2)}) collective-permute-start(f32[5,8,128]{2,1,0:T(8,128)S(1)} %add.19), channel_id=1, source_target_pairs={{0,1},{1,0},{2,3},{3,2},{4,5},{5,4},{6,7},{7,6},{8,9},{9,8},{10,11... | collective-permute-start | bytes 61448 | tf_op jit(solution)/shard_map/ppermute | solution.py:292
  28.0 6.4 %collective-permute-start.13 = (f32[2,128,256]{2,1,0:T(8,128)S(1)}, f32[2,128,256]{2,1,0:T(8,128)S(1)}, u32[]{:S(2)}, u32[]{:S(2)}) collective-permute-start(f32[2,128,256]{2,1,0:T(8,128)S(1)} %get-tuple-element.47), channel_id=1, source_target_pairs={{0,8},{1,17},{2,10},{3,19},{4,12},{5,21},{6,14},{7,23},{8,0},{9,25... | collective-permute-start | bytes 786440 | tf_op jit(solution)/shard_map/ppermute | solution.py:310
  29.6 8.0 %collective-permute-start.11 = (f32[2,64,256]{2,1,0:T(8,128)S(1)}, f32[2,64,256]{2,1,0:T(8,128)S(1)}, u32[]{:S(2)}, u32[]{:S(2)}) collective-permute-start(f32[2,64,256]{2,1,0:T(8,128)S(1)} %get-tuple-element.46), channel_id=1, source_target_pairs={{0,8},{1,17},{2,10},{3,19},{4,12},{5,21},{6,14},{7,23},{8,0},{9,25... | collective-permute-start | bytes 393224 | tf_op jit(solution)/shard_map/ppermute | solution.py:310
  34.5 9.6 %collective-permute-start.14 = (f32[2,128,256]{2,1,0:T(8,128)S(1)}, f32[2,128,256]{2,1,0:T(8,128)S(1)}, u32[]{:S(2)}, u32[]{:S(2)}) collective-permute-start(f32[2,128,256]{2,1,0:T(8,128)S(1)} %add.23.total), channel_id=1, source_target_pairs={{0,16},{1,9},{2,18},{3,11},{4,20},{5,13},{6,22},{7,15},{8,24},{9,1... | collective-permute-start | bytes 786440 | tf_op jit(solution)/shard_map/ppermute | solution.py:313
  36.1 6.0 %collective-permute-start.9 = (f32[2,64,256]{2,1,0:T(8,128)S(1)}, f32[2,64,256]{2,1,0:T(8,128)S(1)}, u32[]{:S(2)}, u32[]{:S(2)}) collective-permute-start(f32[2,64,256]{2,1,0:T(8,128)S(1)} %get-tuple-element.45), channel_id=1, source_target_pairs={{0,8},{1,17},{2,10},{3,19},{4,12},{5,21},{6,14},{7,23},{8,0},{9,25... | collective-permute-start | bytes 393224 | tf_op jit(solution)/shard_map/ppermute | solution.py:310
  37.6 7.2 %collective-permute-start.12 = (f32[2,64,256]{2,1,0:T(8,128)S(1)}, f32[2,64,256]{2,1,0:T(8,128)S(1)}, u32[]{:S(2)}, u32[]{:S(2)}) collective-permute-start(f32[2,64,256]{2,1,0:T(8,128)S(1)} %add.22.total), channel_id=1, source_target_pairs={{0,16},{1,9},{2,18},{3,11},{4,20},{5,13},{6,22},{7,15},{8,24},{9,1... | collective-permute-start | bytes 393224 | tf_op jit(solution)/shard_map/ppermute | solution.py:313
  42.1 5.0 %collective-permute-start.10 = (f32[2,64,256]{2,1,0:T(8,128)S(1)}, f32[2,64,256]{2,1,0:T(8,128)S(1)}, u32[]{:S(2)}, u32[]{:S(2)}) collective-permute-start(f32[2,64,256]{2,1,0:T(8,128)S(1)} %add.21.total), channel_id=1, source_target_pairs={{0,16},{1,9},{2,18},{3,11},{4,20},{5,13},{6,22},{7,15},{8,24},{9,1... | collective-permute-start | bytes 393224 | tf_op jit(solution)/shard_map/ppermute | solution.py:313

commit v16 on v9

--- a/solution.py
+++ b/solution.py
@@ -8,7 +8,7 @@
 from jax.sharding import PartitionSpec as P
 
 
-ROWS = 16
+ROWS = 32
 VMEM = pltpu.VMEM
 SMEM = pltpu.SMEM
 SUMS = 5

time: 44.6 us -> 44.7 us (level)
  no operation moved by 1% of the time
where the time goes in v16:
time: 44.7 us; the launch traced here: 44.5 us
  starting transfers between devices  23.6 us (53%)
  waiting for transfers between devices  11.4 us (26%)
  Pallas kernels  7.94 us (18%)
  between operations  1.47 us (3%)
    ppermute x1, starting transfers between devices, local(): arrived = lax.ppermute(sums, 'slab', [(i, i ^ 2) for i in range(slabs)])  6.5 us
    ppermute x3, starting transfers between devices, sum_positions(): lax.ppermute(term, ('pos', 'slab'), partners(step, positions, slabs))  4.75 us
    ppermute x1, starting transfers between devices, local(): near_part_in = lax.ppermute(near_part, 'slab', pairs(slabs, 0))  3.99 us
    ppermute x1, waiting for transfers between devices, local(): arrived = lax.ppermute(sums, 'slab', [(i, i ^ 2) for i in range(slabs)])  3.9 us
    ppermute x3, waiting for transfers between devices, sum_positions(): arrived = lax.ppermute(term, ('pos', 'slab'), partners(0, positions, slabs))  3.88 us
    ppermute x3, starting transfers between devices, sum_positions(): arrived = lax.ppermute(term, ('pos', 'slab'), partners(0, positions, slabs))  3.58 us
    ppermute x2, waiting for transfers between devices, gather_sums(): arrived = lax.ppermute(sums, 'slab', [(i, i ^ step) for i in range(slabs)])  2.59 us
    ppermute x2, starting transfers between devices, gather_sums(): arrived = lax.ppermute(sums, 'slab', [(i, i ^ step) for i in range(slabs)])  2.2 us
  transfers between devices with their start and end apart: 15, of which 7 were waited for; matrix products, arithmetic and copies ran while one was open for 0% of the time, Pallas kernels for 13%

profile of v16, /device:TPU:0, one launch (start us, length us, event | category | flops | bytes accessed | tf_op | source)
XLA Modules:
  0.0 44.5 jit_solution(4248459281520040017)
XLA Ops:
  1.3 1.4 %open.1 = (f32[2,256,256]{2,1,0:T(8,128)S(1)}, f32[2,256,256]{2,1,0:T(8,128)S(1)}, f32[1,256,256]{2,1,0:T(8,128)S(1)}, f32[1,256,256]{2,1,0:T(8,128)S(1)}) custom-call(f32[4]{0:T(128)} %reluctivity.1, s32[1]{0:T(128)S(6)} %copy.12.shift, s32[2,256,256]{2,1,0:T(8,128)} %labels.1, f32[2,256,256]{2,1,0:T(8,128)} %bitcast.5, f32[2,256,256]{2,1,0:T(8,128)} %bitcast.3), custom_call_target="tpu_custom_call" | custom-call | tf_op jit(solution)/shard_map/open/pallas_call | solution.py:328
  3.2 0.7 %collective-permute-start = (f32[2,256,256]{2,1,0:T(8,128)S(1)}, f32[2,256,256]{2,1,0:T(8,128)S(1)}, u32[]{:S(2)}, u32[]{:S(2)}) collective-permute-start(f32[2,256,256]{2,1,0:T(8,128)S(1)} %get-tuple-element.25.far), channel_id=1, source_target_pairs={{1,2},{2,1},{3,4},{4,3},{5,6},{6,5},{9,10},{10,9},{11,12},{12,11},... | collective-permute-start | bytes 1572872 | tf_op jit(solution)/shard_map/ppermute | solution.py:341
  3.9 0.7 %part.1 = (f32[1,256,256]{2,1,0:T(8,128)S(1)}, f32[1,256,256]{2,1,0:T(8,128)S(1)}, f32[1,128,256]{2,1,0:T(8,128)S(1)}, f32[1,384,256]{2,1,0:T(8,128)S(1)}) custom-call(f32[2,256,256]{2,1,0:T(8,128)S(1)} %get-tuple-element.25.far, f32[2,256,256]{2,1,0:T(8,128)S(1)} %get-tuple-element.26.near, f32[1,256,256]{2,1,0:T(8,128)S(1)} %get-tuple-element.27.far_potential), custom_call_target="tpu_custom_call" | custom-call | tf_op jit(solution)/shard_map/part/pallas_call | solution.py:344
  4.6 4.0 %collective-permute-start.3 = (f32[1,256,256]{2,1,0:T(8,128)S(1)}, f32[1,256,256]{2,1,0:T(8,128)S(1)}, u32[]{:S(2)}, u32[]{:S(2)}) collective-permute-start(f32[1,256,256]{2,1,0:T(8,128)S(1)} %get-tuple-element.30.near_part), channel_id=1, source_target_pairs={{0,1},{1,0},{2,3},{3,2},{4,5},{5,4},{6,7},{7,6},{8,9},{9,8},{10,11... | collective-permute-start | bytes 786440 | tf_op jit(solution)/shard_map/ppermute | solution.py:353
  9.3 0.7 %collective-permute-start.6 = (f32[1,384,256]{2,1,0:T(8,128)S(1)}, f32[1,384,256]{2,1,0:T(8,128)S(1)}, u32[]{:S(2)}, u32[]{:S(2)}) collective-permute-start(f32[1,384,256]{2,1,0:T(8,128)S(1)} %get-tuple-element.35), channel_id=1, source_target_pairs={{1,2},{2,1},{3,4},{4,3},{5,6},{6,5},{9,10},{10,9},{11,12},{12,11},... | collective-permute-start | bytes 1179656 | tf_op jit(solution)/shard_map/ppermute | solution.py:354
  10.0 1.3 %sums.1 = (f32[2,256,256]{2,1,0:T(8,128)S(1)}, f32[1,256,256]{2,1,0:T(8,128)S(1)}, f32[8,128]{1,0:T(8,128)S(1)}) custom-call(f32[2,256,256]{2,1,0:T(8,128)S(1)} %get-tuple-element.25.far, f32[2,256,256]{2,1,0:T(8,128)S(1)} %get-tuple-element.26.near, f32[1,256,256]{2,1,0:T(8,128)S(1)} %get-tuple-element.29.far_part, ...), custom_call_target="tpu_custom_call" | custom-call | tf_op jit(solution)/shard_map/sums/pallas_call | solution.py:355
  11.5 6.5 %collective-permute-start.4 = (f32[5,8,128]{2,1,0:T(8,128)S(1)}, f32[5,8,128]{2,1,0:T(8,128)S(1)}, u32[]{:S(2)}, u32[]{:S(2)}) collective-permute-start(f32[5,8,128]{2,1,0:T(8,128)S(1)} %face.1), channel_id=1, source_target_pairs={{0,2},{1,3},{2,0},{3,1},{4,6},{5,7},{6,4},{7,5},{8,10},{9,11},{10,... | collective-permute-start | bytes 61448 | tf_op jit(solution)/shard_map/ppermute | solution.py:371
  18.0 3.9 %collective-permute-done.4 = f32[5,8,128]{2,1,0:T(8,128)S(1)} collective-permute-done((f32[5,8,128]{2,1,0:T(8,128)S(1)}, f32[5,8,128]{2,1,0:T(8,128)S(1)}, u32[]{:S(2)}, u32[]{:S(2)}) %collective-permute-start.4) | collective-permute-done | bytes 20512 | tf_op jit(solution)/shard_map/ppermute | solution.py:371
  21.9 2.2 %collective-permute-start.5 = (f32[5,8,128]{2,1,0:T(8,128)S(1)}, f32[5,8,128]{2,1,0:T(8,128)S(1)}, u32[]{:S(2)}, u32[]{:S(2)}) collective-permute-start(f32[5,8,128]{2,1,0:T(8,128)S(1)} %add.18), channel_id=1, source_target_pairs={{0,4},{1,5},{2,6},{3,7},{4,0},{5,1},{6,2},{7,3},{8,12},{9,13},{10,... | collective-permute-start | bytes 61448 | tf_op jit(solution)/shard_map/ppermute | solution.py:292
  24.1 1.1 %fields.1 = (f32[2,256,256]{2,1,0:T(8,128)S(1)}, f32[2,256,256]{2,1,0:T(8,128)S(1)}, f32[2,256,256]{2,1,0:T(8,128)S(1)}) custom-call(f32[2,256,256]{2,1,0:T(8,128)S(1)} %get-tuple-element.25.far, f32[2,256,256]{2,1,0:T(8,128)S(1)} %get-tuple-element.26.near, f32[2,256,256]{2,1,0:T(8,128)S(1)} %collective-permute-done.far_in, ...), custom_call_target="tpu_custom_call" | custom-call | tf_op jit(solution)/shard_map/fields/pallas_call | solution.py:375
  25.3 1.4 %collective-permute-done.5 = f32[5,8,128]{2,1,0:T(8,128)S(1)} collective-permute-done((f32[5,8,128]{2,1,0:T(8,128)S(1)}, f32[5,8,128]{2,1,0:T(8,128)S(1)}, u32[]{:S(2)}, u32[]{:S(2)}) %collective-permute-start.5) | collective-permute-done | bytes 20512 | tf_op jit(solution)/shard_map/ppermute | solution.py:292
  26.7 1.2 %collective-permute-done.8 = f32[5,8,128]{2,1,0:T(8,128)S(1)} collective-permute-done((f32[5,8,128]{2,1,0:T(8,128)S(1)}, f32[5,8,128]{2,1,0:T(8,128)S(1)}, u32[]{:S(2)}, u32[]{:S(2)}) %collective-permute-start.8) | collective-permute-done | bytes 20512 | tf_op jit(solution)/shard_map/ppermute | solution.py:292
  28.1 1.6 %collective-permute-start.13 = (f32[2,96,256]{2,1,0:T(8,128)S(1)}, f32[2,96,256]{2,1,0:T(8,128)S(1)}, u32[]{:S(2)}, u32[]{:S(2)}) collective-permute-start(f32[2,96,256]{2,1,0:T(8,128)S(1)} %get-tuple-element.47), channel_id=1, source_target_pairs={{0,8},{1,17},{2,10},{3,19},{4,12},{5,21},{6,14},{7,23},{8,0},{9,25... | collective-permute-start | bytes 589832 | tf_op jit(solution)/shard_map/ppermute | solution.py:310
  30.1 1.5 %collective-permute-start.9 = (f32[2,64,256]{2,1,0:T(8,128)S(1)}, f32[2,64,256]{2,1,0:T(8,128)S(1)}, u32[]{:S(2)}, u32[]{:S(2)}) collective-permute-start(f32[2,64,256]{2,1,0:T(8,128)S(1)} %get-tuple-element.45), channel_id=1, source_target_pairs={{0,8},{1,17},{2,10},{3,19},{4,12},{5,21},{6,14},{7,23},{8,0},{9,25... | collective-permute-start | bytes 393224 | tf_op jit(solution)/shard_map/ppermute | solution.py:310
  31.6 2.2 %collective-permute-done.13 = f32[2,96,256]{2,1,0:T(8,128)S(1)} collective-permute-done((f32[2,96,256]{2,1,0:T(8,128)S(1)}, f32[2,96,256]{2,1,0:T(8,128)S(1)}, u32[]{:S(2)}, u32[]{:S(2)}) %collective-permute-start.13) | collective-permute-done | bytes 196640 | tf_op jit(solution)/shard_map/ppermute | solution.py:310
  33.8 1.6 %collective-permute-start.14 = (f32[2,96,256]{2,1,0:T(8,128)S(1)}, f32[2,96,256]{2,1,0:T(8,128)S(1)}, u32[]{:S(2)}, u32[]{:S(2)}) collective-permute-start(f32[2,96,256]{2,1,0:T(8,128)S(1)} %add.23.total), channel_id=1, source_target_pairs={{0,16},{1,9},{2,18},{3,11},{4,20},{5,13},{6,22},{7,15},{8,24},{9,1... | collective-permute-start | bytes 589832 | tf_op jit(solution)/shard_map/ppermute | solution.py:313
  36.0 1.6 %collective-permute-start.12 = (f32[2,96,256]{2,1,0:T(8,128)S(1)}, f32[2,96,256]{2,1,0:T(8,128)S(1)}, u32[]{:S(2)}, u32[]{:S(2)}) collective-permute-start(f32[2,96,256]{2,1,0:T(8,128)S(1)} %add.22.total), channel_id=1, source_target_pairs={{0,16},{1,9},{2,18},{3,11},{4,20},{5,13},{6,22},{7,15},{8,24},{9,1... | collective-permute-start | bytes 589832 | tf_op jit(solution)/shard_map/ppermute | solution.py:313
  37.5 1.2 %collective-permute-done.9 = f32[2,64,256]{2,1,0:T(8,128)S(1)} collective-permute-done((f32[2,64,256]{2,1,0:T(8,128)S(1)}, f32[2,64,256]{2,1,0:T(8,128)S(1)}, u32[]{:S(2)}, u32[]{:S(2)}) %collective-permute-start.9) | collective-permute-done | bytes 131104 | tf_op jit(solution)/shard_map/ppermute | solution.py:310
  38.8 1.6 %collective-permute-start.10 = (f32[2,64,256]{2,1,0:T(8,128)S(1)}, f32[2,64,256]{2,1,0:T(8,128)S(1)}, u32[]{:S(2)}, u32[]{:S(2)}) collective-permute-start(f32[2,64,256]{2,1,0:T(8,128)S(1)} %add.21.total), channel_id=1, source_target_pairs={{0,16},{1,9},{2,18},{3,11},{4,20},{5,13},{6,22},{7,15},{8,24},{9,1... | collective-permute-start | bytes 393224 | tf_op jit(solution)/shard_map/ppermute | solution.py:313
  40.3 1.0 %adjoint.1 = f32[2,256,256]{2,1,0:T(8,128)} custom-call(f32[5,8,128]{2,1,0:T(8,128)S(1)} %add.20.sums, f32[2,256,256]{2,1,0:T(8,128)S(1)} %get-tuple-element.25.far, f32[2,256,256]{2,1,0:T(8,128)S(1)} %get-tuple-element.26.near, f32[2,256,256]{2,1,0:T(8,128)S(1)} %get-tuple-element.31.image), custom_call_target="tpu_custom_call" | custom-call | tf_op jit(solution)/shard_map/adjoint/pallas_call | solution.py:393
  41.3 0.7 %close.3.rest_0_ = f32[2,256,256]{2,1,0:T(8,128)} custom-call(f32[2,96,256]{2,1,0:T(8,128)S(1)} %add.23.total, f32[2,96,256]{2,1,0:T(8,128)S(1)} %collective-permute-done.14.arrived), custom_call_target="tpu_custom_call" | custom-call | tf_op jit(solution)/shard_map/close/pallas_call | solution.py:405
  42.1 0.7 %close.4.rest_0_ = f32[2,256,256]{2,1,0:T(8,128)} custom-call(f32[2,96,256]{2,1,0:T(8,128)S(1)} %add.22.total, f32[2,96,256]{2,1,0:T(8,128)S(1)} %collective-permute-done.12.arrived, f32[2,256,256]{2,1,0:T(8,128)} %close.3.rest_0_), custom_call_target="tpu_custom_call", output_to_operand_aliasing={{}: (2, {})} | custom-call | tf_op jit(solution)/shard_map/close/pallas_call | solution.py:405
  42.8 1.0 %collective-permute-done.10.arrived = f32[2,64,256]{2,1,0:T(8,128)S(1)} collective-permute-done((f32[2,64,256]{2,1,0:T(8,128)S(1)}, f32[2,64,256]{2,1,0:T(8,128)S(1)}, u32[]{:S(2)}, u32[]{:S(2)}) %collective-permute-start.10) | collective-permute-done | bytes 131104 | tf_op jit(solution)/shard_map/ppermute | solution.py:313
  43.8 0.7 %close.5 = f32[2,256,256]{2,1,0:T(8,128)} custom-call(f32[2,64,256]{2,1,0:T(8,128)S(1)} %add.21.total, f32[2,64,256]{2,1,0:T(8,128)S(1)} %collective-permute-done.10.arrived, f32[2,256,256]{2,1,0:T(8,128)} %close.4.rest_0_), custom_call_target="tpu_custom_call", output_to_operand_aliasing={{}: (2, {})} | custom-call | tf_op jit(solution)/shard_map/close/pallas_call | solution.py:405
  (26 shorter events, 2.8 us)
Async XLA Ops:
  2.7 7.3 %collective-permute-start.2 = (f32[2,256,256]{2,1,0:T(8,128)S(1)}, f32[2,256,256]{2,1,0:T(8,128)S(1)}, u32[]{:S(2)}, u32[]{:S(2)}) collective-permute-start(f32[2,256,256]{2,1,0:T(8,128)S(1)} %get-tuple-element.26.near), channel_id=1, source_target_pairs={{0,1},{1,0},{2,3},{3,2},{4,5},{5,4},{6,7},{7,6},{8,9},{9,8},{10,11... | collective-permute-start | bytes 1572872 | tf_op jit(solution)/shard_map/ppermute | solution.py:342
  3.2 6.8 %collective-permute-start = (f32[2,256,256]{2,1,0:T(8,128)S(1)}, f32[2,256,256]{2,1,0:T(8,128)S(1)}, u32[]{:S(2)}, u32[]{:S(2)}) collective-permute-start(f32[2,256,256]{2,1,0:T(8,128)S(1)} %get-tuple-element.25.far), channel_id=1, source_target_pairs={{1,2},{2,1},{3,4},{4,3},{5,6},{6,5},{9,10},{10,9},{11,12},{12,11},... | collective-permute-start | bytes 1572872 | tf_op jit(solution)/shard_map/ppermute | solution.py:341
  4.6 5.4 %collective-permute-start.3 = (f32[1,256,256]{2,1,0:T(8,128)S(1)}, f32[1,256,256]{2,1,0:T(8,128)S(1)}, u32[]{:S(2)}, u32[]{:S(2)}) collective-permute-start(f32[1,256,256]{2,1,0:T(8,128)S(1)} %get-tuple-element.30.near_part), channel_id=1, source_target_pairs={{0,1},{1,0},{2,3},{3,2},{4,5},{5,4},{6,7},{7,6},{8,9},{9,8},{10,11... | collective-permute-start | bytes 786440 | tf_op jit(solution)/shard_map/ppermute | solution.py:353
  8.6 2.7 %collective-permute-start.1 = (f32[1,128,256]{2,1,0:T(8,128)S(1)}, f32[1,128,256]{2,1,0:T(8,128)S(1)}, u32[]{:S(2)}, u32[]{:S(2)}) collective-permute-start(f32[1,128,256]{2,1,0:T(8,128)S(1)} %get-tuple-element.28), channel_id=1, source_target_pairs={{1,2},{2,1},{3,4},{4,3},{5,6},{6,5},{9,10},{10,9},{11,12},{12,11},... | collective-permute-start | bytes 393224 | tf_op jit(solution)/shard_map/ppermute | solution.py:352
  9.3 14.9 %collective-permute-start.6 = (f32[1,384,256]{2,1,0:T(8,128)S(1)}, f32[1,384,256]{2,1,0:T(8,128)S(1)}, u32[]{:S(2)}, u32[]{:S(2)}) collective-permute-start(f32[1,384,256]{2,1,0:T(8,128)S(1)} %get-tuple-element.35), channel_id=1, source_target_pairs={{1,2},{2,1},{3,4},{4,3},{5,6},{6,5},{9,10},{10,9},{11,12},{12,11},... | collective-permute-start | bytes 1179656 | tf_op jit(solution)/shard_map/ppermute | solution.py:354
  11.3 12.9 %copy-start = (f32[1,2,256,256]{3,2,1,0:T(8,128)S(1)}, f32[1,2,256,256]{3,2,1,0:T(8,128)}, u32[]{:S(2)}) copy-start(f32[1,2,256,256]{3,2,1,0:T(8,128)} %param.10) | copy-start | bytes 1572868
  11.3 12.9 %copy-start.1 = (s32[2,256,256]{2,1,0:T(8,128)S(1)}, s32[2,256,256]{2,1,0:T(8,128)}, u32[]{:S(2)}) copy-start(s32[2,256,256]{2,1,0:T(8,128)} %mask.1) | copy-start | bytes 1572868
  11.5 10.4 %collective-permute-start.4 = (f32[5,8,128]{2,1,0:T(8,128)S(1)}, f32[5,8,128]{2,1,0:T(8,128)S(1)}, u32[]{:S(2)}, u32[]{:S(2)}) collective-permute-start(f32[5,8,128]{2,1,0:T(8,128)S(1)} %face.1), channel_id=1, source_target_pairs={{0,2},{1,3},{2,0},{3,1},{4,6},{5,7},{6,4},{7,5},{8,10},{9,11},{10,... | collective-permute-start | bytes 61448 | tf_op jit(solution)/shard_map/ppermute | solution.py:371
  21.9 2.2 %collective-permute-start.7 = (f32[1,256,256]{2,1,0:T(8,128)S(1)}, f32[1,256,256]{2,1,0:T(8,128)S(1)}, u32[]{:S(2)}, u32[]{:S(2)}) collective-permute-start(f32[1,256,256]{2,1,0:T(8,128)S(1)} %get-tuple-element.37), channel_id=1, source_target_pairs={{0,1},{1,0},{2,3},{3,2},{4,5},{5,4},{6,7},{7,6},{8,9},{9,8},{10,11... | collective-permute-start | bytes 786440 | tf_op jit(solution)/shard_map/ppermute | solution.py:373
  21.9 4.7 %collective-permute-start.5 = (f32[5,8,128]{2,1,0:T(8,128)S(1)}, f32[5,8,128]{2,1,0:T(8,128)S(1)}, u32[]{:S(2)}, u32[]{:S(2)}) collective-permute-start(f32[5,8,128]{2,1,0:T(8,128)S(1)} %add.18), channel_id=1, source_target_pairs={{0,4},{1,5},{2,6},{3,7},{4,0},{5,1},{6,2},{7,3},{8,12},{9,13},{10,... | collective-permute-start | bytes 61448 | tf_op jit(solution)/shard_map/ppermute | solution.py:292
  26.7 1.2 %collective-permute-start.8 = (f32[5,8,128]{2,1,0:T(8,128)S(1)}, f32[5,8,128]{2,1,0:T(8,128)S(1)}, u32[]{:S(2)}, u32[]{:S(2)}) collective-permute-start(f32[5,8,128]{2,1,0:T(8,128)S(1)} %add.19), channel_id=1, source_target_pairs={{0,1},{1,0},{2,3},{3,2},{4,5},{5,4},{6,7},{7,6},{8,9},{9,8},{10,11... | collective-permute-start | bytes 61448 | tf_op jit(solution)/shard_map/ppermute | solution.py:292
  28.1 5.7 %collective-permute-start.13 = (f32[2,96,256]{2,1,0:T(8,128)S(1)}, f32[2,96,256]{2,1,0:T(8,128)S(1)}, u32[]{:S(2)}, u32[]{:S(2)}) collective-permute-start(f32[2,96,256]{2,1,0:T(8,128)S(1)} %get-tuple-element.47), channel_id=1, source_target_pairs={{0,8},{1,17},{2,10},{3,19},{4,12},{5,21},{6,14},{7,23},{8,0},{9,25... | collective-permute-start | bytes 589832 | tf_op jit(solution)/shard_map/ppermute | solution.py:310
  29.6 6.3 %collective-permute-start.11 = (f32[2,96,256]{2,1,0:T(8,128)S(1)}, f32[2,96,256]{2,1,0:T(8,128)S(1)}, u32[]{:S(2)}, u32[]{:S(2)}) collective-permute-start(f32[2,96,256]{2,1,0:T(8,128)S(1)} %get-tuple-element.46), channel_id=1, source_target_pairs={{0,8},{1,17},{2,10},{3,19},{4,12},{5,21},{6,14},{7,23},{8,0},{9,25... | collective-permute-start | bytes 589832 | tf_op jit(solution)/shard_map/ppermute | solution.py:310
  30.1 8.6 %collective-permute-start.9 = (f32[2,64,256]{2,1,0:T(8,128)S(1)}, f32[2,64,256]{2,1,0:T(8,128)S(1)}, u32[]{:S(2)}, u32[]{:S(2)}) collective-permute-start(f32[2,64,256]{2,1,0:T(8,128)S(1)} %get-tuple-element.45), channel_id=1, source_target_pairs={{0,8},{1,17},{2,10},{3,19},{4,12},{5,21},{6,14},{7,23},{8,0},{9,25... | collective-permute-start | bytes 393224 | tf_op jit(solution)/shard_map/ppermute | solution.py:310
  33.8 7.5 %collective-permute-start.14 = (f32[2,96,256]{2,1,0:T(8,128)S(1)}, f32[2,96,256]{2,1,0:T(8,128)S(1)}, u32[]{:S(2)}, u32[]{:S(2)}) collective-permute-start(f32[2,96,256]{2,1,0:T(8,128)S(1)} %add.23.total), channel_id=1, source_target_pairs={{0,16},{1,9},{2,18},{3,11},{4,20},{5,13},{6,22},{7,15},{8,24},{9,1... | collective-permute-start | bytes 589832 | tf_op jit(solution)/shard_map/ppermute | solution.py:313
  36.0 6.1 %collective-permute-start.12 = (f32[2,96,256]{2,1,0:T(8,128)S(1)}, f32[2,96,256]{2,1,0:T(8,128)S(1)}, u32[]{:S(2)}, u32[]{:S(2)}) collective-permute-start(f32[2,96,256]{2,1,0:T(8,128)S(1)} %add.22.total), channel_id=1, source_target_pairs={{0,16},{1,9},{2,18},{3,11},{4,20},{5,13},{6,22},{7,15},{8,24},{9,1... | collective-permute-start | bytes 589832 | tf_op jit(solution)/shard_map/ppermute | solution.py:313
  38.8 5.0 %collective-permute-start.10 = (f32[2,64,256]{2,1,0:T(8,128)S(1)}, f32[2,64,256]{2,1,0:T(8,128)S(1)}, u32[]{:S(2)}, u32[]{:S(2)}) collective-permute-start(f32[2,64,256]{2,1,0:T(8,128)S(1)} %add.21.total), channel_id=1, source_target_pairs={{0,16},{1,9},{2,18},{3,11},{4,20},{5,13},{6,22},{7,15},{8,24},{9,1... | collective-permute-start | bytes 393224 | tf_op jit(solution)/shard_map/ppermute | solution.py:313
